TPU v7x, 256 devices: a whole 4x4x8 slice. The times are simulated.
256 devices in a mesh: sub: 4 (over x), tile: 64 (over y, z, core).
Axes of the slice: x: 4, y: 4, z: 8, core: 2. Of those that a mesh axis runs over, the one named last changes fastest.
Arguments:
- displacement: float32 [4, 3, 256, 32, 128], P('sub', None, 'tile'), may hold values from -3 to 3
- velocity: float32 [4, 3, 256, 32, 128], P('sub', None, 'tile'), may hold values from -6 to 6
- external_load: float32 [4, 3, 256, 32, 128], P('sub', None, 'tile'), may hold values from -6 to 6
- node_mass: float32 [4, 256, 32, 128], P('sub', 'tile'), may hold values from 1 to 4
- modulus: float32 [4, 256, 32, 128], P('sub', 'tile'), may hold values from 0.3 to 1.5
- stiffness: float32 [24, 24], replicated
- substeps: int32 [4], P('sub'), may hold values from 1 to 4, as said below
- interface_nodes: int32 [4, 8192], P('sub', 'tile'), may hold values from 0 to 16383, as said below
- factor_inverse: float32 [2, 24576, 384], P(None, 'tile')
- factor_lower: float32 [2, 24576, 384], P(None, 'tile')
Outputs:
- displacement_out: float32 [4, 3, 256, 32, 128], P('sub', None, 'tile')
- velocity_out: float32 [4, 3, 256, 32, 128], P('sub', None, 'tile')
Inputs may be any that keep to these rules, and one draw needn't show every extreme that they name: Each substructure takes 1, 2 or 4 substeps; some substructure takes 4 and some takes 1. `interface_nodes`: within each tile's 128 slots of a substructure the nodes are distinct.
All inputs are finite; a program needn't handle non-finite values.
Results may differ from a plain program's by a relative error of at most 0.00011.
Values sent between devices are 32-bit elements; how exact they have to be, the bound alone decides.
No kernel may reach another device: no remote copies, remote signals or barrier semaphores. Data moves between devices by JAX's collectives and lax.ppermute only.
A program may use at most 192 MiB of HBM per device.

v0:
```python
import jax
import jax.numpy as jnp
from jax import lax
from jax.experimental import pallas as pl
from jax.experimental.pallas import tpu as pltpu
from jax.sharding import PartitionSpec as P

IFC = 128
IB = 384
HALF = IB // 2
GRANT = 12 << 20
CX, CY, CZ = 4, 32, 128
DEEP = 3 * CX
FIELDS = 11
CORE, PAIR, SIDE, LAST, STEPS = 0, 6, 7, 8, 9
GROUPS = CY // 8
MASKS = (1, 2, 4, 12, 16, 48)

coarse_step = 0.1
f32 = jnp.float32
bf16 = jnp.bfloat16
VM = pl.BlockSpec(memory_space=pltpu.VMEM)
SM = pl.BlockSpec(memory_space=pltpu.SMEM)
MAT = jax.ShapeDtypeStruct((IB, IB), f32)
HALFMAT = jax.ShapeDtypeStruct((HALF, IB), f32)
ROW = jax.ShapeDtypeStruct((1, IB), f32)


def swap(value, mask):
    return lax.ppermute(value, "tile", [(i, i ^ mask) for i in range(lax.axis_size("tile"))])


def cost(flops, nbytes):
    return pl.CostEstimate(flops=flops, bytes_accessed=nbytes, transcendentals=0)


def local_call(kernel, flags, operands, outs, flops=0):
    nbytes = sum(o.size * 4 for o in operands)
    return pl.pallas_call(
        kernel,
        out_shape=outs,
        in_specs=[SM] + [VM] * len(operands),
        out_specs=jax.tree.map(lambda _: VM, outs),
        compiler_params=pltpu.CompilerParams(vmem_limit_bytes=GRANT),
        cost_estimate=cost(flops, nbytes),
    )(flags, *operands)


def pair_call(kernel, flags, blocks, operands, outs, flops=0):
    count = len(operands)

    def whole(shape):
        return pl.BlockSpec(shape, lambda i, flags: (0,) * len(shape))

    many = isinstance(outs, (tuple, list))
    return pl.pallas_call(
        kernel,
        out_shape=outs,
        grid_spec=pltpu.PrefetchScalarGridSpec(
            num_scalar_prefetch=1,
            grid=(1,),
            in_specs=[pl.BlockSpec((1, IB, IB), lambda i, flags: (flags[PAIR], 0, 0)) for _ in blocks]
            + [whole(o.shape) for o in operands],
            out_specs=[whole(o.shape) for o in outs] if many else whole(outs.shape),
        ),
        compiler_params=pltpu.CompilerParams(vmem_limit_bytes=GRANT),
        cost_estimate=cost(flops, 4 * IB * IB * len(blocks) + sum(o.size * 4 for o in operands)),
    )(flags, *blocks, *operands)


def halves(value):
    high = value.astype(bf16)
    return high, (value - high.astype(f32)).astype(bf16)


def product(a, b):
    a_high, a_low = halves(a)
    b_high, b_low = halves(b)
    return (
        jnp.dot(a_low, b_high, preferred_element_type=f32)
        + jnp.dot(a_high, b_low, preferred_element_type=f32)
        + jnp.dot(a_high, b_high, preferred_element_type=f32)
    )


def eye_mask(size):
    return lax.broadcasted_iota(jnp.int32, (size, size), 0) == lax.broadcasted_iota(
        jnp.int32, (size, size), 1
    )


def column_to_row(column):
    eye = eye_mask(IFC)
    return jnp.concatenate(
        [
            jnp.sum(jnp.where(eye, column[k : k + IFC], 0.0), axis=0, keepdims=True)
            for k in range(0, IB, IFC)
        ],
        axis=1,
    )


def row_to_column(row):
    eye = eye_mask(IFC)
    return jnp.concatenate(
        [
            jnp.sum(jnp.where(eye, row[:, k : k + IFC], 0.0), axis=1, keepdims=True)
            for k in range(0, IB, IFC)
        ],
        axis=0,
    )


def apply(matrix, row):
    return column_to_row(jnp.sum(matrix * row, axis=1, keepdims=True))


def apply_transposed(matrix, row):
    return jnp.sum(matrix * row_to_column(row), axis=0, keepdims=True)


def triple(value):
    high = value.astype(bf16)
    rest = value - high.astype(f32)
    middle = rest.astype(bf16)
    return high, middle, (rest - middle.astype(f32)).astype(bf16)


def slot_masks(nodes):
    index = lax.broadcasted_iota(jnp.int32, (IFC, IFC), 0)
    return index == nodes // CZ, index == nodes % CZ


def wide(value):
    return jnp.concatenate([value[8 * g : 8 * g + 8] for g in range(GROUPS)], axis=1)


def tall(value):
    return jnp.concatenate([value[:, CZ * g : CZ * g + CZ] for g in range(GROUPS)], axis=0)


def spread(values, parity):
    row = lax.broadcasted_iota(jnp.int32, (192, 24), 0) // 8
    rows = (row == lax.broadcasted_iota(jnp.int32, (192, 24), 1)).astype(f32).astype(bf16)
    block = lax.broadcasted_iota(jnp.int32, (24, 192), 1) // 8
    side = (block // 12 + parity) % 2
    dof = 8 * (block % 12 // 4) + 4 * side + block % 4
    columns = (dof == lax.broadcasted_iota(jnp.int32, (24, 192), 0)).astype(f32).astype(bf16)
    tall_values = jnp.dot(rows, values, preferred_element_type=f32).astype(bf16)
    full = jnp.dot(tall_values, columns, preferred_element_type=f32)
    same = (
        lax.broadcasted_iota(jnp.int32, (192, 192), 0) % 8
        == lax.broadcasted_iota(jnp.int32, (192, 192), 1) % 8
    )
    return jnp.where(same, full, 0.0).astype(bf16)


def substep_kernel(
    flags, step, own, outer, inner, stiffness, nodes,
    displacement_out, velocity_out, picked,
    disp, vel, load, inverse_mass, factor, stiff, features, upper,
):
    first = flags[CORE] == 0

    def place(source, low):
        layers = pl.ds(low, CX)
        for i in range(3):
            disp[i, layers] = source[pl.ds(CX * i, CX)]
            vel[i, layers] = source[pl.ds(CX * (3 + i), CX)]
            load[i, layers] = source[pl.ds(CX * (6 + i), CX)]
        mass = source[pl.ds(CX * 9, CX)]
        present = mass > 0.0
        inverse_mass[layers] = jnp.where(present, 1.0 / jnp.where(present, mass, 1.0), 0.0)
        for x in range(CX):
            value = source[CX * 10 + x]
            row = lax.broadcasted_iota(jnp.int32, (CY, CZ), 0)
            factor[low + x] = wide(jnp.where(row < CY - 1, value, 0.0))

    place(own, CX)

    @pl.when(first)
    def _():
        place(outer, 0)
        place(inner, 2 * CX)

    @pl.when(jnp.logical_not(first))
    def _():
        place(inner, 0)
        place(outer, 2 * CX)

    @pl.when(flags[LAST] == 1)
    def _():
        factor[2 * CX - 1] = jnp.zeros((8, GROUPS * CZ), f32)

    for parity in range(2):
        high, low = [spread(s, parity) for s in halves(stiffness[...])]
        stiff[parity] = jnp.concatenate([high, high, low], axis=1)
    length = step[0]

    def put_features(layer, parity):
        columns = []
        for i in range(3):
            base = disp[i, layer]
            turned = pltpu.roll(base, CZ - 1, 1)
            columns += [base, turned, pltpu.roll(base, CY - 1, 0), pltpu.roll(turned, CY - 1, 0)]
        start = pl.multiple_of(parity * 96, 16)
        for g in range(GROUPS):
            lanes = pl.ds(CZ * g, CZ)
            block = jnp.concatenate([c[8 * g : 8 * g + 8] for c in columns], axis=0)
            high, low = halves(block)
            features[pl.ds(start, 96), lanes] = high
            features[pl.ds(start + 192, 96), lanes] = low
            features[pl.ds(start + 384, 96), lanes] = high

    def element_layer(layer, finish):
        parity = layer % 2
        put_features(layer + 1, 1 - parity)
        force = jnp.dot(stiff[parity], features[...], preferred_element_type=f32)
        scale = factor[layer]
        weight = inverse_mass[layer]

        def corner(i, a, b, c):
            start = 8 * (8 * i + 4 * a + 2 * b + c)
            return force[start : start + 8] * scale

        for i in range(3):
            if finish:
                sums = [corner(i, 0, r // 2, r % 2) + upper[4 * i + r] for r in range(4)]
                s00, s01, s10, s11 = [tall(s) for s in sums]
                base = s00 + pltpu.roll(s10, 1, 0)
                turned = s01 + pltpu.roll(s11, 1, 0)
                internal = base + pltpu.roll(turned, 1, 1)
                speed = vel[i, layer] + length * ((load[i, layer] - internal) * weight)
                vel[i, layer] = speed
                disp[i, layer] = disp[i, layer] + length * speed
            for r in range(4):
                upper[4 * i + r] = corner(i, 1, r // 2, r % 2)

    def one_substep(k, carry):
        put_features(k, k % 2)
        element_layer(k, False)

        def inner_layer(layer, carry):
            element_layer(layer, True)
            return carry

        return lax.fori_loop(k + 1, DEEP - 1 - k, inner_layer, carry)

    lax.fori_loop(0, flags[STEPS], one_substep, 0)
    displacement_out[...] = disp[:, CX : 2 * CX]
    final = vel[:, CX : 2 * CX]
    velocity_out[...] = final
    in_row, in_column = slot_masks(nodes[...])
    chosen = in_column.astype(f32).astype(bf16)
    parts = []
    for i in range(3):
        pieces = triple(final[i].reshape(CX * CY, CZ))
        values = sum(jnp.dot(p, chosen, preferred_element_type=f32) for p in reversed(pieces))
        parts.append(jnp.sum(jnp.where(in_row, values, 0.0), axis=0, keepdims=True))
    picked[...] = jnp.concatenate(parts, axis=1)


def substeps_call(flags, step, own, outer, inner, stiffness, nodes):
    grid_shape = (3, CX, CY, CZ)
    return pl.pallas_call(
        substep_kernel,
        out_shape=(
            jax.ShapeDtypeStruct(grid_shape, f32),
            jax.ShapeDtypeStruct(grid_shape, f32),
            ROW,
        ),
        in_specs=[SM, SM] + [VM] * 5,
        out_specs=(VM, VM, VM),
        scratch_shapes=[
            pltpu.VMEM((3, DEEP, CY, CZ), f32),
            pltpu.VMEM((3, DEEP, CY, CZ), f32),
            pltpu.VMEM((3, DEEP, CY, CZ), f32),
            pltpu.VMEM((DEEP, CY, CZ), f32),
            pltpu.VMEM((DEEP, 8, GROUPS * CZ), f32),
            pltpu.VMEM((2, 192, 576), bf16),
            pltpu.VMEM((576, GROUPS * CZ), bf16),
            pltpu.VMEM((12, 8, GROUPS * CZ), f32),
        ],
        compiler_params=pltpu.CompilerParams(vmem_limit_bytes=20 << 20),
        cost_estimate=cost(32 * 2 * 192 * 576 * 512, 3 * 720896),
    )(flags, step, own, outer, inner, stiffness, nodes)

def transition_kernel(flags, inverse, lower, transition):
    transition[...] = -product(inverse[0], lower[0])


def store_half(flags, half, value_ref):
    @pl.when(flags[CORE] == 0)
    def _():
        half[...] = value_ref[:HALF]

    @pl.when(flags[CORE] == 1)
    def _():
        half[...] = value_ref[HALF:]


def first_merge_kernel(flags, own, other, high_ref, low_ref, merged, half, prefix, suffix):
    is_high = flags[0] == 1
    high = jnp.where(is_high, own[...], other[...])
    low = jnp.where(is_high, other[...], own[...])
    high_ref[...] = high
    low_ref[...] = low
    merged[...] = product(high, low)
    store_half(flags, half, merged)
    identity = eye_mask(IB).astype(f32)
    prefix[...] = jnp.where(is_high, other[...], identity)
    suffix[...] = jnp.where(is_high, identity, other[...])


def merge_kernel(level, last, flags, own, near, far, prefix, suffix, *outs):
    is_high = flags[level] == 1
    first = flags[CORE] == 0
    other = jnp.concatenate(
        [jnp.where(first, near[...], far[...]), jnp.where(first, far[...], near[...])], axis=0
    )
    high = jnp.where(is_high, own[...], other)
    low = jnp.where(is_high, other, own[...])
    high_ref, low_ref, new_prefix, new_suffix = outs[:4]
    high_ref[...] = high
    low_ref[...] = low
    if not last:
        merged, half = outs[4:]
        merged[...] = product(high, low)
        store_half(flags, half, merged)
    longer = product(
        jnp.where(is_high, prefix[...], high), jnp.where(is_high, low, suffix[...])
    )
    new_prefix[...] = jnp.where(is_high, longer, prefix[...])
    new_suffix[...] = jnp.where(is_high, suffix[...], longer)


def start_kernel(flags, inverse, picked, partner, offset):
    sign = (1 - 2 * flags[SIDE]).astype(f32)
    offset[...] = apply(inverse[0], sign * (picked[...] - partner[...]))


def forward_kernel(level, flags, own, other, high_matrix, total):
    is_high = flags[level] == 1
    high = jnp.where(is_high, own[...], other[...])
    low = jnp.where(is_high, other[...], own[...])
    total[...] = high + apply(high_matrix[...], low)


def backward_kernel(level, flags, own, other, low_matrix, total):
    is_high = flags[level] == 1
    high = jnp.where(is_high, own[...], other[...])
    low = jnp.where(is_high, other[...], own[...])
    total[...] = low + apply_transposed(low_matrix[...], high)


def gathered_kernel(wanted, operation, flags, *refs):
    others = refs[:5]
    matrices = refs[5:9]
    result = refs[9]
    result[...] = jnp.where(flags[0] == wanted, others[0][...], 0.0)
    for level in range(1, 5):

        @pl.when(flags[level] == wanted)
        def _():
            result[...] = result[...] + operation(matrices[level - 1][...], others[level][...])


def turn_kernel(flags, entering, other, prefix, transition, offset, solved, returning):
    before = entering[...] + jnp.where(flags[5] == 1, 1.0, 0.0) * apply(prefix[...], other[...])
    current = offset[...] + apply(transition[...], before)
    solved[...] = current
    returning[...] = -apply_transposed(transition[...], current)


def finish_kernel(
    flags, inverse, entering, other, suffix, solved, velocity, node_mass, nodes, velocity_out
):
    after = entering[...] + jnp.where(flags[5] == 0, 1.0, 0.0) * apply_transposed(
        suffix[...], other[...]
    )
    sign = (1 - 2 * flags[SIDE]).astype(f32)
    multiplier = sign * apply_transposed(inverse[0], solved[...] - after)
    in_row, in_column = slot_masks(nodes[...])
    chosen = in_column.astype(f32).astype(bf16)
    weight = 1.0 / node_mass[...]
    for i in range(3):
        held = jnp.where(in_row, multiplier[:, IFC * i : IFC * i + IFC], 0.0)
        change = sum(
            lax.dot_general(p, chosen, (((1,), (1,)), ((), ())), preferred_element_type=f32)
            for p in reversed(triple(held))
        )
        velocity_out[i] = velocity[i] - change.reshape(CX, CY, CZ) * weight


def bound(level, kernel, *fixed):
    def run(*refs):
        kernel(level, *fixed, *refs)

    return run


def first_products(flags, factor_inverse, factor_lower):
    cube = 6 * IB**3
    transition = pair_call(
        transition_kernel, flags, [factor_inverse, factor_lower], [], MAT, cube
    )
    other = swap(transition, MASKS[0])
    high, low, merged, half, prefix, suffix = local_call(
        first_merge_kernel,
        flags,
        [transition, other],
        (MAT, MAT, MAT, HALFMAT, MAT, MAT),
        cube,
    )
    return transition, (merged, half), [(high, low, prefix, suffix)]


def merge_level(flags, level, block, levels, gate=None):
    merged, half = block
    near = swap(half, MASKS[level])
    far = swap(near, 1)
    if gate is not None:
        far, _ = lax.optimization_barrier((far, gate))
    last = level == 4
    made = local_call(
        bound(level, merge_kernel, last),
        flags,
        [merged, near, far, *levels[-1][2:]],
        (MAT,) * 4 if last else (MAT,) * 5 + (HALFMAT,),
        12 * IB**3,
    )
    return made[4:], levels + [tuple(made[:4])]


def coupled_velocity(
    flags, picked, factor_inverse, transition, block, levels, velocity, node_mass, nodes
):
    square = 2 * IB * IB
    count = lax.axis_size("sub")
    partner = lax.ppermute(picked, "sub", [(i, i ^ 1) for i in range(count)])
    offset = pair_call(start_kernel, flags, [factor_inverse], [picked, partner], ROW, square)
    total, others = offset, []
    for level in range(5):
        others.append(swap(total, MASKS[level]))
        if level >= 2:
            gate = picked if level == 2 else total
            block, levels = merge_level(flags, level, block, levels, gate)
        total = local_call(
            bound(level, forward_kernel), flags, [total, others[-1], levels[level][0]], ROW, square
        )
    _, lows, prefixes, suffixes = zip(*levels)
    last_other = swap(total, MASKS[5])
    entering = local_call(
        bound(1, gathered_kernel, apply), flags, others + list(prefixes[:4]), ROW, 4 * square
    )
    solved, returning = local_call(
        turn_kernel,
        flags,
        [entering, last_other, prefixes[4], transition, offset],
        (ROW, ROW),
        3 * square,
    )
    total, others = returning, []
    for level in range(5):
        others.append(swap(total, MASKS[level]))
        total = local_call(
            bound(level, backward_kernel), flags, [total, others[-1], lows[level]], ROW, square
        )
    last_other = swap(total, MASKS[5])
    entering = local_call(
        bound(0, gathered_kernel, apply_transposed), flags, others + list(suffixes[:4]), ROW, 4 * square
    )
    return pair_call(
        finish_kernel,
        flags,
        [factor_inverse],
        [entering, last_other, suffixes[4], solved, velocity, node_mass, nodes],
        jax.ShapeDtypeStruct(velocity.shape, f32),
        2 * square,
    )


def outer_swap(value):
    count = lax.axis_size("tile")
    route = []
    for low in range(1, count - 1, 2):
        route += [(low, low + 1), (low + 1, low)]
    return lax.ppermute(value, "tile", route)


def body(
    displacement,
    velocity,
    external_load,
    node_mass,
    modulus,
    stiffness,
    substeps,
    interface_nodes,
    factor_inverse,
    factor_lower,
):
    sub, tile = lax.axis_index("sub"), lax.axis_index("tile")
    last = tile == lax.axis_size("tile") - 1
    flags = jnp.stack(
        [(tile >> k) & 1 for k in range(6)] + [sub // 2, sub % 2, last, substeps[0]]
    ).astype(jnp.int32)
    step = coarse_step / substeps.astype(f32)
    own = jnp.concatenate(
        [
            displacement.reshape(-1, CY, CZ),
            velocity.reshape(-1, CY, CZ),
            external_load.reshape(-1, CY, CZ),
            node_mass[0],
            modulus[0],
        ],
        axis=0,
    )
    own, factor_inverse, factor_lower = lax.optimization_barrier((own, factor_inverse, factor_lower))
    outer = outer_swap(own)
    inner = swap(own, 1)
    transition, block, levels = first_products(flags, factor_inverse, factor_lower)
    block, levels = merge_level(flags, 1, block, levels)
    outer, inner, block = lax.optimization_barrier((outer, inner, block))
    final_displacement, final_velocity, picked = substeps_call(
        flags, step, own, outer, inner, stiffness, interface_nodes
    )
    coupled = coupled_velocity(
        flags,
        picked,
        factor_inverse,
        transition,
        block,
        levels,
        final_velocity,
        node_mass[0],
        interface_nodes,
    )
    return final_displacement[None], coupled[None]


def solution(mesh):
    in_specs = (
        P("sub", None, "tile", None, None),
        P("sub", None, "tile", None, None),
        P("sub", None, "tile", None, None),
        P("sub", "tile", None, None),
        P("sub", "tile", None, None),
        P(),
        P("sub"),
        P("sub", "tile"),
        P(None, "tile", None),
        P(None, "tile", None),
    )
    out_specs = (P("sub", None, "tile", None, None), P("sub", None, "tile", None, None))
    return jax.shard_map(body, mesh=mesh, in_specs=in_specs, out_specs=out_specs, check_vma=False)
```

profile of v0, /device:TPU:2, one launch (start us, length us, event | category | flops | bytes accessed | tf_op | source)
XLA Modules:
  0.0 157.5 jit_solution(16370897593008481144)
XLA Ops:
  10.5 2.4 %collective-permute-start.3 = (f32[192,384]{1,0:T(8,128)S(1)}, f32[192,384]{1,0:T(8,128)S(1)}, u32[]{:S(2)}, u32[]{:S(2)}) collective-permute-start(f32[192,384]{1,0:T(8,128)S(1)} %get-tuple-element.49), channel_id=1, source_target_pairs={{0,2},{1,3},{2,0},{3,1},{4,6},{5,7},{6,4},{7,5},{8,10},{9,11},{10,... | collective-permute-start | bytes 884744 | tf_op jit(solution)/shard_map/ppermute | solution.py:30
  12.9 14.1 %collective-permute-done.3.refs_2_ = f32[192,384]{1,0:T(8,128)S(1)} collective-permute-done((f32[192,384]{1,0:T(8,128)S(1)}, f32[192,384]{1,0:T(8,128)S(1)}, u32[]{:S(2)}, u32[]{:S(2)}) %collective-permute-start.3) | collective-permute-done | bytes 294944 | tf_op jit(solution)/shard_map/ppermute | solution.py:30
  28.6 2.4 %shard_map.115 = (f32[384,384]{1,0:T(8,128)S(1)}, f32[384,384]{1,0:T(8,128)S(1)}, f32[384,384]{1,0:T(8,128)S(1)}, f32[384,384]{1,0:T(8,128)S(1)}, f32[384,384]{1,0:T(8,128)S(1)}, /*index=5*/f32[192,384]{1,0:T(8,128)S(1)}) custom-call(s32[10]{0:T(128)S(1)} %stack.43.flags.refs_0_, f32[384,384]{1,0:T(8,128)S(1)} %get-tuple-element.48.refs_1_, ...), custom_call_target="tpu_custom_call" | custom-call | flops 679477248 | bytes 2359296 | tf_op jit(solution)/shard_map/pallas_call | solution.py:39
  31.0 3.3 %collective-permute-start.9 = (f32[192,384]{1,0:T(8,128)S(1)}, f32[192,384]{1,0:T(8,128)S(1)}, u32[]{:S(2)}, u32[]{:S(2)}) collective-permute-start(f32[192,384]{1,0:T(8,128)S(1)} %get-tuple-element.61), channel_id=1, source_target_pairs={{0,4},{1,5},{2,6},{3,7},{4,0},{5,1},{6,2},{7,3},{8,12},{9,13},{10,... | collective-permute-start | bytes 884744 | tf_op jit(solution)/shard_map/ppermute | solution.py:30
  34.4 13.6 %collective-permute-done.9.refs_2_ = f32[192,384]{1,0:T(8,128)S(1)} collective-permute-done((f32[192,384]{1,0:T(8,128)S(1)}, f32[192,384]{1,0:T(8,128)S(1)}, u32[]{:S(2)}, u32[]{:S(2)}) %collective-permute-start.9) | collective-permute-done | bytes 294944 | tf_op jit(solution)/shard_map/ppermute | solution.py:30
  48.0 7.8 %shard_map.116 = (f32[3,4,32,128]{3,2,1,0:T(8,128)}, f32[3,4,32,128]{3,2,1,0:T(8,128)S(1)}, f32[1,384]{1,0:T(1,128)S(1)}) custom-call(s32[10]{0:T(128)S(1)} %stack.43.flags.refs_0_, f32[1]{0:T(128)S(6)} %div.14.step, f32[44,32,128]{2,1,0:T(8,128)S(1)} %bitcast_dynamic-update-slice_fusion.own, f32[44,32,128]{2,1,0:T(8,128)S(1)} %collective-permute-done.outer, ...), custom_call_target="tpu_custom_call" | custom-call | flops 3623878656 | bytes 2162688 | tf_op jit(solution)/shard_map/pallas_call | solution.py:265
  55.8 2.4 %shard_map.120 = (f32[384,384]{1,0:T(8,128)S(1)}, f32[384,384]{1,0:T(8,128)S(1)}, f32[384,384]{1,0:T(8,128)S(1)}, f32[384,384]{1,0:T(8,128)S(1)}, f32[384,384]{1,0:T(8,128)S(1)}, /*index=5*/f32[192,384]{1,0:T(8,128)S(1)}) custom-call(s32[10]{0:T(128)S(1)} %stack.43.flags.refs_0_, f32[384,384]{1,0:T(8,128)S(1)} %get-tuple-element.60.refs_1_, ...), custom_call_target="tpu_custom_call" | custom-call | flops 679477248 | bytes 2359296 | tf_op jit(solution)/shard_map/pallas_call | solution.py:39
  58.2 3.5 %collective-permute-start.12 = (f32[192,384]{1,0:T(8,128)S(1)}, f32[192,384]{1,0:T(8,128)S(1)}, u32[]{:S(2)}, u32[]{:S(2)}) collective-permute-start(f32[192,384]{1,0:T(8,128)S(1)} %get-tuple-element.67), channel_id=1, source_target_pairs={{0,12},{1,13},{2,14},{3,15},{4,8},{5,9},{6,10},{7,11},{8,4},{9,5},... | collective-permute-start | bytes 884744 | tf_op jit(solution)/shard_map/ppermute | solution.py:30
  61.7 13.3 %collective-permute-done.12.refs_2_ = f32[192,384]{1,0:T(8,128)S(1)} collective-permute-done((f32[192,384]{1,0:T(8,128)S(1)}, f32[192,384]{1,0:T(8,128)S(1)}, u32[]{:S(2)}, u32[]{:S(2)}) %collective-permute-start.12) | collective-permute-done | bytes 294944 | tf_op jit(solution)/shard_map/ppermute | solution.py:30
  75.0 11.4 %collective-permute-start.5 = (f32[1,384]{1,0:T(1,128)S(1)}, f32[1,384]{1,0:T(1,128)S(1)}, u32[]{:S(2)}, u32[]{:S(2)}) collective-permute-start(f32[1,384]{1,0:T(1,128)S(1)} %get-tuple-element.57.picked), channel_id=1, source_target_pairs={{0,64},{64,0},{128,192},{192,128},{1,65},{65,1},{129,193},{193,129... | collective-permute-start | bytes 4616 | tf_op jit(solution)/shard_map/ppermute | solution.py:440
  90.7 3.3 %collective-permute-start.7 = (f32[1,384]{1,0:T(1,128)S(1)}, f32[1,384]{1,0:T(1,128)S(1)}, u32[]{:S(2)}, u32[]{:S(2)}) collective-permute-start(f32[1,384]{1,0:T(1,128)S(1)} %shard_map.118.refs_1_), channel_id=1, source_target_pairs={{0,2},{1,3},{2,0},{3,1},{4,6},{5,7},{6,4},{7,5},{8,10},{9,11},{10,... | collective-permute-start | bytes 4616 | tf_op jit(solution)/shard_map/ppermute | solution.py:30
  96.3 3.0 %collective-permute-start.8 = (f32[1,384]{1,0:T(1,128)S(1)}, f32[1,384]{1,0:T(1,128)S(1)}, u32[]{:S(2)}, u32[]{:S(2)}) collective-permute-start(f32[1,384]{1,0:T(1,128)S(1)} %shard_map.119.refs_1_), channel_id=1, source_target_pairs={{0,4},{1,5},{2,6},{3,7},{4,0},{5,1},{6,2},{7,3},{8,12},{9,13},{10,... | collective-permute-start | bytes 4616 | tf_op jit(solution)/shard_map/ppermute | solution.py:30
  101.6 2.4 %shard_map.122 = (f32[384,384]{1,0:T(8,128)S(1)}, f32[384,384]{1,0:T(8,128)S(1)}, f32[384,384]{1,0:T(8,128)S(1)}, f32[384,384]{1,0:T(8,128)S(1)}, f32[384,384]{1,0:T(8,128)S(1)}, /*index=5*/f32[192,384]{1,0:T(8,128)S(1)}) custom-call(s32[10]{0:T(128)S(1)} %stack.43.flags.refs_0_, f32[384,384]{1,0:T(8,128)S(1)} %get-tuple-element.66.refs_1_, ...), custom_call_target="tpu_custom_call" | custom-call | flops 679477248 | bytes 2359296 | tf_op jit(solution)/shard_map/pallas_call | solution.py:39
  105.5 5.6 %collective-permute-done.15.refs_2_ = f32[192,384]{1,0:T(8,128)S(1)} collective-permute-done((f32[192,384]{1,0:T(8,128)S(1)}, f32[192,384]{1,0:T(8,128)S(1)}, u32[]{:S(2)}, u32[]{:S(2)}) %collective-permute-start.15) | collective-permute-done | bytes 294944 | tf_op jit(solution)/shard_map/ppermute | solution.py:30
  111.1 3.1 %collective-permute-start.11 = (f32[1,384]{1,0:T(1,128)S(1)}, f32[1,384]{1,0:T(1,128)S(1)}, u32[]{:S(2)}, u32[]{:S(2)}) collective-permute-start(f32[1,384]{1,0:T(1,128)S(1)} %shard_map.121.refs_1_), channel_id=1, source_target_pairs={{0,12},{1,13},{2,14},{3,15},{4,8},{5,9},{6,10},{7,11},{8,4},{9,5},... | collective-permute-start | bytes 4616 | tf_op jit(solution)/shard_map/ppermute | solution.py:30
  114.2 2.6 %collective-permute-done.11.refs_2_.refs_4_ = f32[1,384]{1,0:T(1,128)S(1)} collective-permute-done((f32[1,384]{1,0:T(1,128)S(1)}, f32[1,384]{1,0:T(1,128)S(1)}, u32[]{:S(2)}, u32[]{:S(2)}) %collective-permute-start.11) | collective-permute-done | bytes 1568 | tf_op jit(solution)/shard_map/ppermute | solution.py:30
  121.9 3.0 %collective-permute-start.17 = (f32[1,384]{1,0:T(1,128)S(1)}, f32[1,384]{1,0:T(1,128)S(1)}, u32[]{:S(2)}, u32[]{:S(2)}) collective-permute-start(f32[1,384]{1,0:T(1,128)S(1)} %shard_map.126), channel_id=1, source_target_pairs={{0,48},{1,49},{2,50},{3,51},{4,52},{5,53},{6,54},{7,55},{8,56},{9,... | collective-permute-start | bytes 4616 | tf_op jit(solution)/shard_map/ppermute | solution.py:30
  134.2 2.7 %collective-permute-start.20 = (f32[1,384]{1,0:T(1,128)S(1)}, f32[1,384]{1,0:T(1,128)S(1)}, u32[]{:S(2)}, u32[]{:S(2)}) collective-permute-start(f32[1,384]{1,0:T(1,128)S(1)} %shard_map.129.refs_1_), channel_id=1, source_target_pairs={{0,4},{1,5},{2,6},{3,7},{4,0},{5,1},{6,2},{7,3},{8,12},{9,13},{10,... | collective-permute-start | bytes 4616 | tf_op jit(solution)/shard_map/ppermute | solution.py:30
  136.9 1.9 %collective-permute-done.20.refs_2_.refs_3_ = f32[1,384]{1,0:T(1,128)S(1)} collective-permute-done((f32[1,384]{1,0:T(1,128)S(1)}, f32[1,384]{1,0:T(1,128)S(1)}, u32[]{:S(2)}, u32[]{:S(2)}) %collective-permute-start.20) | collective-permute-done | bytes 1568 | tf_op jit(solution)/shard_map/ppermute | solution.py:30
  139.6 3.2 %collective-permute-start.21 = (f32[1,384]{1,0:T(1,128)S(1)}, f32[1,384]{1,0:T(1,128)S(1)}, u32[]{:S(2)}, u32[]{:S(2)}) collective-permute-start(f32[1,384]{1,0:T(1,128)S(1)} %shard_map.130.refs_1_), channel_id=1, source_target_pairs={{0,12},{1,13},{2,14},{3,15},{4,8},{5,9},{6,10},{7,11},{8,4},{9,5},... | collective-permute-start | bytes 4616 | tf_op jit(solution)/shard_map/ppermute | solution.py:30
  142.7 2.6 %collective-permute-done.21.refs_2_.refs_4_ = f32[1,384]{1,0:T(1,128)S(1)} collective-permute-done((f32[1,384]{1,0:T(1,128)S(1)}, f32[1,384]{1,0:T(1,128)S(1)}, u32[]{:S(2)}, u32[]{:S(2)}) %collective-permute-start.21) | collective-permute-done | bytes 1568 | tf_op jit(solution)/shard_map/ppermute | solution.py:30
  146.5 3.3 %collective-permute-done.22.refs_5_.refs_2_ = f32[1,384]{1,0:T(1,128)S(1)} collective-permute-done((f32[1,384]{1,0:T(1,128)S(1)}, f32[1,384]{1,0:T(1,128)S(1)}, u32[]{:S(2)}, u32[]{:S(2)}) %collective-permute-start.22) | collective-permute-done | bytes 1568 | tf_op jit(solution)/shard_map/ppermute | solution.py:30
  150.6 3.0 %collective-permute-start.23 = (f32[1,384]{1,0:T(1,128)S(1)}, f32[1,384]{1,0:T(1,128)S(1)}, u32[]{:S(2)}, u32[]{:S(2)}) collective-permute-start(f32[1,384]{1,0:T(1,128)S(1)} %shard_map.133), channel_id=1, source_target_pairs={{0,48},{1,49},{2,50},{3,51},{4,52},{5,53},{6,54},{7,55},{8,56},{9,... | collective-permute-start | bytes 4616 | tf_op jit(solution)/shard_map/ppermute | solution.py:30
  155.5 2.0 %shard_map.134 = f32[3,4,32,128]{3,2,1,0:T(8,128)} custom-call(s32[10]{0:T(128)S(1)} %stack.43.flags.refs_0_, f32[2,384,384]{2,1,0:T(8,128)S(1)} %copy-done, f32[1,384]{1,0:T(1,128)S(1)} %shard_map.132.entering, f32[1,384]{1,0:T(1,128)S(1)} %collective-permute-done.23.other, f32[384,384]{1,0:T(8,128)S(1)} %get-tuple-element.85.suffix, ...), custom_call_target="tpu_custom_call" | custom-call | flops 589824 | bytes 1446912 | tf_op jit(solution)/shard_map/pallas_call | solution.py:56
  (64 shorter events, 39.9 us)
Async XLA Ops:
  7.0 2.1 %collective-permute-start.2 = (f32[384,384]{1,0:T(8,128)S(1)}, f32[384,384]{1,0:T(8,128)S(1)}, u32[]{:S(2)}, u32[]{:S(2)}) collective-permute-start(f32[384,384]{1,0:T(8,128)S(1)} %shard_map.113.own.transition), channel_id=1, source_target_pairs={{0,1},{1,0},{2,3},{3,2},{4,5},{5,4},{6,7},{7,6},{8,9},{9,8},{10,11... | collective-permute-start | bytes 1769480 | tf_op jit(solution)/shard_map/ppermute | solution.py:30
  7.1 23.9 %collective-permute-start.1 = (f32[44,32,128]{2,1,0:T(8,128)S(1)}, f32[44,32,128]{2,1,0:T(8,128)S(1)}, u32[]{:S(2)}, u32[]{:S(2)}) collective-permute-start(f32[44,32,128]{2,1,0:T(8,128)S(1)} %bitcast_dynamic-update-slice_fusion.own), channel_id=1, source_target_pairs={{0,1},{1,0},{2,3},{3,2},{4,5},{5,4},{6,7},{7,6},{8,9},{9,8},{10,11... | collective-permute-start | bytes 2162696 | tf_op jit(solution)/shard_map/ppermute | solution.py:30
  7.6 23.4 %collective-permute-start = (f32[44,32,128]{2,1,0:T(8,128)S(1)}, f32[44,32,128]{2,1,0:T(8,128)S(1)}, u32[]{:S(2)}, u32[]{:S(2)}) collective-permute-start(f32[44,32,128]{2,1,0:T(8,128)S(1)} %bitcast_dynamic-update-slice_fusion.own), channel_id=1, source_target_pairs={{1,2},{2,1},{3,4},{4,3},{5,6},{6,5},{7,8},{8,7},{9,10},{10,9},{11,... | collective-permute-start | bytes 2162696 | tf_op jit(solution)/shard_map/ppermute | solution.py:488
  10.5 16.5 %collective-permute-start.3 = (f32[192,384]{1,0:T(8,128)S(1)}, f32[192,384]{1,0:T(8,128)S(1)}, u32[]{:S(2)}, u32[]{:S(2)}) collective-permute-start(f32[192,384]{1,0:T(8,128)S(1)} %get-tuple-element.49), channel_id=1, source_target_pairs={{0,2},{1,3},{2,0},{3,1},{4,6},{5,7},{6,4},{7,5},{8,10},{9,11},{10,... | collective-permute-start | bytes 884744 | tf_op jit(solution)/shard_map/ppermute | solution.py:30
  27.0 1.6 %collective-permute-start.4 = (f32[192,384]{1,0:T(8,128)S(1)}, f32[192,384]{1,0:T(8,128)S(1)}, u32[]{:S(2)}, u32[]{:S(2)}) collective-permute-start(f32[192,384]{1,0:T(8,128)S(1)} %collective-permute-done.3.refs_2_), channel_id=1, source_target_pairs={{0,1},{1,0},{2,3},{3,2},{4,5},{5,4},{6,7},{7,6},{8,9},{9,8},{10,11... | collective-permute-start | bytes 884744 | tf_op jit(solution)/shard_map/ppermute | solution.py:30
  31.0 17.0 %collective-permute-start.9 = (f32[192,384]{1,0:T(8,128)S(1)}, f32[192,384]{1,0:T(8,128)S(1)}, u32[]{:S(2)}, u32[]{:S(2)}) collective-permute-start(f32[192,384]{1,0:T(8,128)S(1)} %get-tuple-element.61), channel_id=1, source_target_pairs={{0,4},{1,5},{2,6},{3,7},{4,0},{5,1},{6,2},{7,3},{8,12},{9,13},{10,... | collective-permute-start | bytes 884744 | tf_op jit(solution)/shard_map/ppermute | solution.py:30
  48.0 7.8 %collective-permute-start.10 = (f32[192,384]{1,0:T(8,128)S(1)}, f32[192,384]{1,0:T(8,128)S(1)}, u32[]{:S(2)}, u32[]{:S(2)}) collective-permute-start(f32[192,384]{1,0:T(8,128)S(1)} %collective-permute-done.9.refs_2_), channel_id=1, source_target_pairs={{0,1},{1,0},{2,3},{3,2},{4,5},{5,4},{6,7},{7,6},{8,9},{9,8},{10,11... | collective-permute-start | bytes 884744 | tf_op jit(solution)/shard_map/ppermute | solution.py:30
  58.2 16.8 %collective-permute-start.12 = (f32[192,384]{1,0:T(8,128)S(1)}, f32[192,384]{1,0:T(8,128)S(1)}, u32[]{:S(2)}, u32[]{:S(2)}) collective-permute-start(f32[192,384]{1,0:T(8,128)S(1)} %get-tuple-element.67), channel_id=1, source_target_pairs={{0,12},{1,13},{2,14},{3,15},{4,8},{5,9},{6,10},{7,11},{8,4},{9,5},... | collective-permute-start | bytes 884744 | tf_op jit(solution)/shard_map/ppermute | solution.py:30
  75.0 26.6 %collective-permute-start.13 = (f32[192,384]{1,0:T(8,128)S(1)}, f32[192,384]{1,0:T(8,128)S(1)}, u32[]{:S(2)}, u32[]{:S(2)}) collective-permute-start(f32[192,384]{1,0:T(8,128)S(1)} %collective-permute-done.12.refs_2_), channel_id=1, source_target_pairs={{0,1},{1,0},{2,3},{3,2},{4,5},{5,4},{6,7},{7,6},{8,9},{9,8},{10,11... | collective-permute-start | bytes 884744 | tf_op jit(solution)/shard_map/ppermute | solution.py:30
  75.0 12.9 %collective-permute-start.5 = (f32[1,384]{1,0:T(1,128)S(1)}, f32[1,384]{1,0:T(1,128)S(1)}, u32[]{:S(2)}, u32[]{:S(2)}) collective-permute-start(f32[1,384]{1,0:T(1,128)S(1)} %get-tuple-element.57.picked), channel_id=1, source_target_pairs={{0,64},{64,0},{128,192},{192,128},{1,65},{65,1},{129,193},{193,129... | collective-permute-start | bytes 4616 | tf_op jit(solution)/shard_map/ppermute | solution.py:440
  88.6 1.4 collective-permute-start.6
  90.7 4.9 %collective-permute-start.7 = (f32[1,384]{1,0:T(1,128)S(1)}, f32[1,384]{1,0:T(1,128)S(1)}, u32[]{:S(2)}, u32[]{:S(2)}) collective-permute-start(f32[1,384]{1,0:T(1,128)S(1)} %shard_map.118.refs_1_), channel_id=1, source_target_pairs={{0,2},{1,3},{2,0},{3,1},{4,6},{5,7},{6,4},{7,5},{8,10},{9,11},{10,... | collective-permute-start | bytes 4616 | tf_op jit(solution)/shard_map/ppermute | solution.py:30
  96.3 4.6 %collective-permute-start.8 = (f32[1,384]{1,0:T(1,128)S(1)}, f32[1,384]{1,0:T(1,128)S(1)}, u32[]{:S(2)}, u32[]{:S(2)}) collective-permute-start(f32[1,384]{1,0:T(1,128)S(1)} %shard_map.119.refs_1_), channel_id=1, source_target_pairs={{0,4},{1,5},{2,6},{3,7},{4,0},{5,1},{6,2},{7,3},{8,12},{9,13},{10,... | collective-permute-start | bytes 4616 | tf_op jit(solution)/shard_map/ppermute | solution.py:30
  104.0 7.2 %collective-permute-start.15 = (f32[192,384]{1,0:T(8,128)S(1)}, f32[192,384]{1,0:T(8,128)S(1)}, u32[]{:S(2)}, u32[]{:S(2)}) collective-permute-start(f32[192,384]{1,0:T(8,128)S(1)} %get-tuple-element.74), channel_id=1, source_target_pairs={{0,16},{1,17},{2,18},{3,19},{4,20},{5,21},{6,22},{7,23},{8,24},{9,... | collective-permute-start | bytes 884744 | tf_op jit(solution)/shard_map/ppermute | solution.py:30
  111.1 8.0 %collective-permute-start.16 = (f32[192,384]{1,0:T(8,128)S(1)}, f32[192,384]{1,0:T(8,128)S(1)}, u32[]{:S(2)}, u32[]{:S(2)}) collective-permute-start(f32[192,384]{1,0:T(8,128)S(1)} %collective-permute-done.15.refs_2_), channel_id=1, source_target_pairs={{0,1},{1,0},{2,3},{3,2},{4,5},{5,4},{6,7},{7,6},{8,9},{9,8},{10,11... | collective-permute-start | bytes 884744 | tf_op jit(solution)/shard_map/ppermute | solution.py:30
  111.1 5.7 %collective-permute-start.11 = (f32[1,384]{1,0:T(1,128)S(1)}, f32[1,384]{1,0:T(1,128)S(1)}, u32[]{:S(2)}, u32[]{:S(2)}) collective-permute-start(f32[1,384]{1,0:T(1,128)S(1)} %shard_map.121.refs_1_), channel_id=1, source_target_pairs={{0,12},{1,13},{2,14},{3,15},{4,8},{5,9},{6,10},{7,11},{8,4},{9,5},... | collective-permute-start | bytes 4616 | tf_op jit(solution)/shard_map/ppermute | solution.py:30
  117.5 3.7 %collective-permute-start.14 = (f32[1,384]{1,0:T(1,128)S(1)}, f32[1,384]{1,0:T(1,128)S(1)}, u32[]{:S(2)}, u32[]{:S(2)}) collective-permute-start(f32[1,384]{1,0:T(1,128)S(1)} %shard_map.123.refs_1_), channel_id=1, source_target_pairs={{0,16},{1,17},{2,18},{3,19},{4,20},{5,21},{6,22},{7,23},{8,24},{9,... | collective-permute-start | bytes 4616 | tf_op jit(solution)/shard_map/ppermute | solution.py:30
  121.9 4.9 %collective-permute-start.17 = (f32[1,384]{1,0:T(1,128)S(1)}, f32[1,384]{1,0:T(1,128)S(1)}, u32[]{:S(2)}, u32[]{:S(2)}) collective-permute-start(f32[1,384]{1,0:T(1,128)S(1)} %shard_map.126), channel_id=1, source_target_pairs={{0,48},{1,49},{2,50},{3,51},{4,52},{5,53},{6,54},{7,55},{8,56},{9,... | collective-permute-start | bytes 4616 | tf_op jit(solution)/shard_map/ppermute | solution.py:30
  127.8 1.2 collective-permute-start.18
  129.8 3.7 %collective-permute-start.19 = (f32[1,384]{1,0:T(1,128)S(1)}, f32[1,384]{1,0:T(1,128)S(1)}, u32[]{:S(2)}, u32[]{:S(2)}) collective-permute-start(f32[1,384]{1,0:T(1,128)S(1)} %shard_map.128.refs_1_), channel_id=1, source_target_pairs={{0,2},{1,3},{2,0},{3,1},{4,6},{5,7},{6,4},{7,5},{8,10},{9,11},{10,... | collective-permute-start | bytes 4616 | tf_op jit(solution)/shard_map/ppermute | solution.py:30
  134.2 4.6 %collective-permute-start.20 = (f32[1,384]{1,0:T(1,128)S(1)}, f32[1,384]{1,0:T(1,128)S(1)}, u32[]{:S(2)}, u32[]{:S(2)}) collective-permute-start(f32[1,384]{1,0:T(1,128)S(1)} %shard_map.129.refs_1_), channel_id=1, source_target_pairs={{0,4},{1,5},{2,6},{3,7},{4,0},{5,1},{6,2},{7,3},{8,12},{9,13},{10,... | collective-permute-start | bytes 4616 | tf_op jit(solution)/shard_map/ppermute | solution.py:30
  139.6 5.8 %collective-permute-start.21 = (f32[1,384]{1,0:T(1,128)S(1)}, f32[1,384]{1,0:T(1,128)S(1)}, u32[]{:S(2)}, u32[]{:S(2)}) collective-permute-start(f32[1,384]{1,0:T(1,128)S(1)} %shard_map.130.refs_1_), channel_id=1, source_target_pairs={{0,12},{1,13},{2,14},{3,15},{4,8},{5,9},{6,10},{7,11},{8,4},{9,5},... | collective-permute-start | bytes 4616 | tf_op jit(solution)/shard_map/ppermute | solution.py:30
  146.1 3.7 %collective-permute-start.22 = (f32[1,384]{1,0:T(1,128)S(1)}, f32[1,384]{1,0:T(1,128)S(1)}, u32[]{:S(2)}, u32[]{:S(2)}) collective-permute-start(f32[1,384]{1,0:T(1,128)S(1)} %shard_map.131.refs_1_), channel_id=1, source_target_pairs={{0,16},{1,17},{2,18},{3,19},{4,20},{5,21},{6,22},{7,23},{8,24},{9,... | collective-permute-start | bytes 4616 | tf_op jit(solution)/shard_map/ppermute | solution.py:30
  150.6 4.9 %collective-permute-start.23 = (f32[1,384]{1,0:T(1,128)S(1)}, f32[1,384]{1,0:T(1,128)S(1)}, u32[]{:S(2)}, u32[]{:S(2)}) collective-permute-start(f32[1,384]{1,0:T(1,128)S(1)} %shard_map.133), channel_id=1, source_target_pairs={{0,48},{1,49},{2,50},{3,51},{4,52},{5,53},{6,54},{7,55},{8,56},{9,... | collective-permute-start | bytes 4616 | tf_op jit(solution)/shard_map/ppermute | solution.py:30
  (6 other events, 51.2 us)
where the time goes:
time: 159 us; the launch traced here: 157 us
  waiting for transfers between devices  70.6 us (44%)
  starting transfers between devices  48.9 us (31%)
  Pallas kernels  32.1 us (20%)
  local copies, waits for them, and re-layouts  4.22 us (3%)
  between operations  1.74 us (1%)
    ppermute x22, waiting for transfers between devices, swap(): lax.ppermute(value, 'tile', [(i, i ^ mask) for i in range(lax.axis_size('...  69.1 us
    ppermute x22, starting transfers between devices, swap(): lax.ppermute(value, 'tile', [(i, i ^ mask) for i in range(lax.axis_size('...  36.8 us
    pallas_call x18, Pallas kernels, local_call(): pl.pallas_call(kernel, out_shape=outs, in_specs=[SM] + [VM] * len(operand...  20.3 us
    ppermute x1, starting transfers between devices, coupled_velocity(): partner = lax.ppermute(picked, 'sub', [(i, i ^ 1) for i in range(count)])  11.4 us
    pallas_call x1, Pallas kernels, substeps_call(): pl.pallas_call(substep_kernel, out_shape=(jax.ShapeDtypeStruct(grid_shape...  7.82 us
    unnamed x16, local copies, waits for them, and re-layouts  4.12 us
    pallas_call x3, Pallas kernels, pair_call(): pl.pallas_call(kernel, out_shape=outs, grid_spec=pltpu.PrefetchScalarGrid...  3.97 us
  transfers between devices with their start and end apart: 24, of which 19 were waited for; matrix products, arithmetic and copies ran while one was open for 0% of the time, Pallas kernels for 12%

commit v1 on v0

--- a/solution.py
+++ b/solution.py
@@ -11,7 +11,8 @@
 GRANT = 12 << 20
 CX, CY, CZ = 4, 32, 128
 DEEP = 3 * CX
-FIELDS = 11
+NEAR = CX - 1
+PACKED = 37
 CORE, PAIR, SIDE, LAST, STEPS = 0, 6, 7, 8, 9
 GROUPS = CY // 8
 MASKS = (1, 2, 4, 12, 16, 48)
@@ -156,37 +157,47 @@
 
 
 def substep_kernel(
-    flags, step, own, outer, inner, stiffness, nodes,
+    flags, step, displacement, velocity, external_load, node_mass, modulus,
+    outer, inner, stiffness, nodes,
     displacement_out, velocity_out, picked,
     disp, vel, load, inverse_mass, factor, stiff, features, upper,
 ):
     first = flags[CORE] == 0
 
-    def place(source, low):
-        layers = pl.ds(low, CX)
+    def put_mass(low, mass):
+        present = mass > 0.0
+        inverse_mass[pl.ds(low, mass.shape[0])] = jnp.where(
+            present, 1.0 / jnp.where(present, mass, 1.0), 0.0
+        )
+
+    def put_factor(low, source, base):
+        row = lax.broadcasted_iota(jnp.int32, (CY, CZ), 0)
+        for x in range(CX):
+            factor[low + x] = wide(jnp.where(row < CY - 1, source[base + x], 0.0))
+
+    def place(source, low, shift):
         for i in range(3):
-            disp[i, layers] = source[pl.ds(CX * i, CX)]
-            vel[i, layers] = source[pl.ds(CX * (3 + i), CX)]
-            load[i, layers] = source[pl.ds(CX * (6 + i), CX)]
-        mass = source[pl.ds(CX * 9, CX)]
-        present = mass > 0.0
-        inverse_mass[layers] = jnp.where(present, 1.0 / jnp.where(present, mass, 1.0), 0.0)
-        for x in range(CX):
-            value = source[CX * 10 + x]
-            row = lax.broadcasted_iota(jnp.int32, (CY, CZ), 0)
-            factor[low + x] = wide(jnp.where(row < CY - 1, value, 0.0))
-
-    place(own, CX)
+            disp[i, pl.ds(low, CX)] = source[pl.ds(CX * i, CX)]
+            vel[i, pl.ds(low + shift, NEAR)] = source[pl.ds(12 + NEAR * i, NEAR)]
+            load[i, pl.ds(low + shift, NEAR)] = source[pl.ds(21 + NEAR * i, NEAR)]
+        put_mass(low + shift, source[pl.ds(30, NEAR)])
+        put_factor(low, source, 33)
+
+    disp[:, CX : 2 * CX] = displacement[...]
+    vel[:, CX : 2 * CX] = velocity[...]
+    load[:, CX : 2 * CX] = external_load[...]
+    put_mass(CX, node_mass[...])
+    put_factor(CX, modulus, 0)
 
     @pl.when(first)
     def _():
-        place(outer, 0)
-        place(inner, 2 * CX)
+        place(outer, 0, 1)
+        place(inner, 2 * CX, 0)
 
     @pl.when(jnp.logical_not(first))
     def _():
-        place(inner, 0)
-        place(outer, 2 * CX)
+        place(inner, 0, 1)
+        place(outer, 2 * CX, 0)
 
     @pl.when(flags[LAST] == 1)
     def _():
@@ -260,7 +271,17 @@
     picked[...] = jnp.concatenate(parts, axis=1)
 
 
-def substeps_call(flags, step, own, outer, inner, stiffness, nodes):
+def pack_kernel(flags, displacement, velocity, external_load, node_mass, modulus, outer, inner):
+    for target, start in ((outer, flags[CORE]), (inner, 1 - flags[CORE])):
+        for i in range(3):
+            target[pl.ds(CX * i, CX)] = displacement[i]
+            target[pl.ds(12 + NEAR * i, NEAR)] = velocity[i, pl.ds(start, NEAR)]
+            target[pl.ds(21 + NEAR * i, NEAR)] = external_load[i, pl.ds(start, NEAR)]
+        target[pl.ds(30, NEAR)] = node_mass[pl.ds(start, NEAR)]
+        target[pl.ds(33, CX)] = modulus[...]
+
+
+def substeps_call(flags, step, state, outer, inner, stiffness, nodes):
     grid_shape = (3, CX, CY, CZ)
     return pl.pallas_call(
         substep_kernel,
@@ -269,7 +290,7 @@
             jax.ShapeDtypeStruct(grid_shape, f32),
             ROW,
         ),
-        in_specs=[SM, SM] + [VM] * 5,
+        in_specs=[SM, SM] + [VM] * 9,
         out_specs=(VM, VM, VM),
         scratch_shapes=[
             pltpu.VMEM((3, DEEP, CY, CZ), f32),
@@ -283,7 +304,7 @@
         ],
         compiler_params=pltpu.CompilerParams(vmem_limit_bytes=20 << 20),
         cost_estimate=cost(32 * 2 * 192 * 576 * 512, 3 * 720896),
-    )(flags, step, own, outer, inner, stiffness, nodes)
+    )(flags, step, *state, outer, inner, stiffness, nodes)
 
 def transition_kernel(flags, inverse, lower, transition):
     transition[...] = -product(inverse[0], lower[0])
@@ -299,7 +320,7 @@
         half[...] = value_ref[HALF:]
 
 
-def first_merge_kernel(flags, own, other, high_ref, low_ref, merged, half, prefix, suffix):
+def first_merge_kernel(flags, own, other, high_ref, low_ref, merged, half):
     is_high = flags[0] == 1
     high = jnp.where(is_high, own[...], other[...])
     low = jnp.where(is_high, other[...], own[...])
@@ -307,12 +328,16 @@
     low_ref[...] = low
     merged[...] = product(high, low)
     store_half(flags, half, merged)
+
+
+def first_reach_kernel(flags, other, prefix, suffix):
+    is_high = flags[0] == 1
     identity = eye_mask(IB).astype(f32)
     prefix[...] = jnp.where(is_high, other[...], identity)
     suffix[...] = jnp.where(is_high, identity, other[...])
 
 
-def merge_kernel(level, last, flags, own, near, far, prefix, suffix, *outs):
+def merge_kernel(level, last, flags, own, near, far, high_ref, low_ref, *outs):
     is_high = flags[level] == 1
     first = flags[CORE] == 0
     other = jnp.concatenate(
@@ -320,15 +345,18 @@
     )
     high = jnp.where(is_high, own[...], other)
     low = jnp.where(is_high, other, own[...])
-    high_ref, low_ref, new_prefix, new_suffix = outs[:4]
     high_ref[...] = high
     low_ref[...] = low
     if not last:
-        merged, half = outs[4:]
+        merged, half = outs
         merged[...] = product(high, low)
         store_half(flags, half, merged)
+
+
+def reach_kernel(level, flags, high, low, prefix, suffix, new_prefix, new_suffix):
+    is_high = flags[level] == 1
     longer = product(
-        jnp.where(is_high, prefix[...], high), jnp.where(is_high, low, suffix[...])
+        jnp.where(is_high, prefix[...], high[...]), jnp.where(is_high, low[...], suffix[...])
     )
     new_prefix[...] = jnp.where(is_high, longer, prefix[...])
     new_suffix[...] = jnp.where(is_high, suffix[...], longer)
@@ -405,31 +433,32 @@
         transition_kernel, flags, [factor_inverse, factor_lower], [], MAT, cube
     )
     other = swap(transition, MASKS[0])
-    high, low, merged, half, prefix, suffix = local_call(
-        first_merge_kernel,
-        flags,
-        [transition, other],
-        (MAT, MAT, MAT, HALFMAT, MAT, MAT),
-        cube,
-    )
+    high, low, merged, half = local_call(
+        first_merge_kernel, flags, [transition, other], (MAT, MAT, MAT, HALFMAT), cube
+    )
+    prefix, suffix = local_call(first_reach_kernel, flags, [other], (MAT, MAT))
     return transition, (merged, half), [(high, low, prefix, suffix)]
 
 
 def merge_level(flags, level, block, levels, gate=None):
+    cube = 6 * IB**3
     merged, half = block
     near = swap(half, MASKS[level])
+    if gate is not None:
+        near, _ = lax.optimization_barrier((near, gate))
     far = swap(near, 1)
-    if gate is not None:
-        far, _ = lax.optimization_barrier((far, gate))
     last = level == 4
-    made = local_call(
+    high, low, *block = local_call(
         bound(level, merge_kernel, last),
         flags,
-        [merged, near, far, *levels[-1][2:]],
-        (MAT,) * 4 if last else (MAT,) * 5 + (HALFMAT,),
-        12 * IB**3,
-    )
-    return made[4:], levels + [tuple(made[:4])]
+        [merged, near, far],
+        (MAT, MAT) if last else (MAT, MAT, MAT, HALFMAT),
+        cube,
+    )
+    prefix, suffix = local_call(
+        bound(level, reach_kernel), flags, [high, low, *levels[-1][2:]], (MAT, MAT), cube
+    )
+    return block, levels + [(high, low, prefix, suffix)]
 
 
 def coupled_velocity(
@@ -506,24 +535,16 @@
         [(tile >> k) & 1 for k in range(6)] + [sub // 2, sub % 2, last, substeps[0]]
     ).astype(jnp.int32)
     step = coarse_step / substeps.astype(f32)
-    own = jnp.concatenate(
-        [
-            displacement.reshape(-1, CY, CZ),
-            velocity.reshape(-1, CY, CZ),
-            external_load.reshape(-1, CY, CZ),
-            node_mass[0],
-            modulus[0],
-        ],
-        axis=0,
-    )
-    own, factor_inverse, factor_lower = lax.optimization_barrier((own, factor_inverse, factor_lower))
-    outer = outer_swap(own)
-    inner = swap(own, 1)
+    state = [displacement[0], velocity[0], external_load[0], node_mass[0], modulus[0]]
+    packed = jax.ShapeDtypeStruct((PACKED, CY, CZ), f32)
+    outer, inner = local_call(pack_kernel, flags, state, (packed, packed))
+    outer = outer_swap(outer)
+    inner = swap(inner, 1)
     transition, block, levels = first_products(flags, factor_inverse, factor_lower)
     block, levels = merge_level(flags, 1, block, levels)
-    outer, inner, block = lax.optimization_barrier((outer, inner, block))
+    outer, _ = lax.optimization_barrier((outer, block[1]))
     final_displacement, final_velocity, picked = substeps_call(
-        flags, step, own, outer, inner, stiffness, interface_nodes
+        flags, step, state, outer, inner, stiffness, interface_nodes
     )
     coupled = coupled_velocity(
         flags,

time: 159 us -> 125 us (0.79)
  waiting for transfers between devices: 70.6 us -> 39.8 us
  starting transfers between devices: 48.9 us -> 34.9 us
  Pallas kernels: 32.1 us -> 45.4 us
    ppermute x22, waiting for transfers between devices: 69.1 us -> 36.2 us  [swap(): lax.ppermute(value, 'tile', [(i, i ^ mask) for i in range(lax.axis_size('...]
    ppermute x1, starting transfers between devices: 11.4 us -> 0.01 us  [coupled_velocity(): partner = lax.ppermute(picked, 'sub', [(i, i ^ 1) for i in range(count)])]
    pallas_call x1, Pallas kernels: 7.82 us -> 18.6 us  [substeps_call(): pl.pallas_call(substep_kernel, out_shape=(jax.ShapeDtypeStruct(grid_shape...]
    ppermute x22, starting transfers between devices: 36.8 us -> 34.2 us  [swap(): lax.ppermute(value, 'tile', [(i, i ^ mask) for i in range(lax.axis_size('...]
    pallas_call x18 -> x24, Pallas kernels: 20.3 us -> 22.8 us  [local_call(): pl.pallas_call(kernel, out_shape=outs, in_specs=[SM] + [VM] * len(operand...]
    ppermute x1, waiting for transfers between devices: 1.56 us -> 3.58 us  [coupled_velocity(): partner = lax.ppermute(picked, 'sub', [(i, i ^ 1) for i in range(count)])]
    unnamed x16 -> x20, local copies, waits for them, and re-layouts: 4.12 us -> 2.59 us
  transfers between devices with their start and end apart: 24 -> 24, of which waited for: 19 -> 19; matrix products, arithmetic and copies ran while one was open for 0% -> 0% of each run, Pallas kernels for 12% -> 26%
where the time goes in v1:
time: 125 us; the launch traced here: 124 us
  Pallas kernels  45.4 us (36%)
  waiting for transfers between devices  39.8 us (32%)
  starting transfers between devices  34.9 us (28%)
  local copies, waits for them, and re-layouts  2.68 us (2%)
  between operations  1.66 us (1%)
    ppermute x22, waiting for transfers between devices, swap(): lax.ppermute(value, 'tile', [(i, i ^ mask) for i in range(lax.axis_size('...  36.2 us
    ppermute x22, starting transfers between devices, swap(): lax.ppermute(value, 'tile', [(i, i ^ mask) for i in range(lax.axis_size('...  34.2 us
    pallas_call x24, Pallas kernels, local_call(): pl.pallas_call(kernel, out_shape=outs, in_specs=[SM] + [VM] * len(operand...  22.8 us
    pallas_call x1, Pallas kernels, substeps_call(): pl.pallas_call(substep_kernel, out_shape=(jax.ShapeDtypeStruct(grid_shape...  18.6 us
    pallas_call x3, Pallas kernels, pair_call(): pl.pallas_call(kernel, out_shape=outs, grid_spec=pltpu.PrefetchScalarGrid...  3.97 us
    ppermute x1, waiting for transfers between devices, coupled_velocity(): partner = lax.ppermute(picked, 'sub', [(i, i ^ 1) for i in range(count)])  3.58 us
    unnamed x20, local copies, waits for them, and re-layouts  2.59 us
  transfers between devices with their start and end apart: 24, of which 19 were waited for; matrix products, arithmetic and copies ran while one was open for 0% of the time, Pallas kernels for 26%

profile of v1, /device:TPU:2, one launch (start us, length us, event | category | flops | bytes accessed | tf_op | source)
XLA Modules:
  0.0 124.4 jit_solution(13956525442156815414)
XLA Ops:
  5.4 2.0 %collective-permute-done.1.other = f32[384,384]{1,0:T(8,128)S(1)} collective-permute-done((f32[384,384]{1,0:T(8,128)S(1)}, f32[384,384]{1,0:T(8,128)S(1)}, u32[]{:S(2)}, u32[]{:S(2)}) %collective-permute-start.1) | collective-permute-done | bytes 589856 | tf_op jit(solution)/shard_map/ppermute | solution.py:31
  8.7 2.0 %collective-permute-start.2 = (f32[192,384]{1,0:T(8,128)S(1)}, f32[192,384]{1,0:T(8,128)S(1)}, u32[]{:S(2)}, u32[]{:S(2)}) collective-permute-start(f32[192,384]{1,0:T(8,128)S(1)} %get-tuple-element.43), channel_id=1, source_target_pairs={{0,2},{1,3},{2,0},{3,1},{4,6},{5,7},{6,4},{7,5},{8,10},{9,11},{10,... | collective-permute-start | bytes 884744 | tf_op jit(solution)/shard_map/ppermute | solution.py:31
  13.6 4.5 %collective-permute-done.2.refs_2_ = f32[192,384]{1,0:T(8,128)S(1)} collective-permute-done((f32[192,384]{1,0:T(8,128)S(1)}, f32[192,384]{1,0:T(8,128)S(1)}, u32[]{:S(2)}, u32[]{:S(2)}) %collective-permute-start.2) | collective-permute-done | bytes 294944 | tf_op jit(solution)/shard_map/ppermute | solution.py:31
  21.0 3.4 %collective-permute-start.9 = (f32[192,384]{1,0:T(8,128)S(1)}, f32[192,384]{1,0:T(8,128)S(1)}, u32[]{:S(2)}, u32[]{:S(2)}) collective-permute-start(f32[192,384]{1,0:T(8,128)S(1)} %get-tuple-element.44), channel_id=1, source_target_pairs={{0,4},{1,5},{2,6},{3,7},{4,0},{5,1},{6,2},{7,3},{8,12},{9,13},{10,... | collective-permute-start | bytes 884744 | tf_op jit(solution)/shard_map/ppermute | solution.py:31
  24.4 18.6 %shard_map.117 = (f32[3,4,32,128]{3,2,1,0:T(8,128)}, f32[3,4,32,128]{3,2,1,0:T(8,128)S(1)}, f32[1,384]{1,0:T(1,128)S(1)}) custom-call(s32[10]{0:T(128)S(1)} %stack.43.flags.refs_0_, f32[1]{0:T(128)S(6)} %div.14.step, f32[3,4,32,128]{3,2,1,0:T(8,128)S(1)} %bitcast.20, f32[3,4,32,128]{3,2,1,0:T(8,128)S(1)} %bitcast.22, f32[3,4,32,128]{3,2,1,0:T(8,128)S(1)} %bitcast.24, ...), custom_call_target="tpu_custom_call" | custom-call | flops 3623878656 | bytes 2162688 | tf_op jit(solution)/shard_map/pallas_call | solution.py:286
  46.0 5.8 %collective-permute-start.12 = (f32[192,384]{1,0:T(8,128)S(1)}, f32[192,384]{1,0:T(8,128)S(1)}, u32[]{:S(2)}, u32[]{:S(2)}) collective-permute-start(f32[192,384]{1,0:T(8,128)S(1)} %get-tuple-element.55), channel_id=1, source_target_pairs={{0,12},{1,13},{2,14},{3,15},{4,8},{5,9},{6,10},{7,11},{8,4},{9,5},... | collective-permute-start | bytes 884744 | tf_op jit(solution)/shard_map/ppermute | solution.py:31
  51.8 3.6 %collective-permute-done.5.partner = f32[1,384]{1,0:T(1,128)S(1)} collective-permute-done((f32[1,384]{1,0:T(1,128)S(1)}, f32[1,384]{1,0:T(1,128)S(1)}, u32[]{:S(2)}, u32[]{:S(2)}) %collective-permute-start.5) | collective-permute-done | bytes 1568 | tf_op jit(solution)/shard_map/ppermute | solution.py:469
  58.0 1.7 %collective-permute-start.7 = (f32[1,384]{1,0:T(1,128)S(1)}, f32[1,384]{1,0:T(1,128)S(1)}, u32[]{:S(2)}, u32[]{:S(2)}) collective-permute-start(f32[1,384]{1,0:T(1,128)S(1)} %shard_map.119.refs_1_), channel_id=1, source_target_pairs={{0,2},{1,3},{2,0},{3,1},{4,6},{5,7},{6,4},{7,5},{8,10},{9,11},{10,... | collective-permute-start | bytes 4616 | tf_op jit(solution)/shard_map/ppermute | solution.py:31
  59.6 2.0 %collective-permute-done.7.refs_2_ = f32[1,384]{1,0:T(1,128)S(1)} collective-permute-done((f32[1,384]{1,0:T(1,128)S(1)}, f32[1,384]{1,0:T(1,128)S(1)}, u32[]{:S(2)}, u32[]{:S(2)}) %collective-permute-start.7) | collective-permute-done | bytes 1568 | tf_op jit(solution)/shard_map/ppermute | solution.py:31
  64.0 2.9 %collective-permute-done.8.refs_2_.refs_3_ = f32[1,384]{1,0:T(1,128)S(1)} collective-permute-done((f32[1,384]{1,0:T(1,128)S(1)}, f32[1,384]{1,0:T(1,128)S(1)}, u32[]{:S(2)}, u32[]{:S(2)}) %collective-permute-start.8) | collective-permute-done | bytes 1568 | tf_op jit(solution)/shard_map/ppermute | solution.py:31
  70.8 1.7 %collective-permute-start.15 = (f32[192,384]{1,0:T(8,128)S(1)}, f32[192,384]{1,0:T(8,128)S(1)}, u32[]{:S(2)}, u32[]{:S(2)}) collective-permute-start(f32[192,384]{1,0:T(8,128)S(1)} %get-tuple-element.69), channel_id=1, source_target_pairs={{0,16},{1,17},{2,18},{3,19},{4,20},{5,21},{6,22},{7,23},{8,24},{9,... | collective-permute-start | bytes 884744 | tf_op jit(solution)/shard_map/ppermute | solution.py:31
  72.4 1.7 %collective-permute-start.11 = (f32[1,384]{1,0:T(1,128)S(1)}, f32[1,384]{1,0:T(1,128)S(1)}, u32[]{:S(2)}, u32[]{:S(2)}) collective-permute-start(f32[1,384]{1,0:T(1,128)S(1)} %shard_map.122.refs_1_), channel_id=1, source_target_pairs={{0,12},{1,13},{2,14},{3,15},{4,8},{5,9},{6,10},{7,11},{8,4},{9,5},... | collective-permute-start | bytes 4616 | tf_op jit(solution)/shard_map/ppermute | solution.py:31
  74.1 4.0 %collective-permute-done.11.refs_2_.refs_4_ = f32[1,384]{1,0:T(1,128)S(1)} collective-permute-done((f32[1,384]{1,0:T(1,128)S(1)}, f32[1,384]{1,0:T(1,128)S(1)}, u32[]{:S(2)}, u32[]{:S(2)}) %collective-permute-start.11) | collective-permute-done | bytes 1568 | tf_op jit(solution)/shard_map/ppermute | solution.py:31
  83.2 1.7 %collective-permute-start.14 = (f32[1,384]{1,0:T(1,128)S(1)}, f32[1,384]{1,0:T(1,128)S(1)}, u32[]{:S(2)}, u32[]{:S(2)}) collective-permute-start(f32[1,384]{1,0:T(1,128)S(1)} %shard_map.124.refs_1_), channel_id=1, source_target_pairs={{0,16},{1,17},{2,18},{3,19},{4,20},{5,21},{6,22},{7,23},{8,24},{9,... | collective-permute-start | bytes 4616 | tf_op jit(solution)/shard_map/ppermute | solution.py:31
  88.8 3.2 %collective-permute-start.17 = (f32[1,384]{1,0:T(1,128)S(1)}, f32[1,384]{1,0:T(1,128)S(1)}, u32[]{:S(2)}, u32[]{:S(2)}) collective-permute-start(f32[1,384]{1,0:T(1,128)S(1)} %shard_map.131), channel_id=1, source_target_pairs={{0,48},{1,49},{2,50},{3,51},{4,52},{5,53},{6,54},{7,55},{8,56},{9,... | collective-permute-start | bytes 4616 | tf_op jit(solution)/shard_map/ppermute | solution.py:31
  96.8 1.9 %collective-permute-start.19 = (f32[1,384]{1,0:T(1,128)S(1)}, f32[1,384]{1,0:T(1,128)S(1)}, u32[]{:S(2)}, u32[]{:S(2)}) collective-permute-start(f32[1,384]{1,0:T(1,128)S(1)} %shard_map.134.refs_1_), channel_id=1, source_target_pairs={{0,2},{1,3},{2,0},{3,1},{4,6},{5,7},{6,4},{7,5},{8,10},{9,11},{10,... | collective-permute-start | bytes 4616 | tf_op jit(solution)/shard_map/ppermute | solution.py:31
  98.6 1.8 %collective-permute-done.19.refs_2_ = f32[1,384]{1,0:T(1,128)S(1)} collective-permute-done((f32[1,384]{1,0:T(1,128)S(1)}, f32[1,384]{1,0:T(1,128)S(1)}, u32[]{:S(2)}, u32[]{:S(2)}) %collective-permute-start.19) | collective-permute-done | bytes 1568 | tf_op jit(solution)/shard_map/ppermute | solution.py:31
  101.2 1.8 %collective-permute-start.20 = (f32[1,384]{1,0:T(1,128)S(1)}, f32[1,384]{1,0:T(1,128)S(1)}, u32[]{:S(2)}, u32[]{:S(2)}) collective-permute-start(f32[1,384]{1,0:T(1,128)S(1)} %shard_map.135.refs_1_), channel_id=1, source_target_pairs={{0,4},{1,5},{2,6},{3,7},{4,0},{5,1},{6,2},{7,3},{8,12},{9,13},{10,... | collective-permute-start | bytes 4616 | tf_op jit(solution)/shard_map/ppermute | solution.py:31
  103.0 2.8 %collective-permute-done.20.refs_2_.refs_3_ = f32[1,384]{1,0:T(1,128)S(1)} collective-permute-done((f32[1,384]{1,0:T(1,128)S(1)}, f32[1,384]{1,0:T(1,128)S(1)}, u32[]{:S(2)}, u32[]{:S(2)}) %collective-permute-start.20) | collective-permute-done | bytes 1568 | tf_op jit(solution)/shard_map/ppermute | solution.py:31
  106.5 2.0 %collective-permute-start.21 = (f32[1,384]{1,0:T(1,128)S(1)}, f32[1,384]{1,0:T(1,128)S(1)}, u32[]{:S(2)}, u32[]{:S(2)}) collective-permute-start(f32[1,384]{1,0:T(1,128)S(1)} %shard_map.136.refs_1_), channel_id=1, source_target_pairs={{0,12},{1,13},{2,14},{3,15},{4,8},{5,9},{6,10},{7,11},{8,4},{9,5},... | collective-permute-start | bytes 4616 | tf_op jit(solution)/shard_map/ppermute | solution.py:31
  108.5 3.8 %collective-permute-done.21.refs_2_.refs_4_ = f32[1,384]{1,0:T(1,128)S(1)} collective-permute-done((f32[1,384]{1,0:T(1,128)S(1)}, f32[1,384]{1,0:T(1,128)S(1)}, u32[]{:S(2)}, u32[]{:S(2)}) %collective-permute-start.21) | collective-permute-done | bytes 1568 | tf_op jit(solution)/shard_map/ppermute | solution.py:31
  113.7 3.1 %collective-permute-done.22.refs_5_.refs_2_ = f32[1,384]{1,0:T(1,128)S(1)} collective-permute-done((f32[1,384]{1,0:T(1,128)S(1)}, f32[1,384]{1,0:T(1,128)S(1)}, u32[]{:S(2)}, u32[]{:S(2)}) %collective-permute-start.22) | collective-permute-done | bytes 1568 | tf_op jit(solution)/shard_map/ppermute | solution.py:31
  117.5 3.2 %collective-permute-start.23 = (f32[1,384]{1,0:T(1,128)S(1)}, f32[1,384]{1,0:T(1,128)S(1)}, u32[]{:S(2)}, u32[]{:S(2)}) collective-permute-start(f32[1,384]{1,0:T(1,128)S(1)} %shard_map.139), channel_id=1, source_target_pairs={{0,48},{1,49},{2,50},{3,51},{4,52},{5,53},{6,54},{7,55},{8,56},{9,... | collective-permute-start | bytes 4616 | tf_op jit(solution)/shard_map/ppermute | solution.py:31
  122.4 2.0 %shard_map.140 = f32[3,4,32,128]{3,2,1,0:T(8,128)} custom-call(s32[10]{0:T(128)S(1)} %stack.43.flags.refs_0_, f32[2,384,384]{2,1,0:T(8,128)S(1)} %copy-done.1, f32[1,384]{1,0:T(1,128)S(1)} %shard_map.138.entering, f32[1,384]{1,0:T(1,128)S(1)} %collective-permute-done.23.other, f32[384,384]{1,0:T(8,128)S(1)} %get-tuple-element.77.suffix, ...), custom_call_target="tpu_custom_call" | custom-call | flops 589824 | bytes 1446912 | tf_op jit(solution)/shard_map/pallas_call | solution.py:57
  (73 shorter events, 41.8 us)
Async XLA Ops:
  5.3 2.1 %collective-permute-start.1 = (f32[384,384]{1,0:T(8,128)S(1)}, f32[384,384]{1,0:T(8,128)S(1)}, u32[]{:S(2)}, u32[]{:S(2)}) collective-permute-start(f32[384,384]{1,0:T(8,128)S(1)} %shard_map.114.own.transition), channel_id=1, source_target_pairs={{0,1},{1,0},{2,3},{3,2},{4,5},{5,4},{6,7},{7,6},{8,9},{9,8},{10,11... | collective-permute-start | bytes 1769480 | tf_op jit(solution)/shard_map/ppermute | solution.py:31
  8.7 9.4 %collective-permute-start.2 = (f32[192,384]{1,0:T(8,128)S(1)}, f32[192,384]{1,0:T(8,128)S(1)}, u32[]{:S(2)}, u32[]{:S(2)}) collective-permute-start(f32[192,384]{1,0:T(8,128)S(1)} %get-tuple-element.43), channel_id=1, source_target_pairs={{0,2},{1,3},{2,0},{3,1},{4,6},{5,7},{6,4},{7,5},{8,10},{9,11},{10,... | collective-permute-start | bytes 884744 | tf_op jit(solution)/shard_map/ppermute | solution.py:31
  11.4 13.0 %collective-permute-start = (f32[37,32,128]{2,1,0:T(8,128)S(1)}, f32[37,32,128]{2,1,0:T(8,128)S(1)}, u32[]{:S(2)}, u32[]{:S(2)}) collective-permute-start(f32[37,32,128]{2,1,0:T(8,128)S(1)} %get-tuple-element.41), channel_id=1, source_target_pairs={{1,2},{2,1},{3,4},{4,3},{5,6},{6,5},{7,8},{8,7},{9,10},{10,9},{11,... | collective-permute-start | bytes 1818632 | tf_op jit(solution)/shard_map/ppermute | solution.py:517
  12.1 12.3 %collective-permute-start.4 = (f32[37,32,128]{2,1,0:T(8,128)S(1)}, f32[37,32,128]{2,1,0:T(8,128)S(1)}, u32[]{:S(2)}, u32[]{:S(2)}) collective-permute-start(f32[37,32,128]{2,1,0:T(8,128)S(1)} %get-tuple-element.46), channel_id=1, source_target_pairs={{0,1},{1,0},{2,3},{3,2},{4,5},{5,4},{6,7},{7,6},{8,9},{9,8},{10,11... | collective-permute-start | bytes 1818632 | tf_op jit(solution)/shard_map/ppermute | solution.py:31
  18.1 1.6 %collective-permute-start.3 = (f32[192,384]{1,0:T(8,128)S(1)}, f32[192,384]{1,0:T(8,128)S(1)}, u32[]{:S(2)}, u32[]{:S(2)}) collective-permute-start(f32[192,384]{1,0:T(8,128)S(1)} %collective-permute-done.2.refs_2_), channel_id=1, source_target_pairs={{0,1},{1,0},{2,3},{3,2},{4,5},{5,4},{6,7},{7,6},{8,9},{9,8},{10,11... | collective-permute-start | bytes 884744 | tf_op jit(solution)/shard_map/ppermute | solution.py:31
  21.0 22.0 %collective-permute-start.9 = (f32[192,384]{1,0:T(8,128)S(1)}, f32[192,384]{1,0:T(8,128)S(1)}, u32[]{:S(2)}, u32[]{:S(2)}) collective-permute-start(f32[192,384]{1,0:T(8,128)S(1)} %get-tuple-element.44), channel_id=1, source_target_pairs={{0,4},{1,5},{2,6},{3,7},{4,0},{5,1},{6,2},{7,3},{8,12},{9,13},{10,... | collective-permute-start | bytes 884744 | tf_op jit(solution)/shard_map/ppermute | solution.py:31
  43.0 1.6 %collective-permute-start.10 = (f32[192,384]{1,0:T(8,128)S(1)}, f32[192,384]{1,0:T(8,128)S(1)}, u32[]{:S(2)}, u32[]{:S(2)}) collective-permute-start(f32[192,384]{1,0:T(8,128)S(1)} %collective-permute-done.9.refs_2_), channel_id=1, source_target_pairs={{0,1},{1,0},{2,3},{3,2},{4,5},{5,4},{6,7},{7,6},{8,9},{9,8},{10,11... | collective-permute-start | bytes 884744 | tf_op jit(solution)/shard_map/ppermute | solution.py:31
  46.0 21.6 %collective-permute-start.12 = (f32[192,384]{1,0:T(8,128)S(1)}, f32[192,384]{1,0:T(8,128)S(1)}, u32[]{:S(2)}, u32[]{:S(2)}) collective-permute-start(f32[192,384]{1,0:T(8,128)S(1)} %get-tuple-element.55), channel_id=1, source_target_pairs={{0,12},{1,13},{2,14},{3,15},{4,8},{5,9},{6,10},{7,11},{8,4},{9,5},... | collective-permute-start | bytes 884744 | tf_op jit(solution)/shard_map/ppermute | solution.py:31
  51.8 3.6 %collective-permute-start.5 = (f32[1,384]{1,0:T(1,128)S(1)}, f32[1,384]{1,0:T(1,128)S(1)}, u32[]{:S(2)}, u32[]{:S(2)}) collective-permute-start(f32[1,384]{1,0:T(1,128)S(1)} %get-tuple-element.48.picked), channel_id=1, source_target_pairs={{0,64},{64,0},{128,192},{192,128},{1,65},{65,1},{129,193},{193,129... | collective-permute-start | bytes 4616 | tf_op jit(solution)/shard_map/ppermute | solution.py:469
  56.0 1.2 collective-permute-start.6
  58.0 3.7 %collective-permute-start.7 = (f32[1,384]{1,0:T(1,128)S(1)}, f32[1,384]{1,0:T(1,128)S(1)}, u32[]{:S(2)}, u32[]{:S(2)}) collective-permute-start(f32[1,384]{1,0:T(1,128)S(1)} %shard_map.119.refs_1_), channel_id=1, source_target_pairs={{0,2},{1,3},{2,0},{3,1},{4,6},{5,7},{6,4},{7,5},{8,10},{9,11},{10,... | collective-permute-start | bytes 4616 | tf_op jit(solution)/shard_map/ppermute | solution.py:31
  62.3 4.6 %collective-permute-start.8 = (f32[1,384]{1,0:T(1,128)S(1)}, f32[1,384]{1,0:T(1,128)S(1)}, u32[]{:S(2)}, u32[]{:S(2)}) collective-permute-start(f32[1,384]{1,0:T(1,128)S(1)} %shard_map.120.refs_1_), channel_id=1, source_target_pairs={{0,4},{1,5},{2,6},{3,7},{4,0},{5,1},{6,2},{7,3},{8,12},{9,13},{10,... | collective-permute-start | bytes 4616 | tf_op jit(solution)/shard_map/ppermute | solution.py:31
  67.6 1.9 %collective-permute-start.13 = (f32[192,384]{1,0:T(8,128)S(1)}, f32[192,384]{1,0:T(8,128)S(1)}, u32[]{:S(2)}, u32[]{:S(2)}) collective-permute-start(f32[192,384]{1,0:T(8,128)S(1)} %collective-permute-done.12.refs_2_), channel_id=1, source_target_pairs={{0,1},{1,0},{2,3},{3,2},{4,5},{5,4},{6,7},{7,6},{8,9},{9,8},{10,11... | collective-permute-start | bytes 884744 | tf_op jit(solution)/shard_map/ppermute | solution.py:31
  70.8 9.1 %collective-permute-start.15 = (f32[192,384]{1,0:T(8,128)S(1)}, f32[192,384]{1,0:T(8,128)S(1)}, u32[]{:S(2)}, u32[]{:S(2)}) collective-permute-start(f32[192,384]{1,0:T(8,128)S(1)} %get-tuple-element.69), channel_id=1, source_target_pairs={{0,16},{1,17},{2,18},{3,19},{4,20},{5,21},{6,22},{7,23},{8,24},{9,... | collective-permute-start | bytes 884744 | tf_op jit(solution)/shard_map/ppermute | solution.py:31
  72.4 5.7 %collective-permute-start.11 = (f32[1,384]{1,0:T(1,128)S(1)}, f32[1,384]{1,0:T(1,128)S(1)}, u32[]{:S(2)}, u32[]{:S(2)}) collective-permute-start(f32[1,384]{1,0:T(1,128)S(1)} %shard_map.122.refs_1_), channel_id=1, source_target_pairs={{0,12},{1,13},{2,14},{3,15},{4,8},{5,9},{6,10},{7,11},{8,4},{9,5},... | collective-permute-start | bytes 4616 | tf_op jit(solution)/shard_map/ppermute | solution.py:31
  79.9 7.5 %collective-permute-start.16 = (f32[192,384]{1,0:T(8,128)S(1)}, f32[192,384]{1,0:T(8,128)S(1)}, u32[]{:S(2)}, u32[]{:S(2)}) collective-permute-start(f32[192,384]{1,0:T(8,128)S(1)} %collective-permute-done.15.refs_2_), channel_id=1, source_target_pairs={{0,1},{1,0},{2,3},{3,2},{4,5},{5,4},{6,7},{7,6},{8,9},{9,8},{10,11... | collective-permute-start | bytes 884744 | tf_op jit(solution)/shard_map/ppermute | solution.py:31
  83.2 3.7 %collective-permute-start.14 = (f32[1,384]{1,0:T(1,128)S(1)}, f32[1,384]{1,0:T(1,128)S(1)}, u32[]{:S(2)}, u32[]{:S(2)}) collective-permute-start(f32[1,384]{1,0:T(1,128)S(1)} %shard_map.124.refs_1_), channel_id=1, source_target_pairs={{0,16},{1,17},{2,18},{3,19},{4,20},{5,21},{6,22},{7,23},{8,24},{9,... | collective-permute-start | bytes 4616 | tf_op jit(solution)/shard_map/ppermute | solution.py:31
  88.8 4.9 %collective-permute-start.17 = (f32[1,384]{1,0:T(1,128)S(1)}, f32[1,384]{1,0:T(1,128)S(1)}, u32[]{:S(2)}, u32[]{:S(2)}) collective-permute-start(f32[1,384]{1,0:T(1,128)S(1)} %shard_map.131), channel_id=1, source_target_pairs={{0,48},{1,49},{2,50},{3,51},{4,52},{5,53},{6,54},{7,55},{8,56},{9,... | collective-permute-start | bytes 4616 | tf_op jit(solution)/shard_map/ppermute | solution.py:31
  94.7 1.2 collective-permute-start.18
  96.8 3.7 %collective-permute-start.19 = (f32[1,384]{1,0:T(1,128)S(1)}, f32[1,384]{1,0:T(1,128)S(1)}, u32[]{:S(2)}, u32[]{:S(2)}) collective-permute-start(f32[1,384]{1,0:T(1,128)S(1)} %shard_map.134.refs_1_), channel_id=1, source_target_pairs={{0,2},{1,3},{2,0},{3,1},{4,6},{5,7},{6,4},{7,5},{8,10},{9,11},{10,... | collective-permute-start | bytes 4616 | tf_op jit(solution)/shard_map/ppermute | solution.py:31
  101.2 4.6 %collective-permute-start.20 = (f32[1,384]{1,0:T(1,128)S(1)}, f32[1,384]{1,0:T(1,128)S(1)}, u32[]{:S(2)}, u32[]{:S(2)}) collective-permute-start(f32[1,384]{1,0:T(1,128)S(1)} %shard_map.135.refs_1_), channel_id=1, source_target_pairs={{0,4},{1,5},{2,6},{3,7},{4,0},{5,1},{6,2},{7,3},{8,12},{9,13},{10,... | collective-permute-start | bytes 4616 | tf_op jit(solution)/shard_map/ppermute | solution.py:31
  106.5 5.8 %collective-permute-start.21 = (f32[1,384]{1,0:T(1,128)S(1)}, f32[1,384]{1,0:T(1,128)S(1)}, u32[]{:S(2)}, u32[]{:S(2)}) collective-permute-start(f32[1,384]{1,0:T(1,128)S(1)} %shard_map.136.refs_1_), channel_id=1, source_target_pairs={{0,12},{1,13},{2,14},{3,15},{4,8},{5,9},{6,10},{7,11},{8,4},{9,5},... | collective-permute-start | bytes 4616 | tf_op jit(solution)/shard_map/ppermute | solution.py:31
  113.1 3.7 %collective-permute-start.22 = (f32[1,384]{1,0:T(1,128)S(1)}, f32[1,384]{1,0:T(1,128)S(1)}, u32[]{:S(2)}, u32[]{:S(2)}) collective-permute-start(f32[1,384]{1,0:T(1,128)S(1)} %shard_map.137.refs_1_), channel_id=1, source_target_pairs={{0,16},{1,17},{2,18},{3,19},{4,20},{5,21},{6,22},{7,23},{8,24},{9,... | collective-permute-start | bytes 4616 | tf_op jit(solution)/shard_map/ppermute | solution.py:31
  117.5 4.9 %collective-permute-start.23 = (f32[1,384]{1,0:T(1,128)S(1)}, f32[1,384]{1,0:T(1,128)S(1)}, u32[]{:S(2)}, u32[]{:S(2)}) collective-permute-start(f32[1,384]{1,0:T(1,128)S(1)} %shard_map.139), channel_id=1, source_target_pairs={{0,48},{1,49},{2,50},{3,51},{4,52},{5,53},{6,54},{7,55},{8,56},{9,... | collective-permute-start | bytes 4616 | tf_op jit(solution)/shard_map/ppermute | solution.py:31
  (10 other events, 73.6 us)

commit v2 on v1

--- a/solution.py
+++ b/solution.py
@@ -9,6 +9,7 @@
 IB = 384
 HALF = IB // 2
 GRANT = 12 << 20
+WIDE_GRANT = 60 << 20
 CX, CY, CZ = 4, 32, 128
 DEEP = 3 * CX
 NEAR = CX - 1
@@ -47,28 +48,6 @@
     )(flags, *operands)
 
 
-def pair_call(kernel, flags, blocks, operands, outs, flops=0):
-    count = len(operands)
-
-    def whole(shape):
-        return pl.BlockSpec(shape, lambda i, flags: (0,) * len(shape))
-
-    many = isinstance(outs, (tuple, list))
-    return pl.pallas_call(
-        kernel,
-        out_shape=outs,
-        grid_spec=pltpu.PrefetchScalarGridSpec(
-            num_scalar_prefetch=1,
-            grid=(1,),
-            in_specs=[pl.BlockSpec((1, IB, IB), lambda i, flags: (flags[PAIR], 0, 0)) for _ in blocks]
-            + [whole(o.shape) for o in operands],
-            out_specs=[whole(o.shape) for o in outs] if many else whole(outs.shape),
-        ),
-        compiler_params=pltpu.CompilerParams(vmem_limit_bytes=GRANT),
-        cost_estimate=cost(flops, 4 * IB * IB * len(blocks) + sum(o.size * 4 for o in operands)),
-    )(flags, *blocks, *operands)
-
-
 def halves(value):
     high = value.astype(bf16)
     return high, (value - high.astype(f32)).astype(bf16)
@@ -140,11 +119,11 @@
     return jnp.concatenate([value[:, CZ * g : CZ * g + CZ] for g in range(GROUPS)], axis=0)
 
 
-def spread(values, parity):
+def spread(values):
     row = lax.broadcasted_iota(jnp.int32, (192, 24), 0) // 8
     rows = (row == lax.broadcasted_iota(jnp.int32, (192, 24), 1)).astype(f32).astype(bf16)
     block = lax.broadcasted_iota(jnp.int32, (24, 192), 1) // 8
-    side = (block // 12 + parity) % 2
+    side = block // 12
     dof = 8 * (block % 12 // 4) + 4 * side + block % 4
     columns = (dof == lax.broadcasted_iota(jnp.int32, (24, 192), 0)).astype(f32).astype(bf16)
     tall_values = jnp.dot(rows, values, preferred_element_type=f32).astype(bf16)
@@ -160,7 +139,7 @@
     flags, step, displacement, velocity, external_load, node_mass, modulus,
     outer, inner, stiffness, nodes,
     displacement_out, velocity_out, picked,
-    disp, vel, load, inverse_mass, factor, stiff, features, upper,
+    disp, vel, load, inverse_mass, factor, stiff, even, odd, even_force, odd_force, upper,
 ):
     first = flags[CORE] == 0
 
@@ -203,59 +182,74 @@
     def _():
         factor[2 * CX - 1] = jnp.zeros((8, GROUPS * CZ), f32)
 
-    for parity in range(2):
-        high, low = [spread(s, parity) for s in halves(stiffness[...])]
-        stiff[parity] = jnp.concatenate([high, high, low], axis=1)
+    high, low = [spread(s) for s in halves(stiffness[...])]
+    stiff[...] = jnp.concatenate([high, high, low], axis=1)
     length = step[0]
 
-    def put_features(layer, parity):
+    def put_features(layer, below, above):
         columns = []
         for i in range(3):
             base = disp[i, layer]
             turned = pltpu.roll(base, CZ - 1, 1)
             columns += [base, turned, pltpu.roll(base, CY - 1, 0), pltpu.roll(turned, CY - 1, 0)]
-        start = pl.multiple_of(parity * 96, 16)
         for g in range(GROUPS):
-            lanes = pl.ds(CZ * g, CZ)
+            lanes = slice(CZ * g, CZ * g + CZ)
             block = jnp.concatenate([c[8 * g : 8 * g + 8] for c in columns], axis=0)
             high, low = halves(block)
-            features[pl.ds(start, 96), lanes] = high
-            features[pl.ds(start + 192, 96), lanes] = low
-            features[pl.ds(start + 384, 96), lanes] = high
-
-    def element_layer(layer, finish):
-        parity = layer % 2
-        put_features(layer + 1, 1 - parity)
-        force = jnp.dot(stiff[parity], features[...], preferred_element_type=f32)
+            for target, start in ((below, 96), (above, 0)):
+                if target is not None:
+                    target[start : start + 96, lanes] = high
+                    target[start + 192 : start + 288, lanes] = low
+                    target[start + 384 : start + 480, lanes] = high
+
+    def put_force(source, target):
+        target[...] = jnp.dot(stiff[...], source[...], preferred_element_type=f32)
+
+    def corner(force, scale, i, a, r):
+        start = 8 * (8 * i + 4 * a + r)
+        return force[start : start + 8] * scale
+
+    def keep_upper(layer, force):
+        scale = factor[layer]
+        for i in range(3):
+            for r in range(4):
+                upper[4 * i + r] = corner(force, scale, i, 1, r)
+
+    def finish_layer(layer, force):
         scale = factor[layer]
         weight = inverse_mass[layer]
-
-        def corner(i, a, b, c):
-            start = 8 * (8 * i + 4 * a + 2 * b + c)
-            return force[start : start + 8] * scale
-
         for i in range(3):
-            if finish:
-                sums = [corner(i, 0, r // 2, r % 2) + upper[4 * i + r] for r in range(4)]
-                s00, s01, s10, s11 = [tall(s) for s in sums]
-                base = s00 + pltpu.roll(s10, 1, 0)
-                turned = s01 + pltpu.roll(s11, 1, 0)
-                internal = base + pltpu.roll(turned, 1, 1)
-                speed = vel[i, layer] + length * ((load[i, layer] - internal) * weight)
-                vel[i, layer] = speed
-                disp[i, layer] = disp[i, layer] + length * speed
-            for r in range(4):
-                upper[4 * i + r] = corner(i, 1, r // 2, r % 2)
+            sums = [corner(force, scale, i, 0, r) + upper[4 * i + r] for r in range(4)]
+            s00, s01, s10, s11 = [tall(s) for s in sums]
+            base = s00 + pltpu.roll(s10, 1, 0)
+            turned = s01 + pltpu.roll(s11, 1, 0)
+            internal = base + pltpu.roll(turned, 1, 1)
+            speed = vel[i, layer] + length * ((load[i, layer] - internal) * weight)
+            vel[i, layer] = speed
+            disp[i, layer] = disp[i, layer] + length * speed
 
     def one_substep(k, carry):
-        put_features(k, k % 2)
-        element_layer(k, False)
-
-        def inner_layer(layer, carry):
-            element_layer(layer, True)
+        put_features(k, None, even)
+        put_features(k + 1, even, odd)
+        put_force(even, even_force)
+        put_features(k + 2, odd, even)
+        keep_upper(k, even_force)
+        put_force(odd, odd_force)
+        put_features(k + 3, even, odd)
+
+        def two_layers(pair, carry):
+            layer = k + 1 + 2 * pair
+            put_force(even, even_force)
+            put_features(layer + 3, odd, even)
+            finish_layer(layer, odd_force)
+            keep_upper(layer, odd_force)
+            put_force(odd, odd_force)
+            put_features(layer + 4, even, odd)
+            finish_layer(layer + 1, even_force)
+            keep_upper(layer + 1, even_force)
             return carry
 
-        return lax.fori_loop(k + 1, DEEP - 1 - k, inner_layer, carry)
+        return lax.fori_loop(0, CX + 1 - k, two_layers, carry)
 
     lax.fori_loop(0, flags[STEPS], one_substep, 0)
     displacement_out[...] = disp[:, CX : 2 * CX]
@@ -293,21 +287,45 @@
         in_specs=[SM, SM] + [VM] * 9,
         out_specs=(VM, VM, VM),
         scratch_shapes=[
-            pltpu.VMEM((3, DEEP, CY, CZ), f32),
+            pltpu.VMEM((3, DEEP + 2, CY, CZ), f32),
             pltpu.VMEM((3, DEEP, CY, CZ), f32),
             pltpu.VMEM((3, DEEP, CY, CZ), f32),
             pltpu.VMEM((DEEP, CY, CZ), f32),
             pltpu.VMEM((DEEP, 8, GROUPS * CZ), f32),
-            pltpu.VMEM((2, 192, 576), bf16),
+            pltpu.VMEM((192, 576), bf16),
             pltpu.VMEM((576, GROUPS * CZ), bf16),
+            pltpu.VMEM((576, GROUPS * CZ), bf16),
+            pltpu.VMEM((192, GROUPS * CZ), f32),
+            pltpu.VMEM((192, GROUPS * CZ), f32),
             pltpu.VMEM((12, 8, GROUPS * CZ), f32),
         ],
         compiler_params=pltpu.CompilerParams(vmem_limit_bytes=20 << 20),
         cost_estimate=cost(32 * 2 * 192 * 576 * 512, 3 * 720896),
     )(flags, step, *state, outer, inner, stiffness, nodes)
 
-def transition_kernel(flags, inverse, lower, transition):
-    transition[...] = -product(inverse[0], lower[0])
+def transition_kernel(flags, inverses, lowers, transition, inverse, lower, arrived):
+    copies = [
+        pltpu.make_async_copy(source.at[flags[PAIR]], target, arrived.at[k])
+        for k, (source, target) in enumerate(((inverses, inverse), (lowers, lower)))
+    ]
+    for copy in copies:
+        copy.start()
+    for copy in copies:
+        copy.wait()
+    transition[...] = -product(inverse[...], lower[...])
+
+
+def transition_call(flags, inverses, lowers):
+    far = pl.BlockSpec(memory_space=pltpu.HBM)
+    return pl.pallas_call(
+        transition_kernel,
+        out_shape=(MAT, MAT),
+        in_specs=[SM, far, far],
+        out_specs=(VM, VM),
+        scratch_shapes=[pltpu.VMEM((IB, IB), f32), pltpu.SemaphoreType.DMA((2,))],
+        compiler_params=pltpu.CompilerParams(vmem_limit_bytes=WIDE_GRANT),
+        cost_estimate=cost(6 * IB**3, 8 * IB * IB),
+    )(flags, inverses, lowers)
 
 
 def store_half(flags, half, value_ref):
@@ -364,7 +382,7 @@
 
 def start_kernel(flags, inverse, picked, partner, offset):
     sign = (1 - 2 * flags[SIDE]).astype(f32)
-    offset[...] = apply(inverse[0], sign * (picked[...] - partner[...]))
+    offset[...] = apply(inverse[...], sign * (picked[...] - partner[...]))
 
 
 def forward_kernel(level, flags, own, other, high_matrix, total):
@@ -407,7 +425,7 @@
         suffix[...], other[...]
     )
     sign = (1 - 2 * flags[SIDE]).astype(f32)
-    multiplier = sign * apply_transposed(inverse[0], solved[...] - after)
+    multiplier = sign * apply_transposed(inverse[...], solved[...] - after)
     in_row, in_column = slot_masks(nodes[...])
     chosen = in_column.astype(f32).astype(bf16)
     weight = 1.0 / node_mass[...]
@@ -427,17 +445,18 @@
     return run
 
 
-def first_products(flags, factor_inverse, factor_lower):
+def after(value, *earlier):
+    return lax.optimization_barrier((value, *earlier))[0]
+
+
+def first_products(flags, transition, gate):
     cube = 6 * IB**3
-    transition = pair_call(
-        transition_kernel, flags, [factor_inverse, factor_lower], [], MAT, cube
-    )
-    other = swap(transition, MASKS[0])
+    other = after(swap(transition, MASKS[0]), gate)
     high, low, merged, half = local_call(
         first_merge_kernel, flags, [transition, other], (MAT, MAT, MAT, HALFMAT), cube
     )
     prefix, suffix = local_call(first_reach_kernel, flags, [other], (MAT, MAT))
-    return transition, (merged, half), [(high, low, prefix, suffix)]
+    return (merged, half), [(high, low, prefix, suffix)]
 
 
 def merge_level(flags, level, block, levels, gate=None):
@@ -445,7 +464,7 @@
     merged, half = block
     near = swap(half, MASKS[level])
     if gate is not None:
-        near, _ = lax.optimization_barrier((near, gate))
+        near = after(near, gate)
     far = swap(near, 1)
     last = level == 4
     high, low, *block = local_call(
@@ -462,18 +481,19 @@
 
 
 def coupled_velocity(
-    flags, picked, factor_inverse, transition, block, levels, velocity, node_mass, nodes
+    flags, picked, inverse, transition, block, levels, velocity, node_mass, nodes
 ):
     square = 2 * IB * IB
     count = lax.axis_size("sub")
     partner = lax.ppermute(picked, "sub", [(i, i ^ 1) for i in range(count)])
-    offset = pair_call(start_kernel, flags, [factor_inverse], [picked, partner], ROW, square)
+    offset = local_call(start_kernel, flags, [inverse, picked, partner], ROW, square)
     total, others = offset, []
     for level in range(5):
         others.append(swap(total, MASKS[level]))
         if level >= 2:
             gate = picked if level == 2 else total
             block, levels = merge_level(flags, level, block, levels, gate)
+        others[-1] = after(others[-1], levels[max(level - 1, 1)][2])
         total = local_call(
             bound(level, forward_kernel), flags, [total, others[-1], levels[level][0]], ROW, square
         )
@@ -499,11 +519,10 @@
     entering = local_call(
         bound(0, gathered_kernel, apply_transposed), flags, others + list(suffixes[:4]), ROW, 4 * square
     )
-    return pair_call(
+    return local_call(
         finish_kernel,
         flags,
-        [factor_inverse],
-        [entering, last_other, suffixes[4], solved, velocity, node_mass, nodes],
+        [inverse, entering, last_other, suffixes[4], solved, velocity, node_mass, nodes],
         jax.ShapeDtypeStruct(velocity.shape, f32),
         2 * square,
     )
@@ -537,19 +556,20 @@
     step = coarse_step / substeps.astype(f32)
     state = [displacement[0], velocity[0], external_load[0], node_mass[0], modulus[0]]
     packed = jax.ShapeDtypeStruct((PACKED, CY, CZ), f32)
+    transition, inverse = transition_call(flags, factor_inverse, factor_lower)
     outer, inner = local_call(pack_kernel, flags, state, (packed, packed))
+    block, levels = first_products(flags, transition, outer)
     outer = outer_swap(outer)
     inner = swap(inner, 1)
-    transition, block, levels = first_products(flags, factor_inverse, factor_lower)
     block, levels = merge_level(flags, 1, block, levels)
-    outer, _ = lax.optimization_barrier((outer, block[1]))
+    outer = after(outer, block[1])
     final_displacement, final_velocity, picked = substeps_call(
         flags, step, state, outer, inner, stiffness, interface_nodes
     )
     coupled = coupled_velocity(
         flags,
         picked,
-        factor_inverse,
+        inverse,
         transition,
         block,
         levels,

time: 125 us -> 118 us (0.944)
  Pallas kernels: 45.4 us -> 34.2 us
  waiting for transfers between devices: 39.8 us -> 46.9 us
  starting transfers between devices: 34.9 us -> 32.9 us
    pallas_call x1, Pallas kernels: 18.6 us -> 5.14 us  [substeps_call(): pl.pallas_call(substep_kernel, out_shape=(jax.ShapeDtypeStruct(grid_shape...]
    ppermute x22, waiting for transfers between devices: 36.2 us -> 44.5 us  [swap(): lax.ppermute(value, 'tile', [(i, i ^ mask) for i in range(lax.axis_size('...]
    pallas_call x24 -> x26, Pallas kernels: 22.8 us -> 25.5 us  [local_call(): pl.pallas_call(kernel, out_shape=outs, in_specs=[SM] + [VM] * len(operand...]
    ppermute x22, starting transfers between devices: 34.2 us -> 31.7 us  [swap(): lax.ppermute(value, 'tile', [(i, i ^ mask) for i in range(lax.axis_size('...]
    unnamed x20 -> x22, local copies, waits for them, and re-layouts: 2.59 us -> 1.11 us
    pallas_call x3 -> x1, Pallas kernels: 3.97 us -> 3.59 us  [transition_call(): pl.pallas_call(transition_kernel, out_shape=(MAT, MAT), in_specs=[SM, far...]
  transfers between devices with their start and end apart: 24 -> 24, of which waited for: 19 -> 19; matrix products, arithmetic and copies ran while one was open for 0% -> 0% of each run, Pallas kernels for 26% -> 16%
where the time goes in v2:
time: 118 us
  waiting for transfers between devices  46.9 us (40%)
  Pallas kernels  34.2 us (29%)
  starting transfers between devices  32.9 us (28%)
  local copies, waits for them, and re-layouts  1.78 us (2%)
  between operations  1.66 us (1%)
    ppermute x22, waiting for transfers between devices, swap(): lax.ppermute(value, 'tile', [(i, i ^ mask) for i in range(lax.axis_size('...  44.5 us
    ppermute x22, starting transfers between devices, swap(): lax.ppermute(value, 'tile', [(i, i ^ mask) for i in range(lax.axis_size('...  31.7 us
    pallas_call x26, Pallas kernels, local_call(): pl.pallas_call(kernel, out_shape=outs, in_specs=[SM] + [VM] * len(operand...  25.5 us
    pallas_call x1, Pallas kernels, substeps_call(): pl.pallas_call(substep_kernel, out_shape=(jax.ShapeDtypeStruct(grid_shape...  5.14 us
    pallas_call x1, Pallas kernels, transition_call(): pl.pallas_call(transition_kernel, out_shape=(MAT, MAT), in_specs=[SM, far...  3.59 us
    ppermute x1, waiting for transfers between devices, coupled_velocity(): partner = lax.ppermute(picked, 'sub', [(i, i ^ 1) for i in range(count)])  2.42 us
  transfers between devices with their start and end apart: 24, of which 19 were waited for; matrix products, arithmetic and copies ran while one was open for 0% of the time, Pallas kernels for 16%

profile of v2, /device:TPU:2, one launch (start us, length us, event | category | flops | bytes accessed | tf_op | source)
XLA Modules:
  0.0 117.5 jit_solution(4860645092270119544)
XLA Ops:
  2.0 3.6 %shard_map.114 = (f32[384,384]{1,0:T(8,128)}, f32[384,384]{1,0:T(8,128)}) custom-call(s32[10]{0:T(128)} %stack.43.flags.refs_0_, f32[2,384,384]{2,1,0:T(8,128)} %inverses.1, f32[2,384,384]{2,1,0:T(8,128)} %lowers.1), custom_call_target="tpu_custom_call" | custom-call | flops 339738624 | bytes 1179648 | tf_op jit(solution)/shard_map/pallas_call | solution.py:320
  10.3 2.0 %collective-permute-start.2 = (f32[192,384]{1,0:T(8,128)S(1)}, f32[192,384]{1,0:T(8,128)S(1)}, u32[]{:S(2)}, u32[]{:S(2)}) collective-permute-start(f32[192,384]{1,0:T(8,128)S(1)} %get-tuple-element.53), channel_id=1, source_target_pairs={{0,2},{1,3},{2,0},{3,1},{4,6},{5,7},{6,4},{7,5},{8,10},{9,11},{10,... | collective-permute-start | bytes 884744 | tf_op jit(solution)/shard_map/ppermute | solution.py:32
  14.5 5.2 %collective-permute-done.2.refs_2_ = f32[192,384]{1,0:T(8,128)S(1)} collective-permute-done((f32[192,384]{1,0:T(8,128)S(1)}, f32[192,384]{1,0:T(8,128)S(1)}, u32[]{:S(2)}, u32[]{:S(2)}) %collective-permute-start.2) | collective-permute-done | bytes 294944 | tf_op jit(solution)/shard_map/ppermute | solution.py:32
  22.6 3.4 %collective-permute-start.9 = (f32[192,384]{1,0:T(8,128)S(1)}, f32[192,384]{1,0:T(8,128)S(1)}, u32[]{:S(2)}, u32[]{:S(2)}) collective-permute-start(f32[192,384]{1,0:T(8,128)S(1)} %get-tuple-element.54), channel_id=1, source_target_pairs={{0,4},{1,5},{2,6},{3,7},{4,0},{5,1},{6,2},{7,3},{8,12},{9,13},{10,... | collective-permute-start | bytes 884744 | tf_op jit(solution)/shard_map/ppermute | solution.py:32
  26.0 5.1 %shard_map.117 = (f32[3,4,32,128]{3,2,1,0:T(8,128)}, f32[3,4,32,128]{3,2,1,0:T(8,128)S(1)}, f32[1,384]{1,0:T(1,128)S(1)}) custom-call(s32[10]{0:T(128)S(1)} %copy-done.3, f32[1]{0:T(128)S(6)} %div.14.step, f32[3,4,32,128]{3,2,1,0:T(8,128)S(1)} %bitcast.20, f32[3,4,32,128]{3,2,1,0:T(8,128)S(1)} %bitcast.22, f32[3,4,32,128]{3,2,1,0:T(8,128)S(1)} %bitcast.24, ...), custom_call_target="tpu_custom_call" | custom-call | flops 3623878656 | bytes 2162688 | tf_op jit(solution)/shard_map/pallas_call | solution.py:280
  31.1 8.5 %collective-permute-done.9.refs_2_ = f32[192,384]{1,0:T(8,128)S(1)} collective-permute-done((f32[192,384]{1,0:T(8,128)S(1)}, f32[192,384]{1,0:T(8,128)S(1)}, u32[]{:S(2)}, u32[]{:S(2)}) %collective-permute-start.9) | collective-permute-done | bytes 294944 | tf_op jit(solution)/shard_map/ppermute | solution.py:32
  39.6 1.6 %collective-permute-done.10.refs_3_ = f32[192,384]{1,0:T(8,128)S(1)} collective-permute-done((f32[192,384]{1,0:T(8,128)S(1)}, f32[192,384]{1,0:T(8,128)S(1)}, u32[]{:S(2)}, u32[]{:S(2)}) %collective-permute-start.10) | collective-permute-done | bytes 294944 | tf_op jit(solution)/shard_map/ppermute | solution.py:32
  42.5 3.6 %collective-permute-start.12 = (f32[192,384]{1,0:T(8,128)S(1)}, f32[192,384]{1,0:T(8,128)S(1)}, u32[]{:S(2)}, u32[]{:S(2)}) collective-permute-start(f32[192,384]{1,0:T(8,128)S(1)} %get-tuple-element.77), channel_id=1, source_target_pairs={{0,12},{1,13},{2,14},{3,15},{4,8},{5,9},{6,10},{7,11},{8,4},{9,5},... | collective-permute-start | bytes 884744 | tf_op jit(solution)/shard_map/ppermute | solution.py:32
  47.3 2.4 %collective-permute-done.5.partner = f32[1,384]{1,0:T(1,128)S(1)} collective-permute-done((f32[1,384]{1,0:T(1,128)S(1)}, f32[1,384]{1,0:T(1,128)S(1)}, u32[]{:S(2)}, u32[]{:S(2)}) %collective-permute-start.5) | collective-permute-done | bytes 1568 | tf_op jit(solution)/shard_map/ppermute | solution.py:488
  52.5 3.8 %collective-permute-start.7 = (f32[1,384]{1,0:T(1,128)S(1)}, f32[1,384]{1,0:T(1,128)S(1)}, u32[]{:S(2)}, u32[]{:S(2)}) collective-permute-start(f32[1,384]{1,0:T(1,128)S(1)} %shard_map.121.refs_1_), channel_id=1, source_target_pairs={{0,2},{1,3},{2,0},{3,1},{4,6},{5,7},{6,4},{7,5},{8,10},{9,11},{10,... | collective-permute-start | bytes 4616 | tf_op jit(solution)/shard_map/ppermute | solution.py:32
  58.5 2.1 %collective-permute-start.8 = (f32[1,384]{1,0:T(1,128)S(1)}, f32[1,384]{1,0:T(1,128)S(1)}, u32[]{:S(2)}, u32[]{:S(2)}) collective-permute-start(f32[1,384]{1,0:T(1,128)S(1)} %shard_map.122.refs_1_), channel_id=1, source_target_pairs={{0,4},{1,5},{2,6},{3,7},{4,0},{5,1},{6,2},{7,3},{8,12},{9,13},{10,... | collective-permute-start | bytes 4616 | tf_op jit(solution)/shard_map/ppermute | solution.py:32
  60.6 2.7 %collective-permute-done.8.refs_2_.refs_3_ = f32[1,384]{1,0:T(1,128)S(1)} collective-permute-done((f32[1,384]{1,0:T(1,128)S(1)}, f32[1,384]{1,0:T(1,128)S(1)}, u32[]{:S(2)}, u32[]{:S(2)}) %collective-permute-start.8) | collective-permute-done | bytes 1568 | tf_op jit(solution)/shard_map/ppermute | solution.py:32
  64.1 1.6 %collective-permute-done.13.refs_3_ = f32[192,384]{1,0:T(8,128)S(1)} collective-permute-done((f32[192,384]{1,0:T(8,128)S(1)}, f32[192,384]{1,0:T(8,128)S(1)}, u32[]{:S(2)}, u32[]{:S(2)}) %collective-permute-start.13) | collective-permute-done | bytes 294944 | tf_op jit(solution)/shard_map/ppermute | solution.py:32
  67.0 1.7 %collective-permute-start.15 = (f32[192,384]{1,0:T(8,128)S(1)}, f32[192,384]{1,0:T(8,128)S(1)}, u32[]{:S(2)}, u32[]{:S(2)}) collective-permute-start(f32[192,384]{1,0:T(8,128)S(1)} %get-tuple-element.85), channel_id=1, source_target_pairs={{0,16},{1,17},{2,18},{3,19},{4,20},{5,21},{6,22},{7,23},{8,24},{9,... | collective-permute-start | bytes 884744 | tf_op jit(solution)/shard_map/ppermute | solution.py:32
  70.1 4.2 %collective-permute-done.11.refs_2_.refs_4_ = f32[1,384]{1,0:T(1,128)S(1)} collective-permute-done((f32[1,384]{1,0:T(1,128)S(1)}, f32[1,384]{1,0:T(1,128)S(1)}, u32[]{:S(2)}, u32[]{:S(2)}) %collective-permute-start.11) | collective-permute-done | bytes 1568 | tf_op jit(solution)/shard_map/ppermute | solution.py:32
  76.1 1.6 %collective-permute-start.14 = (f32[1,384]{1,0:T(1,128)S(1)}, f32[1,384]{1,0:T(1,128)S(1)}, u32[]{:S(2)}, u32[]{:S(2)}) collective-permute-start(f32[1,384]{1,0:T(1,128)S(1)} %shard_map.127.refs_1_), channel_id=1, source_target_pairs={{0,16},{1,17},{2,18},{3,19},{4,20},{5,21},{6,22},{7,23},{8,24},{9,... | collective-permute-start | bytes 4616 | tf_op jit(solution)/shard_map/ppermute | solution.py:32
  81.7 3.2 %collective-permute-start.17 = (f32[1,384]{1,0:T(1,128)S(1)}, f32[1,384]{1,0:T(1,128)S(1)}, u32[]{:S(2)}, u32[]{:S(2)}) collective-permute-start(f32[1,384]{1,0:T(1,128)S(1)} %shard_map.131), channel_id=1, source_target_pairs={{0,48},{1,49},{2,50},{3,51},{4,52},{5,53},{6,54},{7,55},{8,56},{9,... | collective-permute-start | bytes 4616 | tf_op jit(solution)/shard_map/ppermute | solution.py:32
  89.6 2.3 %collective-permute-start.19 = (f32[1,384]{1,0:T(1,128)S(1)}, f32[1,384]{1,0:T(1,128)S(1)}, u32[]{:S(2)}, u32[]{:S(2)}) collective-permute-start(f32[1,384]{1,0:T(1,128)S(1)} %shard_map.134.refs_1_), channel_id=1, source_target_pairs={{0,2},{1,3},{2,0},{3,1},{4,6},{5,7},{6,4},{7,5},{8,10},{9,11},{10,... | collective-permute-start | bytes 4616 | tf_op jit(solution)/shard_map/ppermute | solution.py:32
  94.3 1.8 %collective-permute-start.20 = (f32[1,384]{1,0:T(1,128)S(1)}, f32[1,384]{1,0:T(1,128)S(1)}, u32[]{:S(2)}, u32[]{:S(2)}) collective-permute-start(f32[1,384]{1,0:T(1,128)S(1)} %shard_map.135.refs_1_), channel_id=1, source_target_pairs={{0,4},{1,5},{2,6},{3,7},{4,0},{5,1},{6,2},{7,3},{8,12},{9,13},{10,... | collective-permute-start | bytes 4616 | tf_op jit(solution)/shard_map/ppermute | solution.py:32
  96.1 2.8 %collective-permute-done.20.refs_2_.refs_3_ = f32[1,384]{1,0:T(1,128)S(1)} collective-permute-done((f32[1,384]{1,0:T(1,128)S(1)}, f32[1,384]{1,0:T(1,128)S(1)}, u32[]{:S(2)}, u32[]{:S(2)}) %collective-permute-start.20) | collective-permute-done | bytes 1568 | tf_op jit(solution)/shard_map/ppermute | solution.py:32
  100.0 5.4 %collective-permute-done.21.refs_2_.refs_4_ = f32[1,384]{1,0:T(1,128)S(1)} collective-permute-done((f32[1,384]{1,0:T(1,128)S(1)}, f32[1,384]{1,0:T(1,128)S(1)}, u32[]{:S(2)}, u32[]{:S(2)}) %collective-permute-start.21) | collective-permute-done | bytes 1568 | tf_op jit(solution)/shard_map/ppermute | solution.py:32
  106.8 3.1 %collective-permute-done.22.refs_5_.refs_2_ = f32[1,384]{1,0:T(1,128)S(1)} collective-permute-done((f32[1,384]{1,0:T(1,128)S(1)}, f32[1,384]{1,0:T(1,128)S(1)}, u32[]{:S(2)}, u32[]{:S(2)}) %collective-permute-start.22) | collective-permute-done | bytes 1568 | tf_op jit(solution)/shard_map/ppermute | solution.py:32
  110.6 3.2 %collective-permute-start.23 = (f32[1,384]{1,0:T(1,128)S(1)}, f32[1,384]{1,0:T(1,128)S(1)}, u32[]{:S(2)}, u32[]{:S(2)}) collective-permute-start(f32[1,384]{1,0:T(1,128)S(1)} %shard_map.139), channel_id=1, source_target_pairs={{0,48},{1,49},{2,50},{3,51},{4,52},{5,53},{6,54},{7,55},{8,56},{9,... | collective-permute-start | bytes 4616 | tf_op jit(solution)/shard_map/ppermute | solution.py:32
  115.5 2.0 %shard_map.140 = f32[3,4,32,128]{3,2,1,0:T(8,128)} custom-call(s32[10]{0:T(128)S(1)} %copy-done.3, f32[384,384]{1,0:T(8,128)S(1)} %copy-done, f32[1,384]{1,0:T(1,128)S(1)} %shard_map.138.entering, f32[1,384]{1,0:T(1,128)S(1)} %collective-permute-done.23.other, f32[384,384]{1,0:T(8,128)S(1)} %get-tuple-element.93.suffix, ...), custom_call_target="tpu_custom_call" | custom-call | flops 589824 | bytes 1446912 | tf_op jit(solution)/shard_map/pallas_call | solution.py:41
  (75 shorter events, 39.1 us)
Async XLA Ops:
  5.6 2.3 %collective-permute-start.1 = (f32[384,384]{1,0:T(8,128)}, f32[384,384]{1,0:T(8,128)S(1)}, u32[]{:S(2)}, u32[]{:S(2)}) collective-permute-start(f32[384,384]{1,0:T(8,128)} %get-tuple-element.50.own.transition), channel_id=1, source_target_pairs={{0,1},{1,0},{2,3},{3,2},{4,5},{5,4},{6,7},{7,6},{8,9},{9,8},{10,11... | collective-permute-start | bytes 1769480 | tf_op jit(solution)/shard_map/ppermute | solution.py:32
  10.3 9.4 %collective-permute-start.2 = (f32[192,384]{1,0:T(8,128)S(1)}, f32[192,384]{1,0:T(8,128)S(1)}, u32[]{:S(2)}, u32[]{:S(2)}) collective-permute-start(f32[192,384]{1,0:T(8,128)S(1)} %get-tuple-element.53), channel_id=1, source_target_pairs={{0,2},{1,3},{2,0},{3,1},{4,6},{5,7},{6,4},{7,5},{8,10},{9,11},{10,... | collective-permute-start | bytes 884744 | tf_op jit(solution)/shard_map/ppermute | solution.py:32
  12.3 13.6 %collective-permute-start = (f32[37,32,128]{2,1,0:T(8,128)S(1)}, f32[37,32,128]{2,1,0:T(8,128)S(1)}, u32[]{:S(2)}, u32[]{:S(2)}) collective-permute-start(f32[37,32,128]{2,1,0:T(8,128)S(1)} %get-tuple-element.49), channel_id=1, source_target_pairs={{1,2},{2,1},{3,4},{4,3},{5,6},{6,5},{7,8},{8,7},{9,10},{10,9},{11,... | collective-permute-start | bytes 1818632 | tf_op jit(solution)/shard_map/ppermute | solution.py:536
  13.0 13.0 %collective-permute-start.4 = (f32[37,32,128]{2,1,0:T(8,128)S(1)}, f32[37,32,128]{2,1,0:T(8,128)S(1)}, u32[]{:S(2)}, u32[]{:S(2)}) collective-permute-start(f32[37,32,128]{2,1,0:T(8,128)S(1)} %get-tuple-element.56), channel_id=1, source_target_pairs={{0,1},{1,0},{2,3},{3,2},{4,5},{5,4},{6,7},{7,6},{8,9},{9,8},{10,11... | collective-permute-start | bytes 1818632 | tf_op jit(solution)/shard_map/ppermute | solution.py:32
  19.7 1.6 %collective-permute-start.3 = (f32[192,384]{1,0:T(8,128)S(1)}, f32[192,384]{1,0:T(8,128)S(1)}, u32[]{:S(2)}, u32[]{:S(2)}) collective-permute-start(f32[192,384]{1,0:T(8,128)S(1)} %collective-permute-done.2.refs_2_), channel_id=1, source_target_pairs={{0,1},{1,0},{2,3},{3,2},{4,5},{5,4},{6,7},{7,6},{8,9},{9,8},{10,11... | collective-permute-start | bytes 884744 | tf_op jit(solution)/shard_map/ppermute | solution.py:32
  22.6 17.0 %collective-permute-start.9 = (f32[192,384]{1,0:T(8,128)S(1)}, f32[192,384]{1,0:T(8,128)S(1)}, u32[]{:S(2)}, u32[]{:S(2)}) collective-permute-start(f32[192,384]{1,0:T(8,128)S(1)} %get-tuple-element.54), channel_id=1, source_target_pairs={{0,4},{1,5},{2,6},{3,7},{4,0},{5,1},{6,2},{7,3},{8,12},{9,13},{10,... | collective-permute-start | bytes 884744 | tf_op jit(solution)/shard_map/ppermute | solution.py:32
  39.6 1.6 %collective-permute-start.10 = (f32[192,384]{1,0:T(8,128)S(1)}, f32[192,384]{1,0:T(8,128)S(1)}, u32[]{:S(2)}, u32[]{:S(2)}) collective-permute-start(f32[192,384]{1,0:T(8,128)S(1)} %collective-permute-done.9.refs_2_), channel_id=1, source_target_pairs={{0,1},{1,0},{2,3},{3,2},{4,5},{5,4},{6,7},{7,6},{8,9},{9,8},{10,11... | collective-permute-start | bytes 884744 | tf_op jit(solution)/shard_map/ppermute | solution.py:32
  42.5 21.4 %collective-permute-start.12 = (f32[192,384]{1,0:T(8,128)S(1)}, f32[192,384]{1,0:T(8,128)S(1)}, u32[]{:S(2)}, u32[]{:S(2)}) collective-permute-start(f32[192,384]{1,0:T(8,128)S(1)} %get-tuple-element.77), channel_id=1, source_target_pairs={{0,12},{1,13},{2,14},{3,15},{4,8},{5,9},{6,10},{7,11},{8,4},{9,5},... | collective-permute-start | bytes 884744 | tf_op jit(solution)/shard_map/ppermute | solution.py:32
  46.1 3.6 %collective-permute-start.5 = (f32[1,384]{1,0:T(1,128)S(1)}, f32[1,384]{1,0:T(1,128)S(1)}, u32[]{:S(2)}, u32[]{:S(2)}) collective-permute-start(f32[1,384]{1,0:T(1,128)S(1)} %get-tuple-element.59.picked), channel_id=1, source_target_pairs={{0,64},{64,0},{128,192},{192,128},{1,65},{65,1},{129,193},{193,129... | collective-permute-start | bytes 4616 | tf_op jit(solution)/shard_map/ppermute | solution.py:488
  50.4 1.4 %collective-permute-start.6 = (f32[1,384]{1,0:T(1,128)S(1)}, f32[1,384]{1,0:T(1,128)S(1)}, u32[]{:S(2)}, u32[]{:S(2)}) collective-permute-start(f32[1,384]{1,0:T(1,128)S(1)} %shard_map.118.refs_1_.offset), channel_id=1, source_target_pairs={{0,1},{1,0},{2,3},{3,2},{4,5},{5,4},{6,7},{7,6},{8,9},{9,8},{10,11... | collective-permute-start | bytes 4616 | tf_op jit(solution)/shard_map/ppermute | solution.py:32
  52.5 5.3 %collective-permute-start.7 = (f32[1,384]{1,0:T(1,128)S(1)}, f32[1,384]{1,0:T(1,128)S(1)}, u32[]{:S(2)}, u32[]{:S(2)}) collective-permute-start(f32[1,384]{1,0:T(1,128)S(1)} %shard_map.121.refs_1_), channel_id=1, source_target_pairs={{0,2},{1,3},{2,0},{3,1},{4,6},{5,7},{6,4},{7,5},{8,10},{9,11},{10,... | collective-permute-start | bytes 4616 | tf_op jit(solution)/shard_map/ppermute | solution.py:32
  58.5 4.7 %collective-permute-start.8 = (f32[1,384]{1,0:T(1,128)S(1)}, f32[1,384]{1,0:T(1,128)S(1)}, u32[]{:S(2)}, u32[]{:S(2)}) collective-permute-start(f32[1,384]{1,0:T(1,128)S(1)} %shard_map.122.refs_1_), channel_id=1, source_target_pairs={{0,4},{1,5},{2,6},{3,7},{4,0},{5,1},{6,2},{7,3},{8,12},{9,13},{10,... | collective-permute-start | bytes 4616 | tf_op jit(solution)/shard_map/ppermute | solution.py:32
  64.0 1.7 %collective-permute-start.13 = (f32[192,384]{1,0:T(8,128)S(1)}, f32[192,384]{1,0:T(8,128)S(1)}, u32[]{:S(2)}, u32[]{:S(2)}) collective-permute-start(f32[192,384]{1,0:T(8,128)S(1)} %collective-permute-done.12.refs_2_), channel_id=1, source_target_pairs={{0,1},{1,0},{2,3},{3,2},{4,5},{5,4},{6,7},{7,6},{8,9},{9,8},{10,11... | collective-permute-start | bytes 884744 | tf_op jit(solution)/shard_map/ppermute | solution.py:32
  67.0 9.1 %collective-permute-start.15 = (f32[192,384]{1,0:T(8,128)S(1)}, f32[192,384]{1,0:T(8,128)S(1)}, u32[]{:S(2)}, u32[]{:S(2)}) collective-permute-start(f32[192,384]{1,0:T(8,128)S(1)} %get-tuple-element.85), channel_id=1, source_target_pairs={{0,16},{1,17},{2,18},{3,19},{4,20},{5,21},{6,22},{7,23},{8,24},{9,... | collective-permute-start | bytes 884744 | tf_op jit(solution)/shard_map/ppermute | solution.py:32
  68.6 5.7 %collective-permute-start.11 = (f32[1,384]{1,0:T(1,128)S(1)}, f32[1,384]{1,0:T(1,128)S(1)}, u32[]{:S(2)}, u32[]{:S(2)}) collective-permute-start(f32[1,384]{1,0:T(1,128)S(1)} %shard_map.124.refs_1_), channel_id=1, source_target_pairs={{0,12},{1,13},{2,14},{3,15},{4,8},{5,9},{6,10},{7,11},{8,4},{9,5},... | collective-permute-start | bytes 4616 | tf_op jit(solution)/shard_map/ppermute | solution.py:32
  76.1 4.2 %collective-permute-start.16 = (f32[192,384]{1,0:T(8,128)S(1)}, f32[192,384]{1,0:T(8,128)S(1)}, u32[]{:S(2)}, u32[]{:S(2)}) collective-permute-start(f32[192,384]{1,0:T(8,128)S(1)} %collective-permute-done.15.refs_2_), channel_id=1, source_target_pairs={{0,1},{1,0},{2,3},{3,2},{4,5},{5,4},{6,7},{7,6},{8,9},{9,8},{10,11... | collective-permute-start | bytes 884744 | tf_op jit(solution)/shard_map/ppermute | solution.py:32
  76.1 3.6 %collective-permute-start.14 = (f32[1,384]{1,0:T(1,128)S(1)}, f32[1,384]{1,0:T(1,128)S(1)}, u32[]{:S(2)}, u32[]{:S(2)}) collective-permute-start(f32[1,384]{1,0:T(1,128)S(1)} %shard_map.127.refs_1_), channel_id=1, source_target_pairs={{0,16},{1,17},{2,18},{3,19},{4,20},{5,21},{6,22},{7,23},{8,24},{9,... | collective-permute-start | bytes 4616 | tf_op jit(solution)/shard_map/ppermute | solution.py:32
  81.7 4.9 %collective-permute-start.17 = (f32[1,384]{1,0:T(1,128)S(1)}, f32[1,384]{1,0:T(1,128)S(1)}, u32[]{:S(2)}, u32[]{:S(2)}) collective-permute-start(f32[1,384]{1,0:T(1,128)S(1)} %shard_map.131), channel_id=1, source_target_pairs={{0,48},{1,49},{2,50},{3,51},{4,52},{5,53},{6,54},{7,55},{8,56},{9,... | collective-permute-start | bytes 4616 | tf_op jit(solution)/shard_map/ppermute | solution.py:32
  87.6 1.2 %collective-permute-start.18 = (f32[1,384]{1,0:T(1,128)S(1)}, f32[1,384]{1,0:T(1,128)S(1)}, u32[]{:S(2)}, u32[]{:S(2)}) collective-permute-start(f32[1,384]{1,0:T(1,128)S(1)} %get-tuple-element.91.refs_1_), channel_id=1, source_target_pairs={{0,1},{1,0},{2,3},{3,2},{4,5},{5,4},{6,7},{7,6},{8,9},{9,8},{10,11... | collective-permute-start | bytes 4616 | tf_op jit(solution)/shard_map/ppermute | solution.py:32
  89.6 3.9 %collective-permute-start.19 = (f32[1,384]{1,0:T(1,128)S(1)}, f32[1,384]{1,0:T(1,128)S(1)}, u32[]{:S(2)}, u32[]{:S(2)}) collective-permute-start(f32[1,384]{1,0:T(1,128)S(1)} %shard_map.134.refs_1_), channel_id=1, source_target_pairs={{0,2},{1,3},{2,0},{3,1},{4,6},{5,7},{6,4},{7,5},{8,10},{9,11},{10,... | collective-permute-start | bytes 4616 | tf_op jit(solution)/shard_map/ppermute | solution.py:32
  94.3 4.6 %collective-permute-start.20 = (f32[1,384]{1,0:T(1,128)S(1)}, f32[1,384]{1,0:T(1,128)S(1)}, u32[]{:S(2)}, u32[]{:S(2)}) collective-permute-start(f32[1,384]{1,0:T(1,128)S(1)} %shard_map.135.refs_1_), channel_id=1, source_target_pairs={{0,4},{1,5},{2,6},{3,7},{4,0},{5,1},{6,2},{7,3},{8,12},{9,13},{10,... | collective-permute-start | bytes 4616 | tf_op jit(solution)/shard_map/ppermute | solution.py:32
  99.6 5.8 %collective-permute-start.21 = (f32[1,384]{1,0:T(1,128)S(1)}, f32[1,384]{1,0:T(1,128)S(1)}, u32[]{:S(2)}, u32[]{:S(2)}) collective-permute-start(f32[1,384]{1,0:T(1,128)S(1)} %shard_map.136.refs_1_), channel_id=1, source_target_pairs={{0,12},{1,13},{2,14},{3,15},{4,8},{5,9},{6,10},{7,11},{8,4},{9,5},... | collective-permute-start | bytes 4616 | tf_op jit(solution)/shard_map/ppermute | solution.py:32
  106.2 3.7 %collective-permute-start.22 = (f32[1,384]{1,0:T(1,128)S(1)}, f32[1,384]{1,0:T(1,128)S(1)}, u32[]{:S(2)}, u32[]{:S(2)}) collective-permute-start(f32[1,384]{1,0:T(1,128)S(1)} %shard_map.137.refs_1_), channel_id=1, source_target_pairs={{0,16},{1,17},{2,18},{3,19},{4,20},{5,21},{6,22},{7,23},{8,24},{9,... | collective-permute-start | bytes 4616 | tf_op jit(solution)/shard_map/ppermute | solution.py:32
  110.6 4.9 %collective-permute-start.23 = (f32[1,384]{1,0:T(1,128)S(1)}, f32[1,384]{1,0:T(1,128)S(1)}, u32[]{:S(2)}, u32[]{:S(2)}) collective-permute-start(f32[1,384]{1,0:T(1,128)S(1)} %shard_map.139), channel_id=1, source_target_pairs={{0,48},{1,49},{2,50},{3,51},{4,52},{5,53},{6,54},{7,55},{8,56},{9,... | collective-permute-start | bytes 4616 | tf_op jit(solution)/shard_map/ppermute | solution.py:32
  (11 other events, 77.8 us)

commit v3 on v2

--- a/solution.py
+++ b/solution.py
@@ -9,7 +9,6 @@
 IB = 384
 HALF = IB // 2
 GRANT = 12 << 20
-WIDE_GRANT = 60 << 20
 CX, CY, CZ = 4, 32, 128
 DEEP = 3 * CX
 NEAR = CX - 1
@@ -17,6 +16,7 @@
 CORE, PAIR, SIDE, LAST, STEPS = 0, 6, 7, 8, 9
 GROUPS = CY // 8
 MASKS = (1, 2, 4, 12, 16, 48)
+OPPOSITE = 10
 
 coarse_step = 0.1
 f32 = jnp.float32
@@ -303,29 +303,9 @@
         cost_estimate=cost(32 * 2 * 192 * 576 * 512, 3 * 720896),
     )(flags, step, *state, outer, inner, stiffness, nodes)
 
-def transition_kernel(flags, inverses, lowers, transition, inverse, lower, arrived):
-    copies = [
-        pltpu.make_async_copy(source.at[flags[PAIR]], target, arrived.at[k])
-        for k, (source, target) in enumerate(((inverses, inverse), (lowers, lower)))
-    ]
-    for copy in copies:
-        copy.start()
-    for copy in copies:
-        copy.wait()
-    transition[...] = -product(inverse[...], lower[...])
-
-
-def transition_call(flags, inverses, lowers):
-    far = pl.BlockSpec(memory_space=pltpu.HBM)
-    return pl.pallas_call(
-        transition_kernel,
-        out_shape=(MAT, MAT),
-        in_specs=[SM, far, far],
-        out_specs=(VM, VM),
-        scratch_shapes=[pltpu.VMEM((IB, IB), f32), pltpu.SemaphoreType.DMA((2,))],
-        compiler_params=pltpu.CompilerParams(vmem_limit_bytes=WIDE_GRANT),
-        cost_estimate=cost(6 * IB**3, 8 * IB * IB),
-    )(flags, inverses, lowers)
+def transition_kernel(flags, inverses, lowers, transition, inverse):
+    inverse[...] = inverses[flags[PAIR]]
+    transition[...] = -product(inverse[...], lowers[flags[PAIR]])
 
 
 def store_half(flags, half, value_ref):
@@ -355,12 +335,15 @@
     suffix[...] = jnp.where(is_high, identity, other[...])
 
 
+def whole(first, near, far):
+    return jnp.concatenate(
+        [jnp.where(first, near[...], far[...]), jnp.where(first, far[...], near[...])], axis=0
+    )
+
+
 def merge_kernel(level, last, flags, own, near, far, high_ref, low_ref, *outs):
     is_high = flags[level] == 1
-    first = flags[CORE] == 0
-    other = jnp.concatenate(
-        [jnp.where(first, near[...], far[...]), jnp.where(first, far[...], near[...])], axis=0
-    )
+    other = whole(flags[CORE] == 0, near, far)
     high = jnp.where(is_high, own[...], other)
     low = jnp.where(is_high, other, own[...])
     high_ref[...] = high
@@ -369,6 +352,32 @@
         merged, half = outs
         merged[...] = product(high, low)
         store_half(flags, half, merged)
+
+
+def row_kernel(
+    flags, own, near, far, near_across, far_across, near_opposite, far_opposite,
+    high_ref, low_ref, row_high_ref, row_low_ref, merged, half,
+):
+    first = flags[CORE] == 0
+    is_high = flags[2] == 1
+    in_upper = flags[3] == 1
+    other = whole(first, near, far)
+    across = whole(first, near_across, far_across)
+    opposite = whole(first, near_opposite, far_opposite)
+    high = jnp.where(is_high, own[...], other)
+    low = jnp.where(is_high, other, own[...])
+    high_ref[...] = high
+    low_ref[...] = low
+    mine = product(high, low)
+    theirs = product(
+        jnp.where(is_high, opposite, across), jnp.where(is_high, across, opposite)
+    )
+    row_high = jnp.where(in_upper, mine, theirs)
+    row_low = jnp.where(in_upper, theirs, mine)
+    row_high_ref[...] = row_high
+    row_low_ref[...] = row_low
+    merged[...] = product(row_high, row_low)
+    store_half(flags, half, merged)
 
 
 def reach_kernel(level, flags, high, low, prefix, suffix, new_prefix, new_suffix):
@@ -480,6 +489,24 @@
     return block, levels + [(high, low, prefix, suffix)]
 
 
+def row_levels(flags, block, levels, gate):
+    cube = 6 * IB**3
+    merged, half = block
+    blocks = []
+    for mask in (MASKS[2], MASKS[3], OPPOSITE):
+        near = after(swap(half, mask), gate)
+        blocks += [near, swap(near, 1)]
+    high, low, row_high, row_low, *block = local_call(
+        row_kernel, flags, [merged, *blocks], (MAT,) * 5 + (HALFMAT,), 3 * cube
+    )
+    for level, pair in ((2, (high, low)), (3, (row_high, row_low))):
+        reach = local_call(
+            bound(level, reach_kernel), flags, [*pair, *levels[-1][2:]], (MAT, MAT), cube
+        )
+        levels = levels + [(*pair, *reach)]
+    return block, levels
+
+
 def coupled_velocity(
     flags, picked, inverse, transition, block, levels, velocity, node_mass, nodes
 ):
@@ -490,9 +517,10 @@
     total, others = offset, []
     for level in range(5):
         others.append(swap(total, MASKS[level]))
-        if level >= 2:
-            gate = picked if level == 2 else total
-            block, levels = merge_level(flags, level, block, levels, gate)
+        if level == 2:
+            block, levels = row_levels(flags, block, levels, others[-1])
+        if level == 4:
+            block, levels = merge_level(flags, level, block, levels, others[-1])
         others[-1] = after(others[-1], levels[max(level - 1, 1)][2])
         total = local_call(
             bound(level, forward_kernel), flags, [total, others[-1], levels[level][0]], ROW, square
@@ -556,7 +584,9 @@
     step = coarse_step / substeps.astype(f32)
     state = [displacement[0], velocity[0], external_load[0], node_mass[0], modulus[0]]
     packed = jax.ShapeDtypeStruct((PACKED, CY, CZ), f32)
-    transition, inverse = transition_call(flags, factor_inverse, factor_lower)
+    transition, inverse = local_call(
+        transition_kernel, flags, [factor_inverse, factor_lower], (MAT, MAT), 6 * IB**3
+    )
     outer, inner = local_call(pack_kernel, flags, state, (packed, packed))
     block, levels = first_products(flags, transition, outer)
     outer = outer_swap(outer)

time: 118 us -> 114 us (0.966)
  waiting for transfers between devices: 46.9 us -> 33 us
  starting transfers between devices: 32.9 us -> 43 us
  Pallas kernels: 34.2 us -> 32.1 us
    ppermute x22 -> x24, waiting for transfers between devices: 44.5 us -> 32.1 us  [swap(): lax.ppermute(value, 'tile', [(i, i ^ mask) for i in range(lax.axis_size('...]
    ppermute x1, starting transfers between devices: 0.53 us -> 7.08 us  [coupled_velocity(): partner = lax.ppermute(picked, 'sub', [(i, i ^ 1) for i in range(count)])]
    pallas_call x1 -> x0, Pallas kernels: 3.59 us -> none  [transition_call(): pl.pallas_call(transition_kernel, out_shape=(MAT, MAT), in_specs=[SM, far...]
    ppermute x22 -> x24, starting transfers between devices: 31.7 us -> 35.2 us  [swap(): lax.ppermute(value, 'tile', [(i, i ^ mask) for i in range(lax.axis_size('...]
    ppermute x1, waiting for transfers between devices: 2.42 us -> 0.92 us  [coupled_velocity(): partner = lax.ppermute(picked, 'sub', [(i, i ^ 1) for i in range(count)])]
    unnamed x22 -> x18, local copies, waits for them, and re-layouts: 1.11 us -> 2.57 us
    pallas_call x26, Pallas kernels: 25.5 us -> 27 us  [local_call(): pl.pallas_call(kernel, out_shape=outs, in_specs=[SM] + [VM] * len(operand...]
  transfers between devices with their start and end apart: 24 -> 26, of which waited for: 19 -> 18; matrix products, arithmetic and copies ran while one was open for 0% -> 0% of each run, Pallas kernels for 16% -> 16%
where the time goes in v3:
time: 114 us; the launch traced here: 112 us
  starting transfers between devices  43 us (38%)
  waiting for transfers between devices  33 us (29%)
  Pallas kernels  32.1 us (28%)
  local copies, waits for them, and re-layouts  2.66 us (2%)
  between operations  1.64 us (1%)
    ppermute x24, starting transfers between devices, swap(): lax.ppermute(value, 'tile', [(i, i ^ mask) for i in range(lax.axis_size('...  35.2 us
    ppermute x24, waiting for transfers between devices, swap(): lax.ppermute(value, 'tile', [(i, i ^ mask) for i in range(lax.axis_size('...  32.1 us
    pallas_call x26, Pallas kernels, local_call(): pl.pallas_call(kernel, out_shape=outs, in_specs=[SM] + [VM] * len(operand...  27 us
    ppermute x1, starting transfers between devices, coupled_velocity(): partner = lax.ppermute(picked, 'sub', [(i, i ^ 1) for i in range(count)])  7.08 us
    pallas_call x1, Pallas kernels, substeps_call(): pl.pallas_call(substep_kernel, out_shape=(jax.ShapeDtypeStruct(grid_shape...  5.17 us
    unnamed x18, local copies, waits for them, and re-layouts  2.57 us
  transfers between devices with their start and end apart: 26, of which 18 were waited for; matrix products, arithmetic and copies ran while one was open for 0% of the time, Pallas kernels for 16%

profile of v3, /device:TPU:2, one launch (start us, length us, event | category | flops | bytes accessed | tf_op | source)
XLA Modules:
  0.0 112.5 jit_solution(13631531840321905619)
XLA Ops:
  8.7 2.0 %collective-permute-start.2 = (f32[192,384]{1,0:T(8,128)S(1)}, f32[192,384]{1,0:T(8,128)S(1)}, u32[]{:S(2)}, u32[]{:S(2)}) collective-permute-start(f32[192,384]{1,0:T(8,128)S(1)} %get-tuple-element.52), channel_id=1, source_target_pairs={{0,2},{1,3},{2,0},{3,1},{4,6},{5,7},{6,4},{7,5},{8,10},{9,11},{10,... | collective-permute-start | bytes 884744 | tf_op jit(solution)/shard_map/ppermute | solution.py:32
  11.4 1.5 %collective-permute-start.4 = (f32[37,32,128]{2,1,0:T(8,128)S(1)}, f32[37,32,128]{2,1,0:T(8,128)S(1)}, u32[]{:S(2)}, u32[]{:S(2)}) collective-permute-start(f32[37,32,128]{2,1,0:T(8,128)S(1)} %get-tuple-element.55), channel_id=1, source_target_pairs={{0,1},{1,0},{2,3},{3,2},{4,5},{5,4},{6,7},{7,6},{8,9},{9,8},{10,11... | collective-permute-start | bytes 1818632 | tf_op jit(solution)/shard_map/ppermute | solution.py:32
  12.9 5.2 %collective-permute-done.2.refs_2_ = f32[192,384]{1,0:T(8,128)S(1)} collective-permute-done((f32[192,384]{1,0:T(8,128)S(1)}, f32[192,384]{1,0:T(8,128)S(1)}, u32[]{:S(2)}, u32[]{:S(2)}) %collective-permute-start.2) | collective-permute-done | bytes 294944 | tf_op jit(solution)/shard_map/ppermute | solution.py:32
  18.1 1.5 %collective-permute-done.3.refs_3_ = f32[192,384]{1,0:T(8,128)S(1)} collective-permute-done((f32[192,384]{1,0:T(8,128)S(1)}, f32[192,384]{1,0:T(8,128)S(1)}, u32[]{:S(2)}, u32[]{:S(2)}) %collective-permute-start.3) | collective-permute-done | bytes 294944 | tf_op jit(solution)/shard_map/ppermute | solution.py:32
  21.0 7.4 %collective-permute-start.13 = (f32[192,384]{1,0:T(8,128)S(1)}, f32[192,384]{1,0:T(8,128)S(1)}, u32[]{:S(2)}, u32[]{:S(2)}) collective-permute-start(f32[192,384]{1,0:T(8,128)S(1)} %get-tuple-element.53), channel_id=1, source_target_pairs={{0,10},{1,11},{2,8},{3,9},{4,14},{5,15},{6,12},{7,13},{8,2},{9,3},... | collective-permute-start | bytes 884744 | tf_op jit(solution)/shard_map/ppermute | solution.py:32
  29.9 5.2 %shard_map.117 = (f32[3,4,32,128]{3,2,1,0:T(8,128)}, f32[3,4,32,128]{3,2,1,0:T(8,128)S(1)}, f32[1,384]{1,0:T(1,128)S(1)}) custom-call(s32[10]{0:T(128)S(1)} %stack.43.flags.refs_0_, f32[1]{0:T(128)S(6)} %div.14.step, f32[3,4,32,128]{3,2,1,0:T(8,128)S(1)} %bitcast.20, f32[3,4,32,128]{3,2,1,0:T(8,128)S(1)} %bitcast.22, f32[3,4,32,128]{3,2,1,0:T(8,128)S(1)} %bitcast.24, ...), custom_call_target="tpu_custom_call" | custom-call | flops 3623878656 | bytes 2162688 | tf_op jit(solution)/shard_map/pallas_call | solution.py:280
  35.0 7.1 %collective-permute-start.5 = (f32[1,384]{1,0:T(1,128)S(1)}, f32[1,384]{1,0:T(1,128)S(1)}, u32[]{:S(2)}, u32[]{:S(2)}) collective-permute-start(f32[1,384]{1,0:T(1,128)S(1)} %get-tuple-element.58.picked), channel_id=1, source_target_pairs={{0,64},{64,0},{128,192},{192,128},{1,65},{65,1},{129,193},{193,129... | collective-permute-start | bytes 4616 | tf_op jit(solution)/shard_map/ppermute | solution.py:515
  47.2 3.0 %collective-permute-done.7.refs_2_ = f32[1,384]{1,0:T(1,128)S(1)} collective-permute-done((f32[1,384]{1,0:T(1,128)S(1)}, f32[1,384]{1,0:T(1,128)S(1)}, u32[]{:S(2)}, u32[]{:S(2)}) %collective-permute-start.7) | collective-permute-done | bytes 1568 | tf_op jit(solution)/shard_map/ppermute | solution.py:32
  50.9 2.1 %collective-permute-start.8 = (f32[1,384]{1,0:T(1,128)S(1)}, f32[1,384]{1,0:T(1,128)S(1)}, u32[]{:S(2)}, u32[]{:S(2)}) collective-permute-start(f32[1,384]{1,0:T(1,128)S(1)} %shard_map.122.refs_1_), channel_id=1, source_target_pairs={{0,4},{1,5},{2,6},{3,7},{4,0},{5,1},{6,2},{7,3},{8,12},{9,13},{10,... | collective-permute-start | bytes 4616 | tf_op jit(solution)/shard_map/ppermute | solution.py:32
  53.0 2.5 %collective-permute-done.8.refs_2_.refs_3_ = f32[1,384]{1,0:T(1,128)S(1)} collective-permute-done((f32[1,384]{1,0:T(1,128)S(1)}, f32[1,384]{1,0:T(1,128)S(1)}, u32[]{:S(2)}, u32[]{:S(2)}) %collective-permute-start.8) | collective-permute-done | bytes 1568 | tf_op jit(solution)/shard_map/ppermute | solution.py:32
  58.0 2.8 %shard_map.123 = (f32[384,384]{1,0:T(8,128)S(1)}, f32[384,384]{1,0:T(8,128)S(1)}, f32[384,384]{1,0:T(8,128)S(1)}, f32[384,384]{1,0:T(8,128)S(1)}, f32[384,384]{1,0:T(8,128)S(1)}, /*index=5*/f32[192,384]{1,0:T(8,128)S(1)}) custom-call(s32[10]{0:T(128)S(1)} %stack.43.flags.refs_0_, f32[384,384]{1,0:T(8,128)S(1)} %get-tuple-element.68.own, ...), custom_call_target="tpu_custom_call" | custom-call | flops 1019215872 | bytes 2359296 | tf_op jit(solution)/shard_map/pallas_call | solution.py:41
  60.8 1.6 %collective-permute-start.17 = (f32[192,384]{1,0:T(8,128)S(1)}, f32[192,384]{1,0:T(8,128)S(1)}, u32[]{:S(2)}, u32[]{:S(2)}) collective-permute-start(f32[192,384]{1,0:T(8,128)S(1)} %get-tuple-element.83), channel_id=1, source_target_pairs={{0,16},{1,17},{2,18},{3,19},{4,20},{5,21},{6,22},{7,23},{8,24},{9,... | collective-permute-start | bytes 884744 | tf_op jit(solution)/shard_map/ppermute | solution.py:32
  63.2 4.2 %collective-permute-start.15 = (f32[1,384]{1,0:T(1,128)S(1)}, f32[1,384]{1,0:T(1,128)S(1)}, u32[]{:S(2)}, u32[]{:S(2)}) collective-permute-start(f32[1,384]{1,0:T(1,128)S(1)} %shard_map.124.refs_1_), channel_id=1, source_target_pairs={{0,12},{1,13},{2,14},{3,15},{4,8},{5,9},{6,10},{7,11},{8,4},{9,5},... | collective-permute-start | bytes 4616 | tf_op jit(solution)/shard_map/ppermute | solution.py:32
  70.2 3.1 %collective-permute-done.16.refs_5_.refs_2_ = f32[1,384]{1,0:T(1,128)S(1)} collective-permute-done((f32[1,384]{1,0:T(1,128)S(1)}, f32[1,384]{1,0:T(1,128)S(1)}, u32[]{:S(2)}, u32[]{:S(2)}) %collective-permute-start.16) | collective-permute-done | bytes 1568 | tf_op jit(solution)/shard_map/ppermute | solution.py:32
  76.6 2.4 %collective-permute-start.19 = (f32[1,384]{1,0:T(1,128)S(1)}, f32[1,384]{1,0:T(1,128)S(1)}, u32[]{:S(2)}, u32[]{:S(2)}) collective-permute-start(f32[1,384]{1,0:T(1,128)S(1)} %shard_map.130), channel_id=1, source_target_pairs={{0,48},{1,49},{2,50},{3,51},{4,52},{5,53},{6,54},{7,55},{8,56},{9,... | collective-permute-start | bytes 4616 | tf_op jit(solution)/shard_map/ppermute | solution.py:32
  85.4 2.8 %collective-permute-done.21.refs_2_ = f32[1,384]{1,0:T(1,128)S(1)} collective-permute-done((f32[1,384]{1,0:T(1,128)S(1)}, f32[1,384]{1,0:T(1,128)S(1)}, u32[]{:S(2)}, u32[]{:S(2)}) %collective-permute-start.21) | collective-permute-done | bytes 1568 | tf_op jit(solution)/shard_map/ppermute | solution.py:32
  89.0 2.2 %collective-permute-start.22 = (f32[1,384]{1,0:T(1,128)S(1)}, f32[1,384]{1,0:T(1,128)S(1)}, u32[]{:S(2)}, u32[]{:S(2)}) collective-permute-start(f32[1,384]{1,0:T(1,128)S(1)} %shard_map.134.refs_1_), channel_id=1, source_target_pairs={{0,4},{1,5},{2,6},{3,7},{4,0},{5,1},{6,2},{7,3},{8,12},{9,13},{10,... | collective-permute-start | bytes 4616 | tf_op jit(solution)/shard_map/ppermute | solution.py:32
  91.2 2.4 %collective-permute-done.22.refs_2_.refs_3_ = f32[1,384]{1,0:T(1,128)S(1)} collective-permute-done((f32[1,384]{1,0:T(1,128)S(1)}, f32[1,384]{1,0:T(1,128)S(1)}, u32[]{:S(2)}, u32[]{:S(2)}) %collective-permute-start.22) | collective-permute-done | bytes 1568 | tf_op jit(solution)/shard_map/ppermute | solution.py:32
  94.3 4.5 %collective-permute-start.23 = (f32[1,384]{1,0:T(1,128)S(1)}, f32[1,384]{1,0:T(1,128)S(1)}, u32[]{:S(2)}, u32[]{:S(2)}) collective-permute-start(f32[1,384]{1,0:T(1,128)S(1)} %shard_map.135.refs_1_), channel_id=1, source_target_pairs={{0,12},{1,13},{2,14},{3,15},{4,8},{5,9},{6,10},{7,11},{8,4},{9,5},... | collective-permute-start | bytes 4616 | tf_op jit(solution)/shard_map/ppermute | solution.py:32
  98.8 1.6 %collective-permute-done.23.refs_2_.refs_4_ = f32[1,384]{1,0:T(1,128)S(1)} collective-permute-done((f32[1,384]{1,0:T(1,128)S(1)}, f32[1,384]{1,0:T(1,128)S(1)}, u32[]{:S(2)}, u32[]{:S(2)}) %collective-permute-start.23) | collective-permute-done | bytes 1568 | tf_op jit(solution)/shard_map/ppermute | solution.py:32
  101.2 3.6 %collective-permute-done.24.refs_5_.refs_2_ = f32[1,384]{1,0:T(1,128)S(1)} collective-permute-done((f32[1,384]{1,0:T(1,128)S(1)}, f32[1,384]{1,0:T(1,128)S(1)}, u32[]{:S(2)}, u32[]{:S(2)}) %collective-permute-start.24) | collective-permute-done | bytes 1568 | tf_op jit(solution)/shard_map/ppermute | solution.py:32
  105.6 2.4 %collective-permute-start.25 = (f32[1,384]{1,0:T(1,128)S(1)}, f32[1,384]{1,0:T(1,128)S(1)}, u32[]{:S(2)}, u32[]{:S(2)}) collective-permute-start(f32[1,384]{1,0:T(1,128)S(1)} %shard_map.138), channel_id=1, source_target_pairs={{0,48},{1,49},{2,50},{3,51},{4,52},{5,53},{6,54},{7,55},{8,56},{9,... | collective-permute-start | bytes 4616 | tf_op jit(solution)/shard_map/ppermute | solution.py:32
  108.0 1.5 %shard_map.137.entering = f32[1,384]{1,0:T(1,128)S(1)} custom-call(s32[10]{0:T(128)S(1)} %stack.43.flags.refs_0_, f32[1,384]{1,0:T(1,128)S(1)} %collective-permute-done.20.refs_2_.refs_1_, f32[1,384]{1,0:T(1,128)S(1)} %collective-permute-done.21.refs_2_, f32[1,384]{1,0:T(1,128)S(1)} %collective-permute-done.22.refs_2_.refs_3_, ...), custom_call_target="tpu_custom_call" | custom-call | flops 1179648 | bytes 2366976 | tf_op jit(solution)/shard_map/pallas_call | solution.py:41
  110.5 2.0 %shard_map.139 = f32[3,4,32,128]{3,2,1,0:T(8,128)} custom-call(s32[10]{0:T(128)S(1)} %stack.43.flags.refs_0_, f32[384,384]{1,0:T(8,128)S(1)} %get-tuple-element.57.inverse, f32[1,384]{1,0:T(1,128)S(1)} %shard_map.137.entering, f32[1,384]{1,0:T(1,128)S(1)} %collective-permute-done.25.other, f32[384,384]{1,0:T(8,128)S(1)} %get-tuple-element.91.suffix, ...), custom_call_target="tpu_custom_call" | custom-call | flops 589824 | bytes 1446912 | tf_op jit(solution)/shard_map/pallas_call | solution.py:41
  (74 shorter events, 36.4 us)
Async XLA Ops:
  5.3 2.1 %collective-permute-start.1 = (f32[384,384]{1,0:T(8,128)S(1)}, f32[384,384]{1,0:T(8,128)S(1)}, u32[]{:S(2)}, u32[]{:S(2)}) collective-permute-start(f32[384,384]{1,0:T(8,128)S(1)} %get-tuple-element.49.own.transition), channel_id=1, source_target_pairs={{0,1},{1,0},{2,3},{3,2},{4,5},{5,4},{6,7},{7,6},{8,9},{9,8},{10,11... | collective-permute-start | bytes 1769480 | tf_op jit(solution)/shard_map/ppermute | solution.py:32
  8.7 9.4 %collective-permute-start.2 = (f32[192,384]{1,0:T(8,128)S(1)}, f32[192,384]{1,0:T(8,128)S(1)}, u32[]{:S(2)}, u32[]{:S(2)}) collective-permute-start(f32[192,384]{1,0:T(8,128)S(1)} %get-tuple-element.52), channel_id=1, source_target_pairs={{0,2},{1,3},{2,0},{3,1},{4,6},{5,7},{6,4},{7,5},{8,10},{9,11},{10,... | collective-permute-start | bytes 884744 | tf_op jit(solution)/shard_map/ppermute | solution.py:32
  10.7 19.2 %collective-permute-start = (f32[37,32,128]{2,1,0:T(8,128)S(1)}, f32[37,32,128]{2,1,0:T(8,128)S(1)}, u32[]{:S(2)}, u32[]{:S(2)}) collective-permute-start(f32[37,32,128]{2,1,0:T(8,128)S(1)} %get-tuple-element.48), channel_id=1, source_target_pairs={{1,2},{2,1},{3,4},{4,3},{5,6},{6,5},{7,8},{8,7},{9,10},{10,9},{11,... | collective-permute-start | bytes 1818632 | tf_op jit(solution)/shard_map/ppermute | solution.py:564
  11.4 18.5 %collective-permute-start.4 = (f32[37,32,128]{2,1,0:T(8,128)S(1)}, f32[37,32,128]{2,1,0:T(8,128)S(1)}, u32[]{:S(2)}, u32[]{:S(2)}) collective-permute-start(f32[37,32,128]{2,1,0:T(8,128)S(1)} %get-tuple-element.55), channel_id=1, source_target_pairs={{0,1},{1,0},{2,3},{3,2},{4,5},{5,4},{6,7},{7,6},{8,9},{9,8},{10,11... | collective-permute-start | bytes 1818632 | tf_op jit(solution)/shard_map/ppermute | solution.py:32
  18.1 1.6 %collective-permute-start.3 = (f32[192,384]{1,0:T(8,128)S(1)}, f32[192,384]{1,0:T(8,128)S(1)}, u32[]{:S(2)}, u32[]{:S(2)}) collective-permute-start(f32[192,384]{1,0:T(8,128)S(1)} %collective-permute-done.2.refs_2_), channel_id=1, source_target_pairs={{0,1},{1,0},{2,3},{3,2},{4,5},{5,4},{6,7},{7,6},{8,9},{9,8},{10,11... | collective-permute-start | bytes 884744 | tf_op jit(solution)/shard_map/ppermute | solution.py:32
  21.0 34.5 %collective-permute-start.13 = (f32[192,384]{1,0:T(8,128)S(1)}, f32[192,384]{1,0:T(8,128)S(1)}, u32[]{:S(2)}, u32[]{:S(2)}) collective-permute-start(f32[192,384]{1,0:T(8,128)S(1)} %get-tuple-element.53), channel_id=1, source_target_pairs={{0,10},{1,11},{2,8},{3,9},{4,14},{5,15},{6,12},{7,13},{8,2},{9,3},... | collective-permute-start | bytes 884744 | tf_op jit(solution)/shard_map/ppermute | solution.py:32
  28.4 27.1 %collective-permute-start.11 = (f32[192,384]{1,0:T(8,128)S(1)}, f32[192,384]{1,0:T(8,128)S(1)}, u32[]{:S(2)}, u32[]{:S(2)}) collective-permute-start(f32[192,384]{1,0:T(8,128)S(1)} %get-tuple-element.53), channel_id=1, source_target_pairs={{0,12},{1,13},{2,14},{3,15},{4,8},{5,9},{6,10},{7,11},{8,4},{9,5},... | collective-permute-start | bytes 884744 | tf_op jit(solution)/shard_map/ppermute | solution.py:32
  28.9 26.6 %collective-permute-start.9 = (f32[192,384]{1,0:T(8,128)S(1)}, f32[192,384]{1,0:T(8,128)S(1)}, u32[]{:S(2)}, u32[]{:S(2)}) collective-permute-start(f32[192,384]{1,0:T(8,128)S(1)} %get-tuple-element.53), channel_id=1, source_target_pairs={{0,4},{1,5},{2,6},{3,7},{4,0},{5,1},{6,2},{7,3},{8,12},{9,13},{10,... | collective-permute-start | bytes 884744 | tf_op jit(solution)/shard_map/ppermute | solution.py:32
  35.0 8.6 %collective-permute-start.5 = (f32[1,384]{1,0:T(1,128)S(1)}, f32[1,384]{1,0:T(1,128)S(1)}, u32[]{:S(2)}, u32[]{:S(2)}) collective-permute-start(f32[1,384]{1,0:T(1,128)S(1)} %get-tuple-element.58.picked), channel_id=1, source_target_pairs={{0,64},{64,0},{128,192},{192,128},{1,65},{65,1},{129,193},{193,129... | collective-permute-start | bytes 4616 | tf_op jit(solution)/shard_map/ppermute | solution.py:515
  46.5 3.8 %collective-permute-start.7 = (f32[1,384]{1,0:T(1,128)S(1)}, f32[1,384]{1,0:T(1,128)S(1)}, u32[]{:S(2)}, u32[]{:S(2)}) collective-permute-start(f32[1,384]{1,0:T(1,128)S(1)} %shard_map.121.refs_1_), channel_id=1, source_target_pairs={{0,2},{1,3},{2,0},{3,1},{4,6},{5,7},{6,4},{7,5},{8,10},{9,11},{10,... | collective-permute-start | bytes 4616 | tf_op jit(solution)/shard_map/ppermute | solution.py:32
  50.9 4.6 %collective-permute-start.8 = (f32[1,384]{1,0:T(1,128)S(1)}, f32[1,384]{1,0:T(1,128)S(1)}, u32[]{:S(2)}, u32[]{:S(2)}) collective-permute-start(f32[1,384]{1,0:T(1,128)S(1)} %shard_map.122.refs_1_), channel_id=1, source_target_pairs={{0,4},{1,5},{2,6},{3,7},{4,0},{5,1},{6,2},{7,3},{8,12},{9,13},{10,... | collective-permute-start | bytes 4616 | tf_op jit(solution)/shard_map/ppermute | solution.py:32
  55.5 1.7 %collective-permute-start.10 = (f32[192,384]{1,0:T(8,128)S(1)}, f32[192,384]{1,0:T(8,128)S(1)}, u32[]{:S(2)}, u32[]{:S(2)}) collective-permute-start(f32[192,384]{1,0:T(8,128)S(1)} %collective-permute-done.9.near), channel_id=1, source_target_pairs={{0,1},{1,0},{2,3},{3,2},{4,5},{5,4},{6,7},{7,6},{8,9},{9,8},{10,11... | collective-permute-start | bytes 884744 | tf_op jit(solution)/shard_map/ppermute | solution.py:32
  55.6 2.0 %collective-permute-start.12 = (f32[192,384]{1,0:T(8,128)S(1)}, f32[192,384]{1,0:T(8,128)S(1)}, u32[]{:S(2)}, u32[]{:S(2)}) collective-permute-start(f32[192,384]{1,0:T(8,128)S(1)} %collective-permute-done.11.near_across), channel_id=1, source_target_pairs={{0,1},{1,0},{2,3},{3,2},{4,5},{5,4},{6,7},{7,6},{8,9},{9,8},{10,11... | collective-permute-start | bytes 884744 | tf_op jit(solution)/shard_map/ppermute | solution.py:32
  56.1 1.9 %collective-permute-start.14 = (f32[192,384]{1,0:T(8,128)S(1)}, f32[192,384]{1,0:T(8,128)S(1)}, u32[]{:S(2)}, u32[]{:S(2)}) collective-permute-start(f32[192,384]{1,0:T(8,128)S(1)} %collective-permute-done.13.near_opposite), channel_id=1, source_target_pairs={{0,1},{1,0},{2,3},{3,2},{4,5},{5,4},{6,7},{7,6},{8,9},{9,8},{10,11... | collective-permute-start | bytes 884744 | tf_op jit(solution)/shard_map/ppermute | solution.py:32
  60.8 12.5 %collective-permute-start.17 = (f32[192,384]{1,0:T(8,128)S(1)}, f32[192,384]{1,0:T(8,128)S(1)}, u32[]{:S(2)}, u32[]{:S(2)}) collective-permute-start(f32[192,384]{1,0:T(8,128)S(1)} %get-tuple-element.83), channel_id=1, source_target_pairs={{0,16},{1,17},{2,18},{3,19},{4,20},{5,21},{6,22},{7,23},{8,24},{9,... | collective-permute-start | bytes 884744 | tf_op jit(solution)/shard_map/ppermute | solution.py:32
  63.2 5.8 %collective-permute-start.15 = (f32[1,384]{1,0:T(1,128)S(1)}, f32[1,384]{1,0:T(1,128)S(1)}, u32[]{:S(2)}, u32[]{:S(2)}) collective-permute-start(f32[1,384]{1,0:T(1,128)S(1)} %shard_map.124.refs_1_), channel_id=1, source_target_pairs={{0,12},{1,13},{2,14},{3,15},{4,8},{5,9},{6,10},{7,11},{8,4},{9,5},... | collective-permute-start | bytes 4616 | tf_op jit(solution)/shard_map/ppermute | solution.py:32
  69.6 3.7 %collective-permute-start.16 = (f32[1,384]{1,0:T(1,128)S(1)}, f32[1,384]{1,0:T(1,128)S(1)}, u32[]{:S(2)}, u32[]{:S(2)}) collective-permute-start(f32[1,384]{1,0:T(1,128)S(1)} %shard_map.126.refs_1_), channel_id=1, source_target_pairs={{0,16},{1,17},{2,18},{3,19},{4,20},{5,21},{6,22},{7,23},{8,24},{9,... | collective-permute-start | bytes 4616 | tf_op jit(solution)/shard_map/ppermute | solution.py:32
  73.3 1.9 %collective-permute-start.18 = (f32[192,384]{1,0:T(8,128)S(1)}, f32[192,384]{1,0:T(8,128)S(1)}, u32[]{:S(2)}, u32[]{:S(2)}) collective-permute-start(f32[192,384]{1,0:T(8,128)S(1)} %collective-permute-done.17.refs_2_), channel_id=1, source_target_pairs={{0,1},{1,0},{2,3},{3,2},{4,5},{5,4},{6,7},{7,6},{8,9},{9,8},{10,11... | collective-permute-start | bytes 884744 | tf_op jit(solution)/shard_map/ppermute | solution.py:32
  76.6 4.9 %collective-permute-start.19 = (f32[1,384]{1,0:T(1,128)S(1)}, f32[1,384]{1,0:T(1,128)S(1)}, u32[]{:S(2)}, u32[]{:S(2)}) collective-permute-start(f32[1,384]{1,0:T(1,128)S(1)} %shard_map.130), channel_id=1, source_target_pairs={{0,48},{1,49},{2,50},{3,51},{4,52},{5,53},{6,54},{7,55},{8,56},{9,... | collective-permute-start | bytes 4616 | tf_op jit(solution)/shard_map/ppermute | solution.py:32
  84.5 3.7 %collective-permute-start.21 = (f32[1,384]{1,0:T(1,128)S(1)}, f32[1,384]{1,0:T(1,128)S(1)}, u32[]{:S(2)}, u32[]{:S(2)}) collective-permute-start(f32[1,384]{1,0:T(1,128)S(1)} %shard_map.133.refs_1_), channel_id=1, source_target_pairs={{0,2},{1,3},{2,0},{3,1},{4,6},{5,7},{6,4},{7,5},{8,10},{9,11},{10,... | collective-permute-start | bytes 4616 | tf_op jit(solution)/shard_map/ppermute | solution.py:32
  89.0 4.6 %collective-permute-start.22 = (f32[1,384]{1,0:T(1,128)S(1)}, f32[1,384]{1,0:T(1,128)S(1)}, u32[]{:S(2)}, u32[]{:S(2)}) collective-permute-start(f32[1,384]{1,0:T(1,128)S(1)} %shard_map.134.refs_1_), channel_id=1, source_target_pairs={{0,4},{1,5},{2,6},{3,7},{4,0},{5,1},{6,2},{7,3},{8,12},{9,13},{10,... | collective-permute-start | bytes 4616 | tf_op jit(solution)/shard_map/ppermute | solution.py:32
  94.3 6.0 %collective-permute-start.23 = (f32[1,384]{1,0:T(1,128)S(1)}, f32[1,384]{1,0:T(1,128)S(1)}, u32[]{:S(2)}, u32[]{:S(2)}) collective-permute-start(f32[1,384]{1,0:T(1,128)S(1)} %shard_map.135.refs_1_), channel_id=1, source_target_pairs={{0,12},{1,13},{2,14},{3,15},{4,8},{5,9},{6,10},{7,11},{8,4},{9,5},... | collective-permute-start | bytes 4616 | tf_op jit(solution)/shard_map/ppermute | solution.py:32
  101.1 3.7 %collective-permute-start.24 = (f32[1,384]{1,0:T(1,128)S(1)}, f32[1,384]{1,0:T(1,128)S(1)}, u32[]{:S(2)}, u32[]{:S(2)}) collective-permute-start(f32[1,384]{1,0:T(1,128)S(1)} %shard_map.136.refs_1_), channel_id=1, source_target_pairs={{0,16},{1,17},{2,18},{3,19},{4,20},{5,21},{6,22},{7,23},{8,24},{9,... | collective-permute-start | bytes 4616 | tf_op jit(solution)/shard_map/ppermute | solution.py:32
  105.6 4.9 %collective-permute-start.25 = (f32[1,384]{1,0:T(1,128)S(1)}, f32[1,384]{1,0:T(1,128)S(1)}, u32[]{:S(2)}, u32[]{:S(2)}) collective-permute-start(f32[1,384]{1,0:T(1,128)S(1)} %shard_map.138), channel_id=1, source_target_pairs={{0,48},{1,49},{2,50},{3,51},{4,52},{5,53},{6,54},{7,55},{8,56},{9,... | collective-permute-start | bytes 4616 | tf_op jit(solution)/shard_map/ppermute | solution.py:32
  (11 other events, 57.4 us)

commit v4 on v2

--- a/solution.py
+++ b/solution.py
@@ -9,7 +9,6 @@
 IB = 384
 HALF = IB // 2
 GRANT = 12 << 20
-WIDE_GRANT = 60 << 20
 CX, CY, CZ = 4, 32, 128
 DEEP = 3 * CX
 NEAR = CX - 1
@@ -17,6 +16,8 @@
 CORE, PAIR, SIDE, LAST, STEPS = 0, 6, 7, 8, 9
 GROUPS = CY // 8
 MASKS = (1, 2, 4, 12, 16, 48)
+ROW_MASKS = (4, 10, 12)
+ROW_TILES = 16
 
 coarse_step = 0.1
 f32 = jnp.float32
@@ -303,29 +304,8 @@
         cost_estimate=cost(32 * 2 * 192 * 576 * 512, 3 * 720896),
     )(flags, step, *state, outer, inner, stiffness, nodes)
 
-def transition_kernel(flags, inverses, lowers, transition, inverse, lower, arrived):
-    copies = [
-        pltpu.make_async_copy(source.at[flags[PAIR]], target, arrived.at[k])
-        for k, (source, target) in enumerate(((inverses, inverse), (lowers, lower)))
-    ]
-    for copy in copies:
-        copy.start()
-    for copy in copies:
-        copy.wait()
+def transition_kernel(flags, inverse, lower, transition):
     transition[...] = -product(inverse[...], lower[...])
-
-
-def transition_call(flags, inverses, lowers):
-    far = pl.BlockSpec(memory_space=pltpu.HBM)
-    return pl.pallas_call(
-        transition_kernel,
-        out_shape=(MAT, MAT),
-        in_specs=[SM, far, far],
-        out_specs=(VM, VM),
-        scratch_shapes=[pltpu.VMEM((IB, IB), f32), pltpu.SemaphoreType.DMA((2,))],
-        compiler_params=pltpu.CompilerParams(vmem_limit_bytes=WIDE_GRANT),
-        cost_estimate=cost(6 * IB**3, 8 * IB * IB),
-    )(flags, inverses, lowers)
 
 
 def store_half(flags, half, value_ref):
@@ -355,12 +335,15 @@
     suffix[...] = jnp.where(is_high, identity, other[...])
 
 
+def whole(first, near, far):
+    return jnp.concatenate(
+        [jnp.where(first, near[...], far[...]), jnp.where(first, far[...], near[...])], axis=0
+    )
+
+
 def merge_kernel(level, last, flags, own, near, far, high_ref, low_ref, *outs):
     is_high = flags[level] == 1
-    first = flags[CORE] == 0
-    other = jnp.concatenate(
-        [jnp.where(first, near[...], far[...]), jnp.where(first, far[...], near[...])], axis=0
-    )
+    other = whole(flags[CORE] == 0, near, far)
     high = jnp.where(is_high, own[...], other)
     low = jnp.where(is_high, other, own[...])
     high_ref[...] = high
@@ -371,6 +354,86 @@
         store_half(flags, half, merged)
 
 
+def block_index(flags):
+    return flags[2] + 2 * flags[3]
+
+
+def sort_kernel(flags, own, near, far, near_far, far_far, near_across, far_across, blocks):
+    first = flags[CORE] == 0
+    mine = block_index(flags)
+    blocks[mine] = own[...]
+    for change, pieces in enumerate(((near, far), (near_far, far_far), (near_across, far_across))):
+        blocks[mine ^ (change + 1)] = whole(first, *pieces)
+
+
+def row_kernel(flags, blocks, high, low, merged, half):
+    low[...] = product(blocks[1], blocks[0])
+    high[...] = product(blocks[3], blocks[2])
+    merged[...] = product(high[...], low[...])
+    store_half(flags, half, merged)
+
+
+def row_reach_kernel(flags, blocks, high, low, prefix, suffix, new_prefix, new_suffix):
+    base = 2 * flags[3]
+    is_high = flags[2] == 1
+    longer = product(
+        jnp.where(is_high, prefix[...], blocks[base + 1]),
+        jnp.where(is_high, blocks[base], suffix[...]),
+    )
+    new_prefix[...] = jnp.where(is_high, longer, prefix[...])
+    new_suffix[...] = jnp.where(is_high, suffix[...], longer)
+    in_upper = flags[3] == 1
+    longer = product(
+        jnp.where(in_upper, new_prefix[...], high[...]),
+        jnp.where(in_upper, low[...], new_suffix[...]),
+    )
+    new_prefix[...] = jnp.where(in_upper, longer, new_prefix[...])
+    new_suffix[...] = jnp.where(in_upper, new_suffix[...], longer)
+
+
+def ordered(flags, rows):
+    mine = block_index(flags)
+    result = []
+    for block in range(4):
+        change = mine ^ block
+        value = rows[0][...]
+        for k in range(1, 4):
+            value = jnp.where(change == k, rows[k][...], value)
+        result.append(value)
+    return mine, result
+
+
+def row_forward_kernel(flags, own, one, two, three, blocks, total, entering):
+    mine, rows = ordered(flags, (own, one, two, three))
+    state = rows[0]
+    before = jnp.zeros_like(state)
+    for block in range(1, 4):
+        before = jnp.where(mine == block, state, before)
+        state = rows[block] + apply(blocks[block], state)
+    total[...] = state
+    entering[...] = before
+
+
+def row_backward_kernel(flags, own, one, two, three, blocks, total, entering):
+    mine, rows = ordered(flags, (own, one, two, three))
+    state = rows[3]
+    before = jnp.zeros_like(state)
+    for block in range(2, -1, -1):
+        before = jnp.where(mine == block, state, before)
+        state = rows[block] + apply_transposed(blocks[block], state)
+    total[...] = state
+    entering[...] = before
+
+
+def below_row(flags, hop):
+    first_row = flags[4] + flags[5] == 0
+    return jnp.where(first_row, 0.0, hop[...])
+
+
+def hop_kernel(flags, total, hop, merged, leaving):
+    leaving[...] = total[...] + apply(merged[...], below_row(flags, hop))
+
+
 def reach_kernel(level, flags, high, low, prefix, suffix, new_prefix, new_suffix):
     is_high = flags[level] == 1
     longer = product(
@@ -399,20 +462,32 @@
     total[...] = low + apply_transposed(low_matrix[...], high)
 
 
-def gathered_kernel(wanted, operation, flags, *refs):
-    others = refs[:5]
-    matrices = refs[5:9]
-    result = refs[9]
-    result[...] = jnp.where(flags[0] == wanted, others[0][...], 0.0)
-    for level in range(1, 5):
-
-        @pl.when(flags[level] == wanted)
-        def _():
-            result[...] = result[...] + operation(matrices[level - 1][...], others[level][...])
-
-
-def turn_kernel(flags, entering, other, prefix, transition, offset, solved, returning):
-    before = entering[...] + jnp.where(flags[5] == 1, 1.0, 0.0) * apply(prefix[...], other[...])
+def forward_part_kernel(flags, other_0, other_1, in_row, prefix_0, prefix_1, result):
+    result[...] = jnp.where(flags[0] == 1, other_0[...], 0.0) + apply(prefix_1[...], in_row[...])
+
+    @pl.when(flags[1] == 1)
+    def _():
+        result[...] = result[...] + apply(prefix_0[...], other_1[...])
+
+
+def backward_part_kernel(
+    flags, other_0, other_1, in_row, other_4, suffix_0, suffix_1, suffix_3, result
+):
+    result[...] = jnp.where(flags[0] == 0, other_0[...], 0.0) + apply_transposed(
+        suffix_1[...], in_row[...]
+    )
+
+    @pl.when(flags[1] == 0)
+    def _():
+        result[...] = result[...] + apply_transposed(suffix_0[...], other_1[...])
+
+    @pl.when(flags[4] == 0)
+    def _():
+        result[...] = result[...] + apply_transposed(suffix_3[...], other_4[...])
+
+
+def turn_kernel(flags, entering, hop, prefix, transition, offset, solved, returning):
+    before = entering[...] + apply(prefix[...], below_row(flags, hop))
     current = offset[...] + apply(transition[...], before)
     solved[...] = current
     returning[...] = -apply_transposed(transition[...], current)
@@ -480,52 +555,103 @@
     return block, levels + [(high, low, prefix, suffix)]
 
 
+def sorted_blocks(flags, block, gate):
+    merged, half = block
+    pieces = []
+    for mask in ROW_MASKS:
+        near = after(swap(half, mask), gate)
+        pieces += [near, swap(near, 1)]
+    return local_call(
+        sort_kernel, flags, [merged, *pieces], jax.ShapeDtypeStruct((4, IB, IB), f32)
+    )
+
+
 def coupled_velocity(
     flags, picked, inverse, transition, block, levels, velocity, node_mass, nodes
 ):
     square = 2 * IB * IB
+    cube = 6 * IB**3
+    prefix_0, suffix_0 = levels[0][2:]
+    prefix_1, suffix_1 = levels[1][2:]
     count = lax.axis_size("sub")
     partner = lax.ppermute(picked, "sub", [(i, i ^ 1) for i in range(count)])
     offset = local_call(start_kernel, flags, [inverse, picked, partner], ROW, square)
     total, others = offset, []
-    for level in range(5):
-        others.append(swap(total, MASKS[level]))
-        if level >= 2:
-            gate = picked if level == 2 else total
-            block, levels = merge_level(flags, level, block, levels, gate)
-        others[-1] = after(others[-1], levels[max(level - 1, 1)][2])
+    for level in range(2):
+        others.append(after(swap(total, MASKS[level]), prefix_1))
         total = local_call(
             bound(level, forward_kernel), flags, [total, others[-1], levels[level][0]], ROW, square
         )
-    _, lows, prefixes, suffixes = zip(*levels)
-    last_other = swap(total, MASKS[5])
+    arrived = [swap(total, mask) for mask in ROW_MASKS]
+    blocks = sorted_blocks(flags, block, total)
+    total, in_row = local_call(
+        row_forward_kernel, flags, [total, *arrived, blocks], (ROW, ROW), 3 * square
+    )
+    high, low, *row = local_call(
+        row_kernel, flags, [after(blocks, total)], (MAT, MAT, MAT, HALFMAT), 3 * cube
+    )
+    merged = row[0]
+    hop = up_row(total)
+    hop = after(hop, merged)
+    leaving = local_call(hop_kernel, flags, [total, hop, merged], ROW, square)
+    hop = up_row(leaving)
+    prefix_3, suffix_3 = local_call(
+        row_reach_kernel, flags, [blocks, high, low, prefix_1, suffix_1], (MAT, MAT), 2 * cube
+    )
+    row[1] = after(row[1], hop)
+    hop = after(hop, prefix_3)
+    leaving = local_call(hop_kernel, flags, [total, hop, merged], ROW, square)
+    hop = up_row(leaving)
     entering = local_call(
-        bound(1, gathered_kernel, apply), flags, others + list(prefixes[:4]), ROW, 4 * square
-    )
+        forward_part_kernel, flags, [*others, in_row, prefix_0, prefix_1], ROW, 2 * square
+    )
+    hop = after(hop, entering)
     solved, returning = local_call(
         turn_kernel,
         flags,
-        [entering, last_other, prefixes[4], transition, offset],
+        [entering, hop, prefix_3, transition, offset],
         (ROW, ROW),
         3 * square,
     )
     total, others = returning, []
-    for level in range(5):
+    for level in range(2):
         others.append(swap(total, MASKS[level]))
         total = local_call(
-            bound(level, backward_kernel), flags, [total, others[-1], lows[level]], ROW, square
+            bound(level, backward_kernel), flags, [total, others[-1], levels[level][1]], ROW, square
         )
+    arrived = [swap(total, mask) for mask in ROW_MASKS]
+    row, levels = merge_level(
+        flags, 4, row, levels + [None, (None, None, prefix_3, suffix_3)], solved
+    )
+    _, low, _, suffix_4 = levels[4]
+    arrived[-1] = after(arrived[-1], low)
+    total, in_row = local_call(
+        row_backward_kernel, flags, [total, *arrived, blocks], (ROW, ROW), 3 * square
+    )
+    others.append(swap(total, MASKS[4]))
+    total = local_call(
+        bound(4, backward_kernel), flags, [total, after(others[-1], suffix_4), low], ROW, square
+    )
     last_other = swap(total, MASKS[5])
     entering = local_call(
-        bound(0, gathered_kernel, apply_transposed), flags, others + list(suffixes[:4]), ROW, 4 * square
+        backward_part_kernel,
+        flags,
+        [others[0], others[1], in_row, others[2], suffix_0, suffix_1, suffix_3],
+        ROW,
+        3 * square,
     )
     return local_call(
         finish_kernel,
         flags,
-        [inverse, entering, last_other, suffixes[4], solved, velocity, node_mass, nodes],
+        [inverse, entering, after(last_other, entering), suffix_4, solved, velocity, node_mass, nodes],
         jax.ShapeDtypeStruct(velocity.shape, f32),
         2 * square,
     )
+
+
+def up_row(value):
+    count = lax.axis_size("tile")
+    return lax.ppermute(value, "tile", [(i, (i + ROW_TILES) % count) for i in range(count)])
 
 
 def outer_swap(value):
@@ -556,11 +682,14 @@
     step = coarse_step / substeps.astype(f32)
     state = [displacement[0], velocity[0], external_load[0], node_mass[0], modulus[0]]
     packed = jax.ShapeDtypeStruct((PACKED, CY, CZ), f32)
-    transition, inverse = transition_call(flags, factor_inverse, factor_lower)
+    inverse = lax.dynamic_index_in_dim(factor_inverse, sub // 2, 0, keepdims=False)
+    lower = lax.dynamic_index_in_dim(factor_lower, sub // 2, 0, keepdims=False)
+    transition = local_call(transition_kernel, flags, [inverse, lower], MAT, 6 * IB**3)
     outer, inner = local_call(pack_kernel, flags, state, (packed, packed))
     block, levels = first_products(flags, transition, outer)
     outer = outer_swap(outer)
     inner = swap(inner, 1)
+    block = (block[0], after(block[1], inner))
     block, levels = merge_level(flags, 1, block, levels)
     outer = after(outer, block[1])
     final_displacement, final_velocity, picked = substeps_call(

time: 118 us -> 114 us (0.966)
  waiting for transfers between devices: 46.9 us -> 35.5 us
  starting transfers between devices: 32.9 us -> 39.4 us
  Pallas kernels: 34.2 us -> 35.6 us
    ppermute x22 -> x24, waiting for transfers between devices: 44.5 us -> 28.3 us  [swap(): lax.ppermute(value, 'tile', [(i, i ^ mask) for i in range(lax.axis_size('...]
    ppermute x0 -> x3, waiting for transfers between devices: none -> 6.34 us  [up_row(): lax.ppermute(value, 'tile', [(i, (i + ROW_TILES) % count) for i in range(...]
    ppermute x0 -> x3, starting transfers between devices: none -> 4.89 us  [up_row(): lax.ppermute(value, 'tile', [(i, (i + ROW_TILES) % count) for i in range(...]
    ppermute x1, starting transfers between devices: 0.53 us -> 4.4 us  [coupled_velocity(): partner = lax.ppermute(picked, 'sub', [(i, i ^ 1) for i in range(count)])]
    pallas_call x1 -> x0, Pallas kernels: 3.59 us -> none  [transition_call(): pl.pallas_call(transition_kernel, out_shape=(MAT, MAT), in_specs=[SM, far...]
    pallas_call x1, Pallas kernels: 5.14 us -> 7.84 us  [substeps_call(): pl.pallas_call(substep_kernel, out_shape=(jax.ShapeDtypeStruct(grid_shape...]
    pallas_call x26 -> x25, Pallas kernels: 25.5 us -> 27.7 us  [local_call(): pl.pallas_call(kernel, out_shape=outs, in_specs=[SM] + [VM] * len(operand...]
    ppermute x22 -> x24, starting transfers between devices: 31.7 us -> 29.5 us  [swap(): lax.ppermute(value, 'tile', [(i, i ^ mask) for i in range(lax.axis_size('...]
  transfers between devices with their start and end apart: 24 -> 29, of which waited for: 19 -> 15; matrix products, arithmetic and copies ran while one was open for 0% -> 0% of each run, Pallas kernels for 16% -> 25%
where the time goes in v4:
time: 114 us
  starting transfers between devices  39.4 us (35%)
  Pallas kernels  35.6 us (31%)
  waiting for transfers between devices  35.5 us (31%)
  between operations  1.68 us (1%)
  local copies, waits for them, and re-layouts  1.45 us (1%)
    ppermute x24, starting transfers between devices, swap(): lax.ppermute(value, 'tile', [(i, i ^ mask) for i in range(lax.axis_size('...  29.5 us
    ppermute x24, waiting for transfers between devices, swap(): lax.ppermute(value, 'tile', [(i, i ^ mask) for i in range(lax.axis_size('...  28.3 us
    pallas_call x25, Pallas kernels, local_call(): pl.pallas_call(kernel, out_shape=outs, in_specs=[SM] + [VM] * len(operand...  27.7 us
    pallas_call x1, Pallas kernels, substeps_call(): pl.pallas_call(substep_kernel, out_shape=(jax.ShapeDtypeStruct(grid_shape...  7.84 us
    ppermute x3, waiting for transfers between devices, up_row(): lax.ppermute(value, 'tile', [(i, (i + ROW_TILES) % count) for i in range(...  6.34 us
    ppermute x3, starting transfers between devices, up_row(): lax.ppermute(value, 'tile', [(i, (i + ROW_TILES) % count) for i in range(...  4.89 us
    ppermute x1, starting transfers between devices, coupled_velocity(): partner = lax.ppermute(picked, 'sub', [(i, i ^ 1) for i in range(count)])  4.4 us
  transfers between devices with their start and end apart: 29, of which 15 were waited for; matrix products, arithmetic and copies ran while one was open for 0% of the time, Pallas kernels for 25%

profile of v4, /device:TPU:2, one launch (start us, length us, event | category | flops | bytes accessed | tf_op | source)
XLA Modules:
  0.0 113.7 jit_solution(13822316928355116985)
XLA Ops:
  7.5 2.0 %collective-permute-start.3 = (f32[192,384]{1,0:T(8,128)S(1)}, f32[192,384]{1,0:T(8,128)S(1)}, u32[]{:S(2)}, u32[]{:S(2)}) collective-permute-start(f32[192,384]{1,0:T(8,128)S(1)} %get-tuple-element.56), channel_id=1, source_target_pairs={{0,2},{1,3},{2,0},{3,1},{4,6},{5,7},{6,4},{7,5},{8,10},{9,11},{10,... | collective-permute-start | bytes 884744 | tf_op jit(solution)/shard_map/ppermute | solution.py:33
  10.2 6.7 %collective-permute-done.3.refs_2_ = f32[192,384]{1,0:T(8,128)S(1)} collective-permute-done((f32[192,384]{1,0:T(8,128)S(1)}, f32[192,384]{1,0:T(8,128)S(1)}, u32[]{:S(2)}, u32[]{:S(2)}) %collective-permute-start.3) | collective-permute-done | bytes 294944 | tf_op jit(solution)/shard_map/ppermute | solution.py:33
  19.8 6.2 %collective-permute-start.15 = (f32[192,384]{1,0:T(8,128)S(1)}, f32[192,384]{1,0:T(8,128)S(1)}, u32[]{:S(2)}, u32[]{:S(2)}) collective-permute-start(f32[192,384]{1,0:T(8,128)S(1)} %get-tuple-element.57), channel_id=1, source_target_pairs={{0,12},{1,13},{2,14},{3,15},{4,8},{5,9},{6,10},{7,11},{8,4},{9,5},... | collective-permute-start | bytes 884744 | tf_op jit(solution)/shard_map/ppermute | solution.py:33
  25.9 1.8 %collective-permute-start.13 = (f32[192,384]{1,0:T(8,128)S(1)}, f32[192,384]{1,0:T(8,128)S(1)}, u32[]{:S(2)}, u32[]{:S(2)}) collective-permute-start(f32[192,384]{1,0:T(8,128)S(1)} %get-tuple-element.57), channel_id=1, source_target_pairs={{0,10},{1,11},{2,8},{3,9},{4,14},{5,15},{6,12},{7,13},{8,2},{9,3},... | collective-permute-start | bytes 884744 | tf_op jit(solution)/shard_map/ppermute | solution.py:33
  28.8 7.8 %shard_map.117 = (f32[3,4,32,128]{3,2,1,0:T(8,128)}, f32[3,4,32,128]{3,2,1,0:T(8,128)S(1)}, f32[1,384]{1,0:T(1,128)S(1)}) custom-call(s32[10]{0:T(128)S(1)} %stack.43.flags.refs_0_, f32[1]{0:T(128)S(6)} %div.16.step, f32[3,4,32,128]{3,2,1,0:T(8,128)S(1)} %bitcast.24, f32[3,4,32,128]{3,2,1,0:T(8,128)S(1)} %bitcast.26, f32[3,4,32,128]{3,2,1,0:T(8,128)S(1)} %bitcast.28, ...), custom_call_target="tpu_custom_call" | custom-call | flops 3623878656 | bytes 2162688 | tf_op jit(solution)/shard_map/pallas_call | solution.py:281
  36.6 4.4 %collective-permute-start.5 = (f32[1,384]{1,0:T(1,128)S(1)}, f32[1,384]{1,0:T(1,128)S(1)}, u32[]{:S(2)}, u32[]{:S(2)}) collective-permute-start(f32[1,384]{1,0:T(1,128)S(1)} %get-tuple-element.60.picked), channel_id=1, source_target_pairs={{0,64},{64,0},{128,192},{192,128},{1,65},{65,1},{129,193},{193,129... | collective-permute-start | bytes 4616 | tf_op jit(solution)/shard_map/ppermute | solution.py:577
  45.9 3.1 %collective-permute-done.7.refs_2_.other_1 = f32[1,384]{1,0:T(1,128)S(1)} collective-permute-done((f32[1,384]{1,0:T(1,128)S(1)}, f32[1,384]{1,0:T(1,128)S(1)}, u32[]{:S(2)}, u32[]{:S(2)}) %collective-permute-start.7) | collective-permute-done | bytes 1568 | tf_op jit(solution)/shard_map/ppermute | solution.py:33
  49.7 5.1 %collective-permute-done.11.near = f32[192,384]{1,0:T(8,128)S(1)} collective-permute-done((f32[192,384]{1,0:T(8,128)S(1)}, f32[192,384]{1,0:T(8,128)S(1)}, u32[]{:S(2)}, u32[]{:S(2)}) %collective-permute-start.11) | collective-permute-done | bytes 294944 | tf_op jit(solution)/shard_map/ppermute | solution.py:33
  55.6 2.0 %collective-permute-start.10 = (f32[1,384]{1,0:T(1,128)S(1)}, f32[1,384]{1,0:T(1,128)S(1)}, u32[]{:S(2)}, u32[]{:S(2)}) collective-permute-start(f32[1,384]{1,0:T(1,128)S(1)} %shard_map.122.own), channel_id=1, source_target_pairs={{0,12},{1,13},{2,14},{3,15},{4,8},{5,9},{6,10},{7,11},{8,4},{9,5},... | collective-permute-start | bytes 4616 | tf_op jit(solution)/shard_map/ppermute | solution.py:33
  57.6 2.1 %collective-permute-start.9 = (f32[1,384]{1,0:T(1,128)S(1)}, f32[1,384]{1,0:T(1,128)S(1)}, u32[]{:S(2)}, u32[]{:S(2)}) collective-permute-start(f32[1,384]{1,0:T(1,128)S(1)} %shard_map.122.own), channel_id=1, source_target_pairs={{0,10},{1,11},{2,8},{3,9},{4,14},{5,15},{6,12},{7,13},{8,2},{9,3},... | collective-permute-start | bytes 4616 | tf_op jit(solution)/shard_map/ppermute | solution.py:33
  61.5 2.7 %collective-permute-done.9.two = f32[1,384]{1,0:T(1,128)S(1)} collective-permute-done((f32[1,384]{1,0:T(1,128)S(1)}, f32[1,384]{1,0:T(1,128)S(1)}, u32[]{:S(2)}, u32[]{:S(2)}) %collective-permute-start.9) | collective-permute-done | bytes 1568 | tf_op jit(solution)/shard_map/ppermute | solution.py:33
  66.8 2.7 %shard_map.126 = (f32[384,384]{1,0:T(8,128)S(1)}, f32[384,384]{1,0:T(8,128)S(1)}, f32[384,384]{1,0:T(8,128)S(1)}, f32[192,384]{1,0:T(8,128)S(1)}) custom-call(s32[10]{0:T(128)S(1)} %stack.43.flags.refs_0_, f32[4,384,384]{2,1,0:T(8,128)S(1)} %shard_map.123.blocks), custom_call_target="tpu_custom_call" | custom-call | flops 1019215872 | bytes 2359296 | tf_op jit(solution)/shard_map/pallas_call | solution.py:42
  71.8 3.7 %collective-permute-done.18.hop = f32[1,384]{1,0:T(1,128)S(1)} collective-permute-done((f32[1,384]{1,0:T(1,128)S(1)}, f32[1,384]{1,0:T(1,128)S(1)}, u32[]{:S(2)}, u32[]{:S(2)}) %collective-permute-start.18) | collective-permute-done | bytes 1568 | tf_op jit(solution)/shard_map/ppermute | solution.py:654
  75.6 2.2 %shard_map.128 = (f32[384,384]{1,0:T(8,128)S(1)}, f32[384,384]{1,0:T(8,128)S(1)}) custom-call(s32[10]{0:T(128)S(1)} %stack.43.flags.refs_0_, f32[4,384,384]{2,1,0:T(8,128)S(1)} %shard_map.123.blocks, f32[384,384]{1,0:T(8,128)S(1)} %get-tuple-element.78.high, f32[384,384]{1,0:T(8,128)S(1)} %get-tuple-element.79.low, ...), custom_call_target="tpu_custom_call" | custom-call | flops 679477248 | bytes 4718592 | tf_op jit(solution)/shard_map/pallas_call | solution.py:42
  78.5 2.1 %collective-permute-start.19 = (f32[1,384]{1,0:T(1,128)S(1)}, f32[1,384]{1,0:T(1,128)S(1)}, u32[]{:S(2)}, u32[]{:S(2)}) collective-permute-start(f32[1,384]{1,0:T(1,128)S(1)} %shard_map.129), channel_id=1, source_target_pairs={{0,16},{1,17},{2,18},{3,19},{4,20},{5,21},{6,22},{7,23},{8,24},{9,... | collective-permute-start | bytes 4616 | tf_op jit(solution)/shard_map/ppermute | solution.py:654
  81.3 2.1 %collective-permute-done.19.hop = f32[1,384]{1,0:T(1,128)S(1)} collective-permute-done((f32[1,384]{1,0:T(1,128)S(1)}, f32[1,384]{1,0:T(1,128)S(1)}, u32[]{:S(2)}, u32[]{:S(2)}) %collective-permute-start.19) | collective-permute-done | bytes 1568 | tf_op jit(solution)/shard_map/ppermute | solution.py:654
  86.9 2.1 %collective-permute-start.21 = (f32[1,384]{1,0:T(1,128)S(1)}, f32[1,384]{1,0:T(1,128)S(1)}, u32[]{:S(2)}, u32[]{:S(2)}) collective-permute-start(f32[1,384]{1,0:T(1,128)S(1)} %shard_map.131.refs_1_), channel_id=1, source_target_pairs={{0,2},{1,3},{2,0},{3,1},{4,6},{5,7},{6,4},{7,5},{8,10},{9,11},{10,... | collective-permute-start | bytes 4616 | tf_op jit(solution)/shard_map/ppermute | solution.py:33
  91.3 3.3 %collective-permute-start.24 = (f32[1,384]{1,0:T(1,128)S(1)}, f32[1,384]{1,0:T(1,128)S(1)}, u32[]{:S(2)}, u32[]{:S(2)}) collective-permute-start(f32[1,384]{1,0:T(1,128)S(1)} %shard_map.132.own), channel_id=1, source_target_pairs={{0,12},{1,13},{2,14},{3,15},{4,8},{5,9},{6,10},{7,11},{8,4},{9,5},... | collective-permute-start | bytes 4616 | tf_op jit(solution)/shard_map/ppermute | solution.py:33
  94.6 2.1 %collective-permute-start.23 = (f32[1,384]{1,0:T(1,128)S(1)}, f32[1,384]{1,0:T(1,128)S(1)}, u32[]{:S(2)}, u32[]{:S(2)}) collective-permute-start(f32[1,384]{1,0:T(1,128)S(1)} %shard_map.132.own), channel_id=1, source_target_pairs={{0,10},{1,11},{2,8},{3,9},{4,14},{5,15},{6,12},{7,13},{8,2},{9,3},... | collective-permute-start | bytes 4616 | tf_op jit(solution)/shard_map/ppermute | solution.py:33
  96.7 1.7 %collective-permute-start.22 = (f32[1,384]{1,0:T(1,128)S(1)}, f32[1,384]{1,0:T(1,128)S(1)}, u32[]{:S(2)}, u32[]{:S(2)}) collective-permute-start(f32[1,384]{1,0:T(1,128)S(1)} %shard_map.132.own), channel_id=1, source_target_pairs={{0,4},{1,5},{2,6},{3,7},{4,0},{5,1},{6,2},{7,3},{8,12},{9,13},{10,... | collective-permute-start | bytes 4616 | tf_op jit(solution)/shard_map/ppermute | solution.py:33
  99.1 2.0 %collective-permute-done.23.two = f32[1,384]{1,0:T(1,128)S(1)} collective-permute-done((f32[1,384]{1,0:T(1,128)S(1)}, f32[1,384]{1,0:T(1,128)S(1)}, u32[]{:S(2)}, u32[]{:S(2)}) %collective-permute-start.23) | collective-permute-done | bytes 1568 | tf_op jit(solution)/shard_map/ppermute | solution.py:33
  103.2 2.1 %shard_map.136 = (f32[384,384]{1,0:T(8,128)}, f32[384,384]{1,0:T(8,128)S(1)}) custom-call(s32[10]{0:T(128)S(1)} %stack.43.flags.refs_0_, f32[384,384]{1,0:T(8,128)S(1)} %get-tuple-element.95.refs_1_, f32[384,384]{1,0:T(8,128)S(1)} %get-tuple-element.90.refs_2_.refs_3_, f32[384,384]{1,0:T(8,128)S(1)} %get-tuple-element.81.prefix.refs_3_, ...), custom_call_target="tpu_custom_call" | custom-call | flops 339738624 | bytes 2359296 | tf_op jit(solution)/shard_map/pallas_call | solution.py:42
  108.6 3.0 %collective-permute-done.28.other = f32[1,384]{1,0:T(1,128)S(1)} collective-permute-done((f32[1,384]{1,0:T(1,128)S(1)}, f32[1,384]{1,0:T(1,128)S(1)}, u32[]{:S(2)}, u32[]{:S(2)}) %collective-permute-start.28) | collective-permute-done | bytes 1568 | tf_op jit(solution)/shard_map/ppermute | solution.py:33
  111.7 2.0 %shard_map.138 = f32[3,4,32,128]{3,2,1,0:T(8,128)} custom-call(s32[10]{0:T(128)S(1)} %stack.43.flags.refs_0_, f32[384,384]{1,0:T(8,128)S(1)} %get-tuple-element.101.inverse, f32[1,384]{1,0:T(1,128)S(1)} %shard_map.135.entering, f32[1,384]{1,0:T(1,128)S(1)} %collective-permute-done.28.other, f32[384,384]{1,0:T(8,128)S(1)} %get-tuple-element.96.suffix, ...), custom_call_target="tpu_custom_call" | custom-call | flops 589824 | bytes 1446912 | tf_op jit(solution)/shard_map/pallas_call | solution.py:42
  (76 shorter events, 37.0 us)
Async XLA Ops:
  7.5 9.4 %collective-permute-start.3 = (f32[192,384]{1,0:T(8,128)S(1)}, f32[192,384]{1,0:T(8,128)S(1)}, u32[]{:S(2)}, u32[]{:S(2)}) collective-permute-start(f32[192,384]{1,0:T(8,128)S(1)} %get-tuple-element.56), channel_id=1, source_target_pairs={{0,2},{1,3},{2,0},{3,1},{4,6},{5,7},{6,4},{7,5},{8,10},{9,11},{10,... | collective-permute-start | bytes 884744 | tf_op jit(solution)/shard_map/ppermute | solution.py:33
  9.5 19.3 %collective-permute-start = (f32[37,32,128]{2,1,0:T(8,128)S(1)}, f32[37,32,128]{2,1,0:T(8,128)S(1)}, u32[]{:S(2)}, u32[]{:S(2)}) collective-permute-start(f32[37,32,128]{2,1,0:T(8,128)S(1)} %get-tuple-element.51), channel_id=1, source_target_pairs={{1,2},{2,1},{3,4},{4,3},{5,6},{6,5},{7,8},{8,7},{9,10},{10,9},{11,... | collective-permute-start | bytes 1818632 | tf_op jit(solution)/shard_map/ppermute | solution.py:662
  19.8 35.0 %collective-permute-start.15 = (f32[192,384]{1,0:T(8,128)S(1)}, f32[192,384]{1,0:T(8,128)S(1)}, u32[]{:S(2)}, u32[]{:S(2)}) collective-permute-start(f32[192,384]{1,0:T(8,128)S(1)} %get-tuple-element.57), channel_id=1, source_target_pairs={{0,12},{1,13},{2,14},{3,15},{4,8},{5,9},{6,10},{7,11},{8,4},{9,5},... | collective-permute-start | bytes 884744 | tf_op jit(solution)/shard_map/ppermute | solution.py:33
  25.9 28.9 %collective-permute-start.13 = (f32[192,384]{1,0:T(8,128)S(1)}, f32[192,384]{1,0:T(8,128)S(1)}, u32[]{:S(2)}, u32[]{:S(2)}) collective-permute-start(f32[192,384]{1,0:T(8,128)S(1)} %get-tuple-element.57), channel_id=1, source_target_pairs={{0,10},{1,11},{2,8},{3,9},{4,14},{5,15},{6,12},{7,13},{8,2},{9,3},... | collective-permute-start | bytes 884744 | tf_op jit(solution)/shard_map/ppermute | solution.py:33
  27.7 27.1 %collective-permute-start.11 = (f32[192,384]{1,0:T(8,128)S(1)}, f32[192,384]{1,0:T(8,128)S(1)}, u32[]{:S(2)}, u32[]{:S(2)}) collective-permute-start(f32[192,384]{1,0:T(8,128)S(1)} %get-tuple-element.57), channel_id=1, source_target_pairs={{0,4},{1,5},{2,6},{3,7},{4,0},{5,1},{6,2},{7,3},{8,12},{9,13},{10,... | collective-permute-start | bytes 884744 | tf_op jit(solution)/shard_map/ppermute | solution.py:33
  36.6 6.0 %collective-permute-start.5 = (f32[1,384]{1,0:T(1,128)S(1)}, f32[1,384]{1,0:T(1,128)S(1)}, u32[]{:S(2)}, u32[]{:S(2)}) collective-permute-start(f32[1,384]{1,0:T(1,128)S(1)} %get-tuple-element.60.picked), channel_id=1, source_target_pairs={{0,64},{64,0},{128,192},{192,128},{1,65},{65,1},{129,193},{193,129... | collective-permute-start | bytes 4616 | tf_op jit(solution)/shard_map/ppermute | solution.py:577
  45.4 3.7 %collective-permute-start.7 = (f32[1,384]{1,0:T(1,128)S(1)}, f32[1,384]{1,0:T(1,128)S(1)}, u32[]{:S(2)}, u32[]{:S(2)}) collective-permute-start(f32[1,384]{1,0:T(1,128)S(1)} %shard_map.121.refs_1_), channel_id=1, source_target_pairs={{0,2},{1,3},{2,0},{3,1},{4,6},{5,7},{6,4},{7,5},{8,10},{9,11},{10,... | collective-permute-start | bytes 4616 | tf_op jit(solution)/shard_map/ppermute | solution.py:33
  54.8 4.9 %collective-permute-start.12 = (f32[192,384]{1,0:T(8,128)S(1)}, f32[192,384]{1,0:T(8,128)S(1)}, u32[]{:S(2)}, u32[]{:S(2)}) collective-permute-start(f32[192,384]{1,0:T(8,128)S(1)} %collective-permute-done.11.near), channel_id=1, source_target_pairs={{0,1},{1,0},{2,3},{3,2},{4,5},{5,4},{6,7},{7,6},{8,9},{9,8},{10,11... | collective-permute-start | bytes 884744 | tf_op jit(solution)/shard_map/ppermute | solution.py:33
  54.8 5.9 %collective-permute-start.14 = (f32[192,384]{1,0:T(8,128)S(1)}, f32[192,384]{1,0:T(8,128)S(1)}, u32[]{:S(2)}, u32[]{:S(2)}) collective-permute-start(f32[192,384]{1,0:T(8,128)S(1)} %collective-permute-done.13.near_far), channel_id=1, source_target_pairs={{0,1},{1,0},{2,3},{3,2},{4,5},{5,4},{6,7},{7,6},{8,9},{9,8},{10,11... | collective-permute-start | bytes 884744 | tf_op jit(solution)/shard_map/ppermute | solution.py:33
  55.3 5.4 %collective-permute-start.16 = (f32[192,384]{1,0:T(8,128)S(1)}, f32[192,384]{1,0:T(8,128)S(1)}, u32[]{:S(2)}, u32[]{:S(2)}) collective-permute-start(f32[192,384]{1,0:T(8,128)S(1)} %collective-permute-done.15.near_across), channel_id=1, source_target_pairs={{0,1},{1,0},{2,3},{3,2},{4,5},{5,4},{6,7},{7,6},{8,9},{9,8},{10,11... | collective-permute-start | bytes 884744 | tf_op jit(solution)/shard_map/ppermute | solution.py:33
  55.6 5.9 %collective-permute-start.10 = (f32[1,384]{1,0:T(1,128)S(1)}, f32[1,384]{1,0:T(1,128)S(1)}, u32[]{:S(2)}, u32[]{:S(2)}) collective-permute-start(f32[1,384]{1,0:T(1,128)S(1)} %shard_map.122.own), channel_id=1, source_target_pairs={{0,12},{1,13},{2,14},{3,15},{4,8},{5,9},{6,10},{7,11},{8,4},{9,5},... | collective-permute-start | bytes 4616 | tf_op jit(solution)/shard_map/ppermute | solution.py:33
  57.6 6.6 %collective-permute-start.9 = (f32[1,384]{1,0:T(1,128)S(1)}, f32[1,384]{1,0:T(1,128)S(1)}, u32[]{:S(2)}, u32[]{:S(2)}) collective-permute-start(f32[1,384]{1,0:T(1,128)S(1)} %shard_map.122.own), channel_id=1, source_target_pairs={{0,10},{1,11},{2,8},{3,9},{4,14},{5,15},{6,12},{7,13},{8,2},{9,3},... | collective-permute-start | bytes 4616 | tf_op jit(solution)/shard_map/ppermute | solution.py:33
  59.7 4.5 %collective-permute-start.8 = (f32[1,384]{1,0:T(1,128)S(1)}, f32[1,384]{1,0:T(1,128)S(1)}, u32[]{:S(2)}, u32[]{:S(2)}) collective-permute-start(f32[1,384]{1,0:T(1,128)S(1)} %shard_map.122.own), channel_id=1, source_target_pairs={{0,4},{1,5},{2,6},{3,7},{4,0},{5,1},{6,2},{7,3},{8,12},{9,13},{10,... | collective-permute-start | bytes 4616 | tf_op jit(solution)/shard_map/ppermute | solution.py:33
  65.1 4.9 %collective-permute-start.17 = (f32[1,384]{1,0:T(1,128)S(1)}, f32[1,384]{1,0:T(1,128)S(1)}, u32[]{:S(2)}, u32[]{:S(2)}) collective-permute-start(f32[1,384]{1,0:T(1,128)S(1)} %get-tuple-element.74.total), channel_id=1, source_target_pairs={{0,16},{1,17},{2,18},{3,19},{4,20},{5,21},{6,22},{7,23},{8,24},{9,... | collective-permute-start | bytes 4616 | tf_op jit(solution)/shard_map/ppermute | solution.py:654
  70.7 4.9 %collective-permute-start.18 = (f32[1,384]{1,0:T(1,128)S(1)}, f32[1,384]{1,0:T(1,128)S(1)}, u32[]{:S(2)}, u32[]{:S(2)}) collective-permute-start(f32[1,384]{1,0:T(1,128)S(1)} %shard_map.127), channel_id=1, source_target_pairs={{0,16},{1,17},{2,18},{3,19},{4,20},{5,21},{6,22},{7,23},{8,24},{9,... | collective-permute-start | bytes 4616 | tf_op jit(solution)/shard_map/ppermute | solution.py:654
  75.6 8.8 %collective-permute-start.25 = (f32[192,384]{1,0:T(8,128)S(1)}, f32[192,384]{1,0:T(8,128)S(1)}, u32[]{:S(2)}, u32[]{:S(2)}) collective-permute-start(f32[192,384]{1,0:T(8,128)S(1)} %get-tuple-element.87), channel_id=1, source_target_pairs={{0,16},{1,17},{2,18},{3,19},{4,20},{5,21},{6,22},{7,23},{8,24},{9,... | collective-permute-start | bytes 884744 | tf_op jit(solution)/shard_map/ppermute | solution.py:33
  78.5 4.9 %collective-permute-start.19 = (f32[1,384]{1,0:T(1,128)S(1)}, f32[1,384]{1,0:T(1,128)S(1)}, u32[]{:S(2)}, u32[]{:S(2)}) collective-permute-start(f32[1,384]{1,0:T(1,128)S(1)} %shard_map.129), channel_id=1, source_target_pairs={{0,16},{1,17},{2,18},{3,19},{4,20},{5,21},{6,22},{7,23},{8,24},{9,... | collective-permute-start | bytes 4616 | tf_op jit(solution)/shard_map/ppermute | solution.py:654
  84.4 14.0 %collective-permute-start.26 = (f32[192,384]{1,0:T(8,128)S(1)}, f32[192,384]{1,0:T(8,128)S(1)}, u32[]{:S(2)}, u32[]{:S(2)}) collective-permute-start(f32[192,384]{1,0:T(8,128)S(1)} %collective-permute-done.25.refs_2_), channel_id=1, source_target_pairs={{0,1},{1,0},{2,3},{3,2},{4,5},{5,4},{6,7},{7,6},{8,9},{9,8},{10,11... | collective-permute-start | bytes 884744 | tf_op jit(solution)/shard_map/ppermute | solution.py:33
  86.9 3.7 %collective-permute-start.21 = (f32[1,384]{1,0:T(1,128)S(1)}, f32[1,384]{1,0:T(1,128)S(1)}, u32[]{:S(2)}, u32[]{:S(2)}) collective-permute-start(f32[1,384]{1,0:T(1,128)S(1)} %shard_map.131.refs_1_), channel_id=1, source_target_pairs={{0,2},{1,3},{2,0},{3,1},{4,6},{5,7},{6,4},{7,5},{8,10},{9,11},{10,... | collective-permute-start | bytes 4616 | tf_op jit(solution)/shard_map/ppermute | solution.py:33
  91.3 7.8 %collective-permute-start.24 = (f32[1,384]{1,0:T(1,128)S(1)}, f32[1,384]{1,0:T(1,128)S(1)}, u32[]{:S(2)}, u32[]{:S(2)}) collective-permute-start(f32[1,384]{1,0:T(1,128)S(1)} %shard_map.132.own), channel_id=1, source_target_pairs={{0,12},{1,13},{2,14},{3,15},{4,8},{5,9},{6,10},{7,11},{8,4},{9,5},... | collective-permute-start | bytes 4616 | tf_op jit(solution)/shard_map/ppermute | solution.py:33
  94.6 6.6 %collective-permute-start.23 = (f32[1,384]{1,0:T(1,128)S(1)}, f32[1,384]{1,0:T(1,128)S(1)}, u32[]{:S(2)}, u32[]{:S(2)}) collective-permute-start(f32[1,384]{1,0:T(1,128)S(1)} %shard_map.132.own), channel_id=1, source_target_pairs={{0,10},{1,11},{2,8},{3,9},{4,14},{5,15},{6,12},{7,13},{8,2},{9,3},... | collective-permute-start | bytes 4616 | tf_op jit(solution)/shard_map/ppermute | solution.py:33
  96.7 4.5 %collective-permute-start.22 = (f32[1,384]{1,0:T(1,128)S(1)}, f32[1,384]{1,0:T(1,128)S(1)}, u32[]{:S(2)}, u32[]{:S(2)}) collective-permute-start(f32[1,384]{1,0:T(1,128)S(1)} %shard_map.132.own), channel_id=1, source_target_pairs={{0,4},{1,5},{2,6},{3,7},{4,0},{5,1},{6,2},{7,3},{8,12},{9,13},{10,... | collective-permute-start | bytes 4616 | tf_op jit(solution)/shard_map/ppermute | solution.py:33
  102.4 3.7 %collective-permute-start.27 = (f32[1,384]{1,0:T(1,128)S(1)}, f32[1,384]{1,0:T(1,128)S(1)}, u32[]{:S(2)}, u32[]{:S(2)}) collective-permute-start(f32[1,384]{1,0:T(1,128)S(1)} %get-tuple-element.93.refs_1_), channel_id=1, source_target_pairs={{0,16},{1,17},{2,18},{3,19},{4,20},{5,21},{6,22},{7,23},{8,24},{9,... | collective-permute-start | bytes 4616 | tf_op jit(solution)/shard_map/ppermute | solution.py:33
  106.8 4.9 %collective-permute-start.28 = (f32[1,384]{1,0:T(1,128)S(1)}, f32[1,384]{1,0:T(1,128)S(1)}, u32[]{:S(2)}, u32[]{:S(2)}) collective-permute-start(f32[1,384]{1,0:T(1,128)S(1)} %shard_map.137), channel_id=1, source_target_pairs={{0,48},{1,49},{2,50},{3,51},{4,52},{5,53},{6,54},{7,55},{8,56},{9,... | collective-permute-start | bytes 4616 | tf_op jit(solution)/shard_map/ppermute | solution.py:33
  (12 other events, 62.1 us)

commit v5 on v4

--- a/solution.py
+++ b/solution.py
@@ -16,7 +16,8 @@
 CORE, PAIR, SIDE, LAST, STEPS = 0, 6, 7, 8, 9
 GROUPS = CY // 8
 MASKS = (1, 2, 4, 12, 16, 48)
-ROW_MASKS = (4, 10, 12)
+SPLIT_MASKS = (4, 12)
+OPPOSITE = 10
 ROW_TILES = 16
 
 coarse_step = 0.1
@@ -393,18 +394,21 @@
 
 def ordered(flags, rows):
     mine = block_index(flags)
+    first = flags[CORE] == 0
+    own, split, other_split, opposite = [row[...] for row in rows]
+    one = jnp.where(first, split, other_split)
+    three = jnp.where(first, other_split, split)
     result = []
     for block in range(4):
         change = mine ^ block
-        value = rows[0][...]
-        for k in range(1, 4):
-            value = jnp.where(change == k, rows[k][...], value)
-        result.append(value)
+        value = jnp.where(change == 1, one, own)
+        value = jnp.where(change == 2, opposite, value)
+        result.append(jnp.where(change == 3, three, value))
     return mine, result
 
 
-def row_forward_kernel(flags, own, one, two, three, blocks, total, entering):
-    mine, rows = ordered(flags, (own, one, two, three))
+def row_forward_kernel(flags, own, split, other_split, opposite, blocks, total, entering):
+    mine, rows = ordered(flags, (own, split, other_split, opposite))
     state = rows[0]
     before = jnp.zeros_like(state)
     for block in range(1, 4):
@@ -414,8 +418,8 @@
     entering[...] = before
 
 
-def row_backward_kernel(flags, own, one, two, three, blocks, total, entering):
-    mine, rows = ordered(flags, (own, one, two, three))
+def row_backward_kernel(flags, own, split, other_split, opposite, blocks, total, entering):
+    mine, rows = ordered(flags, (own, split, other_split, opposite))
     state = rows[3]
     before = jnp.zeros_like(state)
     for block in range(2, -1, -1):
@@ -534,12 +538,9 @@
     return (merged, half), [(high, low, prefix, suffix)]
 
 
-def merge_level(flags, level, block, levels, gate=None):
+def merge_level(flags, level, block, levels, near):
     cube = 6 * IB**3
     merged, half = block
-    near = swap(half, MASKS[level])
-    if gate is not None:
-        near = after(near, gate)
     far = swap(near, 1)
     last = level == 4
     high, low, *block = local_call(
@@ -555,11 +556,22 @@
     return block, levels + [(high, low, prefix, suffix)]
 
 
-def sorted_blocks(flags, block, gate):
-    merged, half = block
+def split_swap(value):
+    masks = [SPLIT_MASKS[i & 1] for i in range(lax.axis_size("tile"))]
+    return lax.ppermute(value, "tile", [(i, i ^ mask) for i, mask in enumerate(masks)])
+
+
+def row_exchange(total):
+    opposite = swap(total, OPPOSITE)
+    split = split_swap(total)
+    return [split, swap(split, 1), opposite]
+
+
+def sorted_blocks(flags, fetched, gate):
+    merged, nears = fetched
     pieces = []
-    for mask in ROW_MASKS:
-        near = after(swap(half, mask), gate)
+    for near in nears:
+        near = after(near, *gate)
         pieces += [near, swap(near, 1)]
     return local_call(
         sort_kernel, flags, [merged, *pieces], jax.ShapeDtypeStruct((4, IB, IB), f32)
@@ -567,7 +579,7 @@
 
 
 def coupled_velocity(
-    flags, picked, inverse, transition, block, levels, velocity, node_mass, nodes
+    flags, picked, inverse, transition, fetched, levels, velocity, node_mass, nodes
 ):
     square = 2 * IB * IB
     cube = 6 * IB**3
@@ -582,8 +594,8 @@
         total = local_call(
             bound(level, forward_kernel), flags, [total, others[-1], levels[level][0]], ROW, square
         )
-    arrived = [swap(total, mask) for mask in ROW_MASKS]
-    blocks = sorted_blocks(flags, block, total)
+    arrived = row_exchange(total)
+    blocks = sorted_blocks(flags, fetched, (arrived[0], arrived[2]))
     total, in_row = local_call(
         row_forward_kernel, flags, [total, *arrived, blocks], (ROW, ROW), 3 * square
     )
@@ -598,7 +610,6 @@
     prefix_3, suffix_3 = local_call(
         row_reach_kernel, flags, [blocks, high, low, prefix_1, suffix_1], (MAT, MAT), 2 * cube
     )
-    row[1] = after(row[1], hop)
     hop = after(hop, prefix_3)
     leaving = local_call(hop_kernel, flags, [total, hop, merged], ROW, square)
     hop = up_row(leaving)
@@ -606,6 +617,7 @@
         forward_part_kernel, flags, [*others, in_row, prefix_0, prefix_1], ROW, 2 * square
     )
     hop = after(hop, entering)
+    row[1] = after(row[1], entering)
     solved, returning = local_call(
         turn_kernel,
         flags,
@@ -619,9 +631,10 @@
         total = local_call(
             bound(level, backward_kernel), flags, [total, others[-1], levels[level][1]], ROW, square
         )
-    arrived = [swap(total, mask) for mask in ROW_MASKS]
+    arrived = row_exchange(total)
+    near = after(swap(row[1], MASKS[4]), total)
     row, levels = merge_level(
-        flags, 4, row, levels + [None, (None, None, prefix_3, suffix_3)], solved
+        flags, 4, row, levels + [None, (None, None, prefix_3, suffix_3)], near
     )
     _, low, _, suffix_4 = levels[4]
     arrived[-1] = after(arrived[-1], low)
@@ -687,11 +700,13 @@
     transition = local_call(transition_kernel, flags, [inverse, lower], MAT, 6 * IB**3)
     outer, inner = local_call(pack_kernel, flags, state, (packed, packed))
     block, levels = first_products(flags, transition, outer)
-    outer = outer_swap(outer)
     inner = swap(inner, 1)
-    block = (block[0], after(block[1], inner))
-    block, levels = merge_level(flags, 1, block, levels)
-    outer = after(outer, block[1])
+    near = swap(after(block[1], inner), MASKS[1])
+    outer = outer_swap(after(outer, near))
+    block, levels = merge_level(flags, 1, block, levels, near)
+    merged, half = block
+    fetched = merged, [swap(half, mask) for mask in (SPLIT_MASKS[0], OPPOSITE, SPLIT_MASKS[1])]
+    outer = after(outer, half)
     final_displacement, final_velocity, picked = substeps_call(
         flags, step, state, outer, inner, stiffness, interface_nodes
     )
@@ -700,7 +715,7 @@
         picked,
         inverse,
         transition,
-        block,
+        fetched,
         levels,
         final_velocity,
         node_mass[0],

time: 114 us -> 132 us (1.16)
  starting transfers between devices: 39.4 us -> 48.4 us
  waiting for transfers between devices: 35.5 us -> 40.8 us
  Pallas kernels: 35.6 us -> 39.4 us
    ppermute x24 -> x22, starting transfers between devices: 29.5 us -> 40.8 us  [swap(): lax.ppermute(value, 'tile', [(i, i ^ mask) for i in range(lax.axis_size('...]
    ppermute x24 -> x22, waiting for transfers between devices: 28.3 us -> 23.2 us  [swap(): lax.ppermute(value, 'tile', [(i, i ^ mask) for i in range(lax.axis_size('...]
    ppermute x3, waiting for transfers between devices: 6.34 us -> 11.1 us  [up_row(): lax.ppermute(value, 'tile', [(i, (i + ROW_TILES) % count) for i in range(...]
    ppermute x1, starting transfers between devices: 4.4 us -> 0.01 us  [coupled_velocity(): partner = lax.ppermute(picked, 'sub', [(i, i ^ 1) for i in range(count)])]
    pallas_call x1, Pallas kernels: 7.84 us -> 11.7 us  [substeps_call(): pl.pallas_call(substep_kernel, out_shape=(jax.ShapeDtypeStruct(grid_shape...]
    ppermute x0 -> x2, waiting for transfers between devices: none -> 3.63 us  [split_swap(): lax.ppermute(value, 'tile', [(i, i ^ mask) for i, mask in enumerate(masks)])]
    ppermute x0 -> x2, starting transfers between devices: none -> 3.17 us  [split_swap(): lax.ppermute(value, 'tile', [(i, i ^ mask) for i, mask in enumerate(masks)])]
    ppermute x1, waiting for transfers between devices: 0.92 us -> 2.94 us  [coupled_velocity(): partner = lax.ppermute(picked, 'sub', [(i, i ^ 1) for i in range(count)])]
  transfers between devices with their start and end apart: 29 -> 29, of which waited for: 15 -> 18; matrix products, arithmetic and copies ran while one was open for 0% -> 0% of each run, Pallas kernels for 25% -> 23%
where the time goes in v5:
time: 132 us
  starting transfers between devices  48.4 us (37%)
  waiting for transfers between devices  40.8 us (31%)
  Pallas kernels  39.4 us (30%)
  between operations  1.69 us (1%)
  local copies, waits for them, and re-layouts  1.45 us (1%)
    ppermute x22, starting transfers between devices, swap(): lax.ppermute(value, 'tile', [(i, i ^ mask) for i in range(lax.axis_size('...  40.8 us
    pallas_call x25, Pallas kernels, local_call(): pl.pallas_call(kernel, out_shape=outs, in_specs=[SM] + [VM] * len(operand...  27.7 us
    ppermute x22, waiting for transfers between devices, swap(): lax.ppermute(value, 'tile', [(i, i ^ mask) for i in range(lax.axis_size('...  23.2 us
    pallas_call x1, Pallas kernels, substeps_call(): pl.pallas_call(substep_kernel, out_shape=(jax.ShapeDtypeStruct(grid_shape...  11.7 us
    ppermute x3, waiting for transfers between devices, up_row(): lax.ppermute(value, 'tile', [(i, (i + ROW_TILES) % count) for i in range(...  11.1 us
    ppermute x3, starting transfers between devices, up_row(): lax.ppermute(value, 'tile', [(i, (i + ROW_TILES) % count) for i in range(...  3.71 us
    ppermute x2, waiting for transfers between devices, split_swap(): lax.ppermute(value, 'tile', [(i, i ^ mask) for i, mask in enumerate(masks)])  3.63 us
    ppermute x2, starting transfers between devices, split_swap(): lax.ppermute(value, 'tile', [(i, i ^ mask) for i, mask in enumerate(masks)])  3.17 us
  transfers between devices with their start and end apart: 29, of which 18 were waited for; matrix products, arithmetic and copies ran while one was open for 0% of the time, Pallas kernels for 23%

profile of v5, /device:TPU:2, one launch (start us, length us, event | category | flops | bytes accessed | tf_op | source)
XLA Modules:
  0.0 131.8 jit_solution(14370748156113875696)
XLA Ops:
  7.5 2.0 %collective-permute-start.2 = (f32[192,384]{1,0:T(8,128)S(1)}, f32[192,384]{1,0:T(8,128)S(1)}, u32[]{:S(2)}, u32[]{:S(2)}) collective-permute-start(f32[192,384]{1,0:T(8,128)S(1)} %get-tuple-element.56), channel_id=1, source_target_pairs={{0,2},{1,3},{2,0},{3,1},{4,6},{5,7},{6,4},{7,5},{8,10},{9,11},{10,... | collective-permute-start | bytes 884744 | tf_op jit(solution)/shard_map/ppermute | solution.py:34
  9.5 7.3 %collective-permute-done.2.refs_2_ = f32[192,384]{1,0:T(8,128)S(1)} collective-permute-done((f32[192,384]{1,0:T(8,128)S(1)}, f32[192,384]{1,0:T(8,128)S(1)}, u32[]{:S(2)}, u32[]{:S(2)}) %collective-permute-start.2) | collective-permute-done | bytes 294944 | tf_op jit(solution)/shard_map/ppermute | solution.py:34
  17.5 3.2 %collective-permute-start.4 = (f32[192,384]{1,0:T(8,128)S(1)}, f32[192,384]{1,0:T(8,128)S(1)}, u32[]{:S(2)}, u32[]{:S(2)}) collective-permute-start(f32[192,384]{1,0:T(8,128)S(1)} %collective-permute-done.2.refs_2_), channel_id=1, source_target_pairs={{0,1},{1,0},{2,3},{3,2},{4,5},{5,4},{6,7},{7,6},{8,9},{9,8},{10,11... | collective-permute-start | bytes 884744 | tf_op jit(solution)/shard_map/ppermute | solution.py:34
  23.2 5.5 %collective-permute-start.15 = (f32[192,384]{1,0:T(8,128)S(1)}, f32[192,384]{1,0:T(8,128)S(1)}, u32[]{:S(2)}, u32[]{:S(2)}) collective-permute-start(f32[192,384]{1,0:T(8,128)S(1)} %get-tuple-element.59), channel_id=1, source_target_pairs={{0,12},{1,13},{2,14},{3,15},{4,8},{5,9},{6,10},{7,11},{8,4},{9,5},... | collective-permute-start | bytes 884744 | tf_op jit(solution)/shard_map/ppermute | solution.py:34
  28.7 3.1 %collective-permute-start.13 = (f32[192,384]{1,0:T(8,128)S(1)}, f32[192,384]{1,0:T(8,128)S(1)}, u32[]{:S(2)}, u32[]{:S(2)}) collective-permute-start(f32[192,384]{1,0:T(8,128)S(1)} %get-tuple-element.59), channel_id=1, source_target_pairs={{0,10},{1,11},{2,8},{3,9},{4,14},{5,15},{6,12},{7,13},{8,2},{9,3},... | collective-permute-start | bytes 884744 | tf_op jit(solution)/shard_map/ppermute | solution.py:34
  31.8 11.7 %shard_map.117 = (f32[3,4,32,128]{3,2,1,0:T(8,128)}, f32[3,4,32,128]{3,2,1,0:T(8,128)S(1)}, f32[1,384]{1,0:T(1,128)S(1)}) custom-call(s32[10]{0:T(128)S(1)} %stack.43.flags.refs_0_, f32[1]{0:T(128)S(6)} %div.16.step, f32[3,4,32,128]{3,2,1,0:T(8,128)S(1)} %bitcast.24, f32[3,4,32,128]{3,2,1,0:T(8,128)S(1)} %bitcast.26, f32[3,4,32,128]{3,2,1,0:T(8,128)S(1)} %bitcast.28, ...), custom_call_target="tpu_custom_call" | custom-call | flops 3623878656 | bytes 2162688 | tf_op jit(solution)/shard_map/pallas_call | solution.py:282
  44.2 2.9 %collective-permute-done.5.partner = f32[1,384]{1,0:T(1,128)S(1)} collective-permute-done((f32[1,384]{1,0:T(1,128)S(1)}, f32[1,384]{1,0:T(1,128)S(1)}, u32[]{:S(2)}, u32[]{:S(2)}) %collective-permute-start.5) | collective-permute-done | bytes 1568 | tf_op jit(solution)/shard_map/ppermute | solution.py:589
  50.0 3.6 %collective-permute-done.7.refs_2_.other_1 = f32[1,384]{1,0:T(1,128)S(1)} collective-permute-done((f32[1,384]{1,0:T(1,128)S(1)}, f32[1,384]{1,0:T(1,128)S(1)}, u32[]{:S(2)}, u32[]{:S(2)}) %collective-permute-start.7) | collective-permute-done | bytes 1568 | tf_op jit(solution)/shard_map/ppermute | solution.py:34
  54.3 17.3 %collective-permute-start.10 = (f32[1,384]{1,0:T(1,128)S(1)}, f32[1,384]{1,0:T(1,128)S(1)}, u32[]{:S(2)}, u32[]{:S(2)}) collective-permute-start(f32[1,384]{1,0:T(1,128)S(1)} %shard_map.122.own), channel_id=1, source_target_pairs={{0,10},{1,11},{2,8},{3,9},{4,14},{5,15},{6,12},{7,13},{8,2},{9,3},... | collective-permute-start | bytes 4616 | tf_op jit(solution)/shard_map/ppermute | solution.py:34
  71.6 1.9 %collective-permute-start.8 = (f32[1,384]{1,0:T(1,128)S(1)}, f32[1,384]{1,0:T(1,128)S(1)}, u32[]{:S(2)}, u32[]{:S(2)}) collective-permute-start(f32[1,384]{1,0:T(1,128)S(1)} %shard_map.122.own), channel_id=1, source_target_pairs={{0,4},{1,13},{2,6},{3,15},{4,0},{5,9},{6,2},{7,11},{8,12},{9,5},{1... | collective-permute-start | bytes 4616 | tf_op jit(solution)/shard_map/ppermute | solution.py:561
  73.6 2.5 %collective-permute-done.8.split = f32[1,384]{1,0:T(1,128)S(1)} collective-permute-done((f32[1,384]{1,0:T(1,128)S(1)}, f32[1,384]{1,0:T(1,128)S(1)}, u32[]{:S(2)}, u32[]{:S(2)}) %collective-permute-start.8) | collective-permute-done | bytes 1568 | tf_op jit(solution)/shard_map/ppermute | solution.py:561
  80.2 2.7 %shard_map.126 = (f32[384,384]{1,0:T(8,128)S(1)}, f32[384,384]{1,0:T(8,128)S(1)}, f32[384,384]{1,0:T(8,128)S(1)}, f32[192,384]{1,0:T(8,128)S(1)}) custom-call(s32[10]{0:T(128)S(1)} %stack.43.flags.refs_0_, f32[4,384,384]{2,1,0:T(8,128)S(1)} %shard_map.123.blocks), custom_call_target="tpu_custom_call" | custom-call | flops 1019215872 | bytes 2359296 | tf_op jit(solution)/shard_map/pallas_call | solution.py:43
  83.6 1.7 %collective-permute-start.25 = (f32[192,384]{1,0:T(8,128)S(1)}, f32[192,384]{1,0:T(8,128)S(1)}, u32[]{:S(2)}, u32[]{:S(2)}) collective-permute-start(f32[192,384]{1,0:T(8,128)S(1)} %get-tuple-element.89), channel_id=1, source_target_pairs={{0,16},{1,17},{2,18},{3,19},{4,20},{5,21},{6,22},{7,23},{8,24},{9,... | collective-permute-start | bytes 884744 | tf_op jit(solution)/shard_map/ppermute | solution.py:34
  85.7 6.2 %collective-permute-done.17.hop = f32[1,384]{1,0:T(1,128)S(1)} collective-permute-done((f32[1,384]{1,0:T(1,128)S(1)}, f32[1,384]{1,0:T(1,128)S(1)}, u32[]{:S(2)}, u32[]{:S(2)}) %collective-permute-start.17) | collective-permute-done | bytes 1568 | tf_op jit(solution)/shard_map/ppermute | solution.py:667
  92.6 2.6 %collective-permute-start.18 = (f32[1,384]{1,0:T(1,128)S(1)}, f32[1,384]{1,0:T(1,128)S(1)}, u32[]{:S(2)}, u32[]{:S(2)}) collective-permute-start(f32[1,384]{1,0:T(1,128)S(1)} %shard_map.127), channel_id=1, source_target_pairs={{0,16},{1,17},{2,18},{3,19},{4,20},{5,21},{6,22},{7,23},{8,24},{9,... | collective-permute-start | bytes 4616 | tf_op jit(solution)/shard_map/ppermute | solution.py:667
  95.2 2.2 %shard_map.128 = (f32[384,384]{1,0:T(8,128)S(1)}, f32[384,384]{1,0:T(8,128)S(1)}) custom-call(s32[10]{0:T(128)S(1)} %stack.43.flags.refs_0_, f32[4,384,384]{2,1,0:T(8,128)S(1)} %shard_map.123.blocks, f32[384,384]{1,0:T(8,128)S(1)} %get-tuple-element.80.high, f32[384,384]{1,0:T(8,128)S(1)} %get-tuple-element.81.low, ...), custom_call_target="tpu_custom_call" | custom-call | flops 679477248 | bytes 4718592 | tf_op jit(solution)/shard_map/pallas_call | solution.py:43
  99.5 4.2 %collective-permute-done.19.hop = f32[1,384]{1,0:T(1,128)S(1)} collective-permute-done((f32[1,384]{1,0:T(1,128)S(1)}, f32[1,384]{1,0:T(1,128)S(1)}, u32[]{:S(2)}, u32[]{:S(2)}) %collective-permute-start.19) | collective-permute-done | bytes 1568 | tf_op jit(solution)/shard_map/ppermute | solution.py:667
  106.7 2.2 %collective-permute-start.21 = (f32[1,384]{1,0:T(1,128)S(1)}, f32[1,384]{1,0:T(1,128)S(1)}, u32[]{:S(2)}, u32[]{:S(2)}) collective-permute-start(f32[1,384]{1,0:T(1,128)S(1)} %shard_map.131.refs_1_), channel_id=1, source_target_pairs={{0,2},{1,3},{2,0},{3,1},{4,6},{5,7},{6,4},{7,5},{8,10},{9,11},{10,... | collective-permute-start | bytes 4616 | tf_op jit(solution)/shard_map/ppermute | solution.py:34
  109.0 1.6 %collective-permute-done.21.refs_2_.other_1 = f32[1,384]{1,0:T(1,128)S(1)} collective-permute-done((f32[1,384]{1,0:T(1,128)S(1)}, f32[1,384]{1,0:T(1,128)S(1)}, u32[]{:S(2)}, u32[]{:S(2)}) %collective-permute-start.21) | collective-permute-done | bytes 1568 | tf_op jit(solution)/shard_map/ppermute | solution.py:34
  112.7 2.2 %collective-permute-start.24 = (f32[1,384]{1,0:T(1,128)S(1)}, f32[1,384]{1,0:T(1,128)S(1)}, u32[]{:S(2)}, u32[]{:S(2)}) collective-permute-start(f32[1,384]{1,0:T(1,128)S(1)} %shard_map.132.own), channel_id=1, source_target_pairs={{0,10},{1,11},{2,8},{3,9},{4,14},{5,15},{6,12},{7,13},{8,2},{9,3},... | collective-permute-start | bytes 4616 | tf_op jit(solution)/shard_map/ppermute | solution.py:34
  117.2 2.1 %collective-permute-done.24.opposite = f32[1,384]{1,0:T(1,128)S(1)} collective-permute-done((f32[1,384]{1,0:T(1,128)S(1)}, f32[1,384]{1,0:T(1,128)S(1)}, u32[]{:S(2)}, u32[]{:S(2)}) %collective-permute-start.24) | collective-permute-done | bytes 1568 | tf_op jit(solution)/shard_map/ppermute | solution.py:34
  120.6 2.1 %shard_map.136 = (f32[384,384]{1,0:T(8,128)}, f32[384,384]{1,0:T(8,128)S(1)}) custom-call(s32[10]{0:T(128)S(1)} %stack.43.flags.refs_0_, f32[384,384]{1,0:T(8,128)S(1)} %get-tuple-element.96.refs_1_, f32[384,384]{1,0:T(8,128)S(1)} %get-tuple-element.91.refs_2_.refs_3_, f32[384,384]{1,0:T(8,128)S(1)} %get-tuple-element.83.prefix.refs_3_, ...), custom_call_target="tpu_custom_call" | custom-call | flops 339738624 | bytes 2359296 | tf_op jit(solution)/shard_map/pallas_call | solution.py:43
  127.0 2.7 %collective-permute-done.28.other = f32[1,384]{1,0:T(1,128)S(1)} collective-permute-done((f32[1,384]{1,0:T(1,128)S(1)}, f32[1,384]{1,0:T(1,128)S(1)}, u32[]{:S(2)}, u32[]{:S(2)}) %collective-permute-start.28) | collective-permute-done | bytes 1568 | tf_op jit(solution)/shard_map/ppermute | solution.py:34
  129.8 2.0 %shard_map.138 = f32[3,4,32,128]{3,2,1,0:T(8,128)} custom-call(s32[10]{0:T(128)S(1)} %stack.43.flags.refs_0_, f32[384,384]{1,0:T(8,128)S(1)} %get-tuple-element.103.inverse, f32[1,384]{1,0:T(1,128)S(1)} %shard_map.135.entering, f32[1,384]{1,0:T(1,128)S(1)} %collective-permute-done.28.other, f32[384,384]{1,0:T(8,128)S(1)} %get-tuple-element.97.suffix, ...), custom_call_target="tpu_custom_call" | custom-call | flops 589824 | bytes 1446912 | tf_op jit(solution)/shard_map/pallas_call | solution.py:43
  (76 shorter events, 34.5 us)
Async XLA Ops:
  4.1 2.1 %collective-permute-start = (f32[384,384]{1,0:T(8,128)S(1)}, f32[384,384]{1,0:T(8,128)S(1)}, u32[]{:S(2)}, u32[]{:S(2)}) collective-permute-start(f32[384,384]{1,0:T(8,128)S(1)} %shard_map.114.own.transition), channel_id=1, source_target_pairs={{0,1},{1,0},{2,3},{3,2},{4,5},{5,4},{6,7},{7,6},{8,9},{9,8},{10,11... | collective-permute-start | bytes 1769480 | tf_op jit(solution)/shard_map/ppermute | solution.py:34
  4.8 2.6 %collective-permute-start.1 = (f32[37,32,128]{2,1,0:T(8,128)S(1)}, f32[37,32,128]{2,1,0:T(8,128)S(1)}, u32[]{:S(2)}, u32[]{:S(2)}) collective-permute-start(f32[37,32,128]{2,1,0:T(8,128)S(1)} %get-tuple-element.55), channel_id=1, source_target_pairs={{0,1},{1,0},{2,3},{3,2},{4,5},{5,4},{6,7},{7,6},{8,9},{9,8},{10,11... | collective-permute-start | bytes 1818632 | tf_op jit(solution)/shard_map/ppermute | solution.py:34
  7.5 9.3 %collective-permute-start.2 = (f32[192,384]{1,0:T(8,128)S(1)}, f32[192,384]{1,0:T(8,128)S(1)}, u32[]{:S(2)}, u32[]{:S(2)}) collective-permute-start(f32[192,384]{1,0:T(8,128)S(1)} %get-tuple-element.56), channel_id=1, source_target_pairs={{0,2},{1,3},{2,0},{3,1},{4,6},{5,7},{6,4},{7,5},{8,10},{9,11},{10,... | collective-permute-start | bytes 884744 | tf_op jit(solution)/shard_map/ppermute | solution.py:34
  16.8 15.0 %collective-permute-start.3 = (f32[37,32,128]{2,1,0:T(8,128)S(1)}, f32[37,32,128]{2,1,0:T(8,128)S(1)}, u32[]{:S(2)}, u32[]{:S(2)}) collective-permute-start(f32[37,32,128]{2,1,0:T(8,128)S(1)} %get-tuple-element.57), channel_id=1, source_target_pairs={{1,2},{2,1},{3,4},{4,3},{5,6},{6,5},{7,8},{8,7},{9,10},{10,9},{11,... | collective-permute-start | bytes 1818632 | tf_op jit(solution)/shard_map/ppermute | solution.py:675
  17.5 4.4 %collective-permute-start.4 = (f32[192,384]{1,0:T(8,128)S(1)}, f32[192,384]{1,0:T(8,128)S(1)}, u32[]{:S(2)}, u32[]{:S(2)}) collective-permute-start(f32[192,384]{1,0:T(8,128)S(1)} %collective-permute-done.2.refs_2_), channel_id=1, source_target_pairs={{0,1},{1,0},{2,3},{3,2},{4,5},{5,4},{6,7},{7,6},{8,9},{9,8},{10,11... | collective-permute-start | bytes 884744 | tf_op jit(solution)/shard_map/ppermute | solution.py:34
  23.2 50.3 %collective-permute-start.15 = (f32[192,384]{1,0:T(8,128)S(1)}, f32[192,384]{1,0:T(8,128)S(1)}, u32[]{:S(2)}, u32[]{:S(2)}) collective-permute-start(f32[192,384]{1,0:T(8,128)S(1)} %get-tuple-element.59), channel_id=1, source_target_pairs={{0,12},{1,13},{2,14},{3,15},{4,8},{5,9},{6,10},{7,11},{8,4},{9,5},... | collective-permute-start | bytes 884744 | tf_op jit(solution)/shard_map/ppermute | solution.py:34
  28.7 47.4 %collective-permute-start.13 = (f32[192,384]{1,0:T(8,128)S(1)}, f32[192,384]{1,0:T(8,128)S(1)}, u32[]{:S(2)}, u32[]{:S(2)}) collective-permute-start(f32[192,384]{1,0:T(8,128)S(1)} %get-tuple-element.59), channel_id=1, source_target_pairs={{0,10},{1,11},{2,8},{3,9},{4,14},{5,15},{6,12},{7,13},{8,2},{9,3},... | collective-permute-start | bytes 884744 | tf_op jit(solution)/shard_map/ppermute | solution.py:34
  31.8 44.8 %collective-permute-start.11 = (f32[192,384]{1,0:T(8,128)S(1)}, f32[192,384]{1,0:T(8,128)S(1)}, u32[]{:S(2)}, u32[]{:S(2)}) collective-permute-start(f32[192,384]{1,0:T(8,128)S(1)} %get-tuple-element.59), channel_id=1, source_target_pairs={{0,4},{1,5},{2,6},{3,7},{4,0},{5,1},{6,2},{7,3},{8,12},{9,13},{10,... | collective-permute-start | bytes 884744 | tf_op jit(solution)/shard_map/ppermute | solution.py:34
  43.5 3.6 %collective-permute-start.5 = (f32[1,384]{1,0:T(1,128)S(1)}, f32[1,384]{1,0:T(1,128)S(1)}, u32[]{:S(2)}, u32[]{:S(2)}) collective-permute-start(f32[1,384]{1,0:T(1,128)S(1)} %get-tuple-element.62.picked), channel_id=1, source_target_pairs={{0,64},{64,0},{128,192},{192,128},{1,65},{65,1},{129,193},{193,129... | collective-permute-start | bytes 4616 | tf_op jit(solution)/shard_map/ppermute | solution.py:589
  49.9 3.7 %collective-permute-start.7 = (f32[1,384]{1,0:T(1,128)S(1)}, f32[1,384]{1,0:T(1,128)S(1)}, u32[]{:S(2)}, u32[]{:S(2)}) collective-permute-start(f32[1,384]{1,0:T(1,128)S(1)} %shard_map.121.refs_1_), channel_id=1, source_target_pairs={{0,2},{1,3},{2,0},{3,1},{4,6},{5,7},{6,4},{7,5},{8,10},{9,11},{10,... | collective-permute-start | bytes 4616 | tf_op jit(solution)/shard_map/ppermute | solution.py:34
  54.3 19.3 %collective-permute-start.10 = (f32[1,384]{1,0:T(1,128)S(1)}, f32[1,384]{1,0:T(1,128)S(1)}, u32[]{:S(2)}, u32[]{:S(2)}) collective-permute-start(f32[1,384]{1,0:T(1,128)S(1)} %shard_map.122.own), channel_id=1, source_target_pairs={{0,10},{1,11},{2,8},{3,9},{4,14},{5,15},{6,12},{7,13},{8,2},{9,3},... | collective-permute-start | bytes 4616 | tf_op jit(solution)/shard_map/ppermute | solution.py:34
  71.6 4.5 %collective-permute-start.8 = (f32[1,384]{1,0:T(1,128)S(1)}, f32[1,384]{1,0:T(1,128)S(1)}, u32[]{:S(2)}, u32[]{:S(2)}) collective-permute-start(f32[1,384]{1,0:T(1,128)S(1)} %shard_map.122.own), channel_id=1, source_target_pairs={{0,4},{1,13},{2,6},{3,15},{4,0},{5,9},{6,2},{7,11},{8,12},{9,5},{1... | collective-permute-start | bytes 4616 | tf_op jit(solution)/shard_map/ppermute | solution.py:561
  76.7 2.5 %collective-permute-start.9 = (f32[1,384]{1,0:T(1,128)S(1)}, f32[1,384]{1,0:T(1,128)S(1)}, u32[]{:S(2)}, u32[]{:S(2)}) collective-permute-start(f32[1,384]{1,0:T(1,128)S(1)} %collective-permute-done.8.split), channel_id=1, source_target_pairs={{0,1},{1,0},{2,3},{3,2},{4,5},{5,4},{6,7},{7,6},{8,9},{9,8},{10,11... | collective-permute-start | bytes 4616 | tf_op jit(solution)/shard_map/ppermute | solution.py:34
  83.6 27.7 %collective-permute-start.25 = (f32[192,384]{1,0:T(8,128)S(1)}, f32[192,384]{1,0:T(8,128)S(1)}, u32[]{:S(2)}, u32[]{:S(2)}) collective-permute-start(f32[192,384]{1,0:T(8,128)S(1)} %get-tuple-element.89), channel_id=1, source_target_pairs={{0,16},{1,17},{2,18},{3,19},{4,20},{5,21},{6,22},{7,23},{8,24},{9,... | collective-permute-start | bytes 884744 | tf_op jit(solution)/shard_map/ppermute | solution.py:34
  85.3 6.6 %collective-permute-start.17 = (f32[1,384]{1,0:T(1,128)S(1)}, f32[1,384]{1,0:T(1,128)S(1)}, u32[]{:S(2)}, u32[]{:S(2)}) collective-permute-start(f32[1,384]{1,0:T(1,128)S(1)} %get-tuple-element.76.total), channel_id=1, source_target_pairs={{0,16},{1,17},{2,18},{3,19},{4,20},{5,21},{6,22},{7,23},{8,24},{9,... | collective-permute-start | bytes 4616 | tf_op jit(solution)/shard_map/ppermute | solution.py:667
  92.6 5.5 %collective-permute-start.18 = (f32[1,384]{1,0:T(1,128)S(1)}, f32[1,384]{1,0:T(1,128)S(1)}, u32[]{:S(2)}, u32[]{:S(2)}) collective-permute-start(f32[1,384]{1,0:T(1,128)S(1)} %shard_map.127), channel_id=1, source_target_pairs={{0,16},{1,17},{2,18},{3,19},{4,20},{5,21},{6,22},{7,23},{8,24},{9,... | collective-permute-start | bytes 4616 | tf_op jit(solution)/shard_map/ppermute | solution.py:667
  98.8 4.9 %collective-permute-start.19 = (f32[1,384]{1,0:T(1,128)S(1)}, f32[1,384]{1,0:T(1,128)S(1)}, u32[]{:S(2)}, u32[]{:S(2)}) collective-permute-start(f32[1,384]{1,0:T(1,128)S(1)} %shard_map.129), channel_id=1, source_target_pairs={{0,16},{1,17},{2,18},{3,19},{4,20},{5,21},{6,22},{7,23},{8,24},{9,... | collective-permute-start | bytes 4616 | tf_op jit(solution)/shard_map/ppermute | solution.py:667
  106.7 3.8 %collective-permute-start.21 = (f32[1,384]{1,0:T(1,128)S(1)}, f32[1,384]{1,0:T(1,128)S(1)}, u32[]{:S(2)}, u32[]{:S(2)}) collective-permute-start(f32[1,384]{1,0:T(1,128)S(1)} %shard_map.131.refs_1_), channel_id=1, source_target_pairs={{0,2},{1,3},{2,0},{3,1},{4,6},{5,7},{6,4},{7,5},{8,10},{9,11},{10,... | collective-permute-start | bytes 4616 | tf_op jit(solution)/shard_map/ppermute | solution.py:34
  111.3 5.1 %collective-permute-start.26 = (f32[192,384]{1,0:T(8,128)S(1)}, f32[192,384]{1,0:T(8,128)S(1)}, u32[]{:S(2)}, u32[]{:S(2)}) collective-permute-start(f32[192,384]{1,0:T(8,128)S(1)} %collective-permute-done.25.refs_2_), channel_id=1, source_target_pairs={{0,1},{1,0},{2,3},{3,2},{4,5},{5,4},{6,7},{7,6},{8,9},{9,8},{10,11... | collective-permute-start | bytes 884744 | tf_op jit(solution)/shard_map/ppermute | solution.py:34
  111.4 4.6 %collective-permute-start.22 = (f32[1,384]{1,0:T(1,128)S(1)}, f32[1,384]{1,0:T(1,128)S(1)}, u32[]{:S(2)}, u32[]{:S(2)}) collective-permute-start(f32[1,384]{1,0:T(1,128)S(1)} %shard_map.132.own), channel_id=1, source_target_pairs={{0,4},{1,13},{2,6},{3,15},{4,0},{5,9},{6,2},{7,11},{8,12},{9,5},{1... | collective-permute-start | bytes 4616 | tf_op jit(solution)/shard_map/ppermute | solution.py:561
  112.7 6.6 %collective-permute-start.24 = (f32[1,384]{1,0:T(1,128)S(1)}, f32[1,384]{1,0:T(1,128)S(1)}, u32[]{:S(2)}, u32[]{:S(2)}) collective-permute-start(f32[1,384]{1,0:T(1,128)S(1)} %shard_map.132.own), channel_id=1, source_target_pairs={{0,10},{1,11},{2,8},{3,9},{4,14},{5,15},{6,12},{7,13},{8,2},{9,3},... | collective-permute-start | bytes 4616 | tf_op jit(solution)/shard_map/ppermute | solution.py:34
  116.0 3.3 %collective-permute-start.23 = (f32[1,384]{1,0:T(1,128)S(1)}, f32[1,384]{1,0:T(1,128)S(1)}, u32[]{:S(2)}, u32[]{:S(2)}) collective-permute-start(f32[1,384]{1,0:T(1,128)S(1)} %collective-permute-done.22.split), channel_id=1, source_target_pairs={{0,1},{1,0},{2,3},{3,2},{4,5},{5,4},{6,7},{7,6},{8,9},{9,8},{10,11... | collective-permute-start | bytes 4616 | tf_op jit(solution)/shard_map/ppermute | solution.py:34
  120.4 3.7 %collective-permute-start.27 = (f32[1,384]{1,0:T(1,128)S(1)}, f32[1,384]{1,0:T(1,128)S(1)}, u32[]{:S(2)}, u32[]{:S(2)}) collective-permute-start(f32[1,384]{1,0:T(1,128)S(1)} %get-tuple-element.94.refs_1_), channel_id=1, source_target_pairs={{0,16},{1,17},{2,18},{3,19},{4,20},{5,21},{6,22},{7,23},{8,24},{9,... | collective-permute-start | bytes 4616 | tf_op jit(solution)/shard_map/ppermute | solution.py:34
  124.9 4.9 %collective-permute-start.28 = (f32[1,384]{1,0:T(1,128)S(1)}, f32[1,384]{1,0:T(1,128)S(1)}, u32[]{:S(2)}, u32[]{:S(2)}) collective-permute-start(f32[1,384]{1,0:T(1,128)S(1)} %shard_map.137), channel_id=1, source_target_pairs={{0,48},{1,49},{2,50},{3,51},{4,52},{5,53},{6,54},{7,55},{8,56},{9,... | collective-permute-start | bytes 4616 | tf_op jit(solution)/shard_map/ppermute | solution.py:34
  (12 other events, 67.1 us)

commit v6 on v5

--- a/solution.py
+++ b/solution.py
@@ -614,10 +614,10 @@
     leaving = local_call(hop_kernel, flags, [total, hop, merged], ROW, square)
     hop = up_row(leaving)
     entering = local_call(
-        forward_part_kernel, flags, [*others, in_row, prefix_0, prefix_1], ROW, 2 * square
+        forward_part_kernel, flags, [*others, after(in_row, leaving), prefix_0, prefix_1], ROW, 2 * square
     )
     hop = after(hop, entering)
-    row[1] = after(row[1], entering)
+    row[1] = after(row[1], hop)
     solved, returning = local_call(
         turn_kernel,
         flags,
@@ -632,12 +632,11 @@
             bound(level, backward_kernel), flags, [total, others[-1], levels[level][1]], ROW, square
         )
     arrived = row_exchange(total)
-    near = after(swap(row[1], MASKS[4]), total)
+    near = after(swap(row[1], MASKS[4]), arrived[0], arrived[2])
     row, levels = merge_level(
         flags, 4, row, levels + [None, (None, None, prefix_3, suffix_3)], near
     )
     _, low, _, suffix_4 = levels[4]
-    arrived[-1] = after(arrived[-1], low)
     total, in_row = local_call(
         row_backward_kernel, flags, [total, *arrived, blocks], (ROW, ROW), 3 * square
     )
@@ -702,7 +701,7 @@
     block, levels = first_products(flags, transition, outer)
     inner = swap(inner, 1)
     near = swap(after(block[1], inner), MASKS[1])
-    outer = outer_swap(after(outer, near))
+    outer = outer_swap(outer)
     block, levels = merge_level(flags, 1, block, levels, near)
     merged, half = block
     fetched = merged, [swap(half, mask) for mask in (SPLIT_MASKS[0], OPPOSITE, SPLIT_MASKS[1])]

time: 132 us -> 111 us (0.84)
  starting transfers between devices: 48.4 us -> 30.4 us
  waiting for transfers between devices: 40.8 us -> 37.7 us
    ppermute x22, starting transfers between devices: 40.8 us -> 23.9 us  [swap(): lax.ppermute(value, 'tile', [(i, i ^ mask) for i in range(lax.axis_size('...]
    ppermute x3, waiting for transfers between devices: 11.1 us -> 6.11 us  [up_row(): lax.ppermute(value, 'tile', [(i, (i + ROW_TILES) % count) for i in range(...]
    ppermute x22, waiting for transfers between devices: 23.2 us -> 26 us  [swap(): lax.ppermute(value, 'tile', [(i, i ^ mask) for i in range(lax.axis_size('...]
  transfers between devices with their start and end apart: 29 -> 29, of which waited for: 18 -> 19; matrix products, arithmetic and copies ran while one was open for 0% -> 0% of each run, Pallas kernels for 23% -> 30%
where the time goes in v6:
time: 111 us
  Pallas kernels  39.4 us (35%)
  waiting for transfers between devices  37.7 us (34%)
  starting transfers between devices  30.4 us (27%)
  between operations  1.68 us (2%)
  local copies, waits for them, and re-layouts  1.45 us (1%)
    pallas_call x25, Pallas kernels, local_call(): pl.pallas_call(kernel, out_shape=outs, in_specs=[SM] + [VM] * len(operand...  27.7 us
    ppermute x22, waiting for transfers between devices, swap(): lax.ppermute(value, 'tile', [(i, i ^ mask) for i in range(lax.axis_size('...  26 us
    ppermute x22, starting transfers between devices, swap(): lax.ppermute(value, 'tile', [(i, i ^ mask) for i in range(lax.axis_size('...  23.9 us
    pallas_call x1, Pallas kernels, substeps_call(): pl.pallas_call(substep_kernel, out_shape=(jax.ShapeDtypeStruct(grid_shape...  11.7 us
    ppermute x3, waiting for transfers between devices, up_row(): lax.ppermute(value, 'tile', [(i, (i + ROW_TILES) % count) for i in range(...  6.11 us
    ppermute x1, waiting for transfers between devices, coupled_velocity(): partner = lax.ppermute(picked, 'sub', [(i, i ^ 1) for i in range(count)])  2.94 us
    ppermute x2, starting transfers between devices, split_swap(): lax.ppermute(value, 'tile', [(i, i ^ mask) for i, mask in enumerate(masks)])  2.9 us
    ppermute x3, starting transfers between devices, up_row(): lax.ppermute(value, 'tile', [(i, (i + ROW_TILES) % count) for i in range(...  2.88 us
  transfers between devices with their start and end apart: 29, of which 19 were waited for; matrix products, arithmetic and copies ran while one was open for 0% of the time, Pallas kernels for 30%

profile of v6, /device:TPU:2, one launch (start us, length us, event | category | flops | bytes accessed | tf_op | source)
XLA Modules:
  0.0 110.6 jit_solution(18151236429391624537)
XLA Ops:
  7.5 2.0 %collective-permute-start.3 = (f32[192,384]{1,0:T(8,128)S(1)}, f32[192,384]{1,0:T(8,128)S(1)}, u32[]{:S(2)}, u32[]{:S(2)}) collective-permute-start(f32[192,384]{1,0:T(8,128)S(1)} %get-tuple-element.56), channel_id=1, source_target_pairs={{0,2},{1,3},{2,0},{3,1},{4,6},{5,7},{6,4},{7,5},{8,10},{9,11},{10,... | collective-permute-start | bytes 884744 | tf_op jit(solution)/shard_map/ppermute | solution.py:34
  10.2 6.7 %collective-permute-done.3.refs_2_ = f32[192,384]{1,0:T(8,128)S(1)} collective-permute-done((f32[192,384]{1,0:T(8,128)S(1)}, f32[192,384]{1,0:T(8,128)S(1)}, u32[]{:S(2)}, u32[]{:S(2)}) %collective-permute-start.3) | collective-permute-done | bytes 294944 | tf_op jit(solution)/shard_map/ppermute | solution.py:34
  16.9 1.5 %collective-permute-done.4.refs_3_ = f32[192,384]{1,0:T(8,128)S(1)} collective-permute-done((f32[192,384]{1,0:T(8,128)S(1)}, f32[192,384]{1,0:T(8,128)S(1)}, u32[]{:S(2)}, u32[]{:S(2)}) %collective-permute-start.4) | collective-permute-done | bytes 294944 | tf_op jit(solution)/shard_map/ppermute | solution.py:34
  19.8 6.1 %collective-permute-start.15 = (f32[192,384]{1,0:T(8,128)S(1)}, f32[192,384]{1,0:T(8,128)S(1)}, u32[]{:S(2)}, u32[]{:S(2)}) collective-permute-start(f32[192,384]{1,0:T(8,128)S(1)} %get-tuple-element.57), channel_id=1, source_target_pairs={{0,12},{1,13},{2,14},{3,15},{4,8},{5,9},{6,10},{7,11},{8,4},{9,5},... | collective-permute-start | bytes 884744 | tf_op jit(solution)/shard_map/ppermute | solution.py:34
  25.9 1.8 %collective-permute-start.13 = (f32[192,384]{1,0:T(8,128)S(1)}, f32[192,384]{1,0:T(8,128)S(1)}, u32[]{:S(2)}, u32[]{:S(2)}) collective-permute-start(f32[192,384]{1,0:T(8,128)S(1)} %get-tuple-element.57), channel_id=1, source_target_pairs={{0,10},{1,11},{2,8},{3,9},{4,14},{5,15},{6,12},{7,13},{8,2},{9,3},... | collective-permute-start | bytes 884744 | tf_op jit(solution)/shard_map/ppermute | solution.py:34
  28.8 11.7 %shard_map.117 = (f32[3,4,32,128]{3,2,1,0:T(8,128)}, f32[3,4,32,128]{3,2,1,0:T(8,128)S(1)}, f32[1,384]{1,0:T(1,128)S(1)}) custom-call(s32[10]{0:T(128)S(1)} %stack.43.flags.refs_0_, f32[1]{0:T(128)S(6)} %div.16.step, f32[3,4,32,128]{3,2,1,0:T(8,128)S(1)} %bitcast.24, f32[3,4,32,128]{3,2,1,0:T(8,128)S(1)} %bitcast.26, f32[3,4,32,128]{3,2,1,0:T(8,128)S(1)} %bitcast.28, ...), custom_call_target="tpu_custom_call" | custom-call | flops 3623878656 | bytes 2162688 | tf_op jit(solution)/shard_map/pallas_call | solution.py:282
  41.1 2.9 %collective-permute-done.5.partner = f32[1,384]{1,0:T(1,128)S(1)} collective-permute-done((f32[1,384]{1,0:T(1,128)S(1)}, f32[1,384]{1,0:T(1,128)S(1)}, u32[]{:S(2)}, u32[]{:S(2)}) %collective-permute-start.5) | collective-permute-done | bytes 1568 | tf_op jit(solution)/shard_map/ppermute | solution.py:589
  47.4 3.1 %collective-permute-done.7.refs_2_.other_1 = f32[1,384]{1,0:T(1,128)S(1)} collective-permute-done((f32[1,384]{1,0:T(1,128)S(1)}, f32[1,384]{1,0:T(1,128)S(1)}, u32[]{:S(2)}, u32[]{:S(2)}) %collective-permute-start.7) | collective-permute-done | bytes 1568 | tf_op jit(solution)/shard_map/ppermute | solution.py:34
  51.2 3.9 %collective-permute-start.10 = (f32[1,384]{1,0:T(1,128)S(1)}, f32[1,384]{1,0:T(1,128)S(1)}, u32[]{:S(2)}, u32[]{:S(2)}) collective-permute-start(f32[1,384]{1,0:T(1,128)S(1)} %shard_map.122.own), channel_id=1, source_target_pairs={{0,10},{1,11},{2,8},{3,9},{4,14},{5,15},{6,12},{7,13},{8,2},{9,3},... | collective-permute-start | bytes 4616 | tf_op jit(solution)/shard_map/ppermute | solution.py:34
  57.9 1.7 %collective-permute-done.8.split = f32[1,384]{1,0:T(1,128)S(1)} collective-permute-done((f32[1,384]{1,0:T(1,128)S(1)}, f32[1,384]{1,0:T(1,128)S(1)}, u32[]{:S(2)}, u32[]{:S(2)}) %collective-permute-start.8) | collective-permute-done | bytes 1568 | tf_op jit(solution)/shard_map/ppermute | solution.py:561
  63.7 1.7 %collective-permute-start.17 = (f32[1,384]{1,0:T(1,128)S(1)}, f32[1,384]{1,0:T(1,128)S(1)}, u32[]{:S(2)}, u32[]{:S(2)}) collective-permute-start(f32[1,384]{1,0:T(1,128)S(1)} %get-tuple-element.74.total), channel_id=1, source_target_pairs={{0,16},{1,17},{2,18},{3,19},{4,20},{5,21},{6,22},{7,23},{8,24},{9,... | collective-permute-start | bytes 4616 | tf_op jit(solution)/shard_map/ppermute | solution.py:666
  65.3 2.7 %shard_map.125 = (f32[384,384]{1,0:T(8,128)S(1)}, f32[384,384]{1,0:T(8,128)S(1)}, f32[384,384]{1,0:T(8,128)S(1)}, f32[192,384]{1,0:T(8,128)S(1)}) custom-call(s32[10]{0:T(128)S(1)} %stack.43.flags.refs_0_, f32[4,384,384]{2,1,0:T(8,128)S(1)} %shard_map.123.blocks), custom_call_target="tpu_custom_call" | custom-call | flops 1019215872 | bytes 2359296 | tf_op jit(solution)/shard_map/pallas_call | solution.py:43
  70.3 2.2 %shard_map.127 = (f32[384,384]{1,0:T(8,128)S(1)}, f32[384,384]{1,0:T(8,128)S(1)}) custom-call(s32[10]{0:T(128)S(1)} %stack.43.flags.refs_0_, f32[4,384,384]{2,1,0:T(8,128)S(1)} %shard_map.123.blocks, f32[384,384]{1,0:T(8,128)S(1)} %get-tuple-element.78.high, f32[384,384]{1,0:T(8,128)S(1)} %get-tuple-element.79.low, ...), custom_call_target="tpu_custom_call" | custom-call | flops 679477248 | bytes 4718592 | tf_op jit(solution)/shard_map/pallas_call | solution.py:43
  72.6 1.5 %collective-permute-done.18.hop = f32[1,384]{1,0:T(1,128)S(1)} collective-permute-done((f32[1,384]{1,0:T(1,128)S(1)}, f32[1,384]{1,0:T(1,128)S(1)}, u32[]{:S(2)}, u32[]{:S(2)}) %collective-permute-start.18) | collective-permute-done | bytes 1568 | tf_op jit(solution)/shard_map/ppermute | solution.py:666
  75.5 4.1 %collective-permute-done.19.hop = f32[1,384]{1,0:T(1,128)S(1)} collective-permute-done((f32[1,384]{1,0:T(1,128)S(1)}, f32[1,384]{1,0:T(1,128)S(1)}, u32[]{:S(2)}, u32[]{:S(2)}) %collective-permute-start.19) | collective-permute-done | bytes 1568 | tf_op jit(solution)/shard_map/ppermute | solution.py:666
  82.7 1.8 %collective-permute-start.21 = (f32[1,384]{1,0:T(1,128)S(1)}, f32[1,384]{1,0:T(1,128)S(1)}, u32[]{:S(2)}, u32[]{:S(2)}) collective-permute-start(f32[1,384]{1,0:T(1,128)S(1)} %shard_map.131.refs_1_), channel_id=1, source_target_pairs={{0,2},{1,3},{2,0},{3,1},{4,6},{5,7},{6,4},{7,5},{8,10},{9,11},{10,... | collective-permute-start | bytes 4616 | tf_op jit(solution)/shard_map/ppermute | solution.py:34
  84.5 1.8 %collective-permute-done.21.refs_2_.other_1 = f32[1,384]{1,0:T(1,128)S(1)} collective-permute-done((f32[1,384]{1,0:T(1,128)S(1)}, f32[1,384]{1,0:T(1,128)S(1)}, u32[]{:S(2)}, u32[]{:S(2)}) %collective-permute-start.21) | collective-permute-done | bytes 1568 | tf_op jit(solution)/shard_map/ppermute | solution.py:34
  87.1 1.5 %collective-permute-start.22 = (f32[1,384]{1,0:T(1,128)S(1)}, f32[1,384]{1,0:T(1,128)S(1)}, u32[]{:S(2)}, u32[]{:S(2)}) collective-permute-start(f32[1,384]{1,0:T(1,128)S(1)} %shard_map.132.own), channel_id=1, source_target_pairs={{0,4},{1,13},{2,6},{3,15},{4,0},{5,9},{6,2},{7,11},{8,12},{9,5},{1... | collective-permute-start | bytes 4616 | tf_op jit(solution)/shard_map/ppermute | solution.py:561
  88.6 2.1 %collective-permute-start.24 = (f32[1,384]{1,0:T(1,128)S(1)}, f32[1,384]{1,0:T(1,128)S(1)}, u32[]{:S(2)}, u32[]{:S(2)}) collective-permute-start(f32[1,384]{1,0:T(1,128)S(1)} %shard_map.132.own), channel_id=1, source_target_pairs={{0,10},{1,11},{2,8},{3,9},{4,14},{5,15},{6,12},{7,13},{8,2},{9,3},... | collective-permute-start | bytes 4616 | tf_op jit(solution)/shard_map/ppermute | solution.py:34
  91.7 3.5 %collective-permute-done.24.opposite = f32[1,384]{1,0:T(1,128)S(1)} collective-permute-done((f32[1,384]{1,0:T(1,128)S(1)}, f32[1,384]{1,0:T(1,128)S(1)}, u32[]{:S(2)}, u32[]{:S(2)}) %collective-permute-start.24) | collective-permute-done | bytes 1568 | tf_op jit(solution)/shard_map/ppermute | solution.py:34
  98.0 2.1 %collective-permute-start.25 = (f32[1,384]{1,0:T(1,128)S(1)}, f32[1,384]{1,0:T(1,128)S(1)}, u32[]{:S(2)}, u32[]{:S(2)}) collective-permute-start(f32[1,384]{1,0:T(1,128)S(1)} %get-tuple-element.88.refs_1_), channel_id=1, source_target_pairs={{0,16},{1,17},{2,18},{3,19},{4,20},{5,21},{6,22},{7,23},{8,24},{9,... | collective-permute-start | bytes 4616 | tf_op jit(solution)/shard_map/ppermute | solution.py:34
  100.8 2.1 %shard_map.136 = (f32[384,384]{1,0:T(8,128)}, f32[384,384]{1,0:T(8,128)S(1)}) custom-call(s32[10]{0:T(128)S(1)} %stack.43.flags.refs_0_, f32[384,384]{1,0:T(8,128)S(1)} %get-tuple-element.93.refs_1_, f32[384,384]{1,0:T(8,128)S(1)} %get-tuple-element.94.refs_2_.refs_3_, f32[384,384]{1,0:T(8,128)S(1)} %get-tuple-element.81.prefix.refs_3_, ...), custom_call_target="tpu_custom_call" | custom-call | flops 339738624 | bytes 2359296 | tf_op jit(solution)/shard_map/pallas_call | solution.py:43
  105.0 3.5 %collective-permute-done.28.other = f32[1,384]{1,0:T(1,128)S(1)} collective-permute-done((f32[1,384]{1,0:T(1,128)S(1)}, f32[1,384]{1,0:T(1,128)S(1)}, u32[]{:S(2)}, u32[]{:S(2)}) %collective-permute-start.28) | collective-permute-done | bytes 1568 | tf_op jit(solution)/shard_map/ppermute | solution.py:34
  108.6 2.0 %shard_map.138 = f32[3,4,32,128]{3,2,1,0:T(8,128)} custom-call(s32[10]{0:T(128)S(1)} %stack.43.flags.refs_0_, f32[384,384]{1,0:T(8,128)S(1)} %get-tuple-element.101.inverse, f32[1,384]{1,0:T(1,128)S(1)} %shard_map.134.entering, f32[1,384]{1,0:T(1,128)S(1)} %collective-permute-done.28.other, f32[384,384]{1,0:T(8,128)S(1)} %get-tuple-element.95.suffix, ...), custom_call_target="tpu_custom_call" | custom-call | flops 589824 | bytes 1446912 | tf_op jit(solution)/shard_map/pallas_call | solution.py:43
  (76 shorter events, 34.7 us)
Async XLA Ops:
  4.1 2.1 %collective-permute-start.1 = (f32[384,384]{1,0:T(8,128)S(1)}, f32[384,384]{1,0:T(8,128)S(1)}, u32[]{:S(2)}, u32[]{:S(2)}) collective-permute-start(f32[384,384]{1,0:T(8,128)S(1)} %shard_map.114.own.transition), channel_id=1, source_target_pairs={{0,1},{1,0},{2,3},{3,2},{4,5},{5,4},{6,7},{7,6},{8,9},{9,8},{10,11... | collective-permute-start | bytes 1769480 | tf_op jit(solution)/shard_map/ppermute | solution.py:34
  4.8 2.6 %collective-permute-start.2 = (f32[37,32,128]{2,1,0:T(8,128)S(1)}, f32[37,32,128]{2,1,0:T(8,128)S(1)}, u32[]{:S(2)}, u32[]{:S(2)}) collective-permute-start(f32[37,32,128]{2,1,0:T(8,128)S(1)} %get-tuple-element.55), channel_id=1, source_target_pairs={{0,1},{1,0},{2,3},{3,2},{4,5},{5,4},{6,7},{7,6},{8,9},{9,8},{10,11... | collective-permute-start | bytes 1818632 | tf_op jit(solution)/shard_map/ppermute | solution.py:34
  7.5 9.4 %collective-permute-start.3 = (f32[192,384]{1,0:T(8,128)S(1)}, f32[192,384]{1,0:T(8,128)S(1)}, u32[]{:S(2)}, u32[]{:S(2)}) collective-permute-start(f32[192,384]{1,0:T(8,128)S(1)} %get-tuple-element.56), channel_id=1, source_target_pairs={{0,2},{1,3},{2,0},{3,1},{4,6},{5,7},{6,4},{7,5},{8,10},{9,11},{10,... | collective-permute-start | bytes 884744 | tf_op jit(solution)/shard_map/ppermute | solution.py:34
  9.5 19.3 %collective-permute-start = (f32[37,32,128]{2,1,0:T(8,128)S(1)}, f32[37,32,128]{2,1,0:T(8,128)S(1)}, u32[]{:S(2)}, u32[]{:S(2)}) collective-permute-start(f32[37,32,128]{2,1,0:T(8,128)S(1)} %get-tuple-element.51), channel_id=1, source_target_pairs={{1,2},{2,1},{3,4},{4,3},{5,6},{6,5},{7,8},{8,7},{9,10},{10,9},{11,... | collective-permute-start | bytes 1818632 | tf_op jit(solution)/shard_map/ppermute | solution.py:674
  19.8 39.7 %collective-permute-start.15 = (f32[192,384]{1,0:T(8,128)S(1)}, f32[192,384]{1,0:T(8,128)S(1)}, u32[]{:S(2)}, u32[]{:S(2)}) collective-permute-start(f32[192,384]{1,0:T(8,128)S(1)} %get-tuple-element.57), channel_id=1, source_target_pairs={{0,12},{1,13},{2,14},{3,15},{4,8},{5,9},{6,10},{7,11},{8,4},{9,5},... | collective-permute-start | bytes 884744 | tf_op jit(solution)/shard_map/ppermute | solution.py:34
  25.9 33.6 %collective-permute-start.13 = (f32[192,384]{1,0:T(8,128)S(1)}, f32[192,384]{1,0:T(8,128)S(1)}, u32[]{:S(2)}, u32[]{:S(2)}) collective-permute-start(f32[192,384]{1,0:T(8,128)S(1)} %get-tuple-element.57), channel_id=1, source_target_pairs={{0,10},{1,11},{2,8},{3,9},{4,14},{5,15},{6,12},{7,13},{8,2},{9,3},... | collective-permute-start | bytes 884744 | tf_op jit(solution)/shard_map/ppermute | solution.py:34
  27.7 32.3 %collective-permute-start.11 = (f32[192,384]{1,0:T(8,128)S(1)}, f32[192,384]{1,0:T(8,128)S(1)}, u32[]{:S(2)}, u32[]{:S(2)}) collective-permute-start(f32[192,384]{1,0:T(8,128)S(1)} %get-tuple-element.57), channel_id=1, source_target_pairs={{0,4},{1,5},{2,6},{3,7},{4,0},{5,1},{6,2},{7,3},{8,12},{9,13},{10,... | collective-permute-start | bytes 884744 | tf_op jit(solution)/shard_map/ppermute | solution.py:34
  40.4 3.6 %collective-permute-start.5 = (f32[1,384]{1,0:T(1,128)S(1)}, f32[1,384]{1,0:T(1,128)S(1)}, u32[]{:S(2)}, u32[]{:S(2)}) collective-permute-start(f32[1,384]{1,0:T(1,128)S(1)} %get-tuple-element.60.picked), channel_id=1, source_target_pairs={{0,64},{64,0},{128,192},{192,128},{1,65},{65,1},{129,193},{193,129... | collective-permute-start | bytes 4616 | tf_op jit(solution)/shard_map/ppermute | solution.py:589
  46.8 3.7 %collective-permute-start.7 = (f32[1,384]{1,0:T(1,128)S(1)}, f32[1,384]{1,0:T(1,128)S(1)}, u32[]{:S(2)}, u32[]{:S(2)}) collective-permute-start(f32[1,384]{1,0:T(1,128)S(1)} %shard_map.121.refs_1_), channel_id=1, source_target_pairs={{0,2},{1,3},{2,0},{3,1},{4,6},{5,7},{6,4},{7,5},{8,10},{9,11},{10,... | collective-permute-start | bytes 4616 | tf_op jit(solution)/shard_map/ppermute | solution.py:34
  51.2 6.7 %collective-permute-start.10 = (f32[1,384]{1,0:T(1,128)S(1)}, f32[1,384]{1,0:T(1,128)S(1)}, u32[]{:S(2)}, u32[]{:S(2)}) collective-permute-start(f32[1,384]{1,0:T(1,128)S(1)} %shard_map.122.own), channel_id=1, source_target_pairs={{0,10},{1,11},{2,8},{3,9},{4,14},{5,15},{6,12},{7,13},{8,2},{9,3},... | collective-permute-start | bytes 4616 | tf_op jit(solution)/shard_map/ppermute | solution.py:34
  55.0 4.5 %collective-permute-start.8 = (f32[1,384]{1,0:T(1,128)S(1)}, f32[1,384]{1,0:T(1,128)S(1)}, u32[]{:S(2)}, u32[]{:S(2)}) collective-permute-start(f32[1,384]{1,0:T(1,128)S(1)} %shard_map.122.own), channel_id=1, source_target_pairs={{0,4},{1,13},{2,6},{3,15},{4,0},{5,9},{6,2},{7,11},{8,12},{9,5},{1... | collective-permute-start | bytes 4616 | tf_op jit(solution)/shard_map/ppermute | solution.py:561
  59.5 2.0 %collective-permute-start.14 = (f32[192,384]{1,0:T(8,128)S(1)}, f32[192,384]{1,0:T(8,128)S(1)}, u32[]{:S(2)}, u32[]{:S(2)}) collective-permute-start(f32[192,384]{1,0:T(8,128)S(1)} %collective-permute-done.13.near_far), channel_id=1, source_target_pairs={{0,1},{1,0},{2,3},{3,2},{4,5},{5,4},{6,7},{7,6},{8,9},{9,8},{10,11... | collective-permute-start | bytes 884744 | tf_op jit(solution)/shard_map/ppermute | solution.py:34
  60.0 1.9 %collective-permute-start.12 = (f32[192,384]{1,0:T(8,128)S(1)}, f32[192,384]{1,0:T(8,128)S(1)}, u32[]{:S(2)}, u32[]{:S(2)}) collective-permute-start(f32[192,384]{1,0:T(8,128)S(1)} %collective-permute-done.11.near), channel_id=1, source_target_pairs={{0,1},{1,0},{2,3},{3,2},{4,5},{5,4},{6,7},{7,6},{8,9},{9,8},{10,11... | collective-permute-start | bytes 884744 | tf_op jit(solution)/shard_map/ppermute | solution.py:34
  60.1 2.5 %collective-permute-start.9 = (f32[1,384]{1,0:T(1,128)S(1)}, f32[1,384]{1,0:T(1,128)S(1)}, u32[]{:S(2)}, u32[]{:S(2)}) collective-permute-start(f32[1,384]{1,0:T(1,128)S(1)} %collective-permute-done.8.split), channel_id=1, source_target_pairs={{0,1},{1,0},{2,3},{3,2},{4,5},{5,4},{6,7},{7,6},{8,9},{9,8},{10,11... | collective-permute-start | bytes 4616 | tf_op jit(solution)/shard_map/ppermute | solution.py:34
  63.7 4.9 %collective-permute-start.17 = (f32[1,384]{1,0:T(1,128)S(1)}, f32[1,384]{1,0:T(1,128)S(1)}, u32[]{:S(2)}, u32[]{:S(2)}) collective-permute-start(f32[1,384]{1,0:T(1,128)S(1)} %get-tuple-element.74.total), channel_id=1, source_target_pairs={{0,16},{1,17},{2,18},{3,19},{4,20},{5,21},{6,22},{7,23},{8,24},{9,... | collective-permute-start | bytes 4616 | tf_op jit(solution)/shard_map/ppermute | solution.py:666
  69.2 4.9 %collective-permute-start.18 = (f32[1,384]{1,0:T(1,128)S(1)}, f32[1,384]{1,0:T(1,128)S(1)}, u32[]{:S(2)}, u32[]{:S(2)}) collective-permute-start(f32[1,384]{1,0:T(1,128)S(1)} %shard_map.126), channel_id=1, source_target_pairs={{0,16},{1,17},{2,18},{3,19},{4,20},{5,21},{6,22},{7,23},{8,24},{9,... | collective-permute-start | bytes 4616 | tf_op jit(solution)/shard_map/ppermute | solution.py:666
  74.8 4.9 %collective-permute-start.19 = (f32[1,384]{1,0:T(1,128)S(1)}, f32[1,384]{1,0:T(1,128)S(1)}, u32[]{:S(2)}, u32[]{:S(2)}) collective-permute-start(f32[1,384]{1,0:T(1,128)S(1)} %shard_map.128), channel_id=1, source_target_pairs={{0,16},{1,17},{2,18},{3,19},{4,20},{5,21},{6,22},{7,23},{8,24},{9,... | collective-permute-start | bytes 4616 | tf_op jit(solution)/shard_map/ppermute | solution.py:666
  79.6 15.6 %collective-permute-start.26 = (f32[192,384]{1,0:T(8,128)S(1)}, f32[192,384]{1,0:T(8,128)S(1)}, u32[]{:S(2)}, u32[]{:S(2)}) collective-permute-start(f32[192,384]{1,0:T(8,128)S(1)} %get-tuple-element.91), channel_id=1, source_target_pairs={{0,16},{1,17},{2,18},{3,19},{4,20},{5,21},{6,22},{7,23},{8,24},{9,... | collective-permute-start | bytes 884744 | tf_op jit(solution)/shard_map/ppermute | solution.py:34
  82.7 3.7 %collective-permute-start.21 = (f32[1,384]{1,0:T(1,128)S(1)}, f32[1,384]{1,0:T(1,128)S(1)}, u32[]{:S(2)}, u32[]{:S(2)}) collective-permute-start(f32[1,384]{1,0:T(1,128)S(1)} %shard_map.131.refs_1_), channel_id=1, source_target_pairs={{0,2},{1,3},{2,0},{3,1},{4,6},{5,7},{6,4},{7,5},{8,10},{9,11},{10,... | collective-permute-start | bytes 4616 | tf_op jit(solution)/shard_map/ppermute | solution.py:34
  87.1 4.6 %collective-permute-start.22 = (f32[1,384]{1,0:T(1,128)S(1)}, f32[1,384]{1,0:T(1,128)S(1)}, u32[]{:S(2)}, u32[]{:S(2)}) collective-permute-start(f32[1,384]{1,0:T(1,128)S(1)} %shard_map.132.own), channel_id=1, source_target_pairs={{0,4},{1,13},{2,6},{3,15},{4,0},{5,9},{6,2},{7,11},{8,12},{9,5},{1... | collective-permute-start | bytes 4616 | tf_op jit(solution)/shard_map/ppermute | solution.py:561
  88.6 6.6 %collective-permute-start.24 = (f32[1,384]{1,0:T(1,128)S(1)}, f32[1,384]{1,0:T(1,128)S(1)}, u32[]{:S(2)}, u32[]{:S(2)}) collective-permute-start(f32[1,384]{1,0:T(1,128)S(1)} %shard_map.132.own), channel_id=1, source_target_pairs={{0,10},{1,11},{2,8},{3,9},{4,14},{5,15},{6,12},{7,13},{8,2},{9,3},... | collective-permute-start | bytes 4616 | tf_op jit(solution)/shard_map/ppermute | solution.py:34
  95.2 4.9 %collective-permute-start.27 = (f32[192,384]{1,0:T(8,128)S(1)}, f32[192,384]{1,0:T(8,128)S(1)}, u32[]{:S(2)}, u32[]{:S(2)}) collective-permute-start(f32[192,384]{1,0:T(8,128)S(1)} %collective-permute-done.26.refs_2_), channel_id=1, source_target_pairs={{0,1},{1,0},{2,3},{3,2},{4,5},{5,4},{6,7},{7,6},{8,9},{9,8},{10,11... | collective-permute-start | bytes 884744 | tf_op jit(solution)/shard_map/ppermute | solution.py:34
  98.0 4.9 %collective-permute-start.25 = (f32[1,384]{1,0:T(1,128)S(1)}, f32[1,384]{1,0:T(1,128)S(1)}, u32[]{:S(2)}, u32[]{:S(2)}) collective-permute-start(f32[1,384]{1,0:T(1,128)S(1)} %get-tuple-element.88.refs_1_), channel_id=1, source_target_pairs={{0,16},{1,17},{2,18},{3,19},{4,20},{5,21},{6,22},{7,23},{8,24},{9,... | collective-permute-start | bytes 4616 | tf_op jit(solution)/shard_map/ppermute | solution.py:34
  103.7 4.9 %collective-permute-start.28 = (f32[1,384]{1,0:T(1,128)S(1)}, f32[1,384]{1,0:T(1,128)S(1)}, u32[]{:S(2)}, u32[]{:S(2)}) collective-permute-start(f32[1,384]{1,0:T(1,128)S(1)} %shard_map.137), channel_id=1, source_target_pairs={{0,48},{1,49},{2,50},{3,51},{4,52},{5,53},{6,54},{7,55},{8,56},{9,... | collective-permute-start | bytes 4616 | tf_op jit(solution)/shard_map/ppermute | solution.py:34
  (12 other events, 60.2 us)

commit v7 on v6

--- a/solution.py
+++ b/solution.py
@@ -13,7 +13,7 @@
 DEEP = 3 * CX
 NEAR = CX - 1
 PACKED = 37
-CORE, PAIR, SIDE, LAST, STEPS = 0, 6, 7, 8, 9
+CORE, PAIR, SIDE, LAST = 0, 6, 7, 8
 GROUPS = CY // 8
 MASKS = (1, 2, 4, 12, 16, 48)
 SPLIT_MASKS = (4, 12)
@@ -38,16 +38,32 @@
     return pl.CostEstimate(flops=flops, bytes_accessed=nbytes, transcendentals=0)
 
 
-def local_call(kernel, flags, operands, outs, flops=0):
+class Place:
+    def __getitem__(self, item):
+        tile, sub = lax.axis_index("tile"), lax.axis_index("sub")
+        if item == PAIR:
+            return sub // 2
+        if item == SIDE:
+            return sub % 2
+        if item == LAST:
+            return (tile == lax.axis_size("tile") - 1).astype(jnp.int32)
+        return (tile >> item) & 1
+
+
+def local_call(kernel, place, operands, outs, flops=0):
     nbytes = sum(o.size * 4 for o in operands)
+
+    def placed(*refs):
+        kernel(place, *refs)
+
     return pl.pallas_call(
-        kernel,
+        placed,
         out_shape=outs,
-        in_specs=[SM] + [VM] * len(operands),
+        in_specs=[VM] * len(operands),
         out_specs=jax.tree.map(lambda _: VM, outs),
         compiler_params=pltpu.CompilerParams(vmem_limit_bytes=GRANT),
         cost_estimate=cost(flops, nbytes),
-    )(flags, *operands)
+    )(*operands)
 
 
 def halves(value):
@@ -138,11 +154,12 @@
 
 
 def substep_kernel(
-    flags, step, displacement, velocity, external_load, node_mass, modulus,
+    count, step, displacement, velocity, external_load, node_mass, modulus,
     outer, inner, stiffness, nodes,
     displacement_out, velocity_out, picked,
     disp, vel, load, inverse_mass, factor, stiff, even, odd, even_force, odd_force, upper,
 ):
+    flags = Place()
     first = flags[CORE] == 0
 
     def put_mass(low, mass):
@@ -253,7 +270,7 @@
 
         return lax.fori_loop(0, CX + 1 - k, two_layers, carry)
 
-    lax.fori_loop(0, flags[STEPS], one_substep, 0)
+    lax.fori_loop(0, count[0], one_substep, 0)
     displacement_out[...] = disp[:, CX : 2 * CX]
     final = vel[:, CX : 2 * CX]
     velocity_out[...] = final
@@ -277,7 +294,7 @@
         target[pl.ds(33, CX)] = modulus[...]
 
 
-def substeps_call(flags, step, state, outer, inner, stiffness, nodes):
+def substeps_call(count, step, state, outer, inner, stiffness, nodes):
     grid_shape = (3, CX, CY, CZ)
     return pl.pallas_call(
         substep_kernel,
@@ -303,7 +320,7 @@
         ],
         compiler_params=pltpu.CompilerParams(vmem_limit_bytes=20 << 20),
         cost_estimate=cost(32 * 2 * 192 * 576 * 512, 3 * 720896),
-    )(flags, step, *state, outer, inner, stiffness, nodes)
+    )(count, step, *state, outer, inner, stiffness, nodes)
 
 def transition_kernel(flags, inverse, lower, transition):
     transition[...] = -product(inverse[...], lower[...])
@@ -686,11 +703,8 @@
     factor_inverse,
     factor_lower,
 ):
-    sub, tile = lax.axis_index("sub"), lax.axis_index("tile")
-    last = tile == lax.axis_size("tile") - 1
-    flags = jnp.stack(
-        [(tile >> k) & 1 for k in range(6)] + [sub // 2, sub % 2, last, substeps[0]]
-    ).astype(jnp.int32)
+    flags = Place()
+    sub = lax.axis_index("sub")
     step = coarse_step / substeps.astype(f32)
     state = [displacement[0], velocity[0], external_load[0], node_mass[0], modulus[0]]
     packed = jax.ShapeDtypeStruct((PACKED, CY, CZ), f32)
@@ -707,7 +721,7 @@
     fetched = merged, [swap(half, mask) for mask in (SPLIT_MASKS[0], OPPOSITE, SPLIT_MASKS[1])]
     outer = after(outer, half)
     final_displacement, final_velocity, picked = substeps_call(
-        flags, step, state, outer, inner, stiffness, interface_nodes
+        substeps, step, state, outer, inner, stiffness, interface_nodes
     )
     coupled = coupled_velocity(
         flags,

time: 111 us -> 99.5 us (0.90)
  Pallas kernels: 39.4 us -> 21.5 us
  waiting for transfers between devices: 37.7 us -> 46.8 us
  starting transfers between devices: 30.4 us -> 27.2 us
    pallas_call x25, Pallas kernels: 27.7 us -> 14.2 us  [local_call(): pl.pallas_call(placed, out_shape=outs, in_specs=[VM] * len(operands), out...]
    ppermute x22, waiting for transfers between devices: 26 us -> 33.7 us  [swap(): lax.ppermute(value, 'tile', [(i, i ^ mask) for i in range(lax.axis_size('...]
    pallas_call x1, Pallas kernels: 11.7 us -> 7.33 us  [substeps_call(): pl.pallas_call(substep_kernel, out_shape=(jax.ShapeDtypeStruct(grid_shape...]
    ppermute x22, starting transfers between devices: 23.9 us -> 21.4 us  [swap(): lax.ppermute(value, 'tile', [(i, i ^ mask) for i in range(lax.axis_size('...]
    ppermute x3, waiting for transfers between devices: 6.11 us -> 8.31 us  [up_row(): lax.ppermute(value, 'tile', [(i, (i + ROW_TILES) % count) for i in range(...]
    ppermute x2, waiting for transfers between devices: 2.63 us -> 1.38 us  [split_swap(): lax.ppermute(value, 'tile', [(i, i ^ mask) for i, mask in enumerate(masks)])]
  transfers between devices with their start and end apart: 29 -> 29, of which waited for: 19 -> 20; matrix products, arithmetic and copies ran while one was open for 0% -> 0% of each run, Pallas kernels for 30% -> 19%
where the time goes in v7:
time: 99.5 us; the launch traced here: 98.8 us
  waiting for transfers between devices  46.8 us (47%)
  starting transfers between devices  27.2 us (27%)
  Pallas kernels  21.5 us (22%)
  between operations  1.62 us (2%)
  local copies, waits for them, and re-layouts  1.61 us (2%)
    ppermute x22, waiting for transfers between devices, swap(): lax.ppermute(value, 'tile', [(i, i ^ mask) for i in range(lax.axis_size('...  33.7 us
    ppermute x22, starting transfers between devices, swap(): lax.ppermute(value, 'tile', [(i, i ^ mask) for i in range(lax.axis_size('...  21.4 us
    pallas_call x25, Pallas kernels, local_call(): pl.pallas_call(placed, out_shape=outs, in_specs=[VM] * len(operands), out...  14.2 us
    ppermute x3, waiting for transfers between devices, up_row(): lax.ppermute(value, 'tile', [(i, (i + ROW_TILES) % count) for i in range(...  8.31 us
    pallas_call x1, Pallas kernels, substeps_call(): pl.pallas_call(substep_kernel, out_shape=(jax.ShapeDtypeStruct(grid_shape...  7.33 us
    ppermute x1, waiting for transfers between devices, coupled_velocity(): partner = lax.ppermute(picked, 'sub', [(i, i ^ 1) for i in range(count)])  3.48 us
    ppermute x2, starting transfers between devices, split_swap(): lax.ppermute(value, 'tile', [(i, i ^ mask) for i, mask in enumerate(masks)])  2.77 us
    ppermute x3, starting transfers between devices, up_row(): lax.ppermute(value, 'tile', [(i, (i + ROW_TILES) % count) for i in range(...  2.33 us
  transfers between devices with their start and end apart: 29, of which 20 were waited for; matrix products, arithmetic and copies ran while one was open for 0% of the time, Pallas kernels for 19%

profile of v7, /device:TPU:2, one launch (start us, length us, event | category | flops | bytes accessed | tf_op | source)
XLA Modules:
  0.0 98.8 jit_solution(9128993194294208680)
XLA Ops:
  0.6 1.3 %dynamic-slice_bitcast_fusion = (f32[384,384]{1,0:T(8,128)S(1)}, f32[384,384]{1,0:T(8,128)S(1)}) fusion(f32[2,384,384]{2,1,0:T(8,128)} %param.19, s32[]{:T(128)S(6)} %select_n.12, f32[2,384,384]{2,1,0:T(8,128)} %param.18), kind=kLoop, calls=%fused_computation | loop fusion | bytes 2359300 | tf_op jit(solution)/shard_map/jit(dynamic_index_in_dim)/squeeze | solution.py:712
  5.7 1.9 %collective-permute-start.3 = (f32[192,384]{1,0:T(8,128)S(1)}, f32[192,384]{1,0:T(8,128)S(1)}, u32[]{:S(2)}, u32[]{:S(2)}) collective-permute-start(f32[192,384]{1,0:T(8,128)S(1)} %get-tuple-element.56), channel_id=1, source_target_pairs={{0,2},{1,3},{2,0},{3,1},{4,6},{5,7},{6,4},{7,5},{8,10},{9,11},{10,... | collective-permute-start | bytes 884744 | tf_op jit(solution)/shard_map/ppermute | solution.py:34
  8.3 6.7 %collective-permute-done.3.refs_1_ = f32[192,384]{1,0:T(8,128)S(1)} collective-permute-done((f32[192,384]{1,0:T(8,128)S(1)}, f32[192,384]{1,0:T(8,128)S(1)}, u32[]{:S(2)}, u32[]{:S(2)}) %collective-permute-start.3) | collective-permute-done | bytes 294944 | tf_op jit(solution)/shard_map/ppermute | solution.py:34
  17.4 6.2 %collective-permute-start.15 = (f32[192,384]{1,0:T(8,128)S(1)}, f32[192,384]{1,0:T(8,128)S(1)}, u32[]{:S(2)}, u32[]{:S(2)}) collective-permute-start(f32[192,384]{1,0:T(8,128)S(1)} %get-tuple-element.57), channel_id=1, source_target_pairs={{0,12},{1,13},{2,14},{3,15},{4,8},{5,9},{6,10},{7,11},{8,4},{9,5},... | collective-permute-start | bytes 884744 | tf_op jit(solution)/shard_map/ppermute | solution.py:34
  23.6 1.8 %collective-permute-start.13 = (f32[192,384]{1,0:T(8,128)S(1)}, f32[192,384]{1,0:T(8,128)S(1)}, u32[]{:S(2)}, u32[]{:S(2)}) collective-permute-start(f32[192,384]{1,0:T(8,128)S(1)} %get-tuple-element.57), channel_id=1, source_target_pairs={{0,10},{1,11},{2,8},{3,9},{4,14},{5,15},{6,12},{7,13},{8,2},{9,3},... | collective-permute-start | bytes 884744 | tf_op jit(solution)/shard_map/ppermute | solution.py:34
  26.4 7.3 %shard_map.117 = (f32[3,4,32,128]{3,2,1,0:T(8,128)}, f32[3,4,32,128]{3,2,1,0:T(8,128)S(1)}, f32[1,384]{1,0:T(1,128)S(1)}) custom-call(s32[1]{0:T(128)S(6)} %copy.12.count, f32[1]{0:T(128)S(6)} %div.12.step, f32[3,4,32,128]{3,2,1,0:T(8,128)S(1)} %bitcast.15, f32[3,4,32,128]{3,2,1,0:T(8,128)S(1)} %bitcast.17, f32[3,4,32,128]{3,2,1,0:T(8,128)S(1)} %bitcast.19, ...), custom_call_target="tpu_custom_call" | custom-call | flops 3623878656 | bytes 2162688 | tf_op jit(solution)/shard_map/pallas_call | solution.py:299
  33.8 3.5 %collective-permute-done.5.refs_2_ = f32[1,384]{1,0:T(1,128)S(1)} collective-permute-done((f32[1,384]{1,0:T(1,128)S(1)}, f32[1,384]{1,0:T(1,128)S(1)}, u32[]{:S(2)}, u32[]{:S(2)}) %collective-permute-start.5) | collective-permute-done | bytes 1568 | tf_op jit(solution)/shard_map/ppermute | solution.py:606
  39.3 3.3 %collective-permute-done.7.refs_1_ = f32[1,384]{1,0:T(1,128)S(1)} collective-permute-done((f32[1,384]{1,0:T(1,128)S(1)}, f32[1,384]{1,0:T(1,128)S(1)}, u32[]{:S(2)}, u32[]{:S(2)}) %collective-permute-start.7) | collective-permute-done | bytes 1568 | tf_op jit(solution)/shard_map/ppermute | solution.py:34
  42.7 3.7 %collective-permute-start.10 = (f32[1,384]{1,0:T(1,128)S(1)}, f32[1,384]{1,0:T(1,128)S(1)}, u32[]{:S(2)}, u32[]{:S(2)}) collective-permute-start(f32[1,384]{1,0:T(1,128)S(1)} %shard_map.122.refs_0_), channel_id=1, source_target_pairs={{0,10},{1,11},{2,8},{3,9},{4,14},{5,15},{6,12},{7,13},{8,2},{9,3},... | collective-permute-start | bytes 4616 | tf_op jit(solution)/shard_map/ppermute | solution.py:34
  46.5 1.5 %collective-permute-start.8 = (f32[1,384]{1,0:T(1,128)S(1)}, f32[1,384]{1,0:T(1,128)S(1)}, u32[]{:S(2)}, u32[]{:S(2)}) collective-permute-start(f32[1,384]{1,0:T(1,128)S(1)} %shard_map.122.refs_0_), channel_id=1, source_target_pairs={{0,4},{1,13},{2,6},{3,15},{4,0},{5,9},{6,2},{7,11},{8,12},{9,5},{1... | collective-permute-start | bytes 4616 | tf_op jit(solution)/shard_map/ppermute | solution.py:578
  47.9 6.5 %collective-permute-done.10.refs_3_ = f32[1,384]{1,0:T(1,128)S(1)} collective-permute-done((f32[1,384]{1,0:T(1,128)S(1)}, f32[1,384]{1,0:T(1,128)S(1)}, u32[]{:S(2)}, u32[]{:S(2)}) %collective-permute-start.10) | collective-permute-done | bytes 1568 | tf_op jit(solution)/shard_map/ppermute | solution.py:34
  57.5 1.7 %collective-permute-start.17 = (f32[1,384]{1,0:T(1,128)S(1)}, f32[1,384]{1,0:T(1,128)S(1)}, u32[]{:S(2)}, u32[]{:S(2)}) collective-permute-start(f32[1,384]{1,0:T(1,128)S(1)} %get-tuple-element.74.refs_0_), channel_id=1, source_target_pairs={{0,16},{1,17},{2,18},{3,19},{4,20},{5,21},{6,22},{7,23},{8,24},{9,... | collective-permute-start | bytes 4616 | tf_op jit(solution)/shard_map/ppermute | solution.py:683
  59.1 2.1 %shard_map.125 = (f32[384,384]{1,0:T(8,128)S(1)}, f32[384,384]{1,0:T(8,128)S(1)}, f32[384,384]{1,0:T(8,128)S(1)}, f32[192,384]{1,0:T(8,128)S(1)}) custom-call(f32[4,384,384]{2,1,0:T(8,128)S(1)} %shard_map.123.refs_4_.refs_0_), custom_call_target="tpu_custom_call" | custom-call | flops 1019215872 | bytes 2359296 | tf_op jit(solution)/shard_map/pallas_call | solution.py:59
  63.1 1.7 %shard_map.127 = (f32[384,384]{1,0:T(8,128)S(1)}, f32[384,384]{1,0:T(8,128)S(1)}) custom-call(f32[4,384,384]{2,1,0:T(8,128)S(1)} %shard_map.123.refs_4_.refs_0_, f32[384,384]{1,0:T(8,128)S(1)} %get-tuple-element.78.refs_1_, f32[384,384]{1,0:T(8,128)S(1)} %get-tuple-element.79.refs_2_, f32[384,384]{1,0:T(8,128)S(1)} %get-tuple-element.65.refs_3_.refs_4_, ...), custom_call_target="tpu_custom_call" | custom-call | flops 679477248 | bytes 4718592 | tf_op jit(solution)/shard_map/pallas_call | solution.py:59
  64.8 2.6 %collective-permute-done.18.refs_1_ = f32[1,384]{1,0:T(1,128)S(1)} collective-permute-done((f32[1,384]{1,0:T(1,128)S(1)}, f32[1,384]{1,0:T(1,128)S(1)}, u32[]{:S(2)}, u32[]{:S(2)}) %collective-permute-start.18) | collective-permute-done | bytes 1568 | tf_op jit(solution)/shard_map/ppermute | solution.py:683
  67.7 4.6 %collective-permute-done.19.refs_1_ = f32[1,384]{1,0:T(1,128)S(1)} collective-permute-done((f32[1,384]{1,0:T(1,128)S(1)}, f32[1,384]{1,0:T(1,128)S(1)}, u32[]{:S(2)}, u32[]{:S(2)}) %collective-permute-start.19) | collective-permute-done | bytes 1568 | tf_op jit(solution)/shard_map/ppermute | solution.py:683
  74.5 3.6 %collective-permute-done.21.refs_1_ = f32[1,384]{1,0:T(1,128)S(1)} collective-permute-done((f32[1,384]{1,0:T(1,128)S(1)}, f32[1,384]{1,0:T(1,128)S(1)}, u32[]{:S(2)}, u32[]{:S(2)}) %collective-permute-start.21) | collective-permute-done | bytes 1568 | tf_op jit(solution)/shard_map/ppermute | solution.py:34
  79.6 1.9 %collective-permute-start.24 = (f32[1,384]{1,0:T(1,128)S(1)}, f32[1,384]{1,0:T(1,128)S(1)}, u32[]{:S(2)}, u32[]{:S(2)}) collective-permute-start(f32[1,384]{1,0:T(1,128)S(1)} %shard_map.132.refs_0_), channel_id=1, source_target_pairs={{0,10},{1,11},{2,8},{3,9},{4,14},{5,15},{6,12},{7,13},{8,2},{9,3},... | collective-permute-start | bytes 4616 | tf_op jit(solution)/shard_map/ppermute | solution.py:34
  81.5 1.4 %collective-permute-done.22.refs_1_ = f32[1,384]{1,0:T(1,128)S(1)} collective-permute-done((f32[1,384]{1,0:T(1,128)S(1)}, f32[1,384]{1,0:T(1,128)S(1)}, u32[]{:S(2)}, u32[]{:S(2)}) %collective-permute-start.22) | collective-permute-done | bytes 1568 | tf_op jit(solution)/shard_map/ppermute | solution.py:578
  82.8 3.3 %collective-permute-done.24.refs_3_ = f32[1,384]{1,0:T(1,128)S(1)} collective-permute-done((f32[1,384]{1,0:T(1,128)S(1)}, f32[1,384]{1,0:T(1,128)S(1)}, u32[]{:S(2)}, u32[]{:S(2)}) %collective-permute-start.24) | collective-permute-done | bytes 1568 | tf_op jit(solution)/shard_map/ppermute | solution.py:34
  88.4 2.1 %collective-permute-start.25 = (f32[1,384]{1,0:T(1,128)S(1)}, f32[1,384]{1,0:T(1,128)S(1)}, u32[]{:S(2)}, u32[]{:S(2)}) collective-permute-start(f32[1,384]{1,0:T(1,128)S(1)} %get-tuple-element.88.refs_0_), channel_id=1, source_target_pairs={{0,16},{1,17},{2,18},{3,19},{4,20},{5,21},{6,22},{7,23},{8,24},{9,... | collective-permute-start | bytes 4616 | tf_op jit(solution)/shard_map/ppermute | solution.py:34
  90.7 1.6 %shard_map.136 = (f32[384,384]{1,0:T(8,128)}, f32[384,384]{1,0:T(8,128)S(1)}) custom-call(f32[384,384]{1,0:T(8,128)S(1)} %get-tuple-element.93.refs_0_, f32[384,384]{1,0:T(8,128)S(1)} %get-tuple-element.94.refs_1_.refs_2_, f32[384,384]{1,0:T(8,128)S(1)} %get-tuple-element.81.refs_2_, f32[384,384]{1,0:T(8,128)S(1)} %get-tuple-element.89.refs_6_.refs_3_), custom_call_target="tpu_custom_call" | custom-call | flops 339738624 | bytes 2359296 | tf_op jit(solution)/shard_map/pallas_call | solution.py:59
  93.3 4.1 %collective-permute-done.28.refs_2_ = f32[1,384]{1,0:T(1,128)S(1)} collective-permute-done((f32[1,384]{1,0:T(1,128)S(1)}, f32[1,384]{1,0:T(1,128)S(1)}, u32[]{:S(2)}, u32[]{:S(2)}) %collective-permute-start.28) | collective-permute-done | bytes 1568 | tf_op jit(solution)/shard_map/ppermute | solution.py:34
  97.3 1.5 %shard_map.138 = f32[3,4,32,128]{3,2,1,0:T(8,128)} custom-call(f32[384,384]{1,0:T(8,128)S(1)} %get-tuple-element.101.refs_0_, f32[1,384]{1,0:T(1,128)S(1)} %shard_map.134.refs_1_, f32[1,384]{1,0:T(1,128)S(1)} %collective-permute-done.28.refs_2_, f32[384,384]{1,0:T(8,128)S(1)} %get-tuple-element.95.refs_3_, f32[1,384]{1,0:T(1,128)S(1)} %get-tuple-element.98.refs_4_, ...), custom_call_target="tpu_custom_call" | custom-call | flops 589824 | bytes 1446912 | tf_op jit(solution)/shard_map/pallas_call | solution.py:59
  (75 shorter events, 21.5 us)
Async XLA Ops:
  2.8 2.1 %collective-permute-start.1 = (f32[384,384]{1,0:T(8,128)S(1)}, f32[384,384]{1,0:T(8,128)S(1)}, u32[]{:S(2)}, u32[]{:S(2)}) collective-permute-start(f32[384,384]{1,0:T(8,128)S(1)} %shard_map.114.refs_0_.refs_3_), channel_id=1, source_target_pairs={{0,1},{1,0},{2,3},{3,2},{4,5},{5,4},{6,7},{7,6},{8,9},{9,8},{10,11... | collective-permute-start | bytes 1769480 | tf_op jit(solution)/shard_map/ppermute | solution.py:34
  3.2 2.5 %collective-permute-start.2 = (f32[37,32,128]{2,1,0:T(8,128)S(1)}, f32[37,32,128]{2,1,0:T(8,128)S(1)}, u32[]{:S(2)}, u32[]{:S(2)}) collective-permute-start(f32[37,32,128]{2,1,0:T(8,128)S(1)} %get-tuple-element.55), channel_id=1, source_target_pairs={{0,1},{1,0},{2,3},{3,2},{4,5},{5,4},{6,7},{7,6},{8,9},{9,8},{10,11... | collective-permute-start | bytes 1818632 | tf_op jit(solution)/shard_map/ppermute | solution.py:34
  5.7 9.3 %collective-permute-start.3 = (f32[192,384]{1,0:T(8,128)S(1)}, f32[192,384]{1,0:T(8,128)S(1)}, u32[]{:S(2)}, u32[]{:S(2)}) collective-permute-start(f32[192,384]{1,0:T(8,128)S(1)} %get-tuple-element.56), channel_id=1, source_target_pairs={{0,2},{1,3},{2,0},{3,1},{4,6},{5,7},{6,4},{7,5},{8,10},{9,11},{10,... | collective-permute-start | bytes 884744 | tf_op jit(solution)/shard_map/ppermute | solution.py:34
  7.6 18.7 %collective-permute-start = (f32[37,32,128]{2,1,0:T(8,128)S(1)}, f32[37,32,128]{2,1,0:T(8,128)S(1)}, u32[]{:S(2)}, u32[]{:S(2)}) collective-permute-start(f32[37,32,128]{2,1,0:T(8,128)S(1)} %get-tuple-element.51), channel_id=1, source_target_pairs={{1,2},{2,1},{3,4},{4,3},{5,6},{6,5},{7,8},{8,7},{9,10},{10,9},{11,... | collective-permute-start | bytes 1818632 | tf_op jit(solution)/shard_map/ppermute | solution.py:691
  17.4 37.0 %collective-permute-start.15 = (f32[192,384]{1,0:T(8,128)S(1)}, f32[192,384]{1,0:T(8,128)S(1)}, u32[]{:S(2)}, u32[]{:S(2)}) collective-permute-start(f32[192,384]{1,0:T(8,128)S(1)} %get-tuple-element.57), channel_id=1, source_target_pairs={{0,12},{1,13},{2,14},{3,15},{4,8},{5,9},{6,10},{7,11},{8,4},{9,5},... | collective-permute-start | bytes 884744 | tf_op jit(solution)/shard_map/ppermute | solution.py:34
  23.6 30.9 %collective-permute-start.13 = (f32[192,384]{1,0:T(8,128)S(1)}, f32[192,384]{1,0:T(8,128)S(1)}, u32[]{:S(2)}, u32[]{:S(2)}) collective-permute-start(f32[192,384]{1,0:T(8,128)S(1)} %get-tuple-element.57), channel_id=1, source_target_pairs={{0,10},{1,11},{2,8},{3,9},{4,14},{5,15},{6,12},{7,13},{8,2},{9,3},... | collective-permute-start | bytes 884744 | tf_op jit(solution)/shard_map/ppermute | solution.py:34
  25.3 29.6 %collective-permute-start.11 = (f32[192,384]{1,0:T(8,128)S(1)}, f32[192,384]{1,0:T(8,128)S(1)}, u32[]{:S(2)}, u32[]{:S(2)}) collective-permute-start(f32[192,384]{1,0:T(8,128)S(1)} %get-tuple-element.57), channel_id=1, source_target_pairs={{0,4},{1,5},{2,6},{3,7},{4,0},{5,1},{6,2},{7,3},{8,12},{9,13},{10,... | collective-permute-start | bytes 884744 | tf_op jit(solution)/shard_map/ppermute | solution.py:34
  33.7 3.6 %collective-permute-start.5 = (f32[1,384]{1,0:T(1,128)S(1)}, f32[1,384]{1,0:T(1,128)S(1)}, u32[]{:S(2)}, u32[]{:S(2)}) collective-permute-start(f32[1,384]{1,0:T(1,128)S(1)} %get-tuple-element.60.refs_1_), channel_id=1, source_target_pairs={{0,64},{64,0},{128,192},{192,128},{1,65},{65,1},{129,193},{193,129... | collective-permute-start | bytes 4616 | tf_op jit(solution)/shard_map/ppermute | solution.py:606
  38.8 3.8 %collective-permute-start.7 = (f32[1,384]{1,0:T(1,128)S(1)}, f32[1,384]{1,0:T(1,128)S(1)}, u32[]{:S(2)}, u32[]{:S(2)}) collective-permute-start(f32[1,384]{1,0:T(1,128)S(1)} %shard_map.121.refs_0_), channel_id=1, source_target_pairs={{0,2},{1,3},{2,0},{3,1},{4,6},{5,7},{6,4},{7,5},{8,10},{9,11},{10,... | collective-permute-start | bytes 4616 | tf_op jit(solution)/shard_map/ppermute | solution.py:34
  42.7 11.7 %collective-permute-start.10 = (f32[1,384]{1,0:T(1,128)S(1)}, f32[1,384]{1,0:T(1,128)S(1)}, u32[]{:S(2)}, u32[]{:S(2)}) collective-permute-start(f32[1,384]{1,0:T(1,128)S(1)} %shard_map.122.refs_0_), channel_id=1, source_target_pairs={{0,10},{1,11},{2,8},{3,9},{4,14},{5,15},{6,12},{7,13},{8,2},{9,3},... | collective-permute-start | bytes 4616 | tf_op jit(solution)/shard_map/ppermute | solution.py:34
  46.5 8.0 %collective-permute-start.8 = (f32[1,384]{1,0:T(1,128)S(1)}, f32[1,384]{1,0:T(1,128)S(1)}, u32[]{:S(2)}, u32[]{:S(2)}) collective-permute-start(f32[1,384]{1,0:T(1,128)S(1)} %shard_map.122.refs_0_), channel_id=1, source_target_pairs={{0,4},{1,13},{2,6},{3,15},{4,0},{5,9},{6,2},{7,11},{8,12},{9,5},{1... | collective-permute-start | bytes 4616 | tf_op jit(solution)/shard_map/ppermute | solution.py:578
  54.4 2.0 %collective-permute-start.14 = (f32[192,384]{1,0:T(8,128)S(1)}, f32[192,384]{1,0:T(8,128)S(1)}, u32[]{:S(2)}, u32[]{:S(2)}) collective-permute-start(f32[192,384]{1,0:T(8,128)S(1)} %collective-permute-done.13.refs_3_), channel_id=1, source_target_pairs={{0,1},{1,0},{2,3},{3,2},{4,5},{5,4},{6,7},{7,6},{8,9},{9,8},{10,11... | collective-permute-start | bytes 884744 | tf_op jit(solution)/shard_map/ppermute | solution.py:34
  54.9 1.9 %collective-permute-start.12 = (f32[192,384]{1,0:T(8,128)S(1)}, f32[192,384]{1,0:T(8,128)S(1)}, u32[]{:S(2)}, u32[]{:S(2)}) collective-permute-start(f32[192,384]{1,0:T(8,128)S(1)} %collective-permute-done.11.refs_1_), channel_id=1, source_target_pairs={{0,1},{1,0},{2,3},{3,2},{4,5},{5,4},{6,7},{7,6},{8,9},{9,8},{10,11... | collective-permute-start | bytes 884744 | tf_op jit(solution)/shard_map/ppermute | solution.py:34
  55.0 2.0 %collective-permute-start.9 = (f32[1,384]{1,0:T(1,128)S(1)}, f32[1,384]{1,0:T(1,128)S(1)}, u32[]{:S(2)}, u32[]{:S(2)}) collective-permute-start(f32[1,384]{1,0:T(1,128)S(1)} %collective-permute-done.8.refs_1_), channel_id=1, source_target_pairs={{0,1},{1,0},{2,3},{3,2},{4,5},{5,4},{6,7},{7,6},{8,9},{9,8},{10,11... | collective-permute-start | bytes 4616 | tf_op jit(solution)/shard_map/ppermute | solution.py:34
  57.5 4.9 %collective-permute-start.17 = (f32[1,384]{1,0:T(1,128)S(1)}, f32[1,384]{1,0:T(1,128)S(1)}, u32[]{:S(2)}, u32[]{:S(2)}) collective-permute-start(f32[1,384]{1,0:T(1,128)S(1)} %get-tuple-element.74.refs_0_), channel_id=1, source_target_pairs={{0,16},{1,17},{2,18},{3,19},{4,20},{5,21},{6,22},{7,23},{8,24},{9,... | collective-permute-start | bytes 4616 | tf_op jit(solution)/shard_map/ppermute | solution.py:683
  62.5 4.9 %collective-permute-start.18 = (f32[1,384]{1,0:T(1,128)S(1)}, f32[1,384]{1,0:T(1,128)S(1)}, u32[]{:S(2)}, u32[]{:S(2)}) collective-permute-start(f32[1,384]{1,0:T(1,128)S(1)} %shard_map.126), channel_id=1, source_target_pairs={{0,16},{1,17},{2,18},{3,19},{4,20},{5,21},{6,22},{7,23},{8,24},{9,... | collective-permute-start | bytes 4616 | tf_op jit(solution)/shard_map/ppermute | solution.py:683
  67.5 4.9 %collective-permute-start.19 = (f32[1,384]{1,0:T(1,128)S(1)}, f32[1,384]{1,0:T(1,128)S(1)}, u32[]{:S(2)}, u32[]{:S(2)}) collective-permute-start(f32[1,384]{1,0:T(1,128)S(1)} %shard_map.128), channel_id=1, source_target_pairs={{0,16},{1,17},{2,18},{3,19},{4,20},{5,21},{6,22},{7,23},{8,24},{9,... | collective-permute-start | bytes 4616 | tf_op jit(solution)/shard_map/ppermute | solution.py:683
  72.4 13.8 %collective-permute-start.26 = (f32[192,384]{1,0:T(8,128)S(1)}, f32[192,384]{1,0:T(8,128)S(1)}, u32[]{:S(2)}, u32[]{:S(2)}) collective-permute-start(f32[192,384]{1,0:T(8,128)S(1)} %get-tuple-element.91), channel_id=1, source_target_pairs={{0,16},{1,17},{2,18},{3,19},{4,20},{5,21},{6,22},{7,23},{8,24},{9,... | collective-permute-start | bytes 884744 | tf_op jit(solution)/shard_map/ppermute | solution.py:34
  74.4 3.7 %collective-permute-start.21 = (f32[1,384]{1,0:T(1,128)S(1)}, f32[1,384]{1,0:T(1,128)S(1)}, u32[]{:S(2)}, u32[]{:S(2)}) collective-permute-start(f32[1,384]{1,0:T(1,128)S(1)} %shard_map.131.refs_0_), channel_id=1, source_target_pairs={{0,2},{1,3},{2,0},{3,1},{4,6},{5,7},{6,4},{7,5},{8,10},{9,11},{10,... | collective-permute-start | bytes 4616 | tf_op jit(solution)/shard_map/ppermute | solution.py:34
  78.3 4.6 %collective-permute-start.22 = (f32[1,384]{1,0:T(1,128)S(1)}, f32[1,384]{1,0:T(1,128)S(1)}, u32[]{:S(2)}, u32[]{:S(2)}) collective-permute-start(f32[1,384]{1,0:T(1,128)S(1)} %shard_map.132.refs_0_), channel_id=1, source_target_pairs={{0,4},{1,13},{2,6},{3,15},{4,0},{5,9},{6,2},{7,11},{8,12},{9,5},{1... | collective-permute-start | bytes 4616 | tf_op jit(solution)/shard_map/ppermute | solution.py:578
  79.6 6.6 %collective-permute-start.24 = (f32[1,384]{1,0:T(1,128)S(1)}, f32[1,384]{1,0:T(1,128)S(1)}, u32[]{:S(2)}, u32[]{:S(2)}) collective-permute-start(f32[1,384]{1,0:T(1,128)S(1)} %shard_map.132.refs_0_), channel_id=1, source_target_pairs={{0,10},{1,11},{2,8},{3,9},{4,14},{5,15},{6,12},{7,13},{8,2},{9,3},... | collective-permute-start | bytes 4616 | tf_op jit(solution)/shard_map/ppermute | solution.py:34
  86.2 4.3 %collective-permute-start.27 = (f32[192,384]{1,0:T(8,128)S(1)}, f32[192,384]{1,0:T(8,128)S(1)}, u32[]{:S(2)}, u32[]{:S(2)}) collective-permute-start(f32[192,384]{1,0:T(8,128)S(1)} %collective-permute-done.26.refs_1_), channel_id=1, source_target_pairs={{0,1},{1,0},{2,3},{3,2},{4,5},{5,4},{6,7},{7,6},{8,9},{9,8},{10,11... | collective-permute-start | bytes 884744 | tf_op jit(solution)/shard_map/ppermute | solution.py:34
  88.4 3.8 %collective-permute-start.25 = (f32[1,384]{1,0:T(1,128)S(1)}, f32[1,384]{1,0:T(1,128)S(1)}, u32[]{:S(2)}, u32[]{:S(2)}) collective-permute-start(f32[1,384]{1,0:T(1,128)S(1)} %get-tuple-element.88.refs_0_), channel_id=1, source_target_pairs={{0,16},{1,17},{2,18},{3,19},{4,20},{5,21},{6,22},{7,23},{8,24},{9,... | collective-permute-start | bytes 4616 | tf_op jit(solution)/shard_map/ppermute | solution.py:34
  92.5 4.9 %collective-permute-start.28 = (f32[1,384]{1,0:T(1,128)S(1)}, f32[1,384]{1,0:T(1,128)S(1)}, u32[]{:S(2)}, u32[]{:S(2)}) collective-permute-start(f32[1,384]{1,0:T(1,128)S(1)} %shard_map.137), channel_id=1, source_target_pairs={{0,48},{1,49},{2,50},{3,51},{4,52},{5,53},{6,54},{7,55},{8,56},{9,... | collective-permute-start | bytes 4616 | tf_op jit(solution)/shard_map/ppermute | solution.py:34
  (12 other events, 55.4 us)

commit v8 on v7

--- a/solution.py
+++ b/solution.py
@@ -24,7 +24,6 @@
 f32 = jnp.float32
 bf16 = jnp.bfloat16
 VM = pl.BlockSpec(memory_space=pltpu.VMEM)
-SM = pl.BlockSpec(memory_space=pltpu.SMEM)
 MAT = jax.ShapeDtypeStruct((IB, IB), f32)
 HALFMAT = jax.ShapeDtypeStruct((HALF, IB), f32)
 ROW = jax.ShapeDtypeStruct((1, IB), f32)
@@ -154,10 +153,10 @@
 
 
 def substep_kernel(
-    count, step, displacement, velocity, external_load, node_mass, modulus,
-    outer, inner, stiffness, nodes,
+    steps, displacement, velocity, external_load, node_mass, modulus,
+    outer, inner, stiff, nodes,
     displacement_out, velocity_out, picked,
-    disp, vel, load, inverse_mass, factor, stiff, even, odd, even_force, odd_force, upper,
+    disp, vel, load, inverse_mass, factor, even, odd, even_force, odd_force, upper,
 ):
     flags = Place()
     first = flags[CORE] == 0
@@ -201,9 +200,7 @@
     def _():
         factor[2 * CX - 1] = jnp.zeros((8, GROUPS * CZ), f32)
 
-    high, low = [spread(s) for s in halves(stiffness[...])]
-    stiff[...] = jnp.concatenate([high, high, low], axis=1)
-    length = step[0]
+    length = steps[1:2]
 
     def put_features(layer, below, above):
         columns = []
@@ -270,7 +267,7 @@
 
         return lax.fori_loop(0, CX + 1 - k, two_layers, carry)
 
-    lax.fori_loop(0, count[0], one_substep, 0)
+    lax.fori_loop(0, jnp.max(steps[0:1]).astype(jnp.int32), one_substep, 0)
     displacement_out[...] = disp[:, CX : 2 * CX]
     final = vel[:, CX : 2 * CX]
     velocity_out[...] = final
@@ -294,7 +291,12 @@
         target[pl.ds(33, CX)] = modulus[...]
 
 
-def substeps_call(count, step, state, outer, inner, stiffness, nodes):
+def spread_kernel(flags, stiffness, stiff):
+    high, low = [spread(s) for s in halves(stiffness[...])]
+    stiff[...] = jnp.concatenate([high, high, low], axis=1)
+
+
+def substeps_call(steps, state, outer, inner, stiff, nodes):
     grid_shape = (3, CX, CY, CZ)
     return pl.pallas_call(
         substep_kernel,
@@ -303,7 +305,7 @@
             jax.ShapeDtypeStruct(grid_shape, f32),
             ROW,
         ),
-        in_specs=[SM, SM] + [VM] * 9,
+        in_specs=[VM] * 10,
         out_specs=(VM, VM, VM),
         scratch_shapes=[
             pltpu.VMEM((3, DEEP + 2, CY, CZ), f32),
@@ -311,7 +313,6 @@
             pltpu.VMEM((3, DEEP, CY, CZ), f32),
             pltpu.VMEM((DEEP, CY, CZ), f32),
             pltpu.VMEM((DEEP, 8, GROUPS * CZ), f32),
-            pltpu.VMEM((192, 576), bf16),
             pltpu.VMEM((576, GROUPS * CZ), bf16),
             pltpu.VMEM((576, GROUPS * CZ), bf16),
             pltpu.VMEM((192, GROUPS * CZ), f32),
@@ -320,7 +321,7 @@
         ],
         compiler_params=pltpu.CompilerParams(vmem_limit_bytes=20 << 20),
         cost_estimate=cost(32 * 2 * 192 * 576 * 512, 3 * 720896),
-    )(count, step, *state, outer, inner, stiffness, nodes)
+    )(steps, *state, outer, inner, stiff, nodes)
 
 def transition_kernel(flags, inverse, lower, transition):
     transition[...] = -product(inverse[...], lower[...])
@@ -649,7 +650,7 @@
             bound(level, backward_kernel), flags, [total, others[-1], levels[level][1]], ROW, square
         )
     arrived = row_exchange(total)
-    near = after(swap(row[1], MASKS[4]), arrived[0], arrived[2])
+    near = after(swap(row[1], MASKS[4]), arrived[1], arrived[2])
     row, levels = merge_level(
         flags, 4, row, levels + [None, (None, None, prefix_3, suffix_3)], near
     )
@@ -705,7 +706,9 @@
 ):
     flags = Place()
     sub = lax.axis_index("sub")
-    step = coarse_step / substeps.astype(f32)
+    count = substeps.astype(f32)
+    steps = jnp.broadcast_to(jnp.stack([count, coarse_step / count]), (2, CZ))
+    stiff = local_call(spread_kernel, flags, [stiffness], jax.ShapeDtypeStruct((192, 576), bf16))
     state = [displacement[0], velocity[0], external_load[0], node_mass[0], modulus[0]]
     packed = jax.ShapeDtypeStruct((PACKED, CY, CZ), f32)
     inverse = lax.dynamic_index_in_dim(factor_inverse, sub // 2, 0, keepdims=False)
@@ -721,7 +724,7 @@
     fetched = merged, [swap(half, mask) for mask in (SPLIT_MASKS[0], OPPOSITE, SPLIT_MASKS[1])]
     outer = after(outer, half)
     final_displacement, final_velocity, picked = substeps_call(
-        substeps, step, state, outer, inner, stiffness, interface_nodes
+        steps, state, outer, inner, stiff, interface_nodes
     )
     coupled = coupled_velocity(
         flags,

time: 99.5 us -> 97.9 us (0.984)
  waiting for transfers between devices: 46.8 us -> 39.3 us
  Pallas kernels: 21.5 us -> 25.7 us
  starting transfers between devices: 27.2 us -> 29.4 us
    ppermute x22, waiting for transfers between devices: 33.7 us -> 26.8 us  [swap(): lax.ppermute(value, 'tile', [(i, i ^ mask) for i in range(lax.axis_size('...]
    pallas_call x1, Pallas kernels: 7.33 us -> 11 us  [substeps_call(): pl.pallas_call(substep_kernel, out_shape=(jax.ShapeDtypeStruct(grid_shape...]
    ppermute x22, starting transfers between devices: 21.4 us -> 23 us  [swap(): lax.ppermute(value, 'tile', [(i, i ^ mask) for i in range(lax.axis_size('...]
    pallas_call x25 -> x26, Pallas kernels: 14.2 us -> 14.7 us  [local_call(): pl.pallas_call(placed, out_shape=outs, in_specs=[VM] * len(operands), out...]
  transfers between devices with their start and end apart: 29 -> 29, of which waited for: 20 -> 20; matrix products, arithmetic and copies ran while one was open for 0% -> 0% of each run, Pallas kernels for 19% -> 23%
where the time goes in v8:
time: 97.9 us; the launch traced here: 97.7 us
  waiting for transfers between devices  39.3 us (40%)
  starting transfers between devices  29.4 us (30%)
  Pallas kernels  25.7 us (26%)
  local copies, waits for them, and re-layouts  1.67 us (2%)
  between operations  1.63 us (2%)
    ppermute x22, waiting for transfers between devices, swap(): lax.ppermute(value, 'tile', [(i, i ^ mask) for i in range(lax.axis_size('...  26.8 us
    ppermute x22, starting transfers between devices, swap(): lax.ppermute(value, 'tile', [(i, i ^ mask) for i in range(lax.axis_size('...  23 us
    pallas_call x26, Pallas kernels, local_call(): pl.pallas_call(placed, out_shape=outs, in_specs=[VM] * len(operands), out...  14.7 us
    pallas_call x1, Pallas kernels, substeps_call(): pl.pallas_call(substep_kernel, out_shape=(jax.ShapeDtypeStruct(grid_shape...  11 us
    ppermute x3, waiting for transfers between devices, up_row(): lax.ppermute(value, 'tile', [(i, (i + ROW_TILES) % count) for i in range(...  8.28 us
    ppermute x1, waiting for transfers between devices, coupled_velocity(): partner = lax.ppermute(picked, 'sub', [(i, i ^ 1) for i in range(count)])  2.95 us
    ppermute x2, starting transfers between devices, split_swap(): lax.ppermute(value, 'tile', [(i, i ^ mask) for i, mask in enumerate(masks)])  2.84 us
    ppermute x3, starting transfers between devices, up_row(): lax.ppermute(value, 'tile', [(i, (i + ROW_TILES) % count) for i in range(...  2.35 us
  transfers between devices with their start and end apart: 29, of which 20 were waited for; matrix products, arithmetic and copies ran while one was open for 0% of the time, Pallas kernels for 23%

profile of v8, /device:TPU:2, one launch (start us, length us, event | category | flops | bytes accessed | tf_op | source)
XLA Modules:
  0.0 97.7 jit_solution(6063450742649407535)
XLA Ops:
  5.7 1.9 %collective-permute-start.3 = (f32[192,384]{1,0:T(8,128)S(1)}, f32[192,384]{1,0:T(8,128)S(1)}, u32[]{:S(2)}, u32[]{:S(2)}) collective-permute-start(f32[192,384]{1,0:T(8,128)S(1)} %get-tuple-element.56), channel_id=1, source_target_pairs={{0,2},{1,3},{2,0},{3,1},{4,6},{5,7},{6,4},{7,5},{8,10},{9,11},{10,... | collective-permute-start | bytes 884744 | tf_op jit(solution)/shard_map/ppermute | solution.py:33
  8.4 6.7 %collective-permute-done.3.refs_1_ = f32[192,384]{1,0:T(8,128)S(1)} collective-permute-done((f32[192,384]{1,0:T(8,128)S(1)}, f32[192,384]{1,0:T(8,128)S(1)}, u32[]{:S(2)}, u32[]{:S(2)}) %collective-permute-start.3) | collective-permute-done | bytes 294944 | tf_op jit(solution)/shard_map/ppermute | solution.py:33
  17.4 6.2 %collective-permute-start.15 = (f32[192,384]{1,0:T(8,128)S(1)}, f32[192,384]{1,0:T(8,128)S(1)}, u32[]{:S(2)}, u32[]{:S(2)}) collective-permute-start(f32[192,384]{1,0:T(8,128)S(1)} %get-tuple-element.57), channel_id=1, source_target_pairs={{0,12},{1,13},{2,14},{3,15},{4,8},{5,9},{6,10},{7,11},{8,4},{9,5},... | collective-permute-start | bytes 884744 | tf_op jit(solution)/shard_map/ppermute | solution.py:33
  23.6 1.8 %collective-permute-start.13 = (f32[192,384]{1,0:T(8,128)S(1)}, f32[192,384]{1,0:T(8,128)S(1)}, u32[]{:S(2)}, u32[]{:S(2)}) collective-permute-start(f32[192,384]{1,0:T(8,128)S(1)} %get-tuple-element.57), channel_id=1, source_target_pairs={{0,10},{1,11},{2,8},{3,9},{4,14},{5,15},{6,12},{7,13},{8,2},{9,3},... | collective-permute-start | bytes 884744 | tf_op jit(solution)/shard_map/ppermute | solution.py:33
  26.5 11.0 %shard_map.118 = (f32[3,4,32,128]{3,2,1,0:T(8,128)}, f32[3,4,32,128]{3,2,1,0:T(8,128)S(1)}, f32[1,384]{1,0:T(1,128)S(1)}) custom-call(f32[2,128]{1,0:T(2,128)S(1)} %broadcast_in_dim.14.steps, f32[3,4,32,128]{3,2,1,0:T(8,128)S(1)} %bitcast.19, f32[3,4,32,128]{3,2,1,0:T(8,128)S(1)} %bitcast.21, f32[3,4,32,128]{3,2,1,0:T(8,128)S(1)} %bitcast.23, ...), custom_call_target="tpu_custom_call" | custom-call | flops 3623878656 | bytes 2162688 | tf_op jit(solution)/shard_map/pallas_call | solution.py:301
  38.0 3.0 %collective-permute-done.5.refs_2_ = f32[1,384]{1,0:T(1,128)S(1)} collective-permute-done((f32[1,384]{1,0:T(1,128)S(1)}, f32[1,384]{1,0:T(1,128)S(1)}, u32[]{:S(2)}, u32[]{:S(2)}) %collective-permute-start.5) | collective-permute-done | bytes 1568 | tf_op jit(solution)/shard_map/ppermute | solution.py:607
  43.1 3.1 %collective-permute-done.7.refs_1_ = f32[1,384]{1,0:T(1,128)S(1)} collective-permute-done((f32[1,384]{1,0:T(1,128)S(1)}, f32[1,384]{1,0:T(1,128)S(1)}, u32[]{:S(2)}, u32[]{:S(2)}) %collective-permute-start.7) | collective-permute-done | bytes 1568 | tf_op jit(solution)/shard_map/ppermute | solution.py:33
  46.3 3.8 %collective-permute-start.10 = (f32[1,384]{1,0:T(1,128)S(1)}, f32[1,384]{1,0:T(1,128)S(1)}, u32[]{:S(2)}, u32[]{:S(2)}) collective-permute-start(f32[1,384]{1,0:T(1,128)S(1)} %shard_map.123.refs_0_), channel_id=1, source_target_pairs={{0,10},{1,11},{2,8},{3,9},{4,14},{5,15},{6,12},{7,13},{8,2},{9,3},... | collective-permute-start | bytes 4616 | tf_op jit(solution)/shard_map/ppermute | solution.py:33
  50.2 1.4 %collective-permute-start.8 = (f32[1,384]{1,0:T(1,128)S(1)}, f32[1,384]{1,0:T(1,128)S(1)}, u32[]{:S(2)}, u32[]{:S(2)}) collective-permute-start(f32[1,384]{1,0:T(1,128)S(1)} %shard_map.123.refs_0_), channel_id=1, source_target_pairs={{0,4},{1,13},{2,6},{3,15},{4,0},{5,9},{6,2},{7,11},{8,12},{9,5},{1... | collective-permute-start | bytes 4616 | tf_op jit(solution)/shard_map/ppermute | solution.py:579
  51.5 2.8 %collective-permute-done.10.refs_3_ = f32[1,384]{1,0:T(1,128)S(1)} collective-permute-done((f32[1,384]{1,0:T(1,128)S(1)}, f32[1,384]{1,0:T(1,128)S(1)}, u32[]{:S(2)}, u32[]{:S(2)}) %collective-permute-start.10) | collective-permute-done | bytes 1568 | tf_op jit(solution)/shard_map/ppermute | solution.py:33
  57.8 1.7 %collective-permute-start.17 = (f32[1,384]{1,0:T(1,128)S(1)}, f32[1,384]{1,0:T(1,128)S(1)}, u32[]{:S(2)}, u32[]{:S(2)}) collective-permute-start(f32[1,384]{1,0:T(1,128)S(1)} %get-tuple-element.74.refs_0_), channel_id=1, source_target_pairs={{0,16},{1,17},{2,18},{3,19},{4,20},{5,21},{6,22},{7,23},{8,24},{9,... | collective-permute-start | bytes 4616 | tf_op jit(solution)/shard_map/ppermute | solution.py:684
  59.5 2.1 %shard_map.126 = (f32[384,384]{1,0:T(8,128)S(1)}, f32[384,384]{1,0:T(8,128)S(1)}, f32[384,384]{1,0:T(8,128)S(1)}, f32[192,384]{1,0:T(8,128)S(1)}) custom-call(f32[4,384,384]{2,1,0:T(8,128)S(1)} %shard_map.124.refs_4_.refs_0_), custom_call_target="tpu_custom_call" | custom-call | flops 1019215872 | bytes 2359296 | tf_op jit(solution)/shard_map/pallas_call | solution.py:58
  63.4 1.7 %shard_map.128 = (f32[384,384]{1,0:T(8,128)S(1)}, f32[384,384]{1,0:T(8,128)S(1)}) custom-call(f32[4,384,384]{2,1,0:T(8,128)S(1)} %shard_map.124.refs_4_.refs_0_, f32[384,384]{1,0:T(8,128)S(1)} %get-tuple-element.78.refs_1_, f32[384,384]{1,0:T(8,128)S(1)} %get-tuple-element.79.refs_2_, f32[384,384]{1,0:T(8,128)S(1)} %get-tuple-element.65.refs_3_.refs_4_, ...), custom_call_target="tpu_custom_call" | custom-call | flops 679477248 | bytes 4718592 | tf_op jit(solution)/shard_map/pallas_call | solution.py:58
  65.1 2.6 %collective-permute-done.18.refs_1_ = f32[1,384]{1,0:T(1,128)S(1)} collective-permute-done((f32[1,384]{1,0:T(1,128)S(1)}, f32[1,384]{1,0:T(1,128)S(1)}, u32[]{:S(2)}, u32[]{:S(2)}) %collective-permute-start.18) | collective-permute-done | bytes 1568 | tf_op jit(solution)/shard_map/ppermute | solution.py:684
  68.1 4.6 %collective-permute-done.19.refs_1_ = f32[1,384]{1,0:T(1,128)S(1)} collective-permute-done((f32[1,384]{1,0:T(1,128)S(1)}, f32[1,384]{1,0:T(1,128)S(1)}, u32[]{:S(2)}, u32[]{:S(2)}) %collective-permute-start.19) | collective-permute-done | bytes 1568 | tf_op jit(solution)/shard_map/ppermute | solution.py:684
  74.7 1.8 %collective-permute-start.21 = (f32[1,384]{1,0:T(1,128)S(1)}, f32[1,384]{1,0:T(1,128)S(1)}, u32[]{:S(2)}, u32[]{:S(2)}) collective-permute-start(f32[1,384]{1,0:T(1,128)S(1)} %shard_map.132.refs_0_), channel_id=1, source_target_pairs={{0,2},{1,3},{2,0},{3,1},{4,6},{5,7},{6,4},{7,5},{8,10},{9,11},{10,... | collective-permute-start | bytes 4616 | tf_op jit(solution)/shard_map/ppermute | solution.py:33
  76.5 1.8 %collective-permute-done.21.refs_1_ = f32[1,384]{1,0:T(1,128)S(1)} collective-permute-done((f32[1,384]{1,0:T(1,128)S(1)}, f32[1,384]{1,0:T(1,128)S(1)}, u32[]{:S(2)}, u32[]{:S(2)}) %collective-permute-start.21) | collective-permute-done | bytes 1568 | tf_op jit(solution)/shard_map/ppermute | solution.py:33
  78.6 1.5 %collective-permute-start.22 = (f32[1,384]{1,0:T(1,128)S(1)}, f32[1,384]{1,0:T(1,128)S(1)}, u32[]{:S(2)}, u32[]{:S(2)}) collective-permute-start(f32[1,384]{1,0:T(1,128)S(1)} %shard_map.133.refs_0_), channel_id=1, source_target_pairs={{0,4},{1,13},{2,6},{3,15},{4,0},{5,9},{6,2},{7,11},{8,12},{9,5},{1... | collective-permute-start | bytes 4616 | tf_op jit(solution)/shard_map/ppermute | solution.py:579
  80.1 2.1 %collective-permute-start.24 = (f32[1,384]{1,0:T(1,128)S(1)}, f32[1,384]{1,0:T(1,128)S(1)}, u32[]{:S(2)}, u32[]{:S(2)}) collective-permute-start(f32[1,384]{1,0:T(1,128)S(1)} %shard_map.133.refs_0_), channel_id=1, source_target_pairs={{0,10},{1,11},{2,8},{3,9},{4,14},{5,15},{6,12},{7,13},{8,2},{9,3},... | collective-permute-start | bytes 4616 | tf_op jit(solution)/shard_map/ppermute | solution.py:33
  83.2 3.5 %collective-permute-done.24.refs_3_ = f32[1,384]{1,0:T(1,128)S(1)} collective-permute-done((f32[1,384]{1,0:T(1,128)S(1)}, f32[1,384]{1,0:T(1,128)S(1)}, u32[]{:S(2)}, u32[]{:S(2)}) %collective-permute-start.24) | collective-permute-done | bytes 1568 | tf_op jit(solution)/shard_map/ppermute | solution.py:33
  87.3 2.1 %collective-permute-start.25 = (f32[1,384]{1,0:T(1,128)S(1)}, f32[1,384]{1,0:T(1,128)S(1)}, u32[]{:S(2)}, u32[]{:S(2)}) collective-permute-start(f32[1,384]{1,0:T(1,128)S(1)} %get-tuple-element.88.refs_0_), channel_id=1, source_target_pairs={{0,16},{1,17},{2,18},{3,19},{4,20},{5,21},{6,22},{7,23},{8,24},{9,... | collective-permute-start | bytes 4616 | tf_op jit(solution)/shard_map/ppermute | solution.py:33
  89.6 1.6 %shard_map.137 = (f32[384,384]{1,0:T(8,128)}, f32[384,384]{1,0:T(8,128)S(1)}) custom-call(f32[384,384]{1,0:T(8,128)S(1)} %get-tuple-element.93.refs_0_, f32[384,384]{1,0:T(8,128)S(1)} %get-tuple-element.94.refs_1_.refs_2_, f32[384,384]{1,0:T(8,128)S(1)} %get-tuple-element.81.refs_2_, f32[384,384]{1,0:T(8,128)S(1)} %get-tuple-element.89.refs_6_.refs_3_), custom_call_target="tpu_custom_call" | custom-call | flops 339738624 | bytes 2359296 | tf_op jit(solution)/shard_map/pallas_call | solution.py:58
  92.2 4.1 %collective-permute-done.28.refs_2_ = f32[1,384]{1,0:T(1,128)S(1)} collective-permute-done((f32[1,384]{1,0:T(1,128)S(1)}, f32[1,384]{1,0:T(1,128)S(1)}, u32[]{:S(2)}, u32[]{:S(2)}) %collective-permute-start.28) | collective-permute-done | bytes 1568 | tf_op jit(solution)/shard_map/ppermute | solution.py:33
  96.3 1.5 %shard_map.139 = f32[3,4,32,128]{3,2,1,0:T(8,128)} custom-call(f32[384,384]{1,0:T(8,128)S(1)} %get-tuple-element.101.refs_0_, f32[1,384]{1,0:T(1,128)S(1)} %shard_map.135.refs_1_, f32[1,384]{1,0:T(1,128)S(1)} %collective-permute-done.28.refs_2_, f32[384,384]{1,0:T(8,128)S(1)} %get-tuple-element.95.refs_3_, f32[1,384]{1,0:T(1,128)S(1)} %get-tuple-element.98.refs_4_, ...), custom_call_target="tpu_custom_call" | custom-call | flops 589824 | bytes 1446912 | tf_op jit(solution)/shard_map/pallas_call | solution.py:58
  (78 shorter events, 21.9 us)
Async XLA Ops:
  2.8 2.1 %collective-permute-start.1 = (f32[384,384]{1,0:T(8,128)S(1)}, f32[384,384]{1,0:T(8,128)S(1)}, u32[]{:S(2)}, u32[]{:S(2)}) collective-permute-start(f32[384,384]{1,0:T(8,128)S(1)} %shard_map.114.refs_0_.refs_3_), channel_id=1, source_target_pairs={{0,1},{1,0},{2,3},{3,2},{4,5},{5,4},{6,7},{7,6},{8,9},{9,8},{10,11... | collective-permute-start | bytes 1769480 | tf_op jit(solution)/shard_map/ppermute | solution.py:33
  3.2 2.5 %collective-permute-start.2 = (f32[37,32,128]{2,1,0:T(8,128)S(1)}, f32[37,32,128]{2,1,0:T(8,128)S(1)}, u32[]{:S(2)}, u32[]{:S(2)}) collective-permute-start(f32[37,32,128]{2,1,0:T(8,128)S(1)} %get-tuple-element.55), channel_id=1, source_target_pairs={{0,1},{1,0},{2,3},{3,2},{4,5},{5,4},{6,7},{7,6},{8,9},{9,8},{10,11... | collective-permute-start | bytes 1818632 | tf_op jit(solution)/shard_map/ppermute | solution.py:33
  5.7 9.3 %collective-permute-start.3 = (f32[192,384]{1,0:T(8,128)S(1)}, f32[192,384]{1,0:T(8,128)S(1)}, u32[]{:S(2)}, u32[]{:S(2)}) collective-permute-start(f32[192,384]{1,0:T(8,128)S(1)} %get-tuple-element.56), channel_id=1, source_target_pairs={{0,2},{1,3},{2,0},{3,1},{4,6},{5,7},{6,4},{7,5},{8,10},{9,11},{10,... | collective-permute-start | bytes 884744 | tf_op jit(solution)/shard_map/ppermute | solution.py:33
  7.7 18.7 %collective-permute-start = (f32[37,32,128]{2,1,0:T(8,128)S(1)}, f32[37,32,128]{2,1,0:T(8,128)S(1)}, u32[]{:S(2)}, u32[]{:S(2)}) collective-permute-start(f32[37,32,128]{2,1,0:T(8,128)S(1)} %get-tuple-element.51), channel_id=1, source_target_pairs={{1,2},{2,1},{3,4},{4,3},{5,6},{6,5},{7,8},{8,7},{9,10},{10,9},{11,... | collective-permute-start | bytes 1818632 | tf_op jit(solution)/shard_map/ppermute | solution.py:692
  17.4 37.2 %collective-permute-start.15 = (f32[192,384]{1,0:T(8,128)S(1)}, f32[192,384]{1,0:T(8,128)S(1)}, u32[]{:S(2)}, u32[]{:S(2)}) collective-permute-start(f32[192,384]{1,0:T(8,128)S(1)} %get-tuple-element.57), channel_id=1, source_target_pairs={{0,12},{1,13},{2,14},{3,15},{4,8},{5,9},{6,10},{7,11},{8,4},{9,5},... | collective-permute-start | bytes 884744 | tf_op jit(solution)/shard_map/ppermute | solution.py:33
  23.6 31.1 %collective-permute-start.13 = (f32[192,384]{1,0:T(8,128)S(1)}, f32[192,384]{1,0:T(8,128)S(1)}, u32[]{:S(2)}, u32[]{:S(2)}) collective-permute-start(f32[192,384]{1,0:T(8,128)S(1)} %get-tuple-element.57), channel_id=1, source_target_pairs={{0,10},{1,11},{2,8},{3,9},{4,14},{5,15},{6,12},{7,13},{8,2},{9,3},... | collective-permute-start | bytes 884744 | tf_op jit(solution)/shard_map/ppermute | solution.py:33
  25.4 29.8 %collective-permute-start.11 = (f32[192,384]{1,0:T(8,128)S(1)}, f32[192,384]{1,0:T(8,128)S(1)}, u32[]{:S(2)}, u32[]{:S(2)}) collective-permute-start(f32[192,384]{1,0:T(8,128)S(1)} %get-tuple-element.57), channel_id=1, source_target_pairs={{0,4},{1,5},{2,6},{3,7},{4,0},{5,1},{6,2},{7,3},{8,12},{9,13},{10,... | collective-permute-start | bytes 884744 | tf_op jit(solution)/shard_map/ppermute | solution.py:33
  37.4 3.6 %collective-permute-start.5 = (f32[1,384]{1,0:T(1,128)S(1)}, f32[1,384]{1,0:T(1,128)S(1)}, u32[]{:S(2)}, u32[]{:S(2)}) collective-permute-start(f32[1,384]{1,0:T(1,128)S(1)} %get-tuple-element.60.refs_1_), channel_id=1, source_target_pairs={{0,64},{64,0},{128,192},{192,128},{1,65},{65,1},{129,193},{193,129... | collective-permute-start | bytes 4616 | tf_op jit(solution)/shard_map/ppermute | solution.py:607
  42.5 3.7 %collective-permute-start.7 = (f32[1,384]{1,0:T(1,128)S(1)}, f32[1,384]{1,0:T(1,128)S(1)}, u32[]{:S(2)}, u32[]{:S(2)}) collective-permute-start(f32[1,384]{1,0:T(1,128)S(1)} %shard_map.122.refs_0_), channel_id=1, source_target_pairs={{0,2},{1,3},{2,0},{3,1},{4,6},{5,7},{6,4},{7,5},{8,10},{9,11},{10,... | collective-permute-start | bytes 4616 | tf_op jit(solution)/shard_map/ppermute | solution.py:33
  46.3 8.0 %collective-permute-start.10 = (f32[1,384]{1,0:T(1,128)S(1)}, f32[1,384]{1,0:T(1,128)S(1)}, u32[]{:S(2)}, u32[]{:S(2)}) collective-permute-start(f32[1,384]{1,0:T(1,128)S(1)} %shard_map.123.refs_0_), channel_id=1, source_target_pairs={{0,10},{1,11},{2,8},{3,9},{4,14},{5,15},{6,12},{7,13},{8,2},{9,3},... | collective-permute-start | bytes 4616 | tf_op jit(solution)/shard_map/ppermute | solution.py:33
  50.2 4.5 %collective-permute-start.8 = (f32[1,384]{1,0:T(1,128)S(1)}, f32[1,384]{1,0:T(1,128)S(1)}, u32[]{:S(2)}, u32[]{:S(2)}) collective-permute-start(f32[1,384]{1,0:T(1,128)S(1)} %shard_map.123.refs_0_), channel_id=1, source_target_pairs={{0,4},{1,13},{2,6},{3,15},{4,0},{5,9},{6,2},{7,11},{8,12},{9,5},{1... | collective-permute-start | bytes 4616 | tf_op jit(solution)/shard_map/ppermute | solution.py:579
  54.7 2.0 %collective-permute-start.14 = (f32[192,384]{1,0:T(8,128)S(1)}, f32[192,384]{1,0:T(8,128)S(1)}, u32[]{:S(2)}, u32[]{:S(2)}) collective-permute-start(f32[192,384]{1,0:T(8,128)S(1)} %collective-permute-done.13.refs_3_), channel_id=1, source_target_pairs={{0,1},{1,0},{2,3},{3,2},{4,5},{5,4},{6,7},{7,6},{8,9},{9,8},{10,11... | collective-permute-start | bytes 884744 | tf_op jit(solution)/shard_map/ppermute | solution.py:33
  55.3 2.1 %collective-permute-start.9 = (f32[1,384]{1,0:T(1,128)S(1)}, f32[1,384]{1,0:T(1,128)S(1)}, u32[]{:S(2)}, u32[]{:S(2)}) collective-permute-start(f32[1,384]{1,0:T(1,128)S(1)} %collective-permute-done.8.refs_1_), channel_id=1, source_target_pairs={{0,1},{1,0},{2,3},{3,2},{4,5},{5,4},{6,7},{7,6},{8,9},{9,8},{10,11... | collective-permute-start | bytes 4616 | tf_op jit(solution)/shard_map/ppermute | solution.py:33
  57.8 4.9 %collective-permute-start.17 = (f32[1,384]{1,0:T(1,128)S(1)}, f32[1,384]{1,0:T(1,128)S(1)}, u32[]{:S(2)}, u32[]{:S(2)}) collective-permute-start(f32[1,384]{1,0:T(1,128)S(1)} %get-tuple-element.74.refs_0_), channel_id=1, source_target_pairs={{0,16},{1,17},{2,18},{3,19},{4,20},{5,21},{6,22},{7,23},{8,24},{9,... | collective-permute-start | bytes 4616 | tf_op jit(solution)/shard_map/ppermute | solution.py:684
  62.8 4.9 %collective-permute-start.18 = (f32[1,384]{1,0:T(1,128)S(1)}, f32[1,384]{1,0:T(1,128)S(1)}, u32[]{:S(2)}, u32[]{:S(2)}) collective-permute-start(f32[1,384]{1,0:T(1,128)S(1)} %shard_map.127), channel_id=1, source_target_pairs={{0,16},{1,17},{2,18},{3,19},{4,20},{5,21},{6,22},{7,23},{8,24},{9,... | collective-permute-start | bytes 4616 | tf_op jit(solution)/shard_map/ppermute | solution.py:684
  67.8 4.9 %collective-permute-start.19 = (f32[1,384]{1,0:T(1,128)S(1)}, f32[1,384]{1,0:T(1,128)S(1)}, u32[]{:S(2)}, u32[]{:S(2)}) collective-permute-start(f32[1,384]{1,0:T(1,128)S(1)} %shard_map.129), channel_id=1, source_target_pairs={{0,16},{1,17},{2,18},{3,19},{4,20},{5,21},{6,22},{7,23},{8,24},{9,... | collective-permute-start | bytes 4616 | tf_op jit(solution)/shard_map/ppermute | solution.py:684
  72.7 13.9 %collective-permute-start.26 = (f32[192,384]{1,0:T(8,128)S(1)}, f32[192,384]{1,0:T(8,128)S(1)}, u32[]{:S(2)}, u32[]{:S(2)}) collective-permute-start(f32[192,384]{1,0:T(8,128)S(1)} %get-tuple-element.91), channel_id=1, source_target_pairs={{0,16},{1,17},{2,18},{3,19},{4,20},{5,21},{6,22},{7,23},{8,24},{9,... | collective-permute-start | bytes 884744 | tf_op jit(solution)/shard_map/ppermute | solution.py:33
  74.7 3.7 %collective-permute-start.21 = (f32[1,384]{1,0:T(1,128)S(1)}, f32[1,384]{1,0:T(1,128)S(1)}, u32[]{:S(2)}, u32[]{:S(2)}) collective-permute-start(f32[1,384]{1,0:T(1,128)S(1)} %shard_map.132.refs_0_), channel_id=1, source_target_pairs={{0,2},{1,3},{2,0},{3,1},{4,6},{5,7},{6,4},{7,5},{8,10},{9,11},{10,... | collective-permute-start | bytes 4616 | tf_op jit(solution)/shard_map/ppermute | solution.py:33
  78.6 4.6 %collective-permute-start.22 = (f32[1,384]{1,0:T(1,128)S(1)}, f32[1,384]{1,0:T(1,128)S(1)}, u32[]{:S(2)}, u32[]{:S(2)}) collective-permute-start(f32[1,384]{1,0:T(1,128)S(1)} %shard_map.133.refs_0_), channel_id=1, source_target_pairs={{0,4},{1,13},{2,6},{3,15},{4,0},{5,9},{6,2},{7,11},{8,12},{9,5},{1... | collective-permute-start | bytes 4616 | tf_op jit(solution)/shard_map/ppermute | solution.py:579
  80.1 6.6 %collective-permute-start.24 = (f32[1,384]{1,0:T(1,128)S(1)}, f32[1,384]{1,0:T(1,128)S(1)}, u32[]{:S(2)}, u32[]{:S(2)}) collective-permute-start(f32[1,384]{1,0:T(1,128)S(1)} %shard_map.133.refs_0_), channel_id=1, source_target_pairs={{0,10},{1,11},{2,8},{3,9},{4,14},{5,15},{6,12},{7,13},{8,2},{9,3},... | collective-permute-start | bytes 4616 | tf_op jit(solution)/shard_map/ppermute | solution.py:33
  83.2 3.5 %collective-permute-start.23 = (f32[1,384]{1,0:T(1,128)S(1)}, f32[1,384]{1,0:T(1,128)S(1)}, u32[]{:S(2)}, u32[]{:S(2)}) collective-permute-start(f32[1,384]{1,0:T(1,128)S(1)} %collective-permute-done.22.refs_1_), channel_id=1, source_target_pairs={{0,1},{1,0},{2,3},{3,2},{4,5},{5,4},{6,7},{7,6},{8,9},{9,8},{10,11... | collective-permute-start | bytes 4616 | tf_op jit(solution)/shard_map/ppermute | solution.py:33
  86.6 2.8 %collective-permute-start.27 = (f32[192,384]{1,0:T(8,128)S(1)}, f32[192,384]{1,0:T(8,128)S(1)}, u32[]{:S(2)}, u32[]{:S(2)}) collective-permute-start(f32[192,384]{1,0:T(8,128)S(1)} %collective-permute-done.26.refs_1_), channel_id=1, source_target_pairs={{0,1},{1,0},{2,3},{3,2},{4,5},{5,4},{6,7},{7,6},{8,9},{9,8},{10,11... | collective-permute-start | bytes 884744 | tf_op jit(solution)/shard_map/ppermute | solution.py:33
  87.3 3.8 %collective-permute-start.25 = (f32[1,384]{1,0:T(1,128)S(1)}, f32[1,384]{1,0:T(1,128)S(1)}, u32[]{:S(2)}, u32[]{:S(2)}) collective-permute-start(f32[1,384]{1,0:T(1,128)S(1)} %get-tuple-element.88.refs_0_), channel_id=1, source_target_pairs={{0,16},{1,17},{2,18},{3,19},{4,20},{5,21},{6,22},{7,23},{8,24},{9,... | collective-permute-start | bytes 4616 | tf_op jit(solution)/shard_map/ppermute | solution.py:33
  91.4 4.9 %collective-permute-start.28 = (f32[1,384]{1,0:T(1,128)S(1)}, f32[1,384]{1,0:T(1,128)S(1)}, u32[]{:S(2)}, u32[]{:S(2)}) collective-permute-start(f32[1,384]{1,0:T(1,128)S(1)} %shard_map.138), channel_id=1, source_target_pairs={{0,48},{1,49},{2,50},{3,51},{4,52},{5,53},{6,54},{7,55},{8,56},{9,... | collective-permute-start | bytes 4616 | tf_op jit(solution)/shard_map/ppermute | solution.py:33
  (12 other events, 47.2 us)

commit v9 on v8

--- a/solution.py
+++ b/solution.py
@@ -613,7 +613,7 @@
             bound(level, forward_kernel), flags, [total, others[-1], levels[level][0]], ROW, square
         )
     arrived = row_exchange(total)
-    blocks = sorted_blocks(flags, fetched, (arrived[0], arrived[2]))
+    blocks = sorted_blocks(flags, fetched, (arrived[1], arrived[2]))
     total, in_row = local_call(
         row_forward_kernel, flags, [total, *arrived, blocks], (ROW, ROW), 3 * square
     )

time: 97.9 us -> 98.1 us (level)
  waiting for transfers between devices: 39.3 us -> 40.6 us
  starting transfers between devices: 29.4 us -> 28.3 us
    ppermute x22, waiting for transfers between devices: 26.8 us -> 27.9 us  [swap(): lax.ppermute(value, 'tile', [(i, i ^ mask) for i in range(lax.axis_size('...]
  transfers between devices with their start and end apart: 29 -> 29, of which waited for: 20 -> 19; matrix products, arithmetic and copies ran while one was open for 0% -> 0% of each run, Pallas kernels for 23% -> 23%
where the time goes in v9:
time: 98.1 us; the launch traced here: 97.9 us
  waiting for transfers between devices  40.6 us (41%)
  starting transfers between devices  28.3 us (29%)
  Pallas kernels  25.7 us (26%)
  local copies, waits for them, and re-layouts  1.67 us (2%)
  between operations  1.61 us (2%)
    ppermute x22, waiting for transfers between devices, swap(): lax.ppermute(value, 'tile', [(i, i ^ mask) for i in range(lax.axis_size('...  27.9 us
    ppermute x22, starting transfers between devices, swap(): lax.ppermute(value, 'tile', [(i, i ^ mask) for i in range(lax.axis_size('...  22.1 us
    pallas_call x26, Pallas kernels, local_call(): pl.pallas_call(placed, out_shape=outs, in_specs=[VM] * len(operands), out...  14.7 us
    pallas_call x1, Pallas kernels, substeps_call(): pl.pallas_call(substep_kernel, out_shape=(jax.ShapeDtypeStruct(grid_shape...  11 us
    ppermute x3, waiting for transfers between devices, up_row(): lax.ppermute(value, 'tile', [(i, (i + ROW_TILES) % count) for i in range(...  8.3 us
    ppermute x1, waiting for transfers between devices, coupled_velocity(): partner = lax.ppermute(picked, 'sub', [(i, i ^ 1) for i in range(count)])  3.48 us
    ppermute x2, starting transfers between devices, split_swap(): lax.ppermute(value, 'tile', [(i, i ^ mask) for i, mask in enumerate(masks)])  3.19 us
    ppermute x3, starting transfers between devices, up_row(): lax.ppermute(value, 'tile', [(i, (i + ROW_TILES) % count) for i in range(...  2.33 us
  transfers between devices with their start and end apart: 29, of which 19 were waited for; matrix products, arithmetic and copies ran while one was open for 0% of the time, Pallas kernels for 23%

profile of v9, /device:TPU:2, one launch (start us, length us, event | category | flops | bytes accessed | tf_op | source)
XLA Modules:
  0.0 97.9 jit_solution(16458244647070007378)
XLA Ops:
  0.6 1.3 %dynamic-slice_bitcast_fusion = (f32[384,384]{1,0:T(8,128)S(1)}, f32[384,384]{1,0:T(8,128)S(1)}) fusion(f32[2,384,384]{2,1,0:T(8,128)} %param.19, s32[]{:T(128)S(6)} %select_n.12, f32[2,384,384]{2,1,0:T(8,128)} %param.18), kind=kLoop, calls=%fused_computation | loop fusion | bytes 2359300 | tf_op jit(solution)/shard_map/jit(dynamic_index_in_dim)/squeeze | solution.py:715
  3.6 1.3 %collective-permute-done.1.refs_1_.refs_0_ = f32[384,384]{1,0:T(8,128)S(1)} collective-permute-done((f32[384,384]{1,0:T(8,128)S(1)}, f32[384,384]{1,0:T(8,128)S(1)}, u32[]{:S(2)}, u32[]{:S(2)}) %collective-permute-start.1) | collective-permute-done | bytes 589856 | tf_op jit(solution)/shard_map/ppermute | solution.py:33
  5.7 1.9 %collective-permute-start.3 = (f32[192,384]{1,0:T(8,128)S(1)}, f32[192,384]{1,0:T(8,128)S(1)}, u32[]{:S(2)}, u32[]{:S(2)}) collective-permute-start(f32[192,384]{1,0:T(8,128)S(1)} %get-tuple-element.56), channel_id=1, source_target_pairs={{0,2},{1,3},{2,0},{3,1},{4,6},{5,7},{6,4},{7,5},{8,10},{9,11},{10,... | collective-permute-start | bytes 884744 | tf_op jit(solution)/shard_map/ppermute | solution.py:33
  8.4 6.7 %collective-permute-done.3.refs_1_ = f32[192,384]{1,0:T(8,128)S(1)} collective-permute-done((f32[192,384]{1,0:T(8,128)S(1)}, f32[192,384]{1,0:T(8,128)S(1)}, u32[]{:S(2)}, u32[]{:S(2)}) %collective-permute-start.3) | collective-permute-done | bytes 294944 | tf_op jit(solution)/shard_map/ppermute | solution.py:33
  17.4 6.2 %collective-permute-start.15 = (f32[192,384]{1,0:T(8,128)S(1)}, f32[192,384]{1,0:T(8,128)S(1)}, u32[]{:S(2)}, u32[]{:S(2)}) collective-permute-start(f32[192,384]{1,0:T(8,128)S(1)} %get-tuple-element.57), channel_id=1, source_target_pairs={{0,12},{1,13},{2,14},{3,15},{4,8},{5,9},{6,10},{7,11},{8,4},{9,5},... | collective-permute-start | bytes 884744 | tf_op jit(solution)/shard_map/ppermute | solution.py:33
  23.6 1.8 %collective-permute-start.13 = (f32[192,384]{1,0:T(8,128)S(1)}, f32[192,384]{1,0:T(8,128)S(1)}, u32[]{:S(2)}, u32[]{:S(2)}) collective-permute-start(f32[192,384]{1,0:T(8,128)S(1)} %get-tuple-element.57), channel_id=1, source_target_pairs={{0,10},{1,11},{2,8},{3,9},{4,14},{5,15},{6,12},{7,13},{8,2},{9,3},... | collective-permute-start | bytes 884744 | tf_op jit(solution)/shard_map/ppermute | solution.py:33
  26.5 11.0 %shard_map.118 = (f32[3,4,32,128]{3,2,1,0:T(8,128)}, f32[3,4,32,128]{3,2,1,0:T(8,128)S(1)}, f32[1,384]{1,0:T(1,128)S(1)}) custom-call(f32[2,128]{1,0:T(2,128)S(1)} %broadcast_in_dim.14.steps, f32[3,4,32,128]{3,2,1,0:T(8,128)S(1)} %bitcast.19, f32[3,4,32,128]{3,2,1,0:T(8,128)S(1)} %bitcast.21, f32[3,4,32,128]{3,2,1,0:T(8,128)S(1)} %bitcast.23, ...), custom_call_target="tpu_custom_call" | custom-call | flops 3623878656 | bytes 2162688 | tf_op jit(solution)/shard_map/pallas_call | solution.py:301
  37.5 3.5 %collective-permute-done.5.refs_2_ = f32[1,384]{1,0:T(1,128)S(1)} collective-permute-done((f32[1,384]{1,0:T(1,128)S(1)}, f32[1,384]{1,0:T(1,128)S(1)}, u32[]{:S(2)}, u32[]{:S(2)}) %collective-permute-start.5) | collective-permute-done | bytes 1568 | tf_op jit(solution)/shard_map/ppermute | solution.py:607
  43.1 3.1 %collective-permute-done.7.refs_1_ = f32[1,384]{1,0:T(1,128)S(1)} collective-permute-done((f32[1,384]{1,0:T(1,128)S(1)}, f32[1,384]{1,0:T(1,128)S(1)}, u32[]{:S(2)}, u32[]{:S(2)}) %collective-permute-start.7) | collective-permute-done | bytes 1568 | tf_op jit(solution)/shard_map/ppermute | solution.py:33
  46.3 2.1 %collective-permute-start.8 = (f32[1,384]{1,0:T(1,128)S(1)}, f32[1,384]{1,0:T(1,128)S(1)}, u32[]{:S(2)}, u32[]{:S(2)}) collective-permute-start(f32[1,384]{1,0:T(1,128)S(1)} %shard_map.123.refs_0_), channel_id=1, source_target_pairs={{0,4},{1,13},{2,6},{3,15},{4,0},{5,9},{6,2},{7,11},{8,12},{9,5},{1... | collective-permute-start | bytes 4616 | tf_op jit(solution)/shard_map/ppermute | solution.py:579
  48.4 3.1 %collective-permute-start.10 = (f32[1,384]{1,0:T(1,128)S(1)}, f32[1,384]{1,0:T(1,128)S(1)}, u32[]{:S(2)}, u32[]{:S(2)}) collective-permute-start(f32[1,384]{1,0:T(1,128)S(1)} %shard_map.123.refs_0_), channel_id=1, source_target_pairs={{0,10},{1,11},{2,8},{3,9},{4,14},{5,15},{6,12},{7,13},{8,2},{9,3},... | collective-permute-start | bytes 4616 | tf_op jit(solution)/shard_map/ppermute | solution.py:33
  52.5 2.5 %collective-permute-done.10.refs_3_ = f32[1,384]{1,0:T(1,128)S(1)} collective-permute-done((f32[1,384]{1,0:T(1,128)S(1)}, f32[1,384]{1,0:T(1,128)S(1)}, u32[]{:S(2)}, u32[]{:S(2)}) %collective-permute-start.10) | collective-permute-done | bytes 1568 | tf_op jit(solution)/shard_map/ppermute | solution.py:33
  58.1 1.7 %collective-permute-start.17 = (f32[1,384]{1,0:T(1,128)S(1)}, f32[1,384]{1,0:T(1,128)S(1)}, u32[]{:S(2)}, u32[]{:S(2)}) collective-permute-start(f32[1,384]{1,0:T(1,128)S(1)} %get-tuple-element.74.refs_0_), channel_id=1, source_target_pairs={{0,16},{1,17},{2,18},{3,19},{4,20},{5,21},{6,22},{7,23},{8,24},{9,... | collective-permute-start | bytes 4616 | tf_op jit(solution)/shard_map/ppermute | solution.py:684
  59.8 2.1 %shard_map.126 = (f32[384,384]{1,0:T(8,128)S(1)}, f32[384,384]{1,0:T(8,128)S(1)}, f32[384,384]{1,0:T(8,128)S(1)}, f32[192,384]{1,0:T(8,128)S(1)}) custom-call(f32[4,384,384]{2,1,0:T(8,128)S(1)} %shard_map.124.refs_4_.refs_0_), custom_call_target="tpu_custom_call" | custom-call | flops 1019215872 | bytes 2359296 | tf_op jit(solution)/shard_map/pallas_call | solution.py:58
  63.7 1.7 %shard_map.128 = (f32[384,384]{1,0:T(8,128)S(1)}, f32[384,384]{1,0:T(8,128)S(1)}) custom-call(f32[4,384,384]{2,1,0:T(8,128)S(1)} %shard_map.124.refs_4_.refs_0_, f32[384,384]{1,0:T(8,128)S(1)} %get-tuple-element.78.refs_1_, f32[384,384]{1,0:T(8,128)S(1)} %get-tuple-element.79.refs_2_, f32[384,384]{1,0:T(8,128)S(1)} %get-tuple-element.65.refs_3_.refs_4_, ...), custom_call_target="tpu_custom_call" | custom-call | flops 679477248 | bytes 4718592 | tf_op jit(solution)/shard_map/pallas_call | solution.py:58
  65.4 2.6 %collective-permute-done.18.refs_1_ = f32[1,384]{1,0:T(1,128)S(1)} collective-permute-done((f32[1,384]{1,0:T(1,128)S(1)}, f32[1,384]{1,0:T(1,128)S(1)}, u32[]{:S(2)}, u32[]{:S(2)}) %collective-permute-start.18) | collective-permute-done | bytes 1568 | tf_op jit(solution)/shard_map/ppermute | solution.py:684
  68.4 4.6 %collective-permute-done.19.refs_1_ = f32[1,384]{1,0:T(1,128)S(1)} collective-permute-done((f32[1,384]{1,0:T(1,128)S(1)}, f32[1,384]{1,0:T(1,128)S(1)}, u32[]{:S(2)}, u32[]{:S(2)}) %collective-permute-start.19) | collective-permute-done | bytes 1568 | tf_op jit(solution)/shard_map/ppermute | solution.py:684
  75.1 3.6 %collective-permute-done.21.refs_1_ = f32[1,384]{1,0:T(1,128)S(1)} collective-permute-done((f32[1,384]{1,0:T(1,128)S(1)}, f32[1,384]{1,0:T(1,128)S(1)}, u32[]{:S(2)}, u32[]{:S(2)}) %collective-permute-start.21) | collective-permute-done | bytes 1568 | tf_op jit(solution)/shard_map/ppermute | solution.py:33
  80.1 3.6 %collective-permute-start.24 = (f32[1,384]{1,0:T(1,128)S(1)}, f32[1,384]{1,0:T(1,128)S(1)}, u32[]{:S(2)}, u32[]{:S(2)}) collective-permute-start(f32[1,384]{1,0:T(1,128)S(1)} %shard_map.133.refs_0_), channel_id=1, source_target_pairs={{0,10},{1,11},{2,8},{3,9},{4,14},{5,15},{6,12},{7,13},{8,2},{9,3},... | collective-permute-start | bytes 4616 | tf_op jit(solution)/shard_map/ppermute | solution.py:33
  83.7 2.9 %collective-permute-done.24.refs_3_ = f32[1,384]{1,0:T(1,128)S(1)} collective-permute-done((f32[1,384]{1,0:T(1,128)S(1)}, f32[1,384]{1,0:T(1,128)S(1)}, u32[]{:S(2)}, u32[]{:S(2)}) %collective-permute-start.24) | collective-permute-done | bytes 1568 | tf_op jit(solution)/shard_map/ppermute | solution.py:33
  87.7 2.0 %collective-permute-start.25 = (f32[1,384]{1,0:T(1,128)S(1)}, f32[1,384]{1,0:T(1,128)S(1)}, u32[]{:S(2)}, u32[]{:S(2)}) collective-permute-start(f32[1,384]{1,0:T(1,128)S(1)} %get-tuple-element.88.refs_0_), channel_id=1, source_target_pairs={{0,16},{1,17},{2,18},{3,19},{4,20},{5,21},{6,22},{7,23},{8,24},{9,... | collective-permute-start | bytes 4616 | tf_op jit(solution)/shard_map/ppermute | solution.py:33
  89.8 1.6 %shard_map.137 = (f32[384,384]{1,0:T(8,128)}, f32[384,384]{1,0:T(8,128)S(1)}) custom-call(f32[384,384]{1,0:T(8,128)S(1)} %get-tuple-element.93.refs_0_, f32[384,384]{1,0:T(8,128)S(1)} %get-tuple-element.94.refs_1_.refs_2_, f32[384,384]{1,0:T(8,128)S(1)} %get-tuple-element.81.refs_2_, f32[384,384]{1,0:T(8,128)S(1)} %get-tuple-element.89.refs_6_.refs_3_), custom_call_target="tpu_custom_call" | custom-call | flops 339738624 | bytes 2359296 | tf_op jit(solution)/shard_map/pallas_call | solution.py:58
  92.5 4.0 %collective-permute-done.28.refs_2_ = f32[1,384]{1,0:T(1,128)S(1)} collective-permute-done((f32[1,384]{1,0:T(1,128)S(1)}, f32[1,384]{1,0:T(1,128)S(1)}, u32[]{:S(2)}, u32[]{:S(2)}) %collective-permute-start.28) | collective-permute-done | bytes 1568 | tf_op jit(solution)/shard_map/ppermute | solution.py:33
  96.5 1.5 %shard_map.139 = f32[3,4,32,128]{3,2,1,0:T(8,128)} custom-call(f32[384,384]{1,0:T(8,128)S(1)} %get-tuple-element.101.refs_0_, f32[1,384]{1,0:T(1,128)S(1)} %shard_map.135.refs_1_, f32[1,384]{1,0:T(1,128)S(1)} %collective-permute-done.28.refs_2_, f32[384,384]{1,0:T(8,128)S(1)} %get-tuple-element.95.refs_3_, f32[1,384]{1,0:T(1,128)S(1)} %get-tuple-element.98.refs_4_, ...), custom_call_target="tpu_custom_call" | custom-call | flops 589824 | bytes 1446912 | tf_op jit(solution)/shard_map/pallas_call | solution.py:58
  (78 shorter events, 20.1 us)
Async XLA Ops:
  2.8 2.1 %collective-permute-start.1 = (f32[384,384]{1,0:T(8,128)S(1)}, f32[384,384]{1,0:T(8,128)S(1)}, u32[]{:S(2)}, u32[]{:S(2)}) collective-permute-start(f32[384,384]{1,0:T(8,128)S(1)} %shard_map.114.refs_0_.refs_3_), channel_id=1, source_target_pairs={{0,1},{1,0},{2,3},{3,2},{4,5},{5,4},{6,7},{7,6},{8,9},{9,8},{10,11... | collective-permute-start | bytes 1769480 | tf_op jit(solution)/shard_map/ppermute | solution.py:33
  3.2 2.5 %collective-permute-start.2 = (f32[37,32,128]{2,1,0:T(8,128)S(1)}, f32[37,32,128]{2,1,0:T(8,128)S(1)}, u32[]{:S(2)}, u32[]{:S(2)}) collective-permute-start(f32[37,32,128]{2,1,0:T(8,128)S(1)} %get-tuple-element.55), channel_id=1, source_target_pairs={{0,1},{1,0},{2,3},{3,2},{4,5},{5,4},{6,7},{7,6},{8,9},{9,8},{10,11... | collective-permute-start | bytes 1818632 | tf_op jit(solution)/shard_map/ppermute | solution.py:33
  5.7 9.3 %collective-permute-start.3 = (f32[192,384]{1,0:T(8,128)S(1)}, f32[192,384]{1,0:T(8,128)S(1)}, u32[]{:S(2)}, u32[]{:S(2)}) collective-permute-start(f32[192,384]{1,0:T(8,128)S(1)} %get-tuple-element.56), channel_id=1, source_target_pairs={{0,2},{1,3},{2,0},{3,1},{4,6},{5,7},{6,4},{7,5},{8,10},{9,11},{10,... | collective-permute-start | bytes 884744 | tf_op jit(solution)/shard_map/ppermute | solution.py:33
  7.7 18.7 %collective-permute-start = (f32[37,32,128]{2,1,0:T(8,128)S(1)}, f32[37,32,128]{2,1,0:T(8,128)S(1)}, u32[]{:S(2)}, u32[]{:S(2)}) collective-permute-start(f32[37,32,128]{2,1,0:T(8,128)S(1)} %get-tuple-element.51), channel_id=1, source_target_pairs={{1,2},{2,1},{3,4},{4,3},{5,6},{6,5},{7,8},{8,7},{9,10},{10,9},{11,... | collective-permute-start | bytes 1818632 | tf_op jit(solution)/shard_map/ppermute | solution.py:692
  17.4 37.6 %collective-permute-start.15 = (f32[192,384]{1,0:T(8,128)S(1)}, f32[192,384]{1,0:T(8,128)S(1)}, u32[]{:S(2)}, u32[]{:S(2)}) collective-permute-start(f32[192,384]{1,0:T(8,128)S(1)} %get-tuple-element.57), channel_id=1, source_target_pairs={{0,12},{1,13},{2,14},{3,15},{4,8},{5,9},{6,10},{7,11},{8,4},{9,5},... | collective-permute-start | bytes 884744 | tf_op jit(solution)/shard_map/ppermute | solution.py:33
  23.6 31.6 %collective-permute-start.13 = (f32[192,384]{1,0:T(8,128)S(1)}, f32[192,384]{1,0:T(8,128)S(1)}, u32[]{:S(2)}, u32[]{:S(2)}) collective-permute-start(f32[192,384]{1,0:T(8,128)S(1)} %get-tuple-element.57), channel_id=1, source_target_pairs={{0,10},{1,11},{2,8},{3,9},{4,14},{5,15},{6,12},{7,13},{8,2},{9,3},... | collective-permute-start | bytes 884744 | tf_op jit(solution)/shard_map/ppermute | solution.py:33
  25.4 30.2 %collective-permute-start.11 = (f32[192,384]{1,0:T(8,128)S(1)}, f32[192,384]{1,0:T(8,128)S(1)}, u32[]{:S(2)}, u32[]{:S(2)}) collective-permute-start(f32[192,384]{1,0:T(8,128)S(1)} %get-tuple-element.57), channel_id=1, source_target_pairs={{0,4},{1,5},{2,6},{3,7},{4,0},{5,1},{6,2},{7,3},{8,12},{9,13},{10,... | collective-permute-start | bytes 884744 | tf_op jit(solution)/shard_map/ppermute | solution.py:33
  37.4 3.6 %collective-permute-start.5 = (f32[1,384]{1,0:T(1,128)S(1)}, f32[1,384]{1,0:T(1,128)S(1)}, u32[]{:S(2)}, u32[]{:S(2)}) collective-permute-start(f32[1,384]{1,0:T(1,128)S(1)} %get-tuple-element.60.refs_1_), channel_id=1, source_target_pairs={{0,64},{64,0},{128,192},{192,128},{1,65},{65,1},{129,193},{193,129... | collective-permute-start | bytes 4616 | tf_op jit(solution)/shard_map/ppermute | solution.py:607
  42.5 3.7 %collective-permute-start.7 = (f32[1,384]{1,0:T(1,128)S(1)}, f32[1,384]{1,0:T(1,128)S(1)}, u32[]{:S(2)}, u32[]{:S(2)}) collective-permute-start(f32[1,384]{1,0:T(1,128)S(1)} %shard_map.122.refs_0_), channel_id=1, source_target_pairs={{0,2},{1,3},{2,0},{3,1},{4,6},{5,7},{6,4},{7,5},{8,10},{9,11},{10,... | collective-permute-start | bytes 4616 | tf_op jit(solution)/shard_map/ppermute | solution.py:33
  46.3 6.2 %collective-permute-start.8 = (f32[1,384]{1,0:T(1,128)S(1)}, f32[1,384]{1,0:T(1,128)S(1)}, u32[]{:S(2)}, u32[]{:S(2)}) collective-permute-start(f32[1,384]{1,0:T(1,128)S(1)} %shard_map.123.refs_0_), channel_id=1, source_target_pairs={{0,4},{1,13},{2,6},{3,15},{4,0},{5,9},{6,2},{7,11},{8,12},{9,5},{1... | collective-permute-start | bytes 4616 | tf_op jit(solution)/shard_map/ppermute | solution.py:579
  48.4 6.6 %collective-permute-start.10 = (f32[1,384]{1,0:T(1,128)S(1)}, f32[1,384]{1,0:T(1,128)S(1)}, u32[]{:S(2)}, u32[]{:S(2)}) collective-permute-start(f32[1,384]{1,0:T(1,128)S(1)} %shard_map.123.refs_0_), channel_id=1, source_target_pairs={{0,10},{1,11},{2,8},{3,9},{4,14},{5,15},{6,12},{7,13},{8,2},{9,3},... | collective-permute-start | bytes 4616 | tf_op jit(solution)/shard_map/ppermute | solution.py:33
  52.5 2.5 %collective-permute-start.9 = (f32[1,384]{1,0:T(1,128)S(1)}, f32[1,384]{1,0:T(1,128)S(1)}, u32[]{:S(2)}, u32[]{:S(2)}) collective-permute-start(f32[1,384]{1,0:T(1,128)S(1)} %collective-permute-done.8.refs_1_), channel_id=1, source_target_pairs={{0,1},{1,0},{2,3},{3,2},{4,5},{5,4},{6,7},{7,6},{8,9},{9,8},{10,11... | collective-permute-start | bytes 4616 | tf_op jit(solution)/shard_map/ppermute | solution.py:33
  55.5 1.9 %collective-permute-start.12 = (f32[192,384]{1,0:T(8,128)S(1)}, f32[192,384]{1,0:T(8,128)S(1)}, u32[]{:S(2)}, u32[]{:S(2)}) collective-permute-start(f32[192,384]{1,0:T(8,128)S(1)} %collective-permute-done.11.refs_1_), channel_id=1, source_target_pairs={{0,1},{1,0},{2,3},{3,2},{4,5},{5,4},{6,7},{7,6},{8,9},{9,8},{10,11... | collective-permute-start | bytes 884744 | tf_op jit(solution)/shard_map/ppermute | solution.py:33
  58.1 4.9 %collective-permute-start.17 = (f32[1,384]{1,0:T(1,128)S(1)}, f32[1,384]{1,0:T(1,128)S(1)}, u32[]{:S(2)}, u32[]{:S(2)}) collective-permute-start(f32[1,384]{1,0:T(1,128)S(1)} %get-tuple-element.74.refs_0_), channel_id=1, source_target_pairs={{0,16},{1,17},{2,18},{3,19},{4,20},{5,21},{6,22},{7,23},{8,24},{9,... | collective-permute-start | bytes 4616 | tf_op jit(solution)/shard_map/ppermute | solution.py:684
  63.2 4.9 %collective-permute-start.18 = (f32[1,384]{1,0:T(1,128)S(1)}, f32[1,384]{1,0:T(1,128)S(1)}, u32[]{:S(2)}, u32[]{:S(2)}) collective-permute-start(f32[1,384]{1,0:T(1,128)S(1)} %shard_map.127), channel_id=1, source_target_pairs={{0,16},{1,17},{2,18},{3,19},{4,20},{5,21},{6,22},{7,23},{8,24},{9,... | collective-permute-start | bytes 4616 | tf_op jit(solution)/shard_map/ppermute | solution.py:684
  68.2 4.9 %collective-permute-start.19 = (f32[1,384]{1,0:T(1,128)S(1)}, f32[1,384]{1,0:T(1,128)S(1)}, u32[]{:S(2)}, u32[]{:S(2)}) collective-permute-start(f32[1,384]{1,0:T(1,128)S(1)} %shard_map.129), channel_id=1, source_target_pairs={{0,16},{1,17},{2,18},{3,19},{4,20},{5,21},{6,22},{7,23},{8,24},{9,... | collective-permute-start | bytes 4616 | tf_op jit(solution)/shard_map/ppermute | solution.py:684
  73.0 13.6 %collective-permute-start.26 = (f32[192,384]{1,0:T(8,128)S(1)}, f32[192,384]{1,0:T(8,128)S(1)}, u32[]{:S(2)}, u32[]{:S(2)}) collective-permute-start(f32[192,384]{1,0:T(8,128)S(1)} %get-tuple-element.91), channel_id=1, source_target_pairs={{0,16},{1,17},{2,18},{3,19},{4,20},{5,21},{6,22},{7,23},{8,24},{9,... | collective-permute-start | bytes 884744 | tf_op jit(solution)/shard_map/ppermute | solution.py:33
  75.0 3.7 %collective-permute-start.21 = (f32[1,384]{1,0:T(1,128)S(1)}, f32[1,384]{1,0:T(1,128)S(1)}, u32[]{:S(2)}, u32[]{:S(2)}) collective-permute-start(f32[1,384]{1,0:T(1,128)S(1)} %shard_map.132.refs_0_), channel_id=1, source_target_pairs={{0,2},{1,3},{2,0},{3,1},{4,6},{5,7},{6,4},{7,5},{8,10},{9,11},{10,... | collective-permute-start | bytes 4616 | tf_op jit(solution)/shard_map/ppermute | solution.py:33
  78.9 4.8 %collective-permute-start.22 = (f32[1,384]{1,0:T(1,128)S(1)}, f32[1,384]{1,0:T(1,128)S(1)}, u32[]{:S(2)}, u32[]{:S(2)}) collective-permute-start(f32[1,384]{1,0:T(1,128)S(1)} %shard_map.133.refs_0_), channel_id=1, source_target_pairs={{0,4},{1,13},{2,6},{3,15},{4,0},{5,9},{6,2},{7,11},{8,12},{9,5},{1... | collective-permute-start | bytes 4616 | tf_op jit(solution)/shard_map/ppermute | solution.py:579
  80.1 6.6 %collective-permute-start.24 = (f32[1,384]{1,0:T(1,128)S(1)}, f32[1,384]{1,0:T(1,128)S(1)}, u32[]{:S(2)}, u32[]{:S(2)}) collective-permute-start(f32[1,384]{1,0:T(1,128)S(1)} %shard_map.133.refs_0_), channel_id=1, source_target_pairs={{0,10},{1,11},{2,8},{3,9},{4,14},{5,15},{6,12},{7,13},{8,2},{9,3},... | collective-permute-start | bytes 4616 | tf_op jit(solution)/shard_map/ppermute | solution.py:33
  83.7 2.9 %collective-permute-start.23 = (f32[1,384]{1,0:T(1,128)S(1)}, f32[1,384]{1,0:T(1,128)S(1)}, u32[]{:S(2)}, u32[]{:S(2)}) collective-permute-start(f32[1,384]{1,0:T(1,128)S(1)} %collective-permute-done.22.refs_1_), channel_id=1, source_target_pairs={{0,1},{1,0},{2,3},{3,2},{4,5},{5,4},{6,7},{7,6},{8,9},{9,8},{10,11... | collective-permute-start | bytes 4616 | tf_op jit(solution)/shard_map/ppermute | solution.py:33
  86.6 3.0 %collective-permute-start.27 = (f32[192,384]{1,0:T(8,128)S(1)}, f32[192,384]{1,0:T(8,128)S(1)}, u32[]{:S(2)}, u32[]{:S(2)}) collective-permute-start(f32[192,384]{1,0:T(8,128)S(1)} %collective-permute-done.26.refs_1_), channel_id=1, source_target_pairs={{0,1},{1,0},{2,3},{3,2},{4,5},{5,4},{6,7},{7,6},{8,9},{9,8},{10,11... | collective-permute-start | bytes 884744 | tf_op jit(solution)/shard_map/ppermute | solution.py:33
  87.7 3.7 %collective-permute-start.25 = (f32[1,384]{1,0:T(1,128)S(1)}, f32[1,384]{1,0:T(1,128)S(1)}, u32[]{:S(2)}, u32[]{:S(2)}) collective-permute-start(f32[1,384]{1,0:T(1,128)S(1)} %get-tuple-element.88.refs_0_), channel_id=1, source_target_pairs={{0,16},{1,17},{2,18},{3,19},{4,20},{5,21},{6,22},{7,23},{8,24},{9,... | collective-permute-start | bytes 4616 | tf_op jit(solution)/shard_map/ppermute | solution.py:33
  91.6 4.9 %collective-permute-start.28 = (f32[1,384]{1,0:T(1,128)S(1)}, f32[1,384]{1,0:T(1,128)S(1)}, u32[]{:S(2)}, u32[]{:S(2)}) collective-permute-start(f32[1,384]{1,0:T(1,128)S(1)} %shard_map.138), channel_id=1, source_target_pairs={{0,48},{1,49},{2,50},{3,51},{4,52},{5,53},{6,54},{7,55},{8,56},{9,... | collective-permute-start | bytes 4616 | tf_op jit(solution)/shard_map/ppermute | solution.py:33
  (12 other events, 47.2 us)

commit v10 on v9

--- a/solution.py
+++ b/solution.py
@@ -18,7 +18,6 @@
 MASKS = (1, 2, 4, 12, 16, 48)
 SPLIT_MASKS = (4, 12)
 OPPOSITE = 10
-ROW_TILES = 16
 
 coarse_step = 0.1
 f32 = jnp.float32
@@ -447,13 +446,8 @@
     entering[...] = before
 
 
-def below_row(flags, hop):
-    first_row = flags[4] + flags[5] == 0
-    return jnp.where(first_row, 0.0, hop[...])
-
-
 def hop_kernel(flags, total, hop, merged, leaving):
-    leaving[...] = total[...] + apply(merged[...], below_row(flags, hop))
+    leaving[...] = total[...] + apply(merged[...], hop[...])
 
 
 def reach_kernel(level, flags, high, low, prefix, suffix, new_prefix, new_suffix):
@@ -508,8 +502,14 @@
         result[...] = result[...] + apply_transposed(suffix_3[...], other_4[...])
 
 
-def turn_kernel(flags, entering, hop, prefix, transition, offset, solved, returning):
-    before = entering[...] + apply(prefix[...], below_row(flags, hop))
+def turn_kernel(
+    flags, entering, hop_1, hop_2, hop_3, prefix, transition, offset, solved, returning
+):
+    row = flags[4] + 2 * flags[5]
+    state = jnp.zeros_like(hop_1[...])
+    for index, hop in ((1, hop_1), (2, hop_2), (3, hop_3)):
+        state = jnp.where(row == index, hop[...], state)
+    before = entering[...] + apply(prefix[...], state)
     current = offset[...] + apply(transition[...], before)
     solved[...] = current
     returning[...] = -apply_transposed(transition[...], current)
@@ -621,25 +621,24 @@
         row_kernel, flags, [after(blocks, total)], (MAT, MAT, MAT, HALFMAT), 3 * cube
     )
     merged = row[0]
-    hop = up_row(total)
-    hop = after(hop, merged)
-    leaving = local_call(hop_kernel, flags, [total, hop, merged], ROW, square)
-    hop = up_row(leaving)
+    hop_1 = after(swap(total, MASKS[4]), merged)
+    leaving = local_call(hop_kernel, flags, [total, hop_1, merged], ROW, square)
+    hop_2 = swap(leaving, MASKS[5])
     prefix_3, suffix_3 = local_call(
         row_reach_kernel, flags, [blocks, high, low, prefix_1, suffix_1], (MAT, MAT), 2 * cube
     )
-    hop = after(hop, prefix_3)
-    leaving = local_call(hop_kernel, flags, [total, hop, merged], ROW, square)
-    hop = up_row(leaving)
+    hop_2 = after(hop_2, prefix_3)
+    leaving = local_call(hop_kernel, flags, [total, hop_2, merged], ROW, square)
+    hop_3 = swap(leaving, MASKS[4])
     entering = local_call(
         forward_part_kernel, flags, [*others, after(in_row, leaving), prefix_0, prefix_1], ROW, 2 * square
     )
-    hop = after(hop, entering)
-    row[1] = after(row[1], hop)
+    hop_3 = after(hop_3, entering)
+    row[1] = after(row[1], hop_3)
     solved, returning = local_call(
         turn_kernel,
         flags,
-        [entering, hop, prefix_3, transition, offset],
+        [entering, hop_1, hop_2, hop_3, prefix_3, transition, offset],
         (ROW, ROW),
         3 * square,
     )
@@ -677,11 +676,6 @@
         jax.ShapeDtypeStruct(velocity.shape, f32),
         2 * square,
     )
-
-
-def up_row(value):
-    count = lax.axis_size("tile")
-    return lax.ppermute(value, "tile", [(i, (i + ROW_TILES) % count) for i in range(count)])
 
 
 def outer_swap(value):

time: 98.1 us -> 96 us (0.979)
  waiting for transfers between devices: 40.6 us -> 32.7 us
  starting transfers between devices: 28.3 us -> 34.2 us
    ppermute x3 -> x0, waiting for transfers between devices: 8.3 us -> none  [up_row(): lax.ppermute(value, 'tile', [(i, (i + ROW_TILES) % count) for i in range(...]
    ppermute x22 -> x25, starting transfers between devices: 22.1 us -> 29.8 us  [swap(): lax.ppermute(value, 'tile', [(i, i ^ mask) for i in range(lax.axis_size('...]
    ppermute x3 -> x0, starting transfers between devices: 2.33 us -> none  [up_row(): lax.ppermute(value, 'tile', [(i, (i + ROW_TILES) % count) for i in range(...]
    ppermute x22 -> x25, waiting for transfers between devices: 27.9 us -> 28.8 us  [swap(): lax.ppermute(value, 'tile', [(i, i ^ mask) for i in range(lax.axis_size('...]
  transfers between devices with their start and end apart: 29 -> 29, of which waited for: 19 -> 18; matrix products, arithmetic and copies ran while one was open for 0% -> 0% of each run, Pallas kernels for 23% -> 23%
where the time goes in v10:
time: 96 us; the launch traced here: 95.9 us
  starting transfers between devices  34.2 us (36%)
  waiting for transfers between devices  32.7 us (34%)
  Pallas kernels  25.6 us (27%)
  local copies, waits for them, and re-layouts  1.67 us (2%)
  between operations  1.61 us (2%)
    ppermute x25, starting transfers between devices, swap(): lax.ppermute(value, 'tile', [(i, i ^ mask) for i in range(lax.axis_size('...  29.8 us
    ppermute x25, waiting for transfers between devices, swap(): lax.ppermute(value, 'tile', [(i, i ^ mask) for i in range(lax.axis_size('...  28.8 us
    pallas_call x26, Pallas kernels, local_call(): pl.pallas_call(placed, out_shape=outs, in_specs=[VM] * len(operands), out...  14.7 us
    pallas_call x1, Pallas kernels, substeps_call(): pl.pallas_call(substep_kernel, out_shape=(jax.ShapeDtypeStruct(grid_shape...  11 us
    ppermute x2, starting transfers between devices, split_swap(): lax.ppermute(value, 'tile', [(i, i ^ mask) for i, mask in enumerate(masks)])  3.19 us
    ppermute x1, waiting for transfers between devices, coupled_velocity(): partner = lax.ppermute(picked, 'sub', [(i, i ^ 1) for i in range(count)])  2.95 us
  transfers between devices with their start and end apart: 29, of which 18 were waited for; matrix products, arithmetic and copies ran while one was open for 0% of the time, Pallas kernels for 23%

profile of v10, /device:TPU:2, one launch (start us, length us, event | category | flops | bytes accessed | tf_op | source)
XLA Modules:
  0.0 95.9 jit_solution(10558065433167614069)
XLA Ops:
  0.6 1.3 %dynamic-slice_bitcast_fusion = (f32[384,384]{1,0:T(8,128)S(1)}, f32[384,384]{1,0:T(8,128)S(1)}) fusion(f32[2,384,384]{2,1,0:T(8,128)} %param.19, s32[]{:T(128)S(6)} %select_n.12, f32[2,384,384]{2,1,0:T(8,128)} %param.18), kind=kLoop, calls=%fused_computation | loop fusion | bytes 2359300 | tf_op jit(solution)/shard_map/jit(dynamic_index_in_dim)/squeeze | solution.py:709
  5.7 1.9 %collective-permute-start.3 = (f32[192,384]{1,0:T(8,128)S(1)}, f32[192,384]{1,0:T(8,128)S(1)}, u32[]{:S(2)}, u32[]{:S(2)}) collective-permute-start(f32[192,384]{1,0:T(8,128)S(1)} %get-tuple-element.56), channel_id=1, source_target_pairs={{0,2},{1,3},{2,0},{3,1},{4,6},{5,7},{6,4},{7,5},{8,10},{9,11},{10,... | collective-permute-start | bytes 884744 | tf_op jit(solution)/shard_map/ppermute | solution.py:32
  8.4 6.7 %collective-permute-done.3.refs_1_ = f32[192,384]{1,0:T(8,128)S(1)} collective-permute-done((f32[192,384]{1,0:T(8,128)S(1)}, f32[192,384]{1,0:T(8,128)S(1)}, u32[]{:S(2)}, u32[]{:S(2)}) %collective-permute-start.3) | collective-permute-done | bytes 294944 | tf_op jit(solution)/shard_map/ppermute | solution.py:32
  17.4 6.2 %collective-permute-start.15 = (f32[192,384]{1,0:T(8,128)S(1)}, f32[192,384]{1,0:T(8,128)S(1)}, u32[]{:S(2)}, u32[]{:S(2)}) collective-permute-start(f32[192,384]{1,0:T(8,128)S(1)} %get-tuple-element.57), channel_id=1, source_target_pairs={{0,12},{1,13},{2,14},{3,15},{4,8},{5,9},{6,10},{7,11},{8,4},{9,5},... | collective-permute-start | bytes 884744 | tf_op jit(solution)/shard_map/ppermute | solution.py:32
  23.6 1.8 %collective-permute-start.13 = (f32[192,384]{1,0:T(8,128)S(1)}, f32[192,384]{1,0:T(8,128)S(1)}, u32[]{:S(2)}, u32[]{:S(2)}) collective-permute-start(f32[192,384]{1,0:T(8,128)S(1)} %get-tuple-element.57), channel_id=1, source_target_pairs={{0,10},{1,11},{2,8},{3,9},{4,14},{5,15},{6,12},{7,13},{8,2},{9,3},... | collective-permute-start | bytes 884744 | tf_op jit(solution)/shard_map/ppermute | solution.py:32
  26.5 11.0 %shard_map.118 = (f32[3,4,32,128]{3,2,1,0:T(8,128)}, f32[3,4,32,128]{3,2,1,0:T(8,128)S(1)}, f32[1,384]{1,0:T(1,128)S(1)}) custom-call(f32[2,128]{1,0:T(2,128)S(1)} %broadcast_in_dim.14.steps, f32[3,4,32,128]{3,2,1,0:T(8,128)S(1)} %bitcast.19, f32[3,4,32,128]{3,2,1,0:T(8,128)S(1)} %bitcast.21, f32[3,4,32,128]{3,2,1,0:T(8,128)S(1)} %bitcast.23, ...), custom_call_target="tpu_custom_call" | custom-call | flops 3623878656 | bytes 2162688 | tf_op jit(solution)/shard_map/pallas_call | solution.py:300
  38.0 3.0 %collective-permute-done.5.refs_2_ = f32[1,384]{1,0:T(1,128)S(1)} collective-permute-done((f32[1,384]{1,0:T(1,128)S(1)}, f32[1,384]{1,0:T(1,128)S(1)}, u32[]{:S(2)}, u32[]{:S(2)}) %collective-permute-start.5) | collective-permute-done | bytes 1568 | tf_op jit(solution)/shard_map/ppermute | solution.py:607
  43.1 3.1 %collective-permute-done.7.refs_1_ = f32[1,384]{1,0:T(1,128)S(1)} collective-permute-done((f32[1,384]{1,0:T(1,128)S(1)}, f32[1,384]{1,0:T(1,128)S(1)}, u32[]{:S(2)}, u32[]{:S(2)}) %collective-permute-start.7) | collective-permute-done | bytes 1568 | tf_op jit(solution)/shard_map/ppermute | solution.py:32
  46.3 2.1 %collective-permute-start.8 = (f32[1,384]{1,0:T(1,128)S(1)}, f32[1,384]{1,0:T(1,128)S(1)}, u32[]{:S(2)}, u32[]{:S(2)}) collective-permute-start(f32[1,384]{1,0:T(1,128)S(1)} %shard_map.123.refs_0_), channel_id=1, source_target_pairs={{0,4},{1,13},{2,6},{3,15},{4,0},{5,9},{6,2},{7,11},{8,12},{9,5},{1... | collective-permute-start | bytes 4616 | tf_op jit(solution)/shard_map/ppermute | solution.py:579
  48.4 3.1 %collective-permute-start.10 = (f32[1,384]{1,0:T(1,128)S(1)}, f32[1,384]{1,0:T(1,128)S(1)}, u32[]{:S(2)}, u32[]{:S(2)}) collective-permute-start(f32[1,384]{1,0:T(1,128)S(1)} %shard_map.123.refs_0_), channel_id=1, source_target_pairs={{0,10},{1,11},{2,8},{3,9},{4,14},{5,15},{6,12},{7,13},{8,2},{9,3},... | collective-permute-start | bytes 4616 | tf_op jit(solution)/shard_map/ppermute | solution.py:32
  52.5 2.5 %collective-permute-done.10.refs_3_ = f32[1,384]{1,0:T(1,128)S(1)} collective-permute-done((f32[1,384]{1,0:T(1,128)S(1)}, f32[1,384]{1,0:T(1,128)S(1)}, u32[]{:S(2)}, u32[]{:S(2)}) %collective-permute-start.10) | collective-permute-done | bytes 1568 | tf_op jit(solution)/shard_map/ppermute | solution.py:32
  58.1 1.7 %collective-permute-start.17 = (f32[1,384]{1,0:T(1,128)S(1)}, f32[1,384]{1,0:T(1,128)S(1)}, u32[]{:S(2)}, u32[]{:S(2)}) collective-permute-start(f32[1,384]{1,0:T(1,128)S(1)} %get-tuple-element.74.refs_0_), channel_id=1, source_target_pairs={{0,16},{1,17},{2,18},{3,19},{4,20},{5,21},{6,22},{7,23},{8,24},{9,... | collective-permute-start | bytes 4616 | tf_op jit(solution)/shard_map/ppermute | solution.py:32
  59.8 2.1 %shard_map.126 = (f32[384,384]{1,0:T(8,128)S(1)}, f32[384,384]{1,0:T(8,128)S(1)}, f32[384,384]{1,0:T(8,128)S(1)}, f32[192,384]{1,0:T(8,128)S(1)}) custom-call(f32[4,384,384]{2,1,0:T(8,128)S(1)} %shard_map.124.refs_4_.refs_0_), custom_call_target="tpu_custom_call" | custom-call | flops 1019215872 | bytes 2359296 | tf_op jit(solution)/shard_map/pallas_call | solution.py:57
  62.1 3.0 %collective-permute-start.18 = (f32[1,384]{1,0:T(1,128)S(1)}, f32[1,384]{1,0:T(1,128)S(1)}, u32[]{:S(2)}, u32[]{:S(2)}) collective-permute-start(f32[1,384]{1,0:T(1,128)S(1)} %shard_map.127), channel_id=1, source_target_pairs={{0,48},{1,49},{2,50},{3,51},{4,52},{5,53},{6,54},{7,55},{8,56},{9,... | collective-permute-start | bytes 4616 | tf_op jit(solution)/shard_map/ppermute | solution.py:32
  65.1 1.7 %shard_map.128 = (f32[384,384]{1,0:T(8,128)S(1)}, f32[384,384]{1,0:T(8,128)S(1)}) custom-call(f32[4,384,384]{2,1,0:T(8,128)S(1)} %shard_map.124.refs_4_.refs_0_, f32[384,384]{1,0:T(8,128)S(1)} %get-tuple-element.78.refs_1_, f32[384,384]{1,0:T(8,128)S(1)} %get-tuple-element.79.refs_2_, f32[384,384]{1,0:T(8,128)S(1)} %get-tuple-element.65.refs_3_.refs_4_, ...), custom_call_target="tpu_custom_call" | custom-call | flops 679477248 | bytes 4718592 | tf_op jit(solution)/shard_map/pallas_call | solution.py:57
  67.6 3.2 %collective-permute-done.19.refs_3_ = f32[1,384]{1,0:T(1,128)S(1)} collective-permute-done((f32[1,384]{1,0:T(1,128)S(1)}, f32[1,384]{1,0:T(1,128)S(1)}, u32[]{:S(2)}, u32[]{:S(2)}) %collective-permute-start.19) | collective-permute-done | bytes 1568 | tf_op jit(solution)/shard_map/ppermute | solution.py:32
  73.1 3.6 %collective-permute-done.21.refs_1_ = f32[1,384]{1,0:T(1,128)S(1)} collective-permute-done((f32[1,384]{1,0:T(1,128)S(1)}, f32[1,384]{1,0:T(1,128)S(1)}, u32[]{:S(2)}, u32[]{:S(2)}) %collective-permute-start.21) | collective-permute-done | bytes 1568 | tf_op jit(solution)/shard_map/ppermute | solution.py:32
  78.0 3.7 %collective-permute-start.24 = (f32[1,384]{1,0:T(1,128)S(1)}, f32[1,384]{1,0:T(1,128)S(1)}, u32[]{:S(2)}, u32[]{:S(2)}) collective-permute-start(f32[1,384]{1,0:T(1,128)S(1)} %shard_map.133.refs_0_), channel_id=1, source_target_pairs={{0,10},{1,11},{2,8},{3,9},{4,14},{5,15},{6,12},{7,13},{8,2},{9,3},... | collective-permute-start | bytes 4616 | tf_op jit(solution)/shard_map/ppermute | solution.py:32
  81.7 2.9 %collective-permute-done.24.refs_3_ = f32[1,384]{1,0:T(1,128)S(1)} collective-permute-done((f32[1,384]{1,0:T(1,128)S(1)}, f32[1,384]{1,0:T(1,128)S(1)}, u32[]{:S(2)}, u32[]{:S(2)}) %collective-permute-start.24) | collective-permute-done | bytes 1568 | tf_op jit(solution)/shard_map/ppermute | solution.py:32
  85.6 1.9 %collective-permute-start.25 = (f32[1,384]{1,0:T(1,128)S(1)}, f32[1,384]{1,0:T(1,128)S(1)}, u32[]{:S(2)}, u32[]{:S(2)}) collective-permute-start(f32[1,384]{1,0:T(1,128)S(1)} %get-tuple-element.88.refs_0_), channel_id=1, source_target_pairs={{0,16},{1,17},{2,18},{3,19},{4,20},{5,21},{6,22},{7,23},{8,24},{9,... | collective-permute-start | bytes 4616 | tf_op jit(solution)/shard_map/ppermute | solution.py:32
  87.7 1.6 %shard_map.137 = (f32[384,384]{1,0:T(8,128)}, f32[384,384]{1,0:T(8,128)S(1)}) custom-call(f32[384,384]{1,0:T(8,128)S(1)} %get-tuple-element.93.refs_0_, f32[384,384]{1,0:T(8,128)S(1)} %get-tuple-element.94.refs_1_.refs_2_, f32[384,384]{1,0:T(8,128)S(1)} %get-tuple-element.81.refs_4_.refs_2_, f32[384,384]{1,0:T(8,128)S(1)} %get-tuple-element.89.refs_6_.refs_3_), custom_call_target="tpu_custom_call" | custom-call | flops 339738624 | bytes 2359296 | tf_op jit(solution)/shard_map/pallas_call | solution.py:57
  89.5 2.8 %collective-permute-start.28 = (f32[1,384]{1,0:T(1,128)S(1)}, f32[1,384]{1,0:T(1,128)S(1)}, u32[]{:S(2)}, u32[]{:S(2)}) collective-permute-start(f32[1,384]{1,0:T(1,128)S(1)} %shard_map.138), channel_id=1, source_target_pairs={{0,48},{1,49},{2,50},{3,51},{4,52},{5,53},{6,54},{7,55},{8,56},{9,... | collective-permute-start | bytes 4616 | tf_op jit(solution)/shard_map/ppermute | solution.py:32
  93.0 1.4 %collective-permute-done.28.refs_2_ = f32[1,384]{1,0:T(1,128)S(1)} collective-permute-done((f32[1,384]{1,0:T(1,128)S(1)}, f32[1,384]{1,0:T(1,128)S(1)}, u32[]{:S(2)}, u32[]{:S(2)}) %collective-permute-start.28) | collective-permute-done | bytes 1568 | tf_op jit(solution)/shard_map/ppermute | solution.py:32
  94.4 1.5 %shard_map.139 = f32[3,4,32,128]{3,2,1,0:T(8,128)} custom-call(f32[384,384]{1,0:T(8,128)S(1)} %get-tuple-element.101.refs_0_, f32[1,384]{1,0:T(1,128)S(1)} %shard_map.135.refs_1_, f32[1,384]{1,0:T(1,128)S(1)} %collective-permute-done.28.refs_2_, f32[384,384]{1,0:T(8,128)S(1)} %get-tuple-element.95.refs_3_, f32[1,384]{1,0:T(1,128)S(1)} %get-tuple-element.98.refs_4_, ...), custom_call_target="tpu_custom_call" | custom-call | flops 589824 | bytes 1446912 | tf_op jit(solution)/shard_map/pallas_call | solution.py:57
  (78 shorter events, 20.8 us)
Async XLA Ops:
  2.8 2.1 %collective-permute-start.1 = (f32[384,384]{1,0:T(8,128)S(1)}, f32[384,384]{1,0:T(8,128)S(1)}, u32[]{:S(2)}, u32[]{:S(2)}) collective-permute-start(f32[384,384]{1,0:T(8,128)S(1)} %shard_map.114.refs_0_.refs_5_), channel_id=1, source_target_pairs={{0,1},{1,0},{2,3},{3,2},{4,5},{5,4},{6,7},{7,6},{8,9},{9,8},{10,11... | collective-permute-start | bytes 1769480 | tf_op jit(solution)/shard_map/ppermute | solution.py:32
  3.2 2.5 %collective-permute-start.2 = (f32[37,32,128]{2,1,0:T(8,128)S(1)}, f32[37,32,128]{2,1,0:T(8,128)S(1)}, u32[]{:S(2)}, u32[]{:S(2)}) collective-permute-start(f32[37,32,128]{2,1,0:T(8,128)S(1)} %get-tuple-element.55), channel_id=1, source_target_pairs={{0,1},{1,0},{2,3},{3,2},{4,5},{5,4},{6,7},{7,6},{8,9},{9,8},{10,11... | collective-permute-start | bytes 1818632 | tf_op jit(solution)/shard_map/ppermute | solution.py:32
  5.7 9.3 %collective-permute-start.3 = (f32[192,384]{1,0:T(8,128)S(1)}, f32[192,384]{1,0:T(8,128)S(1)}, u32[]{:S(2)}, u32[]{:S(2)}) collective-permute-start(f32[192,384]{1,0:T(8,128)S(1)} %get-tuple-element.56), channel_id=1, source_target_pairs={{0,2},{1,3},{2,0},{3,1},{4,6},{5,7},{6,4},{7,5},{8,10},{9,11},{10,... | collective-permute-start | bytes 884744 | tf_op jit(solution)/shard_map/ppermute | solution.py:32
  7.7 18.7 %collective-permute-start = (f32[37,32,128]{2,1,0:T(8,128)S(1)}, f32[37,32,128]{2,1,0:T(8,128)S(1)}, u32[]{:S(2)}, u32[]{:S(2)}) collective-permute-start(f32[37,32,128]{2,1,0:T(8,128)S(1)} %get-tuple-element.51), channel_id=1, source_target_pairs={{1,2},{2,1},{3,4},{4,3},{5,6},{6,5},{7,8},{8,7},{9,10},{10,9},{11,... | collective-permute-start | bytes 1818632 | tf_op jit(solution)/shard_map/ppermute | solution.py:686
  17.4 37.6 %collective-permute-start.15 = (f32[192,384]{1,0:T(8,128)S(1)}, f32[192,384]{1,0:T(8,128)S(1)}, u32[]{:S(2)}, u32[]{:S(2)}) collective-permute-start(f32[192,384]{1,0:T(8,128)S(1)} %get-tuple-element.57), channel_id=1, source_target_pairs={{0,12},{1,13},{2,14},{3,15},{4,8},{5,9},{6,10},{7,11},{8,4},{9,5},... | collective-permute-start | bytes 884744 | tf_op jit(solution)/shard_map/ppermute | solution.py:32
  23.6 31.6 %collective-permute-start.13 = (f32[192,384]{1,0:T(8,128)S(1)}, f32[192,384]{1,0:T(8,128)S(1)}, u32[]{:S(2)}, u32[]{:S(2)}) collective-permute-start(f32[192,384]{1,0:T(8,128)S(1)} %get-tuple-element.57), channel_id=1, source_target_pairs={{0,10},{1,11},{2,8},{3,9},{4,14},{5,15},{6,12},{7,13},{8,2},{9,3},... | collective-permute-start | bytes 884744 | tf_op jit(solution)/shard_map/ppermute | solution.py:32
  25.4 30.2 %collective-permute-start.11 = (f32[192,384]{1,0:T(8,128)S(1)}, f32[192,384]{1,0:T(8,128)S(1)}, u32[]{:S(2)}, u32[]{:S(2)}) collective-permute-start(f32[192,384]{1,0:T(8,128)S(1)} %get-tuple-element.57), channel_id=1, source_target_pairs={{0,4},{1,5},{2,6},{3,7},{4,0},{5,1},{6,2},{7,3},{8,12},{9,13},{10,... | collective-permute-start | bytes 884744 | tf_op jit(solution)/shard_map/ppermute | solution.py:32
  37.4 3.6 %collective-permute-start.5 = (f32[1,384]{1,0:T(1,128)S(1)}, f32[1,384]{1,0:T(1,128)S(1)}, u32[]{:S(2)}, u32[]{:S(2)}) collective-permute-start(f32[1,384]{1,0:T(1,128)S(1)} %get-tuple-element.60.refs_1_), channel_id=1, source_target_pairs={{0,64},{64,0},{128,192},{192,128},{1,65},{65,1},{129,193},{193,129... | collective-permute-start | bytes 4616 | tf_op jit(solution)/shard_map/ppermute | solution.py:607
  42.5 3.7 %collective-permute-start.7 = (f32[1,384]{1,0:T(1,128)S(1)}, f32[1,384]{1,0:T(1,128)S(1)}, u32[]{:S(2)}, u32[]{:S(2)}) collective-permute-start(f32[1,384]{1,0:T(1,128)S(1)} %shard_map.122.refs_0_), channel_id=1, source_target_pairs={{0,2},{1,3},{2,0},{3,1},{4,6},{5,7},{6,4},{7,5},{8,10},{9,11},{10,... | collective-permute-start | bytes 4616 | tf_op jit(solution)/shard_map/ppermute | solution.py:32
  46.3 6.2 %collective-permute-start.8 = (f32[1,384]{1,0:T(1,128)S(1)}, f32[1,384]{1,0:T(1,128)S(1)}, u32[]{:S(2)}, u32[]{:S(2)}) collective-permute-start(f32[1,384]{1,0:T(1,128)S(1)} %shard_map.123.refs_0_), channel_id=1, source_target_pairs={{0,4},{1,13},{2,6},{3,15},{4,0},{5,9},{6,2},{7,11},{8,12},{9,5},{1... | collective-permute-start | bytes 4616 | tf_op jit(solution)/shard_map/ppermute | solution.py:579
  48.4 6.6 %collective-permute-start.10 = (f32[1,384]{1,0:T(1,128)S(1)}, f32[1,384]{1,0:T(1,128)S(1)}, u32[]{:S(2)}, u32[]{:S(2)}) collective-permute-start(f32[1,384]{1,0:T(1,128)S(1)} %shard_map.123.refs_0_), channel_id=1, source_target_pairs={{0,10},{1,11},{2,8},{3,9},{4,14},{5,15},{6,12},{7,13},{8,2},{9,3},... | collective-permute-start | bytes 4616 | tf_op jit(solution)/shard_map/ppermute | solution.py:32
  52.5 2.5 %collective-permute-start.9 = (f32[1,384]{1,0:T(1,128)S(1)}, f32[1,384]{1,0:T(1,128)S(1)}, u32[]{:S(2)}, u32[]{:S(2)}) collective-permute-start(f32[1,384]{1,0:T(1,128)S(1)} %collective-permute-done.8.refs_1_), channel_id=1, source_target_pairs={{0,1},{1,0},{2,3},{3,2},{4,5},{5,4},{6,7},{7,6},{8,9},{9,8},{10,11... | collective-permute-start | bytes 4616 | tf_op jit(solution)/shard_map/ppermute | solution.py:32
  55.5 1.9 %collective-permute-start.12 = (f32[192,384]{1,0:T(8,128)S(1)}, f32[192,384]{1,0:T(8,128)S(1)}, u32[]{:S(2)}, u32[]{:S(2)}) collective-permute-start(f32[192,384]{1,0:T(8,128)S(1)} %collective-permute-done.11.refs_1_), channel_id=1, source_target_pairs={{0,1},{1,0},{2,3},{3,2},{4,5},{5,4},{6,7},{7,6},{8,9},{9,8},{10,11... | collective-permute-start | bytes 884744 | tf_op jit(solution)/shard_map/ppermute | solution.py:32
  58.1 3.8 %collective-permute-start.17 = (f32[1,384]{1,0:T(1,128)S(1)}, f32[1,384]{1,0:T(1,128)S(1)}, u32[]{:S(2)}, u32[]{:S(2)}) collective-permute-start(f32[1,384]{1,0:T(1,128)S(1)} %get-tuple-element.74.refs_0_), channel_id=1, source_target_pairs={{0,16},{1,17},{2,18},{3,19},{4,20},{5,21},{6,22},{7,23},{8,24},{9,... | collective-permute-start | bytes 4616 | tf_op jit(solution)/shard_map/ppermute | solution.py:32
  62.1 4.9 %collective-permute-start.18 = (f32[1,384]{1,0:T(1,128)S(1)}, f32[1,384]{1,0:T(1,128)S(1)}, u32[]{:S(2)}, u32[]{:S(2)}) collective-permute-start(f32[1,384]{1,0:T(1,128)S(1)} %shard_map.127), channel_id=1, source_target_pairs={{0,48},{1,49},{2,50},{3,51},{4,52},{5,53},{6,54},{7,55},{8,56},{9,... | collective-permute-start | bytes 4616 | tf_op jit(solution)/shard_map/ppermute | solution.py:32
  67.1 3.7 %collective-permute-start.19 = (f32[1,384]{1,0:T(1,128)S(1)}, f32[1,384]{1,0:T(1,128)S(1)}, u32[]{:S(2)}, u32[]{:S(2)}) collective-permute-start(f32[1,384]{1,0:T(1,128)S(1)} %shard_map.129), channel_id=1, source_target_pairs={{0,16},{1,17},{2,18},{3,19},{4,20},{5,21},{6,22},{7,23},{8,24},{9,... | collective-permute-start | bytes 4616 | tf_op jit(solution)/shard_map/ppermute | solution.py:32
  70.8 13.8 %collective-permute-start.26 = (f32[192,384]{1,0:T(8,128)S(1)}, f32[192,384]{1,0:T(8,128)S(1)}, u32[]{:S(2)}, u32[]{:S(2)}) collective-permute-start(f32[192,384]{1,0:T(8,128)S(1)} %get-tuple-element.91), channel_id=1, source_target_pairs={{0,16},{1,17},{2,18},{3,19},{4,20},{5,21},{6,22},{7,23},{8,24},{9,... | collective-permute-start | bytes 884744 | tf_op jit(solution)/shard_map/ppermute | solution.py:32
  73.0 3.7 %collective-permute-start.21 = (f32[1,384]{1,0:T(1,128)S(1)}, f32[1,384]{1,0:T(1,128)S(1)}, u32[]{:S(2)}, u32[]{:S(2)}) collective-permute-start(f32[1,384]{1,0:T(1,128)S(1)} %shard_map.132.refs_0_), channel_id=1, source_target_pairs={{0,2},{1,3},{2,0},{3,1},{4,6},{5,7},{6,4},{7,5},{8,10},{9,11},{10,... | collective-permute-start | bytes 4616 | tf_op jit(solution)/shard_map/ppermute | solution.py:32
  76.9 4.8 %collective-permute-start.22 = (f32[1,384]{1,0:T(1,128)S(1)}, f32[1,384]{1,0:T(1,128)S(1)}, u32[]{:S(2)}, u32[]{:S(2)}) collective-permute-start(f32[1,384]{1,0:T(1,128)S(1)} %shard_map.133.refs_0_), channel_id=1, source_target_pairs={{0,4},{1,13},{2,6},{3,15},{4,0},{5,9},{6,2},{7,11},{8,12},{9,5},{1... | collective-permute-start | bytes 4616 | tf_op jit(solution)/shard_map/ppermute | solution.py:579
  78.0 6.6 %collective-permute-start.24 = (f32[1,384]{1,0:T(1,128)S(1)}, f32[1,384]{1,0:T(1,128)S(1)}, u32[]{:S(2)}, u32[]{:S(2)}) collective-permute-start(f32[1,384]{1,0:T(1,128)S(1)} %shard_map.133.refs_0_), channel_id=1, source_target_pairs={{0,10},{1,11},{2,8},{3,9},{4,14},{5,15},{6,12},{7,13},{8,2},{9,3},... | collective-permute-start | bytes 4616 | tf_op jit(solution)/shard_map/ppermute | solution.py:32
  81.7 2.9 %collective-permute-start.23 = (f32[1,384]{1,0:T(1,128)S(1)}, f32[1,384]{1,0:T(1,128)S(1)}, u32[]{:S(2)}, u32[]{:S(2)}) collective-permute-start(f32[1,384]{1,0:T(1,128)S(1)} %collective-permute-done.22.refs_1_), channel_id=1, source_target_pairs={{0,1},{1,0},{2,3},{3,2},{4,5},{5,4},{6,7},{7,6},{8,9},{9,8},{10,11... | collective-permute-start | bytes 4616 | tf_op jit(solution)/shard_map/ppermute | solution.py:32
  84.6 2.9 %collective-permute-start.27 = (f32[192,384]{1,0:T(8,128)S(1)}, f32[192,384]{1,0:T(8,128)S(1)}, u32[]{:S(2)}, u32[]{:S(2)}) collective-permute-start(f32[192,384]{1,0:T(8,128)S(1)} %collective-permute-done.26.refs_1_), channel_id=1, source_target_pairs={{0,1},{1,0},{2,3},{3,2},{4,5},{5,4},{6,7},{7,6},{8,9},{9,8},{10,11... | collective-permute-start | bytes 884744 | tf_op jit(solution)/shard_map/ppermute | solution.py:32
  85.6 3.7 %collective-permute-start.25 = (f32[1,384]{1,0:T(1,128)S(1)}, f32[1,384]{1,0:T(1,128)S(1)}, u32[]{:S(2)}, u32[]{:S(2)}) collective-permute-start(f32[1,384]{1,0:T(1,128)S(1)} %get-tuple-element.88.refs_0_), channel_id=1, source_target_pairs={{0,16},{1,17},{2,18},{3,19},{4,20},{5,21},{6,22},{7,23},{8,24},{9,... | collective-permute-start | bytes 4616 | tf_op jit(solution)/shard_map/ppermute | solution.py:32
  89.5 4.9 %collective-permute-start.28 = (f32[1,384]{1,0:T(1,128)S(1)}, f32[1,384]{1,0:T(1,128)S(1)}, u32[]{:S(2)}, u32[]{:S(2)}) collective-permute-start(f32[1,384]{1,0:T(1,128)S(1)} %shard_map.138), channel_id=1, source_target_pairs={{0,48},{1,49},{2,50},{3,51},{4,52},{5,53},{6,54},{7,55},{8,56},{9,... | collective-permute-start | bytes 4616 | tf_op jit(solution)/shard_map/ppermute | solution.py:32
  (12 other events, 47.2 us)

commit v11 on v10

--- a/solution.py
+++ b/solution.py
@@ -613,7 +613,7 @@
             bound(level, forward_kernel), flags, [total, others[-1], levels[level][0]], ROW, square
         )
     arrived = row_exchange(total)
-    blocks = sorted_blocks(flags, fetched, (arrived[1], arrived[2]))
+    blocks = sorted_blocks(flags, fetched, (arrived[0], arrived[2]))
     total, in_row = local_call(
         row_forward_kernel, flags, [total, *arrived, blocks], (ROW, ROW), 3 * square
     )

time: 96 us -> 95.7 us (level)
  Pallas kernels: 25.6 us -> 19.1 us
  starting transfers between devices: 34.2 us -> 39.9 us
    ppermute x1, starting transfers between devices: 0.53 us -> 7.1 us  [coupled_velocity(): partner = lax.ppermute(picked, 'sub', [(i, i ^ 1) for i in range(count)])]
    pallas_call x1, Pallas kernels: 11 us -> 4.39 us  [substeps_call(): pl.pallas_call(substep_kernel, out_shape=(jax.ShapeDtypeStruct(grid_shape...]
    ppermute x1, waiting for transfers between devices: 2.95 us -> 1.46 us  [coupled_velocity(): partner = lax.ppermute(picked, 'sub', [(i, i ^ 1) for i in range(count)])]
    ppermute x25, waiting for transfers between devices: 28.8 us -> 30 us  [swap(): lax.ppermute(value, 'tile', [(i, i ^ mask) for i in range(lax.axis_size('...]
  transfers between devices with their start and end apart: 29 -> 29, of which waited for: 18 -> 19; matrix products, arithmetic and copies ran while one was open for 0% -> 0% of each run, Pallas kernels for 23% -> 17%
where the time goes in v11:
time: 95.7 us; the launch traced here: 95.1 us
  starting transfers between devices  39.9 us (42%)
  waiting for transfers between devices  32.8 us (34%)
  Pallas kernels  19.1 us (20%)
  local copies, waits for them, and re-layouts  1.67 us (2%)
  between operations  1.64 us (2%)
    ppermute x25, waiting for transfers between devices, swap(): lax.ppermute(value, 'tile', [(i, i ^ mask) for i in range(lax.axis_size('...  30 us
    ppermute x25, starting transfers between devices, swap(): lax.ppermute(value, 'tile', [(i, i ^ mask) for i in range(lax.axis_size('...  29.3 us
    pallas_call x26, Pallas kernels, local_call(): pl.pallas_call(placed, out_shape=outs, in_specs=[VM] * len(operands), out...  14.7 us
    ppermute x1, starting transfers between devices, coupled_velocity(): partner = lax.ppermute(picked, 'sub', [(i, i ^ 1) for i in range(count)])  7.1 us
    pallas_call x1, Pallas kernels, substeps_call(): pl.pallas_call(substep_kernel, out_shape=(jax.ShapeDtypeStruct(grid_shape...  4.39 us
    ppermute x2, starting transfers between devices, split_swap(): lax.ppermute(value, 'tile', [(i, i ^ mask) for i, mask in enumerate(masks)])  2.81 us
  transfers between devices with their start and end apart: 29, of which 19 were waited for; matrix products, arithmetic and copies ran while one was open for 0% of the time, Pallas kernels for 17%

profile of v11, /device:TPU:2, one launch (start us, length us, event | category | flops | bytes accessed | tf_op | source)
XLA Modules:
  0.0 95.1 jit_solution(5938191912794654506)
XLA Ops:
  5.7 1.9 %collective-permute-start.3 = (f32[192,384]{1,0:T(8,128)S(1)}, f32[192,384]{1,0:T(8,128)S(1)}, u32[]{:S(2)}, u32[]{:S(2)}) collective-permute-start(f32[192,384]{1,0:T(8,128)S(1)} %get-tuple-element.56), channel_id=1, source_target_pairs={{0,2},{1,3},{2,0},{3,1},{4,6},{5,7},{6,4},{7,5},{8,10},{9,11},{10,... | collective-permute-start | bytes 884744 | tf_op jit(solution)/shard_map/ppermute | solution.py:32
  8.4 6.7 %collective-permute-done.3.refs_1_ = f32[192,384]{1,0:T(8,128)S(1)} collective-permute-done((f32[192,384]{1,0:T(8,128)S(1)}, f32[192,384]{1,0:T(8,128)S(1)}, u32[]{:S(2)}, u32[]{:S(2)}) %collective-permute-start.3) | collective-permute-done | bytes 294944 | tf_op jit(solution)/shard_map/ppermute | solution.py:32
  17.4 6.2 %collective-permute-start.15 = (f32[192,384]{1,0:T(8,128)S(1)}, f32[192,384]{1,0:T(8,128)S(1)}, u32[]{:S(2)}, u32[]{:S(2)}) collective-permute-start(f32[192,384]{1,0:T(8,128)S(1)} %get-tuple-element.57), channel_id=1, source_target_pairs={{0,12},{1,13},{2,14},{3,15},{4,8},{5,9},{6,10},{7,11},{8,4},{9,5},... | collective-permute-start | bytes 884744 | tf_op jit(solution)/shard_map/ppermute | solution.py:32
  23.6 1.8 %collective-permute-start.13 = (f32[192,384]{1,0:T(8,128)S(1)}, f32[192,384]{1,0:T(8,128)S(1)}, u32[]{:S(2)}, u32[]{:S(2)}) collective-permute-start(f32[192,384]{1,0:T(8,128)S(1)} %get-tuple-element.57), channel_id=1, source_target_pairs={{0,10},{1,11},{2,8},{3,9},{4,14},{5,15},{6,12},{7,13},{8,2},{9,3},... | collective-permute-start | bytes 884744 | tf_op jit(solution)/shard_map/ppermute | solution.py:32
  26.5 4.4 %shard_map.118 = (f32[3,4,32,128]{3,2,1,0:T(8,128)}, f32[3,4,32,128]{3,2,1,0:T(8,128)S(1)}, f32[1,384]{1,0:T(1,128)S(1)}) custom-call(f32[2,128]{1,0:T(2,128)S(1)} %broadcast_in_dim.14.steps, f32[3,4,32,128]{3,2,1,0:T(8,128)S(1)} %bitcast.19, f32[3,4,32,128]{3,2,1,0:T(8,128)S(1)} %bitcast.21, f32[3,4,32,128]{3,2,1,0:T(8,128)S(1)} %bitcast.23, ...), custom_call_target="tpu_custom_call" | custom-call | flops 3623878656 | bytes 2162688 | tf_op jit(solution)/shard_map/pallas_call | solution.py:300
  30.8 7.1 %collective-permute-start.5 = (f32[1,384]{1,0:T(1,128)S(1)}, f32[1,384]{1,0:T(1,128)S(1)}, u32[]{:S(2)}, u32[]{:S(2)}) collective-permute-start(f32[1,384]{1,0:T(1,128)S(1)} %get-tuple-element.60.refs_1_), channel_id=1, source_target_pairs={{0,64},{64,0},{128,192},{192,128},{1,65},{65,1},{129,193},{193,129... | collective-permute-start | bytes 4616 | tf_op jit(solution)/shard_map/ppermute | solution.py:607
  38.0 1.5 %collective-permute-done.5.refs_2_ = f32[1,384]{1,0:T(1,128)S(1)} collective-permute-done((f32[1,384]{1,0:T(1,128)S(1)}, f32[1,384]{1,0:T(1,128)S(1)}, u32[]{:S(2)}, u32[]{:S(2)}) %collective-permute-start.5) | collective-permute-done | bytes 1568 | tf_op jit(solution)/shard_map/ppermute | solution.py:607
  41.6 3.2 %collective-permute-done.7.refs_1_ = f32[1,384]{1,0:T(1,128)S(1)} collective-permute-done((f32[1,384]{1,0:T(1,128)S(1)}, f32[1,384]{1,0:T(1,128)S(1)}, u32[]{:S(2)}, u32[]{:S(2)}) %collective-permute-start.7) | collective-permute-done | bytes 1568 | tf_op jit(solution)/shard_map/ppermute | solution.py:32
  44.9 3.8 %collective-permute-start.10 = (f32[1,384]{1,0:T(1,128)S(1)}, f32[1,384]{1,0:T(1,128)S(1)}, u32[]{:S(2)}, u32[]{:S(2)}) collective-permute-start(f32[1,384]{1,0:T(1,128)S(1)} %shard_map.123.refs_0_), channel_id=1, source_target_pairs={{0,10},{1,11},{2,8},{3,9},{4,14},{5,15},{6,12},{7,13},{8,2},{9,3},... | collective-permute-start | bytes 4616 | tf_op jit(solution)/shard_map/ppermute | solution.py:32
  48.7 1.5 %collective-permute-start.8 = (f32[1,384]{1,0:T(1,128)S(1)}, f32[1,384]{1,0:T(1,128)S(1)}, u32[]{:S(2)}, u32[]{:S(2)}) collective-permute-start(f32[1,384]{1,0:T(1,128)S(1)} %shard_map.123.refs_0_), channel_id=1, source_target_pairs={{0,4},{1,13},{2,6},{3,15},{4,0},{5,9},{6,2},{7,11},{8,12},{9,5},{1... | collective-permute-start | bytes 4616 | tf_op jit(solution)/shard_map/ppermute | solution.py:579
  50.2 4.2 %collective-permute-done.10.refs_3_ = f32[1,384]{1,0:T(1,128)S(1)} collective-permute-done((f32[1,384]{1,0:T(1,128)S(1)}, f32[1,384]{1,0:T(1,128)S(1)}, u32[]{:S(2)}, u32[]{:S(2)}) %collective-permute-start.10) | collective-permute-done | bytes 1568 | tf_op jit(solution)/shard_map/ppermute | solution.py:32
  57.6 1.7 %collective-permute-start.17 = (f32[1,384]{1,0:T(1,128)S(1)}, f32[1,384]{1,0:T(1,128)S(1)}, u32[]{:S(2)}, u32[]{:S(2)}) collective-permute-start(f32[1,384]{1,0:T(1,128)S(1)} %get-tuple-element.74.refs_0_), channel_id=1, source_target_pairs={{0,16},{1,17},{2,18},{3,19},{4,20},{5,21},{6,22},{7,23},{8,24},{9,... | collective-permute-start | bytes 4616 | tf_op jit(solution)/shard_map/ppermute | solution.py:32
  59.2 2.1 %shard_map.126 = (f32[384,384]{1,0:T(8,128)S(1)}, f32[384,384]{1,0:T(8,128)S(1)}, f32[384,384]{1,0:T(8,128)S(1)}, f32[192,384]{1,0:T(8,128)S(1)}) custom-call(f32[4,384,384]{2,1,0:T(8,128)S(1)} %shard_map.124.refs_4_.refs_0_), custom_call_target="tpu_custom_call" | custom-call | flops 1019215872 | bytes 2359296 | tf_op jit(solution)/shard_map/pallas_call | solution.py:57
  61.5 3.0 %collective-permute-start.18 = (f32[1,384]{1,0:T(1,128)S(1)}, f32[1,384]{1,0:T(1,128)S(1)}, u32[]{:S(2)}, u32[]{:S(2)}) collective-permute-start(f32[1,384]{1,0:T(1,128)S(1)} %shard_map.127), channel_id=1, source_target_pairs={{0,48},{1,49},{2,50},{3,51},{4,52},{5,53},{6,54},{7,55},{8,56},{9,... | collective-permute-start | bytes 4616 | tf_op jit(solution)/shard_map/ppermute | solution.py:32
  64.5 1.7 %shard_map.128 = (f32[384,384]{1,0:T(8,128)S(1)}, f32[384,384]{1,0:T(8,128)S(1)}) custom-call(f32[4,384,384]{2,1,0:T(8,128)S(1)} %shard_map.124.refs_4_.refs_0_, f32[384,384]{1,0:T(8,128)S(1)} %get-tuple-element.78.refs_1_, f32[384,384]{1,0:T(8,128)S(1)} %get-tuple-element.79.refs_2_, f32[384,384]{1,0:T(8,128)S(1)} %get-tuple-element.65.refs_3_.refs_4_, ...), custom_call_target="tpu_custom_call" | custom-call | flops 679477248 | bytes 4718592 | tf_op jit(solution)/shard_map/pallas_call | solution.py:57
  67.0 3.2 %collective-permute-done.19.refs_3_ = f32[1,384]{1,0:T(1,128)S(1)} collective-permute-done((f32[1,384]{1,0:T(1,128)S(1)}, f32[1,384]{1,0:T(1,128)S(1)}, u32[]{:S(2)}, u32[]{:S(2)}) %collective-permute-start.19) | collective-permute-done | bytes 1568 | tf_op jit(solution)/shard_map/ppermute | solution.py:32
  73.0 3.1 %collective-permute-done.21.refs_1_ = f32[1,384]{1,0:T(1,128)S(1)} collective-permute-done((f32[1,384]{1,0:T(1,128)S(1)}, f32[1,384]{1,0:T(1,128)S(1)}, u32[]{:S(2)}, u32[]{:S(2)}) %collective-permute-start.21) | collective-permute-done | bytes 1568 | tf_op jit(solution)/shard_map/ppermute | solution.py:32
  77.6 1.9 %collective-permute-start.24 = (f32[1,384]{1,0:T(1,128)S(1)}, f32[1,384]{1,0:T(1,128)S(1)}, u32[]{:S(2)}, u32[]{:S(2)}) collective-permute-start(f32[1,384]{1,0:T(1,128)S(1)} %shard_map.133.refs_0_), channel_id=1, source_target_pairs={{0,10},{1,11},{2,8},{3,9},{4,14},{5,15},{6,12},{7,13},{8,2},{9,3},... | collective-permute-start | bytes 4616 | tf_op jit(solution)/shard_map/ppermute | solution.py:32
  79.5 1.4 %collective-permute-done.22.refs_1_ = f32[1,384]{1,0:T(1,128)S(1)} collective-permute-done((f32[1,384]{1,0:T(1,128)S(1)}, f32[1,384]{1,0:T(1,128)S(1)}, u32[]{:S(2)}, u32[]{:S(2)}) %collective-permute-start.22) | collective-permute-done | bytes 1568 | tf_op jit(solution)/shard_map/ppermute | solution.py:579
  80.9 3.3 %collective-permute-done.24.refs_3_ = f32[1,384]{1,0:T(1,128)S(1)} collective-permute-done((f32[1,384]{1,0:T(1,128)S(1)}, f32[1,384]{1,0:T(1,128)S(1)}, u32[]{:S(2)}, u32[]{:S(2)}) %collective-permute-start.24) | collective-permute-done | bytes 1568 | tf_op jit(solution)/shard_map/ppermute | solution.py:32
  84.9 1.9 %collective-permute-start.25 = (f32[1,384]{1,0:T(1,128)S(1)}, f32[1,384]{1,0:T(1,128)S(1)}, u32[]{:S(2)}, u32[]{:S(2)}) collective-permute-start(f32[1,384]{1,0:T(1,128)S(1)} %get-tuple-element.88.refs_0_), channel_id=1, source_target_pairs={{0,16},{1,17},{2,18},{3,19},{4,20},{5,21},{6,22},{7,23},{8,24},{9,... | collective-permute-start | bytes 4616 | tf_op jit(solution)/shard_map/ppermute | solution.py:32
  86.9 1.6 %shard_map.137 = (f32[384,384]{1,0:T(8,128)}, f32[384,384]{1,0:T(8,128)S(1)}) custom-call(f32[384,384]{1,0:T(8,128)S(1)} %get-tuple-element.93.refs_0_, f32[384,384]{1,0:T(8,128)S(1)} %get-tuple-element.94.refs_1_.refs_2_, f32[384,384]{1,0:T(8,128)S(1)} %get-tuple-element.81.refs_4_.refs_2_, f32[384,384]{1,0:T(8,128)S(1)} %get-tuple-element.89.refs_6_.refs_3_), custom_call_target="tpu_custom_call" | custom-call | flops 339738624 | bytes 2359296 | tf_op jit(solution)/shard_map/pallas_call | solution.py:57
  88.8 2.9 %collective-permute-start.28 = (f32[1,384]{1,0:T(1,128)S(1)}, f32[1,384]{1,0:T(1,128)S(1)}, u32[]{:S(2)}, u32[]{:S(2)}) collective-permute-start(f32[1,384]{1,0:T(1,128)S(1)} %shard_map.138), channel_id=1, source_target_pairs={{0,48},{1,49},{2,50},{3,51},{4,52},{5,53},{6,54},{7,55},{8,56},{9,... | collective-permute-start | bytes 4616 | tf_op jit(solution)/shard_map/ppermute | solution.py:32
  93.7 1.5 %shard_map.139 = f32[3,4,32,128]{3,2,1,0:T(8,128)} custom-call(f32[384,384]{1,0:T(8,128)S(1)} %get-tuple-element.101.refs_0_, f32[1,384]{1,0:T(1,128)S(1)} %shard_map.135.refs_1_, f32[1,384]{1,0:T(1,128)S(1)} %collective-permute-done.28.refs_2_, f32[384,384]{1,0:T(8,128)S(1)} %get-tuple-element.95.refs_3_, f32[1,384]{1,0:T(1,128)S(1)} %get-tuple-element.98.refs_4_, ...), custom_call_target="tpu_custom_call" | custom-call | flops 589824 | bytes 1446912 | tf_op jit(solution)/shard_map/pallas_call | solution.py:57
  (78 shorter events, 22.2 us)
Async XLA Ops:
  2.8 2.1 %collective-permute-start.1 = (f32[384,384]{1,0:T(8,128)S(1)}, f32[384,384]{1,0:T(8,128)S(1)}, u32[]{:S(2)}, u32[]{:S(2)}) collective-permute-start(f32[384,384]{1,0:T(8,128)S(1)} %shard_map.114.refs_0_.refs_5_), channel_id=1, source_target_pairs={{0,1},{1,0},{2,3},{3,2},{4,5},{5,4},{6,7},{7,6},{8,9},{9,8},{10,11... | collective-permute-start | bytes 1769480 | tf_op jit(solution)/shard_map/ppermute | solution.py:32
  3.2 2.5 %collective-permute-start.2 = (f32[37,32,128]{2,1,0:T(8,128)S(1)}, f32[37,32,128]{2,1,0:T(8,128)S(1)}, u32[]{:S(2)}, u32[]{:S(2)}) collective-permute-start(f32[37,32,128]{2,1,0:T(8,128)S(1)} %get-tuple-element.55), channel_id=1, source_target_pairs={{0,1},{1,0},{2,3},{3,2},{4,5},{5,4},{6,7},{7,6},{8,9},{9,8},{10,11... | collective-permute-start | bytes 1818632 | tf_op jit(solution)/shard_map/ppermute | solution.py:32
  5.7 9.3 %collective-permute-start.3 = (f32[192,384]{1,0:T(8,128)S(1)}, f32[192,384]{1,0:T(8,128)S(1)}, u32[]{:S(2)}, u32[]{:S(2)}) collective-permute-start(f32[192,384]{1,0:T(8,128)S(1)} %get-tuple-element.56), channel_id=1, source_target_pairs={{0,2},{1,3},{2,0},{3,1},{4,6},{5,7},{6,4},{7,5},{8,10},{9,11},{10,... | collective-permute-start | bytes 884744 | tf_op jit(solution)/shard_map/ppermute | solution.py:32
  7.7 18.7 %collective-permute-start = (f32[37,32,128]{2,1,0:T(8,128)S(1)}, f32[37,32,128]{2,1,0:T(8,128)S(1)}, u32[]{:S(2)}, u32[]{:S(2)}) collective-permute-start(f32[37,32,128]{2,1,0:T(8,128)S(1)} %get-tuple-element.51), channel_id=1, source_target_pairs={{1,2},{2,1},{3,4},{4,3},{5,6},{6,5},{7,8},{8,7},{9,10},{10,9},{11,... | collective-permute-start | bytes 1818632 | tf_op jit(solution)/shard_map/ppermute | solution.py:686
  17.4 37.0 %collective-permute-start.15 = (f32[192,384]{1,0:T(8,128)S(1)}, f32[192,384]{1,0:T(8,128)S(1)}, u32[]{:S(2)}, u32[]{:S(2)}) collective-permute-start(f32[192,384]{1,0:T(8,128)S(1)} %get-tuple-element.57), channel_id=1, source_target_pairs={{0,12},{1,13},{2,14},{3,15},{4,8},{5,9},{6,10},{7,11},{8,4},{9,5},... | collective-permute-start | bytes 884744 | tf_op jit(solution)/shard_map/ppermute | solution.py:32
  23.6 30.9 %collective-permute-start.13 = (f32[192,384]{1,0:T(8,128)S(1)}, f32[192,384]{1,0:T(8,128)S(1)}, u32[]{:S(2)}, u32[]{:S(2)}) collective-permute-start(f32[192,384]{1,0:T(8,128)S(1)} %get-tuple-element.57), channel_id=1, source_target_pairs={{0,10},{1,11},{2,8},{3,9},{4,14},{5,15},{6,12},{7,13},{8,2},{9,3},... | collective-permute-start | bytes 884744 | tf_op jit(solution)/shard_map/ppermute | solution.py:32
  25.4 29.6 %collective-permute-start.11 = (f32[192,384]{1,0:T(8,128)S(1)}, f32[192,384]{1,0:T(8,128)S(1)}, u32[]{:S(2)}, u32[]{:S(2)}) collective-permute-start(f32[192,384]{1,0:T(8,128)S(1)} %get-tuple-element.57), channel_id=1, source_target_pairs={{0,4},{1,5},{2,6},{3,7},{4,0},{5,1},{6,2},{7,3},{8,12},{9,13},{10,... | collective-permute-start | bytes 884744 | tf_op jit(solution)/shard_map/ppermute | solution.py:32
  30.8 8.7 %collective-permute-start.5 = (f32[1,384]{1,0:T(1,128)S(1)}, f32[1,384]{1,0:T(1,128)S(1)}, u32[]{:S(2)}, u32[]{:S(2)}) collective-permute-start(f32[1,384]{1,0:T(1,128)S(1)} %get-tuple-element.60.refs_1_), channel_id=1, source_target_pairs={{0,64},{64,0},{128,192},{192,128},{1,65},{65,1},{129,193},{193,129... | collective-permute-start | bytes 4616 | tf_op jit(solution)/shard_map/ppermute | solution.py:607
  41.0 3.7 %collective-permute-start.7 = (f32[1,384]{1,0:T(1,128)S(1)}, f32[1,384]{1,0:T(1,128)S(1)}, u32[]{:S(2)}, u32[]{:S(2)}) collective-permute-start(f32[1,384]{1,0:T(1,128)S(1)} %shard_map.122.refs_0_), channel_id=1, source_target_pairs={{0,2},{1,3},{2,0},{3,1},{4,6},{5,7},{6,4},{7,5},{8,10},{9,11},{10,... | collective-permute-start | bytes 4616 | tf_op jit(solution)/shard_map/ppermute | solution.py:32
  44.9 9.5 %collective-permute-start.10 = (f32[1,384]{1,0:T(1,128)S(1)}, f32[1,384]{1,0:T(1,128)S(1)}, u32[]{:S(2)}, u32[]{:S(2)}) collective-permute-start(f32[1,384]{1,0:T(1,128)S(1)} %shard_map.123.refs_0_), channel_id=1, source_target_pairs={{0,10},{1,11},{2,8},{3,9},{4,14},{5,15},{6,12},{7,13},{8,2},{9,3},... | collective-permute-start | bytes 4616 | tf_op jit(solution)/shard_map/ppermute | solution.py:32
  48.7 5.7 %collective-permute-start.8 = (f32[1,384]{1,0:T(1,128)S(1)}, f32[1,384]{1,0:T(1,128)S(1)}, u32[]{:S(2)}, u32[]{:S(2)}) collective-permute-start(f32[1,384]{1,0:T(1,128)S(1)} %shard_map.123.refs_0_), channel_id=1, source_target_pairs={{0,4},{1,13},{2,6},{3,15},{4,0},{5,9},{6,2},{7,11},{8,12},{9,5},{1... | collective-permute-start | bytes 4616 | tf_op jit(solution)/shard_map/ppermute | solution.py:579
  54.4 2.0 %collective-permute-start.14 = (f32[192,384]{1,0:T(8,128)S(1)}, f32[192,384]{1,0:T(8,128)S(1)}, u32[]{:S(2)}, u32[]{:S(2)}) collective-permute-start(f32[192,384]{1,0:T(8,128)S(1)} %collective-permute-done.13.refs_3_), channel_id=1, source_target_pairs={{0,1},{1,0},{2,3},{3,2},{4,5},{5,4},{6,7},{7,6},{8,9},{9,8},{10,11... | collective-permute-start | bytes 884744 | tf_op jit(solution)/shard_map/ppermute | solution.py:32
  55.0 2.1 %collective-permute-start.9 = (f32[1,384]{1,0:T(1,128)S(1)}, f32[1,384]{1,0:T(1,128)S(1)}, u32[]{:S(2)}, u32[]{:S(2)}) collective-permute-start(f32[1,384]{1,0:T(1,128)S(1)} %collective-permute-done.8.refs_1_), channel_id=1, source_target_pairs={{0,1},{1,0},{2,3},{3,2},{4,5},{5,4},{6,7},{7,6},{8,9},{9,8},{10,11... | collective-permute-start | bytes 4616 | tf_op jit(solution)/shard_map/ppermute | solution.py:32
  57.6 3.8 %collective-permute-start.17 = (f32[1,384]{1,0:T(1,128)S(1)}, f32[1,384]{1,0:T(1,128)S(1)}, u32[]{:S(2)}, u32[]{:S(2)}) collective-permute-start(f32[1,384]{1,0:T(1,128)S(1)} %get-tuple-element.74.refs_0_), channel_id=1, source_target_pairs={{0,16},{1,17},{2,18},{3,19},{4,20},{5,21},{6,22},{7,23},{8,24},{9,... | collective-permute-start | bytes 4616 | tf_op jit(solution)/shard_map/ppermute | solution.py:32
  61.5 4.9 %collective-permute-start.18 = (f32[1,384]{1,0:T(1,128)S(1)}, f32[1,384]{1,0:T(1,128)S(1)}, u32[]{:S(2)}, u32[]{:S(2)}) collective-permute-start(f32[1,384]{1,0:T(1,128)S(1)} %shard_map.127), channel_id=1, source_target_pairs={{0,48},{1,49},{2,50},{3,51},{4,52},{5,53},{6,54},{7,55},{8,56},{9,... | collective-permute-start | bytes 4616 | tf_op jit(solution)/shard_map/ppermute | solution.py:32
  66.5 3.7 %collective-permute-start.19 = (f32[1,384]{1,0:T(1,128)S(1)}, f32[1,384]{1,0:T(1,128)S(1)}, u32[]{:S(2)}, u32[]{:S(2)}) collective-permute-start(f32[1,384]{1,0:T(1,128)S(1)} %shard_map.129), channel_id=1, source_target_pairs={{0,16},{1,17},{2,18},{3,19},{4,20},{5,21},{6,22},{7,23},{8,24},{9,... | collective-permute-start | bytes 4616 | tf_op jit(solution)/shard_map/ppermute | solution.py:32
  70.2 14.0 %collective-permute-start.26 = (f32[192,384]{1,0:T(8,128)S(1)}, f32[192,384]{1,0:T(8,128)S(1)}, u32[]{:S(2)}, u32[]{:S(2)}) collective-permute-start(f32[192,384]{1,0:T(8,128)S(1)} %get-tuple-element.91), channel_id=1, source_target_pairs={{0,16},{1,17},{2,18},{3,19},{4,20},{5,21},{6,22},{7,23},{8,24},{9,... | collective-permute-start | bytes 884744 | tf_op jit(solution)/shard_map/ppermute | solution.py:32
  72.4 3.7 %collective-permute-start.21 = (f32[1,384]{1,0:T(1,128)S(1)}, f32[1,384]{1,0:T(1,128)S(1)}, u32[]{:S(2)}, u32[]{:S(2)}) collective-permute-start(f32[1,384]{1,0:T(1,128)S(1)} %shard_map.132.refs_0_), channel_id=1, source_target_pairs={{0,2},{1,3},{2,0},{3,1},{4,6},{5,7},{6,4},{7,5},{8,10},{9,11},{10,... | collective-permute-start | bytes 4616 | tf_op jit(solution)/shard_map/ppermute | solution.py:32
  76.3 4.6 %collective-permute-start.22 = (f32[1,384]{1,0:T(1,128)S(1)}, f32[1,384]{1,0:T(1,128)S(1)}, u32[]{:S(2)}, u32[]{:S(2)}) collective-permute-start(f32[1,384]{1,0:T(1,128)S(1)} %shard_map.133.refs_0_), channel_id=1, source_target_pairs={{0,4},{1,13},{2,6},{3,15},{4,0},{5,9},{6,2},{7,11},{8,12},{9,5},{1... | collective-permute-start | bytes 4616 | tf_op jit(solution)/shard_map/ppermute | solution.py:579
  77.6 6.6 %collective-permute-start.24 = (f32[1,384]{1,0:T(1,128)S(1)}, f32[1,384]{1,0:T(1,128)S(1)}, u32[]{:S(2)}, u32[]{:S(2)}) collective-permute-start(f32[1,384]{1,0:T(1,128)S(1)} %shard_map.133.refs_0_), channel_id=1, source_target_pairs={{0,10},{1,11},{2,8},{3,9},{4,14},{5,15},{6,12},{7,13},{8,2},{9,3},... | collective-permute-start | bytes 4616 | tf_op jit(solution)/shard_map/ppermute | solution.py:32
  80.9 3.3 %collective-permute-start.23 = (f32[1,384]{1,0:T(1,128)S(1)}, f32[1,384]{1,0:T(1,128)S(1)}, u32[]{:S(2)}, u32[]{:S(2)}) collective-permute-start(f32[1,384]{1,0:T(1,128)S(1)} %collective-permute-done.22.refs_1_), channel_id=1, source_target_pairs={{0,1},{1,0},{2,3},{3,2},{4,5},{5,4},{6,7},{7,6},{8,9},{9,8},{10,11... | collective-permute-start | bytes 4616 | tf_op jit(solution)/shard_map/ppermute | solution.py:32
  84.2 2.6 %collective-permute-start.27 = (f32[192,384]{1,0:T(8,128)S(1)}, f32[192,384]{1,0:T(8,128)S(1)}, u32[]{:S(2)}, u32[]{:S(2)}) collective-permute-start(f32[192,384]{1,0:T(8,128)S(1)} %collective-permute-done.26.refs_1_), channel_id=1, source_target_pairs={{0,1},{1,0},{2,3},{3,2},{4,5},{5,4},{6,7},{7,6},{8,9},{9,8},{10,11... | collective-permute-start | bytes 884744 | tf_op jit(solution)/shard_map/ppermute | solution.py:32
  84.9 3.7 %collective-permute-start.25 = (f32[1,384]{1,0:T(1,128)S(1)}, f32[1,384]{1,0:T(1,128)S(1)}, u32[]{:S(2)}, u32[]{:S(2)}) collective-permute-start(f32[1,384]{1,0:T(1,128)S(1)} %get-tuple-element.88.refs_0_), channel_id=1, source_target_pairs={{0,16},{1,17},{2,18},{3,19},{4,20},{5,21},{6,22},{7,23},{8,24},{9,... | collective-permute-start | bytes 4616 | tf_op jit(solution)/shard_map/ppermute | solution.py:32
  88.8 4.9 %collective-permute-start.28 = (f32[1,384]{1,0:T(1,128)S(1)}, f32[1,384]{1,0:T(1,128)S(1)}, u32[]{:S(2)}, u32[]{:S(2)}) collective-permute-start(f32[1,384]{1,0:T(1,128)S(1)} %shard_map.138), channel_id=1, source_target_pairs={{0,48},{1,49},{2,50},{3,51},{4,52},{5,53},{6,54},{7,55},{8,56},{9,... | collective-permute-start | bytes 4616 | tf_op jit(solution)/shard_map/ppermute | solution.py:32
  (12 other events, 47.2 us)
